TPU v7x, 32 devices: a whole 2x2x4 slice. The times are simulated.
32 devices in a mesh: group: 2 (over y), train: 16 (over z, x, core), layer: 1.
Axes of the slice: x: 2, y: 2, z: 4, core: 2. Of those that a mesh axis runs over, the one named last changes fastest.
Arguments:
- train_grads: bfloat16 [16384, 2, 4096], P(('group', 'train'), 'layer'), parts along dimension 0, may hold values from -6 to 6
- query_grads: bfloat16 [256, 2, 4096], P('train', 'layer'), may hold values from -0.0625 to 0.0625
- basis_in: float32 [2, 64, 64], P('layer'), may hold values from -0.75 to 0.75
- basis_out: float32 [2, 64, 64], P('layer'), may hold values from -0.75 to 0.75
- eigvals: float32 [2, 4096], P('layer'), may hold values from 0.2 to 5
Outputs:
- scores: float32 [16384, 256], P(('group', 'train'), 'layer'), parts along dimension 0
There are 2 independent parts, one for each index of `group`. A program takes and returns all parts, laid end to end along the dimension named above; an argument that names none is the same for every part. Nothing has to cross between parts.
All inputs are finite; a program needn't handle non-finite values.
Results may differ from a plain program's by a relative error of at most 0.0029.
Values may be sent and summed in bfloat16 or wider, within the bound.
No kernel may reach another device: no remote copies, remote signals or barrier semaphores. Data moves between devices by JAX's collectives and lax.ppermute only.
A program may use at most 128 MiB of HBM per device.

v0:
```python
import jax
import jax.numpy as jnp
from jax import lax
from jax.sharding import PartitionSpec as P


def per_device(train_grads, query_grads, basis_in, basis_out, eigvals):
    tr_rows = train_grads.shape[0]
    layers_here = train_grads.shape[1]
    q_rows = query_grads.shape[0]
    p_in = basis_in.shape[1]
    p_out = basis_out.shape[1]
    highest = lax.Precision.HIGHEST
    grads = query_grads.astype(jnp.float32).reshape(q_rows, layers_here, p_in, p_out)
    rotated = jnp.einsum("lai,qlab,lbj->qlij", basis_in, grads, basis_out, precision=highest)
    damping = 0.1 * jnp.mean(eigvals, axis=1)
    scaled = rotated / (eigvals.reshape(layers_here, p_in, p_out) + damping[:, None, None])
    back = jnp.einsum("lia,qlab,ljb->qlij", basis_in, scaled, basis_out, precision=highest)
    precond = back.reshape(q_rows, layers_here * p_in * p_out).astype(jnp.bfloat16)
    flat_train = train_grads.reshape(tr_rows, layers_here * p_in * p_out)
    contract = (((1,), (1,)), ((), ()))
    gathered = lax.all_gather(precond, "train", axis=0, tiled=True)
    partial_scores = lax.dot_general(
        flat_train, gathered, contract, preferred_element_type=jnp.float32
    )
    return lax.psum_scatter(partial_scores, "layer", scatter_dimension=1, tiled=True)


def solution(mesh):
    return jax.shard_map(
        per_device,
        mesh=mesh,
        in_specs=(
            P(("group", "train"), "layer", None),
            P("train", "layer", None),
            P("layer", None, None),
            P("layer", None, None),
            P("layer", None),
        ),
        out_specs=P(("group", "train"), "layer"),
        check_vma=False,
    )
```

profile of v0, /device:TPU:0, one launch (start us, length us, event | category | flops | bytes accessed | tf_op | source)
XLA Modules:
  0.0 84.7 jit_solution(7097296668970545403)
XLA Ops:
  6.5 0.0 copy-start
  6.5 0.0 copy-start.1
  6.5 0.0 all-gather.2.cloned.1.call-start
  6.5 0.9 %reshape.20 = f32[2,64,64]{2,1,0:T(8,128)S(1)} reshape(f32[2,4096]{1,0:T(2,128)} %param.9) | data formatting | bytes 65536 | tf_op jit(solution)/shard_map/reshape | solution.py:17
  7.4 0.9 %reduce_sum.9 = f32[2]{0:T(128)S(1)} reduce(f32[2,4096]{1,0:T(2,128)} %param.9, f32[]{:T(128)} %constant.2.clone.1), dimensions={1}, to_apply=%region_0.0 | reduce | flops 8190 | bytes 32780 | tf_op jit(solution)/shard_map/reduce_sum | solution.py:16
  8.4 1.3 %reshape.19 = bf16[16,2,64,64]{3,2,1,0:T(8,128)(2,1)S(1)} reshape(bf16[16,2,4096]{2,1,0:T(2,128)(2,1)} %param.6) | data formatting | bytes 524288 | tf_op jit(solution)/shard_map/reshape | solution.py:14
  9.7 0.1 broadcast_add_fusion
  9.8 0.0 copy-done
  9.8 0.7 convolution_bitcast_fusion
  10.4 2.6 %fusion = f32[16,2,64,64]{3,2,0,1:T(8,128)S(1)} fusion(f32[16,2,64,64]{3,2,0,1:T(8,128)S(1)} %convolution_bitcast_fusion, f32[2,64,64]{2,1,0:T(8,128)S(1)} %broadcast_add_fusion, f32[2,64,64]{2,1,0:T(8,128)} %param.8), kind=kOutput, calls=%fused_computation.3 | convolution fusion | flops 100794368 | bytes 1114112 | tf_op jit(solution)/shard_map/lai,qlab,lbj->qlij/dot_general | solution.py:15
  13.1 1.1 %convolution_bitcast_fusion.1 = f32[16,2,64,64]{2,3,0,1:T(8,128)S(1)} fusion(f32[16,2,64,64]{3,2,0,1:T(8,128)S(1)} %fusion, f32[2,64,64]{2,1,0:T(8,128)S(1)} %copy-done), kind=kOutput, calls=%fused_computation.1 | convolution fusion | flops 100663296 | bytes 1081344 | tf_op jit(solution)/shard_map/lia,qlab,ljb->qlij/dot_general | solution.py:18
  14.2 0.0 copy-done.1
  14.2 1.0 %fusion.1 = bf16[16,2,64,64]{3,2,0,1:T(8,128)(2,1)S(1)} fusion(f32[16,2,64,64]{2,3,0,1:T(8,128)S(1)} %convolution_bitcast_fusion.1, f32[2,64,64]{2,1,0:T(8,128)S(1)} %copy-done.1), kind=kOutput, calls=%fused_computation.5 | convolution fusion | flops 100794368 | bytes 819200 | tf_op jit(solution)/shard_map/lia,qlab,ljb->qlij/dot_general | solution.py:18
  15.3 1.2 %convert_element_type.12 = bf16[16,8192]{1,0:T(8,128)(2,1)} reshape(bf16[16,2,64,64]{3,2,1,0:T(8,128)(2,1)S(1)} %copy.7) | data formatting | bytes 524288 | tf_op jit(solution)/shard_map/convert_element_type | solution.py:19
  16.4 0.0 all-gather.2.cloned.1.call-update
  16.5 16.4 %copy.12 = bf16[64,8,2,4096]{3,1,2,0:T(8,128)(2,1)} copy(bf16[64,8,2,4096]{3,2,1,0:T(2,128)(2,1)} %bitcast.33) | data formatting | bytes 16777216
  32.9 37.0 %all-gather.2.cloned.1.call-done = bf16[256,8192]{1,0:T(8,128)(2,1)} async-done(((bf16[16,8192]{1,0:T(8,128)(2,1)}), bf16[256,8192]{1,0:T(8,128)(2,1)}) %all-gather.2.cloned.1.call-update) | async-done | bytes 4194320 | tf_op jit(solution)/shard_map/all_gather | solution.py:22
  69.9 7.0 %convolution_bitcast_fusion.2 = f32[512,256]{0,1:T(8,128)S(1)} fusion(bf16[256,8192]{1,0:T(8,128)(2,1)} %all-gather.2.cloned.1.call-done, bf16[512,8192]{1,0:T(8,128)(2,1)} %bitcast.34), kind=kOutput, calls=%fused_computation.6 | convolution fusion | flops 2147483648 | bytes 13107200 | tf_op jit(solution)/shard_map/dot_general | solution.py:23
  76.9 1.0 %copy.8 = f32[512,256]{1,0:T(8,128)} copy(f32[512,256]{0,1:T(8,128)S(1)} %convolution_bitcast_fusion.2) | data formatting | bytes 1048576 | tf_op jit(solution)/shard_map/dot_general | solution.py:23
  (2 shorter events, 0.0 us)
Async XLA Ops:
  6.5 3.2 %copy-start = (f32[2,64,64]{2,1,0:T(8,128)S(1)}, f32[2,64,64]{2,1,0:T(8,128)}, u32[]{:S(2)}) copy-start(f32[2,64,64]{2,1,0:T(8,128)} %param.7) | copy-start | bytes 98308
  6.5 7.6 %copy-start.1 = (f32[2,64,64]{2,1,0:T(8,128)S(1)}, f32[2,64,64]{2,1,0:T(8,128)}, u32[]{:S(2)}) copy-start(f32[2,64,64]{2,1,0:T(8,128)} %param.8) | copy-start | bytes 98308
  6.5 63.3 %all-gather.2.cloned.1.call-start = ((), (), s32[]{:S(2)}) async-start(), calls=%async_computation | async-start | bytes 4456448 | tf_op jit(solution)/shard_map/all_gather | solution.py:22
Sparse Core Ops, SparseCore 0:
  16.6 53.2 all-gather.1
where the time goes:
time: 85.1 us; the launch traced here: 84.7 us
  waiting for transfers between devices  37 us (43%)
  local copies, waits for them, and re-layouts  20.8 us (24%)
  between operations  13.5 us (16%)
  matrix products  12.4 us (15%)
  other arithmetic  0.99 us (1%)
    all_gather x1, waiting for transfers between devices, per_device(): gathered = lax.all_gather(precond, 'train', axis=0, tiled=True)  37 us
    unnamed x5, local copies, waits for them, and re-layouts  16.4 us
    dot_general x1, matrix products, per_device(): lax.dot_general(flat_train, gathered, contract, preferred_element_type=jn...  7.02 us
    dot_general x2, matrix products, per_device(): jnp.einsum('lai,qlab,lbj->qlij', basis_in, grads, basis_out, precision=hi...  3.3 us
    dot_general x2, matrix products, per_device(): jnp.einsum('lia,qlab,ljb->qlij', basis_in, scaled, basis_out, precision=h...  2.1 us
  transfers between devices with their start and end apart: 1, of which 1 were waited for; matrix products, arithmetic and copies ran while one was open for 19% of the time, Pallas kernels for 0%

commit v1 on v0

v1 whole, which is shorter than its diff:
```python
import functools

import jax
import jax.numpy as jnp
from jax import lax
from jax.experimental import pallas as pl
from jax.experimental.pallas import tpu as pltpu
from jax.sharding import PartitionSpec as P

CORES = 2
XS = 2
GROUPS = 2
ROWS = 128


def precondition(query_grads, basis_in, basis_out, eigvals):
    q_rows, layers_here = query_grads.shape[:2]
    p_in = basis_in.shape[1]
    p_out = basis_out.shape[1]
    highest = lax.Precision.HIGHEST
    grads = query_grads.astype(jnp.float32).reshape(q_rows, layers_here, p_in, p_out)
    rotated = jnp.einsum("lai,qlab,lbj->qlij", basis_in, grads, basis_out, precision=highest)
    damping = 0.1 * jnp.mean(eigvals, axis=1)
    scaled = rotated / (eigvals.reshape(layers_here, p_in, p_out) + damping[:, None, None])
    back = jnp.einsum("lia,qlab,ljb->qlij", basis_in, scaled, basis_out, precision=highest)
    return back.reshape(q_rows, layers_here * p_in * p_out).astype(jnp.bfloat16)


def place(n_train):
    t = lax.axis_index("train")
    return t // (XS * CORES), (t // CORES) % XS, t % CORES, lax.axis_index("group")


def hop(array, n_train, dz=0, dx=0, dc=0, dg=0):
    zs = n_train // (XS * CORES)
    perm = []
    for g in range(GROUPS):
        for t in range(n_train):
            z, x, c = t // (XS * CORES), (t // CORES) % XS, t % CORES
            to = (((z + dz) % zs) * XS + (x ^ dx)) * CORES + (c ^ dc)
            perm.append((g * n_train + t, (g ^ dg) * n_train + to))
    return lax.ppermute(array, ("group", "train"), perm)


def score_kernel(ids, n_train, t_ref, *refs):
    pieces, (out_ref, all_ref, sems) = refs[: len(ids)], refs[len(ids) :]
    zs = n_train // (XS * CORES)
    q_rows, width = pieces[0].shape
    z, x, c, g = place(n_train)

    @pl.when(pl.program_id(0) == 0)
    def _():
        copies = []
        for at, (dz, dx, dg, dc) in enumerate(ids):
            block = (lax.rem(z - dz + zs, zs) * XS + (x + dx) % XS) * CORES + (c + dc) % CORES
            part = (g + dg) % GROUPS
            rows = pl.ds(pl.multiple_of(block * q_rows, q_rows), q_rows)
            columns = pl.ds(pl.multiple_of(part * width, width), width)
            copies.append(pltpu.make_async_copy(pieces[at], all_ref.at[rows, columns], sems.at[at]))
        for copy in copies:
            copy.start()
        for copy in copies:
            copy.wait()

    out_ref[...] = lax.dot_general(
        t_ref[...], all_ref[...], (((1,), (1,)), ((), ())), preferred_element_type=jnp.float32
    )


def per_device(n_train, train_grads, query_grads, basis_in, basis_out, eigvals):
    tr_rows = train_grads.shape[0]
    zs = n_train // (XS * CORES)
    precond = precondition(query_grads, basis_in, basis_out, eigvals)
    q_rows, depth = precond.shape
    width = depth // GROUPS
    g = lax.axis_index("group")
    mine = lax.dynamic_slice(precond, (0, g * width), (q_rows, width))
    twin = lax.dynamic_slice(precond, (0, (1 - g) * width), (q_rows, width))
    flat_train = train_grads.reshape(tr_rows, depth)

    ids, pieces = [], []

    def keep(array, dz, dx, dg):
        ids.append((dz, dx, dg, 0))
        pieces.append(array)
        ids.append((dz, dx, dg, 1))
        pieces.append(hop(array, n_train, dc=1))

    for dz in range(zs):
        own = hop(mine, n_train, dz=dz) if dz else mine
        over_x = hop(own, n_train, dx=1)
        over_g = hop(own, n_train, dg=1) if dz else twin
        corner = hop(over_g, n_train, dx=1) if dz % 2 else hop(over_x, n_train, dg=1)
        keep(own, dz, 0, 0)
        keep(over_x, dz, 1, 0)
        keep(over_g, dz, 0, 1)
        keep(corner, dz, 1, 1)

    n_query = n_train * q_rows
    partial_scores = pl.pallas_call(
        functools.partial(score_kernel, tuple(ids), n_train),
        grid=(tr_rows // ROWS,),
        out_shape=jax.ShapeDtypeStruct((tr_rows, n_query), jnp.float32),
        in_specs=[pl.BlockSpec((ROWS, depth), lambda i: (i, 0))]
        + [pl.BlockSpec(memory_space=pl.ANY)] * len(ids),
        out_specs=pl.BlockSpec((ROWS, n_query), lambda i: (i, 0)),
        scratch_shapes=[
            pltpu.VMEM((n_query, depth), jnp.bfloat16),
            pltpu.SemaphoreType.DMA((len(ids),)),
        ],
        compiler_params=pltpu.CompilerParams(vmem_limit_bytes=48 * 1024 * 1024),
        cost_estimate=pl.CostEstimate(
            flops=2 * tr_rows * n_query * depth, bytes_accessed=2 * depth * (tr_rows + n_query), transcendentals=0
        ),
        name="scores",
    )(flat_train, *pieces)
    return lax.psum_scatter(partial_scores, "layer", scatter_dimension=1, tiled=True)


def solution(mesh):
    return jax.shard_map(
        functools.partial(per_device, mesh.shape["train"]),
        mesh=mesh,
        in_specs=(
            P(("group", "train"), "layer", None),
            P("train", "layer", None),
            P("layer", None, None),
            P("layer", None, None),
            P("layer", None),
        ),
        out_specs=P(("group", "train"), "layer"),
        check_vma=False,
    )
```

time: 85.1 us -> 78.2 us (0.919)
  starting transfers between devices: 0.01 us -> 25.2 us
  waiting for transfers between devices: 37 us -> 14.7 us
  between operations: 13.5 us -> 0.28 us
  Pallas kernels: 0 us -> 12.1 us
  matrix products: 12.4 us -> 5.41 us
  local copies, waits for them, and re-layouts: 20.8 us -> 19 us
    all_gather x1 -> x0, waiting for transfers between devices: 37 us -> none  [per_device(): gathered = lax.all_gather(precond, 'train', axis=0, tiled=True)]
    ppermute x0 -> x30, starting transfers between devices: none -> 25.2 us  [hop(): return lax.ppermute(array, ('group', 'train'), perm)]
    ppermute x0 -> x30, waiting for transfers between devices: none -> 14.7 us  [hop(): return lax.ppermute(array, ('group', 'train'), perm)]
    pallas_call x0 -> x1, Pallas kernels: none -> 12.1 us  [per_device(): pl.pallas_call(functools.partial(score_kernel, tuple(ids), n_train), grid...]
    dot_general x5 -> x4, matrix products: 12.4 us -> 5.41 us  [the longest x2 3.3 us: precondition(): jnp.einsum('lai,qlab,lbj->qlij', basis_in, grads, basis_out, precision=hi...]
    dot_general x1 -> x0, local copies, waits for them, and re-layouts: 1 us -> none  [per_device(): lax.dot_general(flat_train, gathered, contract, preferred_element_type=jn...]
  transfers between devices with their start and end apart: 1 -> 30, of which waited for: 1 -> 8; matrix products, arithmetic and copies ran while one was open for 19% -> 21% of each run, Pallas kernels for 0% -> 0%
where the time goes in v1:
time: 78.2 us; the launch traced here: 77.7 us
  starting transfers between devices  25.2 us (32%)
  local copies, waits for them, and re-layouts  19 us (24%)
  waiting for transfers between devices  14.7 us (19%)
  Pallas kernels  12.1 us (15%)
  matrix products  5.41 us (7%)
  other arithmetic  0.99 us (1%)
    ppermute x30, starting transfers between devices, hop(): return lax.ppermute(array, ('group', 'train'), perm)  25.2 us
    unnamed x5, local copies, waits for them, and re-layouts  16.3 us
    ppermute x30, waiting for transfers between devices, hop(): return lax.ppermute(array, ('group', 'train'), perm)  14.7 us
    pallas_call x1, Pallas kernels, per_device(): pl.pallas_call(functools.partial(score_kernel, tuple(ids), n_train), grid...  12.1 us
    dot_general x2, matrix products, precondition(): jnp.einsum('lai,qlab,lbj->qlij', basis_in, grads, basis_out, precision=hi...  3.3 us
    dot_general x2, matrix products, precondition(): jnp.einsum('lia,qlab,ljb->qlij', basis_in, scaled, basis_out, precision=h...  2.1 us
  transfers between devices with their start and end apart: 30, of which 8 were waited for; matrix products, arithmetic and copies ran while one was open for 21% of the time, Pallas kernels for 0%

profile of v1, /device:TPU:0, one launch (start us, length us, event | category | flops | bytes accessed | tf_op | source)
XLA Modules:
  0.0 77.7 jit_solution(8223161689813147413)
XLA Ops:
  0.0 0.9 %reshape.21 = f32[2,64,64]{2,1,0:T(8,128)S(1)} reshape(f32[2,4096]{1,0:T(2,128)} %param.9) | data formatting | bytes 65536 | tf_op jit(solution)/shard_map/reshape | solution.py:24
  0.9 0.9 %reduce_sum.9 = f32[2]{0:T(128)S(1)} reduce(f32[2,4096]{1,0:T(2,128)} %param.9, f32[]{:T(128)} %constant.8.clone.1), dimensions={1}, to_apply=%region_0.0 | reduce | flops 8190 | bytes 32780 | tf_op jit(solution)/shard_map/reduce_sum | solution.py:23
  1.8 1.3 %reshape.20 = bf16[16,2,64,64]{3,2,1,0:T(8,128)(2,1)S(1)} reshape(bf16[16,2,4096]{2,1,0:T(2,128)(2,1)} %param.6) | data formatting | bytes 524288 | tf_op jit(solution)/shard_map/reshape | solution.py:21
  3.2 0.1 broadcast_add_fusion
  3.2 0.7 convolution_bitcast_fusion
  3.9 2.6 %fusion = f32[16,2,64,64]{3,2,0,1:T(8,128)S(1)} fusion(f32[16,2,64,64]{3,2,0,1:T(8,128)S(1)} %convolution_bitcast_fusion, f32[2,64,64]{2,1,0:T(8,128)S(1)} %broadcast_add_fusion, f32[2,64,64]{2,1,0:T(8,128)} %param.8), kind=kOutput, calls=%fused_computation.3 | convolution fusion | flops 100794368 | bytes 1114112 | tf_op jit(solution)/shard_map/lai,qlab,lbj->qlij/dot_general | solution.py:22
  6.5 1.1 %convolution_bitcast_fusion.1 = f32[16,2,64,64]{2,3,0,1:T(8,128)S(1)} fusion(f32[16,2,64,64]{3,2,0,1:T(8,128)S(1)} %fusion, f32[2,64,64]{2,1,0:T(8,128)S(1)} %copy-done), kind=kOutput, calls=%fused_computation.1 | convolution fusion | flops 100663296 | bytes 1081344 | tf_op jit(solution)/shard_map/lia,qlab,ljb->qlij/dot_general | solution.py:25
  7.6 1.0 %fusion.1 = bf16[16,2,64,64]{3,2,0,1:T(8,128)(2,1)S(1)} fusion(f32[16,2,64,64]{2,3,0,1:T(8,128)S(1)} %convolution_bitcast_fusion.1, f32[2,64,64]{2,1,0:T(8,128)S(1)} %copy-done.1), kind=kOutput, calls=%fused_computation.5 | convolution fusion | flops 100794368 | bytes 819200 | tf_op jit(solution)/shard_map/lia,qlab,ljb->qlij/dot_general | solution.py:25
  8.7 0.5 convert_element_type.12
  9.2 0.5 collective-permute-start.3
  9.7 4.7 %collective-permute-start.22 = (bf16[16,4096]{1,0:T(8,128)(2,1)S(1)}, bf16[16,4096]{1,0:T(8,128)(2,1)S(1)}, u32[]{:S(2)}, u32[]{:S(2)}) collective-permute-start(bf16[16,4096]{1,0:T(8,128)(2,1)S(1)} %get-tuple-element.6.refs_0_), channel_id=1, source_target_pairs={{0,12},{1,13},{2,14},{3,15},{4,0},{5,1},{6,2},{7,3},{8,4},{9,5},{1... | collective-permute-start | bytes 393224 | tf_op jit(solution)/shard_map/ppermute | solution.py:42
  14.4 0.0 collective-permute-start.14
  14.4 1.0 %collective-permute-start.6 = (bf16[16,4096]{1,0:T(8,128)(2,1)S(1)}, bf16[16,4096]{1,0:T(8,128)(2,1)S(1)}, u32[]{:S(2)}, u32[]{:S(2)}) collective-permute-start(bf16[16,4096]{1,0:T(8,128)(2,1)S(1)} %get-tuple-element.6.refs_0_), channel_id=1, source_target_pairs={{0,4},{1,5},{2,6},{3,7},{4,8},{5,9},{6,10},{7,11},{8,12},{9,13},{1... | collective-permute-start | bytes 393224 | tf_op jit(solution)/shard_map/ppermute | solution.py:42
  15.4 1.5 %collective-permute-start.1 = (bf16[16,4096]{1,0:T(8,128)(2,1)S(1)}, bf16[16,4096]{1,0:T(8,128)(2,1)S(1)}, u32[]{:S(2)}, u32[]{:S(2)}) collective-permute-start(bf16[16,4096]{1,0:T(8,128)(2,1)S(1)} %get-tuple-element.6.refs_0_), channel_id=1, source_target_pairs={{0,2},{1,3},{2,0},{3,1},{4,6},{5,7},{6,4},{7,5},{8,10},{9,11},{10,... | collective-permute-start | bytes 393224 | tf_op jit(solution)/shard_map/ppermute | solution.py:42
  16.9 0.0 collective-permute-done.3.refs_5_
  16.9 0.0 collective-permute-start
  16.9 1.4 %collective-permute-done.22.refs_24_ = bf16[16,4096]{1,0:T(8,128)(2,1)S(1)} collective-permute-done((bf16[16,4096]{1,0:T(8,128)(2,1)S(1)}, bf16[16,4096]{1,0:T(8,128)(2,1)S(1)}, u32[]{:S(2)}, u32[]{:S(2)}) %collective-permute-start.22) | collective-permute-done | bytes 131104 | tf_op jit(solution)/shard_map/ppermute | solution.py:42
  18.3 1.5 %collective-permute-start.26 = (bf16[16,4096]{1,0:T(8,128)(2,1)S(1)}, bf16[16,4096]{1,0:T(8,128)(2,1)S(1)}, u32[]{:S(2)}, u32[]{:S(2)}) collective-permute-start(bf16[16,4096]{1,0:T(8,128)(2,1)S(1)} %collective-permute-done.22.refs_24_), channel_id=1, source_target_pairs={{0,16},{1,17},{2,18},{3,19},{4,20},{5,21},{6,22},{7,23},{8,24},{9,... | collective-permute-start | bytes 393224 | tf_op jit(solution)/shard_map/ppermute | solution.py:42
  19.8 6.7 %collective-permute-done.14.refs_16_ = bf16[16,4096]{1,0:T(8,128)(2,1)S(1)} collective-permute-done((bf16[16,4096]{1,0:T(8,128)(2,1)S(1)}, bf16[16,4096]{1,0:T(8,128)(2,1)S(1)}, u32[]{:S(2)}, u32[]{:S(2)}) %collective-permute-start.14) | collective-permute-done | bytes 131104 | tf_op jit(solution)/shard_map/ppermute | solution.py:42
  26.5 1.5 %collective-permute-start.24 = (bf16[16,4096]{1,0:T(8,128)(2,1)S(1)}, bf16[16,4096]{1,0:T(8,128)(2,1)S(1)}, u32[]{:S(2)}, u32[]{:S(2)}) collective-permute-start(bf16[16,4096]{1,0:T(8,128)(2,1)S(1)} %collective-permute-done.22.refs_24_), channel_id=1, source_target_pairs={{0,2},{1,3},{2,0},{3,1},{4,6},{5,7},{6,4},{7,5},{8,10},{9,11},{10,... | collective-permute-start | bytes 393224 | tf_op jit(solution)/shard_map/ppermute | solution.py:42
  28.0 0.0 collective-permute-done.6.refs_8_
  28.0 0.0 collective-permute-start.23
  28.0 0.0 collective-permute-done.1.refs_2_
  28.0 1.6 %collective-permute-start.18 = (bf16[16,4096]{1,0:T(8,128)(2,1)S(1)}, bf16[16,4096]{1,0:T(8,128)(2,1)S(1)}, u32[]{:S(2)}, u32[]{:S(2)}) collective-permute-start(bf16[16,4096]{1,0:T(8,128)(2,1)S(1)} %collective-permute-done.14.refs_16_), channel_id=1, source_target_pairs={{0,16},{1,17},{2,18},{3,19},{4,20},{5,21},{6,22},{7,23},{8,24},{9,... | collective-permute-start | bytes 393224 | tf_op jit(solution)/shard_map/ppermute | solution.py:42
  29.6 0.0 collective-permute-done.refs_1_
  29.6 0.5 collective-permute-start.16
  30.1 0.0 collective-permute-done.26.refs_28_
  30.1 0.0 collective-permute-start.15
  30.1 1.4 %collective-permute-done.24.refs_26_ = bf16[16,4096]{1,0:T(8,128)(2,1)S(1)} collective-permute-done((bf16[16,4096]{1,0:T(8,128)(2,1)S(1)}, bf16[16,4096]{1,0:T(8,128)(2,1)S(1)}, u32[]{:S(2)}, u32[]{:S(2)}) %collective-permute-start.24) | collective-permute-done | bytes 131104 | tf_op jit(solution)/shard_map/ppermute | solution.py:42
  31.5 1.7 %collective-permute-start.10 = (bf16[16,4096]{1,0:T(8,128)(2,1)S(1)}, bf16[16,4096]{1,0:T(8,128)(2,1)S(1)}, u32[]{:S(2)}, u32[]{:S(2)}) collective-permute-start(bf16[16,4096]{1,0:T(8,128)(2,1)S(1)} %collective-permute-done.6.refs_8_), channel_id=1, source_target_pairs={{0,16},{1,17},{2,18},{3,19},{4,20},{5,21},{6,22},{7,23},{8,24},{9,... | collective-permute-start | bytes 393224 | tf_op jit(solution)/shard_map/ppermute | solution.py:42
  33.3 0.0 collective-permute-done.23.refs_25_
  33.3 2.5 %collective-permute-start.8 = (bf16[16,4096]{1,0:T(8,128)(2,1)S(1)}, bf16[16,4096]{1,0:T(8,128)(2,1)S(1)}, u32[]{:S(2)}, u32[]{:S(2)}) collective-permute-start(bf16[16,4096]{1,0:T(8,128)(2,1)S(1)} %collective-permute-done.6.refs_8_), channel_id=1, source_target_pairs={{0,2},{1,3},{2,0},{3,1},{4,6},{5,7},{6,4},{7,5},{8,10},{9,11},{10,... | collective-permute-start | bytes 393224 | tf_op jit(solution)/shard_map/ppermute | solution.py:42
  35.7 0.0 collective-permute-done.18.refs_20_
  35.7 0.0 collective-permute-start.7
  35.7 0.2 collective-permute-done.16.refs_18_
  35.9 0.5 collective-permute-start.4
  36.4 0.0 collective-permute-done.15.refs_17_
  36.4 0.0 collective-permute-start.2
  36.4 0.3 collective-permute-done.10.refs_12_
  36.7 2.8 %collective-permute-start.28 = (bf16[16,4096]{1,0:T(8,128)(2,1)S(1)}, bf16[16,4096]{1,0:T(8,128)(2,1)S(1)}, u32[]{:S(2)}, u32[]{:S(2)}) collective-permute-start(bf16[16,4096]{1,0:T(8,128)(2,1)S(1)} %collective-permute-done.26.refs_28_), channel_id=1, source_target_pairs={{0,2},{1,3},{2,0},{3,1},{4,6},{5,7},{6,4},{7,5},{8,10},{9,11},{10,... | collective-permute-start | bytes 393224 | tf_op jit(solution)/shard_map/ppermute | solution.py:42
  39.5 0.0 collective-permute-start.27
  39.5 0.0 collective-permute-done.7.refs_9_
  39.5 0.5 collective-permute-start.25
  40.1 1.6 %collective-permute-done.4.refs_6_ = bf16[16,4096]{1,0:T(8,128)(2,1)S(1)} collective-permute-done((bf16[16,4096]{1,0:T(8,128)(2,1)S(1)}, bf16[16,4096]{1,0:T(8,128)(2,1)S(1)}, u32[]{:S(2)}, u32[]{:S(2)}) %collective-permute-start.4) | collective-permute-done | bytes 131104 | tf_op jit(solution)/shard_map/ppermute | solution.py:42
  41.7 0.0 collective-permute-start.19
  41.7 0.0 collective-permute-done.2.refs_3_
  41.7 0.9 %collective-permute-start.20 = (bf16[16,4096]{1,0:T(8,128)(2,1)S(1)}, bf16[16,4096]{1,0:T(8,128)(2,1)S(1)}, u32[]{:S(2)}, u32[]{:S(2)}) collective-permute-start(bf16[16,4096]{1,0:T(8,128)(2,1)S(1)} %collective-permute-done.16.refs_18_), channel_id=1, source_target_pairs={{0,16},{1,17},{2,18},{3,19},{4,20},{5,21},{6,22},{7,23},{8,24},{9,... | collective-permute-start | bytes 393224 | tf_op jit(solution)/shard_map/ppermute | solution.py:42
  42.6 0.0 collective-permute-done.28.refs_30_
  42.6 0.2 collective-permute-start.17
  42.8 1.7 %collective-permute-start.12 = (bf16[16,4096]{1,0:T(8,128)(2,1)S(1)}, bf16[16,4096]{1,0:T(8,128)(2,1)S(1)}, u32[]{:S(2)}, u32[]{:S(2)}) collective-permute-start(bf16[16,4096]{1,0:T(8,128)(2,1)S(1)} %collective-permute-done.10.refs_12_), channel_id=1, source_target_pairs={{0,2},{1,3},{2,0},{3,1},{4,6},{5,7},{6,4},{7,5},{8,10},{9,11},{10,... | collective-permute-start | bytes 393224 | tf_op jit(solution)/shard_map/ppermute | solution.py:42
  44.5 0.0 collective-permute-done.25.refs_27_
  44.5 0.2 collective-permute-start.11
  44.7 0.3 collective-permute-start.9
  45.0 2.5 %collective-permute-done.20.refs_22_ = bf16[16,4096]{1,0:T(8,128)(2,1)S(1)} collective-permute-done((bf16[16,4096]{1,0:T(8,128)(2,1)S(1)}, bf16[16,4096]{1,0:T(8,128)(2,1)S(1)}, u32[]{:S(2)}, u32[]{:S(2)}) %collective-permute-start.20) | collective-permute-done | bytes 131104 | tf_op jit(solution)/shard_map/ppermute | solution.py:42
  47.6 0.0 collective-permute-start.5
  47.6 0.0 collective-permute-done.17.refs_19_
  47.6 0.5 collective-permute-start.29
  48.1 0.6 collective-permute-done.12.refs_14_
  48.7 0.5 collective-permute-start.13
  49.2 16.3 %copy.10 = bf16[64,8,2,4096]{3,1,2,0:T(8,128)(2,1)} copy(bf16[64,8,2,4096]{3,2,1,0:T(2,128)(2,1)} %bitcast.30) | data formatting | bytes 16777216
  65.5 0.0 collective-permute-done.9.refs_11_
  65.5 0.0 collective-permute-done.5.refs_7_
  65.5 0.0 collective-permute-done.29.refs_31_
  65.5 12.1 %scores.1 = f32[512,256]{1,0:T(8,128)} custom-call(bf16[512,8192]{1,0:T(8,128)(2,1)} %bitcast.29, bf16[16,4096]{1,0:T(8,128)(2,1)S(1)} %get-tuple-element.6.refs_0_, bf16[16,4096]{1,0:T(8,128)(2,1)S(1)} %collective-permute-done.refs_1_, bf16[16,4096]{1,0:T(8,128)(2,1)S(1)} %collective-permute-done.1.refs_2_, ...), custom_call_target="tpu_custom_call" | custom-call | flops 2147483648 | bytes 12582912 | tf_op jit(solution)/shard_map/scores/pallas_call | solution.py:100
  (14 shorter events, 0.1 us)
Async XLA Ops:
  0.0 3.2 %copy-start = (f32[2,64,64]{2,1,0:T(8,128)S(1)}, f32[2,64,64]{2,1,0:T(8,128)}, u32[]{:S(2)}) copy-start(f32[2,64,64]{2,1,0:T(8,128)} %param.7) | copy-start | bytes 98308
  0.0 7.6 %copy-start.1 = (f32[2,64,64]{2,1,0:T(8,128)S(1)}, f32[2,64,64]{2,1,0:T(8,128)}, u32[]{:S(2)}) copy-start(f32[2,64,64]{2,1,0:T(8,128)} %param.8) | copy-start | bytes 98308
  9.2 7.7 %collective-permute-start.3 = (bf16[16,4096]{1,0:T(8,128)(2,1)S(1)}, bf16[16,4096]{1,0:T(8,128)(2,1)S(1)}, u32[]{:S(2)}, u32[]{:S(2)}) collective-permute-start(bf16[16,4096]{1,0:T(8,128)(2,1)S(1)} %get-tuple-element.5.refs_4_), channel_id=1, source_target_pairs={{0,1},{1,0},{2,3},{3,2},{4,5},{5,4},{6,7},{7,6},{8,9},{9,8},{10,11... | collective-permute-start | bytes 393224 | tf_op jit(solution)/shard_map/ppermute | solution.py:42
  9.7 8.6 %collective-permute-start.22 = (bf16[16,4096]{1,0:T(8,128)(2,1)S(1)}, bf16[16,4096]{1,0:T(8,128)(2,1)S(1)}, u32[]{:S(2)}, u32[]{:S(2)}) collective-permute-start(bf16[16,4096]{1,0:T(8,128)(2,1)S(1)} %get-tuple-element.6.refs_0_), channel_id=1, source_target_pairs={{0,12},{1,13},{2,14},{3,15},{4,0},{5,1},{6,2},{7,3},{8,4},{9,5},{1... | collective-permute-start | bytes 393224 | tf_op jit(solution)/shard_map/ppermute | solution.py:42
  14.4 12.1 %collective-permute-start.14 = (bf16[16,4096]{1,0:T(8,128)(2,1)S(1)}, bf16[16,4096]{1,0:T(8,128)(2,1)S(1)}, u32[]{:S(2)}, u32[]{:S(2)}) collective-permute-start(bf16[16,4096]{1,0:T(8,128)(2,1)S(1)} %get-tuple-element.6.refs_0_), channel_id=1, source_target_pairs={{0,8},{1,9},{2,10},{3,11},{4,12},{5,13},{6,14},{7,15},{8,0},{9,1},... | collective-permute-start | bytes 393224 | tf_op jit(solution)/shard_map/ppermute | solution.py:42
  14.4 13.6 %collective-permute-start.6 = (bf16[16,4096]{1,0:T(8,128)(2,1)S(1)}, bf16[16,4096]{1,0:T(8,128)(2,1)S(1)}, u32[]{:S(2)}, u32[]{:S(2)}) collective-permute-start(bf16[16,4096]{1,0:T(8,128)(2,1)S(1)} %get-tuple-element.6.refs_0_), channel_id=1, source_target_pairs={{0,4},{1,5},{2,6},{3,7},{4,8},{5,9},{6,10},{7,11},{8,12},{9,13},{1... | collective-permute-start | bytes 393224 | tf_op jit(solution)/shard_map/ppermute | solution.py:42
  15.4 12.6 %collective-permute-start.1 = (bf16[16,4096]{1,0:T(8,128)(2,1)S(1)}, bf16[16,4096]{1,0:T(8,128)(2,1)S(1)}, u32[]{:S(2)}, u32[]{:S(2)}) collective-permute-start(bf16[16,4096]{1,0:T(8,128)(2,1)S(1)} %get-tuple-element.6.refs_0_), channel_id=1, source_target_pairs={{0,2},{1,3},{2,0},{3,1},{4,6},{5,7},{6,4},{7,5},{8,10},{9,11},{10,... | collective-permute-start | bytes 393224 | tf_op jit(solution)/shard_map/ppermute | solution.py:42
  16.9 12.7 %collective-permute-start = (bf16[16,4096]{1,0:T(8,128)(2,1)S(1)}, bf16[16,4096]{1,0:T(8,128)(2,1)S(1)}, u32[]{:S(2)}, u32[]{:S(2)}) collective-permute-start(bf16[16,4096]{1,0:T(8,128)(2,1)S(1)} %get-tuple-element.6.refs_0_), channel_id=1, source_target_pairs={{0,1},{1,0},{2,3},{3,2},{4,5},{5,4},{6,7},{7,6},{8,9},{9,8},{10,11... | collective-permute-start | bytes 393224 | tf_op jit(solution)/shard_map/ppermute | solution.py:42
  18.3 11.8 %collective-permute-start.26 = (bf16[16,4096]{1,0:T(8,128)(2,1)S(1)}, bf16[16,4096]{1,0:T(8,128)(2,1)S(1)}, u32[]{:S(2)}, u32[]{:S(2)}) collective-permute-start(bf16[16,4096]{1,0:T(8,128)(2,1)S(1)} %collective-permute-done.22.refs_24_), channel_id=1, source_target_pairs={{0,16},{1,17},{2,18},{3,19},{4,20},{5,21},{6,22},{7,23},{8,24},{9,... | collective-permute-start | bytes 393224 | tf_op jit(solution)/shard_map/ppermute | solution.py:42
  26.5 5.1 %collective-permute-start.24 = (bf16[16,4096]{1,0:T(8,128)(2,1)S(1)}, bf16[16,4096]{1,0:T(8,128)(2,1)S(1)}, u32[]{:S(2)}, u32[]{:S(2)}) collective-permute-start(bf16[16,4096]{1,0:T(8,128)(2,1)S(1)} %collective-permute-done.22.refs_24_), channel_id=1, source_target_pairs={{0,2},{1,3},{2,0},{3,1},{4,6},{5,7},{6,4},{7,5},{8,10},{9,11},{10,... | collective-permute-start | bytes 393224 | tf_op jit(solution)/shard_map/ppermute | solution.py:42
  28.0 5.3 %collective-permute-start.23 = (bf16[16,4096]{1,0:T(8,128)(2,1)S(1)}, bf16[16,4096]{1,0:T(8,128)(2,1)S(1)}, u32[]{:S(2)}, u32[]{:S(2)}) collective-permute-start(bf16[16,4096]{1,0:T(8,128)(2,1)S(1)} %collective-permute-done.22.refs_24_), channel_id=1, source_target_pairs={{0,1},{1,0},{2,3},{3,2},{4,5},{5,4},{6,7},{7,6},{8,9},{9,8},{10,11... | collective-permute-start | bytes 393224 | tf_op jit(solution)/shard_map/ppermute | solution.py:42
  28.0 7.8 %collective-permute-start.18 = (bf16[16,4096]{1,0:T(8,128)(2,1)S(1)}, bf16[16,4096]{1,0:T(8,128)(2,1)S(1)}, u32[]{:S(2)}, u32[]{:S(2)}) collective-permute-start(bf16[16,4096]{1,0:T(8,128)(2,1)S(1)} %collective-permute-done.14.refs_16_), channel_id=1, source_target_pairs={{0,16},{1,17},{2,18},{3,19},{4,20},{5,21},{6,22},{7,23},{8,24},{9,... | collective-permute-start | bytes 393224 | tf_op jit(solution)/shard_map/ppermute | solution.py:42
  29.6 6.3 %collective-permute-start.16 = (bf16[16,4096]{1,0:T(8,128)(2,1)S(1)}, bf16[16,4096]{1,0:T(8,128)(2,1)S(1)}, u32[]{:S(2)}, u32[]{:S(2)}) collective-permute-start(bf16[16,4096]{1,0:T(8,128)(2,1)S(1)} %collective-permute-done.14.refs_16_), channel_id=1, source_target_pairs={{0,2},{1,3},{2,0},{3,1},{4,6},{5,7},{6,4},{7,5},{8,10},{9,11},{10,... | collective-permute-start | bytes 393224 | tf_op jit(solution)/shard_map/ppermute | solution.py:42
  30.1 6.3 %collective-permute-start.15 = (bf16[16,4096]{1,0:T(8,128)(2,1)S(1)}, bf16[16,4096]{1,0:T(8,128)(2,1)S(1)}, u32[]{:S(2)}, u32[]{:S(2)}) collective-permute-start(bf16[16,4096]{1,0:T(8,128)(2,1)S(1)} %collective-permute-done.14.refs_16_), channel_id=1, source_target_pairs={{0,1},{1,0},{2,3},{3,2},{4,5},{5,4},{6,7},{7,6},{8,9},{9,8},{10,11... | collective-permute-start | bytes 393224 | tf_op jit(solution)/shard_map/ppermute | solution.py:42
  31.5 5.2 %collective-permute-start.10 = (bf16[16,4096]{1,0:T(8,128)(2,1)S(1)}, bf16[16,4096]{1,0:T(8,128)(2,1)S(1)}, u32[]{:S(2)}, u32[]{:S(2)}) collective-permute-start(bf16[16,4096]{1,0:T(8,128)(2,1)S(1)} %collective-permute-done.6.refs_8_), channel_id=1, source_target_pairs={{0,16},{1,17},{2,18},{3,19},{4,20},{5,21},{6,22},{7,23},{8,24},{9,... | collective-permute-start | bytes 393224 | tf_op jit(solution)/shard_map/ppermute | solution.py:42
  33.3 6.3 %collective-permute-start.8 = (bf16[16,4096]{1,0:T(8,128)(2,1)S(1)}, bf16[16,4096]{1,0:T(8,128)(2,1)S(1)}, u32[]{:S(2)}, u32[]{:S(2)}) collective-permute-start(bf16[16,4096]{1,0:T(8,128)(2,1)S(1)} %collective-permute-done.6.refs_8_), channel_id=1, source_target_pairs={{0,2},{1,3},{2,0},{3,1},{4,6},{5,7},{6,4},{7,5},{8,10},{9,11},{10,... | collective-permute-start | bytes 393224 | tf_op jit(solution)/shard_map/ppermute | solution.py:42
  35.7 3.8 %collective-permute-start.7 = (bf16[16,4096]{1,0:T(8,128)(2,1)S(1)}, bf16[16,4096]{1,0:T(8,128)(2,1)S(1)}, u32[]{:S(2)}, u32[]{:S(2)}) collective-permute-start(bf16[16,4096]{1,0:T(8,128)(2,1)S(1)} %collective-permute-done.6.refs_8_), channel_id=1, source_target_pairs={{0,1},{1,0},{2,3},{3,2},{4,5},{5,4},{6,7},{7,6},{8,9},{9,8},{10,11... | collective-permute-start | bytes 393224 | tf_op jit(solution)/shard_map/ppermute | solution.py:42
  35.9 5.7 %collective-permute-start.4 = (bf16[16,4096]{1,0:T(8,128)(2,1)S(1)}, bf16[16,4096]{1,0:T(8,128)(2,1)S(1)}, u32[]{:S(2)}, u32[]{:S(2)}) collective-permute-start(bf16[16,4096]{1,0:T(8,128)(2,1)S(1)} %collective-permute-done.1.refs_2_), channel_id=1, source_target_pairs={{0,16},{1,17},{2,18},{3,19},{4,20},{5,21},{6,22},{7,23},{8,24},{9,... | collective-permute-start | bytes 393224 | tf_op jit(solution)/shard_map/ppermute | solution.py:42
  36.4 5.2 %collective-permute-start.2 = (bf16[16,4096]{1,0:T(8,128)(2,1)S(1)}, bf16[16,4096]{1,0:T(8,128)(2,1)S(1)}, u32[]{:S(2)}, u32[]{:S(2)}) collective-permute-start(bf16[16,4096]{1,0:T(8,128)(2,1)S(1)} %collective-permute-done.1.refs_2_), channel_id=1, source_target_pairs={{0,1},{1,0},{2,3},{3,2},{4,5},{5,4},{6,7},{7,6},{8,9},{9,8},{10,11... | collective-permute-start | bytes 393224 | tf_op jit(solution)/shard_map/ppermute | solution.py:42
  36.7 5.9 %collective-permute-start.28 = (bf16[16,4096]{1,0:T(8,128)(2,1)S(1)}, bf16[16,4096]{1,0:T(8,128)(2,1)S(1)}, u32[]{:S(2)}, u32[]{:S(2)}) collective-permute-start(bf16[16,4096]{1,0:T(8,128)(2,1)S(1)} %collective-permute-done.26.refs_28_), channel_id=1, source_target_pairs={{0,2},{1,3},{2,0},{3,1},{4,6},{5,7},{6,4},{7,5},{8,10},{9,11},{10,... | collective-permute-start | bytes 393224 | tf_op jit(solution)/shard_map/ppermute | solution.py:42
  39.5 3.2 %collective-permute-start.27 = (bf16[16,4096]{1,0:T(8,128)(2,1)S(1)}, bf16[16,4096]{1,0:T(8,128)(2,1)S(1)}, u32[]{:S(2)}, u32[]{:S(2)}) collective-permute-start(bf16[16,4096]{1,0:T(8,128)(2,1)S(1)} %collective-permute-done.26.refs_28_), channel_id=1, source_target_pairs={{0,1},{1,0},{2,3},{3,2},{4,5},{5,4},{6,7},{7,6},{8,9},{9,8},{10,11... | collective-permute-start | bytes 393224 | tf_op jit(solution)/shard_map/ppermute | solution.py:42
  39.5 5.0 %collective-permute-start.25 = (bf16[16,4096]{1,0:T(8,128)(2,1)S(1)}, bf16[16,4096]{1,0:T(8,128)(2,1)S(1)}, u32[]{:S(2)}, u32[]{:S(2)}) collective-permute-start(bf16[16,4096]{1,0:T(8,128)(2,1)S(1)} %collective-permute-done.24.refs_26_), channel_id=1, source_target_pairs={{0,1},{1,0},{2,3},{3,2},{4,5},{5,4},{6,7},{7,6},{8,9},{9,8},{10,11... | collective-permute-start | bytes 393224 | tf_op jit(solution)/shard_map/ppermute | solution.py:42
  41.7 3.1 %collective-permute-start.19 = (bf16[16,4096]{1,0:T(8,128)(2,1)S(1)}, bf16[16,4096]{1,0:T(8,128)(2,1)S(1)}, u32[]{:S(2)}, u32[]{:S(2)}) collective-permute-start(bf16[16,4096]{1,0:T(8,128)(2,1)S(1)} %collective-permute-done.18.refs_20_), channel_id=1, source_target_pairs={{0,1},{1,0},{2,3},{3,2},{4,5},{5,4},{6,7},{7,6},{8,9},{9,8},{10,11... | collective-permute-start | bytes 393224 | tf_op jit(solution)/shard_map/ppermute | solution.py:42
  41.7 5.9 %collective-permute-start.20 = (bf16[16,4096]{1,0:T(8,128)(2,1)S(1)}, bf16[16,4096]{1,0:T(8,128)(2,1)S(1)}, u32[]{:S(2)}, u32[]{:S(2)}) collective-permute-start(bf16[16,4096]{1,0:T(8,128)(2,1)S(1)} %collective-permute-done.16.refs_18_), channel_id=1, source_target_pairs={{0,16},{1,17},{2,18},{3,19},{4,20},{5,21},{6,22},{7,23},{8,24},{9,... | collective-permute-start | bytes 393224 | tf_op jit(solution)/shard_map/ppermute | solution.py:42
  42.6 5.0 %collective-permute-start.17 = (bf16[16,4096]{1,0:T(8,128)(2,1)S(1)}, bf16[16,4096]{1,0:T(8,128)(2,1)S(1)}, u32[]{:S(2)}, u32[]{:S(2)}) collective-permute-start(bf16[16,4096]{1,0:T(8,128)(2,1)S(1)} %collective-permute-done.16.refs_18_), channel_id=1, source_target_pairs={{0,1},{1,0},{2,3},{3,2},{4,5},{5,4},{6,7},{7,6},{8,9},{9,8},{10,11... | collective-permute-start | bytes 393224 | tf_op jit(solution)/shard_map/ppermute | solution.py:42
  42.8 5.9 %collective-permute-start.12 = (bf16[16,4096]{1,0:T(8,128)(2,1)S(1)}, bf16[16,4096]{1,0:T(8,128)(2,1)S(1)}, u32[]{:S(2)}, u32[]{:S(2)}) collective-permute-start(bf16[16,4096]{1,0:T(8,128)(2,1)S(1)} %collective-permute-done.10.refs_12_), channel_id=1, source_target_pairs={{0,2},{1,3},{2,0},{3,1},{4,6},{5,7},{6,4},{7,5},{8,10},{9,11},{10,... | collective-permute-start | bytes 393224 | tf_op jit(solution)/shard_map/ppermute | solution.py:42
  44.5 4.2 %collective-permute-start.11 = (bf16[16,4096]{1,0:T(8,128)(2,1)S(1)}, bf16[16,4096]{1,0:T(8,128)(2,1)S(1)}, u32[]{:S(2)}, u32[]{:S(2)}) collective-permute-start(bf16[16,4096]{1,0:T(8,128)(2,1)S(1)} %collective-permute-done.10.refs_12_), channel_id=1, source_target_pairs={{0,1},{1,0},{2,3},{3,2},{4,5},{5,4},{6,7},{7,6},{8,9},{9,8},{10,11... | collective-permute-start | bytes 393224 | tf_op jit(solution)/shard_map/ppermute | solution.py:42
  44.7 20.7 %collective-permute-start.9 = (bf16[16,4096]{1,0:T(8,128)(2,1)S(1)}, bf16[16,4096]{1,0:T(8,128)(2,1)S(1)}, u32[]{:S(2)}, u32[]{:S(2)}) collective-permute-start(bf16[16,4096]{1,0:T(8,128)(2,1)S(1)} %collective-permute-done.8.refs_10_), channel_id=1, source_target_pairs={{0,1},{1,0},{2,3},{3,2},{4,5},{5,4},{6,7},{7,6},{8,9},{9,8},{10,11... | collective-permute-start | bytes 393224 | tf_op jit(solution)/shard_map/ppermute | solution.py:42
  47.6 17.9 %collective-permute-start.5 = (bf16[16,4096]{1,0:T(8,128)(2,1)S(1)}, bf16[16,4096]{1,0:T(8,128)(2,1)S(1)}, u32[]{:S(2)}, u32[]{:S(2)}) collective-permute-start(bf16[16,4096]{1,0:T(8,128)(2,1)S(1)} %collective-permute-done.4.refs_6_), channel_id=1, source_target_pairs={{0,1},{1,0},{2,3},{3,2},{4,5},{5,4},{6,7},{7,6},{8,9},{9,8},{10,11... | collective-permute-start | bytes 393224 | tf_op jit(solution)/shard_map/ppermute | solution.py:42
  47.6 17.9 %collective-permute-start.29 = (bf16[16,4096]{1,0:T(8,128)(2,1)S(1)}, bf16[16,4096]{1,0:T(8,128)(2,1)S(1)}, u32[]{:S(2)}, u32[]{:S(2)}) collective-permute-start(bf16[16,4096]{1,0:T(8,128)(2,1)S(1)} %collective-permute-done.28.refs_30_), channel_id=1, source_target_pairs={{0,1},{1,0},{2,3},{3,2},{4,5},{5,4},{6,7},{7,6},{8,9},{9,8},{10,11... | collective-permute-start | bytes 393224 | tf_op jit(solution)/shard_map/ppermute | solution.py:42
  48.7 16.8 %collective-permute-start.21 = (bf16[16,4096]{1,0:T(8,128)(2,1)S(1)}, bf16[16,4096]{1,0:T(8,128)(2,1)S(1)}, u32[]{:S(2)}, u32[]{:S(2)}) collective-permute-start(bf16[16,4096]{1,0:T(8,128)(2,1)S(1)} %collective-permute-done.20.refs_22_), channel_id=1, source_target_pairs={{0,1},{1,0},{2,3},{3,2},{4,5},{5,4},{6,7},{7,6},{8,9},{9,8},{10,11... | collective-permute-start | bytes 393224 | tf_op jit(solution)/shard_map/ppermute | solution.py:42
  48.7 16.8 %collective-permute-start.13 = (bf16[16,4096]{1,0:T(8,128)(2,1)S(1)}, bf16[16,4096]{1,0:T(8,128)(2,1)S(1)}, u32[]{:S(2)}, u32[]{:S(2)}) collective-permute-start(bf16[16,4096]{1,0:T(8,128)(2,1)S(1)} %collective-permute-done.12.refs_14_), channel_id=1, source_target_pairs={{0,1},{1,0},{2,3},{3,2},{4,5},{5,4},{6,7},{7,6},{8,9},{9,8},{10,11... | collective-permute-start | bytes 393224 | tf_op jit(solution)/shard_map/ppermute | solution.py:42

commit v2 on v1

v2 whole, which is shorter than its diff:
```python
import functools

import jax
import jax.numpy as jnp
from jax import lax
from jax.experimental import pallas as pl
from jax.experimental.pallas import tpu as pltpu
from jax.sharding import PartitionSpec as P

CORES = 2
XS = 2
GROUPS = 2
LANES = 128
MIB = 1024 * 1024
VMEM = pl.BlockSpec(memory_space=pltpu.VMEM)
NN = (((1,), (0,)), ((), ()))
NT = (((1,), (1,)), ((), ()))
TN = (((0,), (0,)), ((), ()))


def mxu(a, b, dims=NN):
    return lax.dot_general(a, b, dims, preferred_element_type=jnp.float32)


def halves(a):
    high = a.astype(jnp.bfloat16)
    return high, (a - high.astype(jnp.float32)).astype(jnp.bfloat16)


def place():
    t = lax.axis_index("train")
    return t // (XS * CORES), (t // CORES) % XS, t % CORES, lax.axis_index("group")


def hop(array, n_train, dz=0, dx=0, dc=0, dg=0):
    zs = n_train // (XS * CORES)
    perm = []
    for g in range(GROUPS):
        for t in range(n_train):
            z, x, c = t // (XS * CORES), (t // CORES) % XS, t % CORES
            to = (((z + dz) % zs) * XS + (x ^ dx)) * CORES + (c ^ dc)
            perm.append((g * n_train + t, (g ^ dg) * n_train + to))
    return lax.ppermute(array, ("group", "train"), perm)


def precond_kernel(slot, q_ref, in_ref, out_ref, eig_ref, piece_ref, wide_ref, tall_ref, even_ref):
    layer = (lax.axis_index("group") + slot) % GROUPS
    q_rows, width = piece_ref.shape
    rows = width // LANES
    p_in, p_out = in_ref.shape[1:]
    left = lax.broadcasted_iota(jnp.int32, (1, LANES), 1) < p_out

    eig = eig_ref[pl.ds(layer, 1), :]
    damping = 0.1 / width * jnp.sum(eig, axis=1, keepdims=True)
    for j in range(rows):
        pair = eig[:, j * LANES : (j + 1) * LANES]
        turned = pltpu.roll(pair, p_out, 1)
        even_ref[2 * j : 2 * j + 1, :] = jnp.where(left, pair, turned)
        even_ref[2 * j + 1 : 2 * j + 2, :] = jnp.where(left, turned, pair)
    scale = 1.0 / (even_ref[...] + damping)

    by_row = [in_ref[layer, pl.ds(p, rows, stride=2), :] for p in range(2)]
    back_left = jnp.concatenate(by_row, axis=0)
    fore_left = jnp.concatenate(by_row, axis=1)
    back_high, back_low = halves(back_left)
    fore_high, fore_low = halves(fore_left)
    fore = jnp.concatenate([fore_high, fore_high, fore_low], axis=0)
    back = jnp.concatenate([back_high, back_high, back_low], axis=1)

    basis = out_ref[layer]
    empty = jnp.zeros((p_out, p_out), jnp.bfloat16)

    def twice(a):
        return jnp.concatenate(
            [jnp.concatenate([a, empty], axis=1), jnp.concatenate([empty, a], axis=1)], axis=0
        )

    right_high, right_low = halves(basis)
    turned_high, turned_low = halves(basis.T)
    fore_right = jnp.concatenate([twice(right_high), twice(right_low)], axis=1)
    back_high, back_low = twice(turned_high), twice(turned_low)
    back_right = jnp.concatenate(
        [
            jnp.concatenate([back_high, back_low], axis=1),
            jnp.concatenate([back_high, jnp.zeros_like(back_low)], axis=1),
        ],
        axis=0,
    )

    flat = jnp.where(layer == 0, q_ref[:, 0, :].astype(jnp.float32), q_ref[:, 1, :].astype(jnp.float32))
    flat = flat.astype(jnp.bfloat16)
    stacked = jnp.concatenate([flat[:, j * LANES : (j + 1) * LANES] for j in range(rows)], axis=0)
    both = mxu(stacked, fore_right)
    wide_ref[...] = both[:, :LANES] + both[:, LANES:]
    by_query = jnp.concatenate([wide_ref[pl.ds(q, rows, stride=q_rows), :] for q in range(q_rows)], axis=1)
    high, low = halves(by_query)
    both = mxu(fore, jnp.concatenate([high, low, high], axis=0), TN)
    every = jnp.concatenate([left] * q_rows, axis=1)
    rotated = jnp.where(every, both[:p_in], both[p_in:])
    rotated = jnp.concatenate(
        [
            part + pltpu.roll(part, p_out, 1)
            for part in (rotated[:, q * LANES : (q + 1) * LANES] for q in range(q_rows))
        ],
        axis=1,
    )
    scaled = rotated * jnp.concatenate([scale] * q_rows, axis=1)
    high, low = halves(scaled)
    both = mxu(back, jnp.concatenate([high, low, high], axis=0))
    mixed = jnp.where(every, both[:rows], both[rows:])
    stacked = jnp.concatenate([mixed[:, q * LANES : (q + 1) * LANES] for q in range(q_rows)], axis=0)
    both = mxu(jnp.concatenate(halves(stacked), axis=1), back_right)
    tall_ref[...] = both[:, :LANES] + both[:, LANES:]
    for j in range(rows):
        block = tall_ref[pl.ds(j, q_rows, stride=rows), :]
        piece_ref[:, j * LANES : (j + 1) * LANES] = block.astype(jnp.bfloat16)


def precondition(slot, query_grads, basis_in, basis_out, eigvals):
    q_rows, _, width = query_grads.shape
    return pl.pallas_call(
        functools.partial(precond_kernel, slot),
        out_shape=jax.ShapeDtypeStruct((q_rows, width), jnp.bfloat16),
        in_specs=[VMEM] * 4,
        out_specs=VMEM,
        scratch_shapes=[
            pltpu.VMEM((q_rows * width // LANES, LANES), jnp.float32),
            pltpu.VMEM((q_rows * width // LANES, LANES), jnp.float32),
            pltpu.VMEM((2 * width // LANES, LANES), jnp.float32),
        ],
        compiler_params=pltpu.CompilerParams(vmem_limit_bytes=12 * MIB),
        cost_estimate=pl.CostEstimate(flops=10**9, bytes_accessed=4 * MIB, transcendentals=0),
        name="precond",
    )(query_grads, basis_in, basis_out, eigvals)


def split_kernel(t_ref, flat_ref):
    rows = 32
    width = t_ref.shape[2]

    @pl.loop(0, t_ref.shape[0] // rows)
    def _(i):
        at = pl.ds(pl.multiple_of(i * rows, rows), rows)
        for layer in range(t_ref.shape[1]):
            flat_ref[at, layer * width : (layer + 1) * width] = t_ref[at, layer, :]


def split_layers(train_grads):
    tr_rows, layers, width = train_grads.shape
    return pl.pallas_call(
        split_kernel,
        out_shape=jax.ShapeDtypeStruct((tr_rows, layers * width), jnp.bfloat16),
        in_specs=[VMEM],
        out_specs=VMEM,
        compiler_params=pltpu.CompilerParams(vmem_limit_bytes=20 * MIB),
        cost_estimate=pl.CostEstimate(flops=10**9, bytes_accessed=16 * MIB, transcendentals=0),
        name="split",
    )(train_grads)


def score_kernel(n_train, t_ref, *refs):
    pieces, out_ref = refs[:-1], refs[-1]
    zs = n_train // (XS * CORES)
    q_rows, width = pieces[0].shape
    n_query = n_train * q_rows
    z, x, c, g = place()
    depth = min(width, 1024)
    total = None
    for part in range(GROUPS):
        mine = pieces[part * n_train : (part + 1) * n_train]
        for at in range(0, width, depth):
            columns = pl.ds(pl.multiple_of((g + part) % GROUPS * width + at, depth), depth)
            block = jnp.concatenate([piece[:, at : at + depth] for piece in mine], axis=0)
            term = mxu(t_ref[:, columns], block, NT)
            total = term if total is None else total + term

    came = lax.broadcasted_iota(jnp.int32, (n_query, n_query), 0)
    query = lax.broadcasted_iota(jnp.int32, (n_query, n_query), 1)
    block = came // q_rows
    to_z = (z - block // (XS * CORES) + zs) % zs
    to_x = (x + block // CORES) % XS
    to_c = (c + block) % CORES
    goes = ((to_z * XS + to_x) * CORES + to_c) * q_rows + came % q_rows
    order = jnp.where(goes == query, 1.0, 0.0).astype(jnp.bfloat16)
    high, low = halves(total)
    lowest = (total - high.astype(jnp.float32) - low.astype(jnp.float32)).astype(jnp.bfloat16)
    out_ref[...] = mxu(high, order) + mxu(low, order) + mxu(lowest, order)


def per_device(n_train, train_grads, query_grads, basis_in, basis_out, eigvals):
    tr_rows = train_grads.shape[0]
    zs = n_train // (XS * CORES)
    operands = (query_grads, basis_in, basis_out, eigvals)
    mine = precondition(0, *operands)
    twin = precondition(1, *operands)
    flat_train = split_layers(train_grads)
    q_rows, width = mine.shape

    pieces = {}

    def keep(array, dz, dx, dg):
        pieces[dg, dz, dx, 0] = array
        pieces[dg, dz, dx, 1] = hop(array, n_train, dc=1)

    for dz in range(zs):
        own = hop(mine, n_train, dz=dz) if dz else mine
        over_x = hop(own, n_train, dx=1)
        over_g = hop(own, n_train, dg=1) if dz else twin
        corner = hop(over_g, n_train, dx=1) if dz % 2 else hop(over_x, n_train, dg=1)
        keep(own, dz, 0, 0)
        keep(over_x, dz, 1, 0)
        keep(over_g, dz, 0, 1)
        keep(corner, dz, 1, 1)

    n_query = n_train * q_rows
    ordered = [pieces[key] for key in sorted(pieces)]
    partial_scores = pl.pallas_call(
        functools.partial(score_kernel, n_train),
        out_shape=jax.ShapeDtypeStruct((tr_rows, n_query), jnp.float32),
        in_specs=[VMEM] * (1 + len(ordered)),
        out_specs=VMEM,
        compiler_params=pltpu.CompilerParams(vmem_limit_bytes=36 * MIB),
        cost_estimate=pl.CostEstimate(
            flops=4 * tr_rows * n_query * width, bytes_accessed=2 * width * (tr_rows + n_query), transcendentals=0
        ),
        name="scores",
    )(flat_train, *ordered)
    return lax.psum_scatter(partial_scores, "layer", scatter_dimension=1, tiled=True)


def solution(mesh):
    return jax.shard_map(
        functools.partial(per_device, mesh.shape["train"]),
        mesh=mesh,
        in_specs=(
            P(("group", "train"), "layer", None),
            P("train", "layer", None),
            P("layer", None, None),
            P("layer", None, None),
            P("layer", None),
        ),
        out_specs=P(("group", "train"), "layer"),
        check_vma=False,
    )
```

time: 78.2 us -> 72.6 us (0.928)
  Pallas kernels: 12.1 us -> 25.4 us
  local copies, waits for them, and re-layouts: 19 us -> 6.77 us
  matrix products: 5.41 us -> 0 us
  other arithmetic: 0.99 us -> 0 us
    pallas_call x1 -> x4, Pallas kernels: 12.1 us -> 25.4 us  [the longest x1 18.5 us: split_layers(): pl.pallas_call(split_kernel, out_shape=jax.ShapeDtypeStruct((tr_rows, lay...]
    unnamed x5 -> x10, local copies, waits for them, and re-layouts: 16.3 us -> 6.77 us
    dot_general x4 -> x0, matrix products: 5.41 us -> none  [the longest x2 3.3 us: precondition(): jnp.einsum('lai,qlab,lbj->qlij', basis_in, grads, basis_out, precision=hi...]
    reshape x2 -> x0, local copies, waits for them, and re-layouts: 2.23 us -> none  [the longest x1 1.33 us: precondition(): query_grads.astype(jnp.float32).reshape(q_rows, layers_here, p_in, p_out)]
    reduce_sum x1 -> x0, other arithmetic: 0.91 us -> none  [precondition(): damping = 0.1 * jnp.mean(eigvals, axis=1)]
  transfers between devices with their start and end apart: 30 -> 30, of which waited for: 8 -> 8; matrix products, arithmetic and copies ran while one was open for 21% -> 0% of each run, Pallas kernels for 0% -> 28%
where the time goes in v2:
time: 72.6 us; the launch traced here: 72.2 us
  Pallas kernels  25.4 us (35%)
  starting transfers between devices  25.3 us (35%)
  waiting for transfers between devices  14.8 us (20%)
  local copies, waits for them, and re-layouts  6.77 us (9%)
    ppermute x30, starting transfers between devices, hop(): return lax.ppermute(array, ('group', 'train'), perm)  25.3 us
    pallas_call x1, Pallas kernels, split_layers(): pl.pallas_call(split_kernel, out_shape=jax.ShapeDtypeStruct((tr_rows, lay...  18.5 us
    ppermute x30, waiting for transfers between devices, hop(): return lax.ppermute(array, ('group', 'train'), perm)  14.8 us
    unnamed x10, local copies, waits for them, and re-layouts  6.77 us
    pallas_call x1, Pallas kernels, per_device(): pl.pallas_call(functools.partial(score_kernel, n_train), out_shape=jax.Sh...  3.93 us
    pallas_call x2, Pallas kernels, precondition(): pl.pallas_call(functools.partial(precond_kernel, slot), out_shape=jax.Sha...  2.92 us
  transfers between devices with their start and end apart: 30, of which 8 were waited for; matrix products, arithmetic and copies ran while one was open for 0% of the time, Pallas kernels for 28%

profile of v2, /device:TPU:0, one launch (start us, length us, event | category | flops | bytes accessed | tf_op | source)
XLA Modules:
  0.0 72.2 jit_solution(3064121116768099799)
XLA Ops:
  0.0 0.9 %copy-done.1 = bf16[16,2,4096]{2,1,0:T(2,128)(2,1)S(1)} copy-done((bf16[16,2,4096]{2,1,0:T(2,128)(2,1)S(1)}, bf16[16,2,4096]{2,1,0:T(2,128)(2,1)}, u32[]{:S(2)}) %copy-start.1) | copy-done | bytes 262168
  1.0 0.8 %copy-done.2 = f32[2,64,64]{2,1,0:T(8,128)S(1)} copy-done((f32[2,64,64]{2,1,0:T(8,128)S(1)}, f32[2,64,64]{2,1,0:T(8,128)}, u32[]{:S(2)}) %copy-start.2) | copy-done | bytes 32792
  1.8 0.8 %copy-done.3 = f32[2,64,64]{2,1,0:T(8,128)S(1)} copy-done((f32[2,64,64]{2,1,0:T(8,128)S(1)}, f32[2,64,64]{2,1,0:T(8,128)}, u32[]{:S(2)}) %copy-start.3) | copy-done | bytes 32792
  2.6 0.8 %copy-done.4 = f32[2,4096]{1,0:T(2,128)S(1)} copy-done((f32[2,4096]{1,0:T(2,128)S(1)}, f32[2,4096]{1,0:T(2,128)}, u32[]{:S(2)}) %copy-start.4) | copy-done | bytes 32792
  3.4 1.5 %precond.3.refs_16_ = bf16[16,4096]{1,0:T(8,128)(2,1)S(1)} custom-call(bf16[16,2,4096]{2,1,0:T(2,128)(2,1)S(1)} %copy-done.1, f32[2,64,64]{2,1,0:T(8,128)S(1)} %copy-done.2, f32[2,64,64]{2,1,0:T(8,128)S(1)} %copy-done.3, f32[2,4096]{1,0:T(2,128)S(1)} %copy-done.4), custom_call_target="tpu_custom_call" | custom-call | flops 1000000000 | bytes 4194304 | tf_op jit(solution)/shard_map/precond/pallas_call | solution.py:121
  4.9 0.5 collective-permute-start.15
  5.4 1.5 %precond.2.refs_0_ = bf16[16,4096]{1,0:T(8,128)(2,1)S(1)} custom-call(bf16[16,2,4096]{2,1,0:T(2,128)(2,1)S(1)} %copy-done.1, f32[2,64,64]{2,1,0:T(8,128)S(1)} %copy-done.2, f32[2,64,64]{2,1,0:T(8,128)S(1)} %copy-done.3, f32[2,4096]{1,0:T(2,128)S(1)} %copy-done.4), custom_call_target="tpu_custom_call" | custom-call | flops 1000000000 | bytes 4194304 | tf_op jit(solution)/shard_map/precond/pallas_call | solution.py:121
  6.8 4.7 %collective-permute-start.11 = (bf16[16,4096]{1,0:T(8,128)(2,1)S(1)}, bf16[16,4096]{1,0:T(8,128)(2,1)S(1)}, u32[]{:S(2)}, u32[]{:S(2)}) collective-permute-start(bf16[16,4096]{1,0:T(8,128)(2,1)S(1)} %precond.2.refs_0_), channel_id=1, source_target_pairs={{0,12},{1,13},{2,14},{3,15},{4,0},{5,1},{6,2},{7,3},{8,4},{9,5},{1... | collective-permute-start | bytes 393224 | tf_op jit(solution)/shard_map/ppermute | solution.py:43
  11.5 0.0 collective-permute-start.7
  11.5 1.0 %collective-permute-start.3 = (bf16[16,4096]{1,0:T(8,128)(2,1)S(1)}, bf16[16,4096]{1,0:T(8,128)(2,1)S(1)}, u32[]{:S(2)}, u32[]{:S(2)}) collective-permute-start(bf16[16,4096]{1,0:T(8,128)(2,1)S(1)} %precond.2.refs_0_), channel_id=1, source_target_pairs={{0,4},{1,5},{2,6},{3,7},{4,8},{5,9},{6,10},{7,11},{8,12},{9,13},{1... | collective-permute-start | bytes 393224 | tf_op jit(solution)/shard_map/ppermute | solution.py:43
  12.5 1.5 %collective-permute-start.1 = (bf16[16,4096]{1,0:T(8,128)(2,1)S(1)}, bf16[16,4096]{1,0:T(8,128)(2,1)S(1)}, u32[]{:S(2)}, u32[]{:S(2)}) collective-permute-start(bf16[16,4096]{1,0:T(8,128)(2,1)S(1)} %precond.2.refs_0_), channel_id=1, source_target_pairs={{0,2},{1,3},{2,0},{3,1},{4,6},{5,7},{6,4},{7,5},{8,10},{9,11},{10,... | collective-permute-start | bytes 393224 | tf_op jit(solution)/shard_map/ppermute | solution.py:43
  14.0 0.0 collective-permute-done.15.refs_17_
  14.0 0.0 collective-permute-start
  14.0 1.4 %collective-permute-done.11.refs_12_ = bf16[16,4096]{1,0:T(8,128)(2,1)S(1)} collective-permute-done((bf16[16,4096]{1,0:T(8,128)(2,1)S(1)}, bf16[16,4096]{1,0:T(8,128)(2,1)S(1)}, u32[]{:S(2)}, u32[]{:S(2)}) %collective-permute-start.11) | collective-permute-done | bytes 131104 | tf_op jit(solution)/shard_map/ppermute | solution.py:43
  15.4 1.5 %collective-permute-start.26 = (bf16[16,4096]{1,0:T(8,128)(2,1)S(1)}, bf16[16,4096]{1,0:T(8,128)(2,1)S(1)}, u32[]{:S(2)}, u32[]{:S(2)}) collective-permute-start(bf16[16,4096]{1,0:T(8,128)(2,1)S(1)} %collective-permute-done.11.refs_12_), channel_id=1, source_target_pairs={{0,16},{1,17},{2,18},{3,19},{4,20},{5,21},{6,22},{7,23},{8,24},{9,... | collective-permute-start | bytes 393224 | tf_op jit(solution)/shard_map/ppermute | solution.py:43
  16.9 6.7 %collective-permute-done.7.refs_8_ = bf16[16,4096]{1,0:T(8,128)(2,1)S(1)} collective-permute-done((bf16[16,4096]{1,0:T(8,128)(2,1)S(1)}, bf16[16,4096]{1,0:T(8,128)(2,1)S(1)}, u32[]{:S(2)}, u32[]{:S(2)}) %collective-permute-start.7) | collective-permute-done | bytes 131104 | tf_op jit(solution)/shard_map/ppermute | solution.py:43
  23.6 1.5 %collective-permute-start.13 = (bf16[16,4096]{1,0:T(8,128)(2,1)S(1)}, bf16[16,4096]{1,0:T(8,128)(2,1)S(1)}, u32[]{:S(2)}, u32[]{:S(2)}) collective-permute-start(bf16[16,4096]{1,0:T(8,128)(2,1)S(1)} %collective-permute-done.11.refs_12_), channel_id=1, source_target_pairs={{0,2},{1,3},{2,0},{3,1},{4,6},{5,7},{6,4},{7,5},{8,10},{9,11},{10,... | collective-permute-start | bytes 393224 | tf_op jit(solution)/shard_map/ppermute | solution.py:43
  25.1 0.0 collective-permute-done.3.refs_4_
  25.1 0.0 collective-permute-start.12
  25.1 0.0 collective-permute-done.1.refs_2_
  25.1 1.6 %collective-permute-start.22 = (bf16[16,4096]{1,0:T(8,128)(2,1)S(1)}, bf16[16,4096]{1,0:T(8,128)(2,1)S(1)}, u32[]{:S(2)}, u32[]{:S(2)}) collective-permute-start(bf16[16,4096]{1,0:T(8,128)(2,1)S(1)} %collective-permute-done.7.refs_8_), channel_id=1, source_target_pairs={{0,16},{1,17},{2,18},{3,19},{4,20},{5,21},{6,22},{7,23},{8,24},{9,... | collective-permute-start | bytes 393224 | tf_op jit(solution)/shard_map/ppermute | solution.py:43
  26.7 0.0 collective-permute-done.refs_1_
  26.7 0.5 collective-permute-start.9
  27.3 0.0 collective-permute-done.26.refs_28_
  27.3 0.0 collective-permute-start.8
  27.3 1.4 %collective-permute-done.13.refs_14_ = bf16[16,4096]{1,0:T(8,128)(2,1)S(1)} collective-permute-done((bf16[16,4096]{1,0:T(8,128)(2,1)S(1)}, bf16[16,4096]{1,0:T(8,128)(2,1)S(1)}, u32[]{:S(2)}, u32[]{:S(2)}) %collective-permute-start.13) | collective-permute-done | bytes 131104 | tf_op jit(solution)/shard_map/ppermute | solution.py:43
  28.7 1.7 %collective-permute-start.18 = (bf16[16,4096]{1,0:T(8,128)(2,1)S(1)}, bf16[16,4096]{1,0:T(8,128)(2,1)S(1)}, u32[]{:S(2)}, u32[]{:S(2)}) collective-permute-start(bf16[16,4096]{1,0:T(8,128)(2,1)S(1)} %collective-permute-done.3.refs_4_), channel_id=1, source_target_pairs={{0,16},{1,17},{2,18},{3,19},{4,20},{5,21},{6,22},{7,23},{8,24},{9,... | collective-permute-start | bytes 393224 | tf_op jit(solution)/shard_map/ppermute | solution.py:43
  30.4 0.0 collective-permute-done.12.refs_13_
  30.4 2.5 %collective-permute-start.5 = (bf16[16,4096]{1,0:T(8,128)(2,1)S(1)}, bf16[16,4096]{1,0:T(8,128)(2,1)S(1)}, u32[]{:S(2)}, u32[]{:S(2)}) collective-permute-start(bf16[16,4096]{1,0:T(8,128)(2,1)S(1)} %collective-permute-done.3.refs_4_), channel_id=1, source_target_pairs={{0,2},{1,3},{2,0},{3,1},{4,6},{5,7},{6,4},{7,5},{8,10},{9,11},{10,... | collective-permute-start | bytes 393224 | tf_op jit(solution)/shard_map/ppermute | solution.py:43
  32.9 0.0 collective-permute-done.22.refs_24_
  32.9 0.0 collective-permute-start.4
  32.9 0.2 collective-permute-done.9.refs_10_
  33.1 0.5 collective-permute-start.16
  33.6 0.0 collective-permute-done.8.refs_9_
  33.6 0.3 collective-permute-done.18.refs_20_
  33.9 2.8 %collective-permute-start.28 = (bf16[16,4096]{1,0:T(8,128)(2,1)S(1)}, bf16[16,4096]{1,0:T(8,128)(2,1)S(1)}, u32[]{:S(2)}, u32[]{:S(2)}) collective-permute-start(bf16[16,4096]{1,0:T(8,128)(2,1)S(1)} %collective-permute-done.26.refs_28_), channel_id=1, source_target_pairs={{0,2},{1,3},{2,0},{3,1},{4,6},{5,7},{6,4},{7,5},{8,10},{9,11},{10,... | collective-permute-start | bytes 393224 | tf_op jit(solution)/shard_map/ppermute | solution.py:43
  36.7 0.0 collective-permute-done.5.refs_6_
  36.7 0.0 collective-permute-start.27
  36.7 0.0 collective-permute-done.4.refs_5_
  36.7 0.5 collective-permute-start.14
  37.2 1.6 %collective-permute-done.16.refs_18_ = bf16[16,4096]{1,0:T(8,128)(2,1)S(1)} collective-permute-done((bf16[16,4096]{1,0:T(8,128)(2,1)S(1)}, bf16[16,4096]{1,0:T(8,128)(2,1)S(1)}, u32[]{:S(2)}, u32[]{:S(2)}) %collective-permute-start.16) | collective-permute-done | bytes 131104 | tf_op jit(solution)/shard_map/ppermute | solution.py:43
  38.8 0.0 collective-permute-start.23
  38.8 0.9 %collective-permute-start.24 = (bf16[16,4096]{1,0:T(8,128)(2,1)S(1)}, bf16[16,4096]{1,0:T(8,128)(2,1)S(1)}, u32[]{:S(2)}, u32[]{:S(2)}) collective-permute-start(bf16[16,4096]{1,0:T(8,128)(2,1)S(1)} %collective-permute-done.9.refs_10_), channel_id=1, source_target_pairs={{0,16},{1,17},{2,18},{3,19},{4,20},{5,21},{6,22},{7,23},{8,24},{9,... | collective-permute-start | bytes 393224 | tf_op jit(solution)/shard_map/ppermute | solution.py:43
  39.8 0.2 collective-permute-start.10
  39.9 0.0 collective-permute-done.27.refs_29_
  40.0 1.7 %collective-permute-start.20 = (bf16[16,4096]{1,0:T(8,128)(2,1)S(1)}, bf16[16,4096]{1,0:T(8,128)(2,1)S(1)}, u32[]{:S(2)}, u32[]{:S(2)}) collective-permute-start(bf16[16,4096]{1,0:T(8,128)(2,1)S(1)} %collective-permute-done.18.refs_20_), channel_id=1, source_target_pairs={{0,2},{1,3},{2,0},{3,1},{4,6},{5,7},{6,4},{7,5},{8,10},{9,11},{10,... | collective-permute-start | bytes 393224 | tf_op jit(solution)/shard_map/ppermute | solution.py:43
  41.7 0.0 collective-permute-done.14.refs_15_
  41.7 0.2 collective-permute-start.19
  41.9 0.0 collective-permute-done.23.refs_25_
  41.9 0.3 collective-permute-start.6
  42.2 2.5 %collective-permute-done.24.refs_26_ = bf16[16,4096]{1,0:T(8,128)(2,1)S(1)} collective-permute-done((bf16[16,4096]{1,0:T(8,128)(2,1)S(1)}, bf16[16,4096]{1,0:T(8,128)(2,1)S(1)}, u32[]{:S(2)}, u32[]{:S(2)}) %collective-permute-start.24) | collective-permute-done | bytes 131104 | tf_op jit(solution)/shard_map/ppermute | solution.py:43
  44.8 0.0 collective-permute-start.17
  44.8 0.0 collective-permute-done.10.refs_11_
  44.8 0.5 collective-permute-start.29
  45.3 0.6 collective-permute-done.20.refs_22_
  45.8 0.0 collective-permute-start.25
  45.9 0.0 collective-permute-done.19.refs_21_
  45.9 0.5 collective-permute-start.21
  46.4 3.4 %copy-done = bf16[512,2,4096]{2,1,0:T(2,128)(2,1)S(1)} copy-done((bf16[512,2,4096]{2,1,0:T(2,128)(2,1)S(1)}, bf16[512,2,4096]{2,1,0:T(2,128)(2,1)}, u32[]{:S(2)}) %copy-start) | copy-done | bytes 8388632
  49.7 18.5 %split.1.t_ref = bf16[512,8192]{1,0:T(8,128)(2,1)S(1)} custom-call(bf16[512,2,4096]{2,1,0:T(2,128)(2,1)S(1)} %copy-done), custom_call_target="tpu_custom_call" | custom-call | flops 1000000000 | bytes 16777216 | tf_op jit(solution)/shard_map/split/pallas_call | solution.py:150
  68.3 0.0 collective-permute-done.17.refs_19_
  68.3 0.0 collective-permute-done.29.refs_31_
  68.3 0.0 collective-permute-done.21.refs_23_
  68.3 3.9 %scores.1 = f32[512,256]{1,0:T(8,128)} custom-call(bf16[512,8192]{1,0:T(8,128)(2,1)S(1)} %split.1.t_ref, bf16[16,4096]{1,0:T(8,128)(2,1)S(1)} %precond.2.refs_0_, bf16[16,4096]{1,0:T(8,128)(2,1)S(1)} %collective-permute-done.refs_1_, bf16[16,4096]{1,0:T(8,128)(2,1)S(1)} %collective-permute-done.1.refs_2_, ...), custom_call_target="tpu_custom_call" | custom-call | flops 2147483648 | bytes 6291456 | tf_op jit(solution)/shard_map/scores/pallas_call | solution.py:217
  (10 shorter events, 0.0 us)
Async XLA Ops:
  0.0 0.9 %copy-start.1 = (bf16[16,2,4096]{2,1,0:T(2,128)(2,1)S(1)}, bf16[16,2,4096]{2,1,0:T(2,128)(2,1)}, u32[]{:S(2)}) copy-start(bf16[16,2,4096]{2,1,0:T(2,128)(2,1)} %q_ref.3) | copy-start | bytes 786436
  1.0 0.8 %copy-start.2 = (f32[2,64,64]{2,1,0:T(8,128)S(1)}, f32[2,64,64]{2,1,0:T(8,128)}, u32[]{:S(2)}) copy-start(f32[2,64,64]{2,1,0:T(8,128)} %in_ref.3) | copy-start | bytes 98308
  1.8 0.8 %copy-start.3 = (f32[2,64,64]{2,1,0:T(8,128)S(1)}, f32[2,64,64]{2,1,0:T(8,128)}, u32[]{:S(2)}) copy-start(f32[2,64,64]{2,1,0:T(8,128)} %out_ref.3) | copy-start | bytes 98308
  2.6 0.8 %copy-start.4 = (f32[2,4096]{1,0:T(2,128)S(1)}, f32[2,4096]{1,0:T(2,128)}, u32[]{:S(2)}) copy-start(f32[2,4096]{1,0:T(2,128)} %eig_ref.3) | copy-start | bytes 98308
  4.9 9.2 %collective-permute-start.15 = (bf16[16,4096]{1,0:T(8,128)(2,1)S(1)}, bf16[16,4096]{1,0:T(8,128)(2,1)S(1)}, u32[]{:S(2)}, u32[]{:S(2)}) collective-permute-start(bf16[16,4096]{1,0:T(8,128)(2,1)S(1)} %precond.3.refs_16_), channel_id=1, source_target_pairs={{0,1},{1,0},{2,3},{3,2},{4,5},{5,4},{6,7},{7,6},{8,9},{9,8},{10,11... | collective-permute-start | bytes 393224 | tf_op jit(solution)/shard_map/ppermute | solution.py:43
  6.8 8.6 %collective-permute-start.11 = (bf16[16,4096]{1,0:T(8,128)(2,1)S(1)}, bf16[16,4096]{1,0:T(8,128)(2,1)S(1)}, u32[]{:S(2)}, u32[]{:S(2)}) collective-permute-start(bf16[16,4096]{1,0:T(8,128)(2,1)S(1)} %precond.2.refs_0_), channel_id=1, source_target_pairs={{0,12},{1,13},{2,14},{3,15},{4,0},{5,1},{6,2},{7,3},{8,4},{9,5},{1... | collective-permute-start | bytes 393224 | tf_op jit(solution)/shard_map/ppermute | solution.py:43
  11.5 12.1 %collective-permute-start.7 = (bf16[16,4096]{1,0:T(8,128)(2,1)S(1)}, bf16[16,4096]{1,0:T(8,128)(2,1)S(1)}, u32[]{:S(2)}, u32[]{:S(2)}) collective-permute-start(bf16[16,4096]{1,0:T(8,128)(2,1)S(1)} %precond.2.refs_0_), channel_id=1, source_target_pairs={{0,8},{1,9},{2,10},{3,11},{4,12},{5,13},{6,14},{7,15},{8,0},{9,1},... | collective-permute-start | bytes 393224 | tf_op jit(solution)/shard_map/ppermute | solution.py:43
  11.5 13.6 %collective-permute-start.3 = (bf16[16,4096]{1,0:T(8,128)(2,1)S(1)}, bf16[16,4096]{1,0:T(8,128)(2,1)S(1)}, u32[]{:S(2)}, u32[]{:S(2)}) collective-permute-start(bf16[16,4096]{1,0:T(8,128)(2,1)S(1)} %precond.2.refs_0_), channel_id=1, source_target_pairs={{0,4},{1,5},{2,6},{3,7},{4,8},{5,9},{6,10},{7,11},{8,12},{9,13},{1... | collective-permute-start | bytes 393224 | tf_op jit(solution)/shard_map/ppermute | solution.py:43
  12.5 12.6 %collective-permute-start.1 = (bf16[16,4096]{1,0:T(8,128)(2,1)S(1)}, bf16[16,4096]{1,0:T(8,128)(2,1)S(1)}, u32[]{:S(2)}, u32[]{:S(2)}) collective-permute-start(bf16[16,4096]{1,0:T(8,128)(2,1)S(1)} %precond.2.refs_0_), channel_id=1, source_target_pairs={{0,2},{1,3},{2,0},{3,1},{4,6},{5,7},{6,4},{7,5},{8,10},{9,11},{10,... | collective-permute-start | bytes 393224 | tf_op jit(solution)/shard_map/ppermute | solution.py:43
  14.0 12.7 %collective-permute-start = (bf16[16,4096]{1,0:T(8,128)(2,1)S(1)}, bf16[16,4096]{1,0:T(8,128)(2,1)S(1)}, u32[]{:S(2)}, u32[]{:S(2)}) collective-permute-start(bf16[16,4096]{1,0:T(8,128)(2,1)S(1)} %precond.2.refs_0_), channel_id=1, source_target_pairs={{0,1},{1,0},{2,3},{3,2},{4,5},{5,4},{6,7},{7,6},{8,9},{9,8},{10,11... | collective-permute-start | bytes 393224 | tf_op jit(solution)/shard_map/ppermute | solution.py:43
  15.4 11.9 %collective-permute-start.26 = (bf16[16,4096]{1,0:T(8,128)(2,1)S(1)}, bf16[16,4096]{1,0:T(8,128)(2,1)S(1)}, u32[]{:S(2)}, u32[]{:S(2)}) collective-permute-start(bf16[16,4096]{1,0:T(8,128)(2,1)S(1)} %collective-permute-done.11.refs_12_), channel_id=1, source_target_pairs={{0,16},{1,17},{2,18},{3,19},{4,20},{5,21},{6,22},{7,23},{8,24},{9,... | collective-permute-start | bytes 393224 | tf_op jit(solution)/shard_map/ppermute | solution.py:43
  23.6 5.1 %collective-permute-start.13 = (bf16[16,4096]{1,0:T(8,128)(2,1)S(1)}, bf16[16,4096]{1,0:T(8,128)(2,1)S(1)}, u32[]{:S(2)}, u32[]{:S(2)}) collective-permute-start(bf16[16,4096]{1,0:T(8,128)(2,1)S(1)} %collective-permute-done.11.refs_12_), channel_id=1, source_target_pairs={{0,2},{1,3},{2,0},{3,1},{4,6},{5,7},{6,4},{7,5},{8,10},{9,11},{10,... | collective-permute-start | bytes 393224 | tf_op jit(solution)/shard_map/ppermute | solution.py:43
  25.1 5.3 %collective-permute-start.12 = (bf16[16,4096]{1,0:T(8,128)(2,1)S(1)}, bf16[16,4096]{1,0:T(8,128)(2,1)S(1)}, u32[]{:S(2)}, u32[]{:S(2)}) collective-permute-start(bf16[16,4096]{1,0:T(8,128)(2,1)S(1)} %collective-permute-done.11.refs_12_), channel_id=1, source_target_pairs={{0,1},{1,0},{2,3},{3,2},{4,5},{5,4},{6,7},{7,6},{8,9},{9,8},{10,11... | collective-permute-start | bytes 393224 | tf_op jit(solution)/shard_map/ppermute | solution.py:43
  25.1 7.8 %collective-permute-start.22 = (bf16[16,4096]{1,0:T(8,128)(2,1)S(1)}, bf16[16,4096]{1,0:T(8,128)(2,1)S(1)}, u32[]{:S(2)}, u32[]{:S(2)}) collective-permute-start(bf16[16,4096]{1,0:T(8,128)(2,1)S(1)} %collective-permute-done.7.refs_8_), channel_id=1, source_target_pairs={{0,16},{1,17},{2,18},{3,19},{4,20},{5,21},{6,22},{7,23},{8,24},{9,... | collective-permute-start | bytes 393224 | tf_op jit(solution)/shard_map/ppermute | solution.py:43
  26.7 6.3 %collective-permute-start.9 = (bf16[16,4096]{1,0:T(8,128)(2,1)S(1)}, bf16[16,4096]{1,0:T(8,128)(2,1)S(1)}, u32[]{:S(2)}, u32[]{:S(2)}) collective-permute-start(bf16[16,4096]{1,0:T(8,128)(2,1)S(1)} %collective-permute-done.7.refs_8_), channel_id=1, source_target_pairs={{0,2},{1,3},{2,0},{3,1},{4,6},{5,7},{6,4},{7,5},{8,10},{9,11},{10,... | collective-permute-start | bytes 393224 | tf_op jit(solution)/shard_map/ppermute | solution.py:43
  27.3 6.3 %collective-permute-start.8 = (bf16[16,4096]{1,0:T(8,128)(2,1)S(1)}, bf16[16,4096]{1,0:T(8,128)(2,1)S(1)}, u32[]{:S(2)}, u32[]{:S(2)}) collective-permute-start(bf16[16,4096]{1,0:T(8,128)(2,1)S(1)} %collective-permute-done.7.refs_8_), channel_id=1, source_target_pairs={{0,1},{1,0},{2,3},{3,2},{4,5},{5,4},{6,7},{7,6},{8,9},{9,8},{10,11... | collective-permute-start | bytes 393224 | tf_op jit(solution)/shard_map/ppermute | solution.py:43
  28.7 5.2 %collective-permute-start.18 = (bf16[16,4096]{1,0:T(8,128)(2,1)S(1)}, bf16[16,4096]{1,0:T(8,128)(2,1)S(1)}, u32[]{:S(2)}, u32[]{:S(2)}) collective-permute-start(bf16[16,4096]{1,0:T(8,128)(2,1)S(1)} %collective-permute-done.3.refs_4_), channel_id=1, source_target_pairs={{0,16},{1,17},{2,18},{3,19},{4,20},{5,21},{6,22},{7,23},{8,24},{9,... | collective-permute-start | bytes 393224 | tf_op jit(solution)/shard_map/ppermute | solution.py:43
  30.4 6.3 %collective-permute-start.5 = (bf16[16,4096]{1,0:T(8,128)(2,1)S(1)}, bf16[16,4096]{1,0:T(8,128)(2,1)S(1)}, u32[]{:S(2)}, u32[]{:S(2)}) collective-permute-start(bf16[16,4096]{1,0:T(8,128)(2,1)S(1)} %collective-permute-done.3.refs_4_), channel_id=1, source_target_pairs={{0,2},{1,3},{2,0},{3,1},{4,6},{5,7},{6,4},{7,5},{8,10},{9,11},{10,... | collective-permute-start | bytes 393224 | tf_op jit(solution)/shard_map/ppermute | solution.py:43
  32.9 3.8 %collective-permute-start.4 = (bf16[16,4096]{1,0:T(8,128)(2,1)S(1)}, bf16[16,4096]{1,0:T(8,128)(2,1)S(1)}, u32[]{:S(2)}, u32[]{:S(2)}) collective-permute-start(bf16[16,4096]{1,0:T(8,128)(2,1)S(1)} %collective-permute-done.3.refs_4_), channel_id=1, source_target_pairs={{0,1},{1,0},{2,3},{3,2},{4,5},{5,4},{6,7},{7,6},{8,9},{9,8},{10,11... | collective-permute-start | bytes 393224 | tf_op jit(solution)/shard_map/ppermute | solution.py:43
  33.1 5.8 %collective-permute-start.16 = (bf16[16,4096]{1,0:T(8,128)(2,1)S(1)}, bf16[16,4096]{1,0:T(8,128)(2,1)S(1)}, u32[]{:S(2)}, u32[]{:S(2)}) collective-permute-start(bf16[16,4096]{1,0:T(8,128)(2,1)S(1)} %collective-permute-done.1.refs_2_), channel_id=1, source_target_pairs={{0,16},{1,17},{2,18},{3,19},{4,20},{5,21},{6,22},{7,23},{8,24},{9,... | collective-permute-start | bytes 393224 | tf_op jit(solution)/shard_map/ppermute | solution.py:43
  33.6 5.2 %collective-permute-start.2 = (bf16[16,4096]{1,0:T(8,128)(2,1)S(1)}, bf16[16,4096]{1,0:T(8,128)(2,1)S(1)}, u32[]{:S(2)}, u32[]{:S(2)}) collective-permute-start(bf16[16,4096]{1,0:T(8,128)(2,1)S(1)} %collective-permute-done.1.refs_2_), channel_id=1, source_target_pairs={{0,1},{1,0},{2,3},{3,2},{4,5},{5,4},{6,7},{7,6},{8,9},{9,8},{10,11... | collective-permute-start | bytes 393224 | tf_op jit(solution)/shard_map/ppermute | solution.py:43
  33.9 5.9 %collective-permute-start.28 = (bf16[16,4096]{1,0:T(8,128)(2,1)S(1)}, bf16[16,4096]{1,0:T(8,128)(2,1)S(1)}, u32[]{:S(2)}, u32[]{:S(2)}) collective-permute-start(bf16[16,4096]{1,0:T(8,128)(2,1)S(1)} %collective-permute-done.26.refs_28_), channel_id=1, source_target_pairs={{0,2},{1,3},{2,0},{3,1},{4,6},{5,7},{6,4},{7,5},{8,10},{9,11},{10,... | collective-permute-start | bytes 393224 | tf_op jit(solution)/shard_map/ppermute | solution.py:43
  36.7 3.2 %collective-permute-start.27 = (bf16[16,4096]{1,0:T(8,128)(2,1)S(1)}, bf16[16,4096]{1,0:T(8,128)(2,1)S(1)}, u32[]{:S(2)}, u32[]{:S(2)}) collective-permute-start(bf16[16,4096]{1,0:T(8,128)(2,1)S(1)} %collective-permute-done.26.refs_28_), channel_id=1, source_target_pairs={{0,1},{1,0},{2,3},{3,2},{4,5},{5,4},{6,7},{7,6},{8,9},{9,8},{10,11... | collective-permute-start | bytes 393224 | tf_op jit(solution)/shard_map/ppermute | solution.py:43
  36.7 5.0 %collective-permute-start.14 = (bf16[16,4096]{1,0:T(8,128)(2,1)S(1)}, bf16[16,4096]{1,0:T(8,128)(2,1)S(1)}, u32[]{:S(2)}, u32[]{:S(2)}) collective-permute-start(bf16[16,4096]{1,0:T(8,128)(2,1)S(1)} %collective-permute-done.13.refs_14_), channel_id=1, source_target_pairs={{0,1},{1,0},{2,3},{3,2},{4,5},{5,4},{6,7},{7,6},{8,9},{9,8},{10,11... | collective-permute-start | bytes 393224 | tf_op jit(solution)/shard_map/ppermute | solution.py:43
  38.8 3.1 %collective-permute-start.23 = (bf16[16,4096]{1,0:T(8,128)(2,1)S(1)}, bf16[16,4096]{1,0:T(8,128)(2,1)S(1)}, u32[]{:S(2)}, u32[]{:S(2)}) collective-permute-start(bf16[16,4096]{1,0:T(8,128)(2,1)S(1)} %collective-permute-done.22.refs_24_), channel_id=1, source_target_pairs={{0,1},{1,0},{2,3},{3,2},{4,5},{5,4},{6,7},{7,6},{8,9},{9,8},{10,11... | collective-permute-start | bytes 393224 | tf_op jit(solution)/shard_map/ppermute | solution.py:43
  38.8 5.9 %collective-permute-start.24 = (bf16[16,4096]{1,0:T(8,128)(2,1)S(1)}, bf16[16,4096]{1,0:T(8,128)(2,1)S(1)}, u32[]{:S(2)}, u32[]{:S(2)}) collective-permute-start(bf16[16,4096]{1,0:T(8,128)(2,1)S(1)} %collective-permute-done.9.refs_10_), channel_id=1, source_target_pairs={{0,16},{1,17},{2,18},{3,19},{4,20},{5,21},{6,22},{7,23},{8,24},{9,... | collective-permute-start | bytes 393224 | tf_op jit(solution)/shard_map/ppermute | solution.py:43
  39.8 5.0 %collective-permute-start.10 = (bf16[16,4096]{1,0:T(8,128)(2,1)S(1)}, bf16[16,4096]{1,0:T(8,128)(2,1)S(1)}, u32[]{:S(2)}, u32[]{:S(2)}) collective-permute-start(bf16[16,4096]{1,0:T(8,128)(2,1)S(1)} %collective-permute-done.9.refs_10_), channel_id=1, source_target_pairs={{0,1},{1,0},{2,3},{3,2},{4,5},{5,4},{6,7},{7,6},{8,9},{9,8},{10,11... | collective-permute-start | bytes 393224 | tf_op jit(solution)/shard_map/ppermute | solution.py:43
  40.0 5.9 %collective-permute-start.20 = (bf16[16,4096]{1,0:T(8,128)(2,1)S(1)}, bf16[16,4096]{1,0:T(8,128)(2,1)S(1)}, u32[]{:S(2)}, u32[]{:S(2)}) collective-permute-start(bf16[16,4096]{1,0:T(8,128)(2,1)S(1)} %collective-permute-done.18.refs_20_), channel_id=1, source_target_pairs={{0,2},{1,3},{2,0},{3,1},{4,6},{5,7},{6,4},{7,5},{8,10},{9,11},{10,... | collective-permute-start | bytes 393224 | tf_op jit(solution)/shard_map/ppermute | solution.py:43
  41.7 4.2 %collective-permute-start.19 = (bf16[16,4096]{1,0:T(8,128)(2,1)S(1)}, bf16[16,4096]{1,0:T(8,128)(2,1)S(1)}, u32[]{:S(2)}, u32[]{:S(2)}) collective-permute-start(bf16[16,4096]{1,0:T(8,128)(2,1)S(1)} %collective-permute-done.18.refs_20_), channel_id=1, source_target_pairs={{0,1},{1,0},{2,3},{3,2},{4,5},{5,4},{6,7},{7,6},{8,9},{9,8},{10,11... | collective-permute-start | bytes 393224 | tf_op jit(solution)/shard_map/ppermute | solution.py:43
  41.9 26.3 %collective-permute-start.6 = (bf16[16,4096]{1,0:T(8,128)(2,1)S(1)}, bf16[16,4096]{1,0:T(8,128)(2,1)S(1)}, u32[]{:S(2)}, u32[]{:S(2)}) collective-permute-start(bf16[16,4096]{1,0:T(8,128)(2,1)S(1)} %collective-permute-done.5.refs_6_), channel_id=1, source_target_pairs={{0,1},{1,0},{2,3},{3,2},{4,5},{5,4},{6,7},{7,6},{8,9},{9,8},{10,11... | collective-permute-start | bytes 393224 | tf_op jit(solution)/shard_map/ppermute | solution.py:43
  44.8 23.5 %collective-permute-start.17 = (bf16[16,4096]{1,0:T(8,128)(2,1)S(1)}, bf16[16,4096]{1,0:T(8,128)(2,1)S(1)}, u32[]{:S(2)}, u32[]{:S(2)}) collective-permute-start(bf16[16,4096]{1,0:T(8,128)(2,1)S(1)} %collective-permute-done.16.refs_18_), channel_id=1, source_target_pairs={{0,1},{1,0},{2,3},{3,2},{4,5},{5,4},{6,7},{7,6},{8,9},{9,8},{10,11... | collective-permute-start | bytes 393224 | tf_op jit(solution)/shard_map/ppermute | solution.py:43
  44.8 23.5 %collective-permute-start.29 = (bf16[16,4096]{1,0:T(8,128)(2,1)S(1)}, bf16[16,4096]{1,0:T(8,128)(2,1)S(1)}, u32[]{:S(2)}, u32[]{:S(2)}) collective-permute-start(bf16[16,4096]{1,0:T(8,128)(2,1)S(1)} %collective-permute-done.28.refs_30_), channel_id=1, source_target_pairs={{0,1},{1,0},{2,3},{3,2},{4,5},{5,4},{6,7},{7,6},{8,9},{9,8},{10,11... | collective-permute-start | bytes 393224 | tf_op jit(solution)/shard_map/ppermute | solution.py:43
  45.8 22.4 %collective-permute-start.25 = (bf16[16,4096]{1,0:T(8,128)(2,1)S(1)}, bf16[16,4096]{1,0:T(8,128)(2,1)S(1)}, u32[]{:S(2)}, u32[]{:S(2)}) collective-permute-start(bf16[16,4096]{1,0:T(8,128)(2,1)S(1)} %collective-permute-done.24.refs_26_), channel_id=1, source_target_pairs={{0,1},{1,0},{2,3},{3,2},{4,5},{5,4},{6,7},{7,6},{8,9},{9,8},{10,11... | collective-permute-start | bytes 393224 | tf_op jit(solution)/shard_map/ppermute | solution.py:43
  45.9 22.4 %collective-permute-start.21 = (bf16[16,4096]{1,0:T(8,128)(2,1)S(1)}, bf16[16,4096]{1,0:T(8,128)(2,1)S(1)}, u32[]{:S(2)}, u32[]{:S(2)}) collective-permute-start(bf16[16,4096]{1,0:T(8,128)(2,1)S(1)} %collective-permute-done.20.refs_22_), channel_id=1, source_target_pairs={{0,1},{1,0},{2,3},{3,2},{4,5},{5,4},{6,7},{7,6},{8,9},{9,8},{10,11... | collective-permute-start | bytes 393224 | tf_op jit(solution)/shard_map/ppermute | solution.py:43
  46.4 3.4 %copy-start = (bf16[512,2,4096]{2,1,0:T(2,128)(2,1)S(1)}, bf16[512,2,4096]{2,1,0:T(2,128)(2,1)}, u32[]{:S(2)}) copy-start(bf16[512,2,4096]{2,1,0:T(2,128)(2,1)} %t_ref.1) | copy-start | bytes 25165828

commit v3 on v2

--- a/solution.py
+++ b/solution.py
@@ -11,6 +11,7 @@
 XS = 2
 GROUPS = 2
 LANES = 128
+BLOCK = 16
 MIB = 1024 * 1024
 VMEM = pl.BlockSpec(memory_space=pltpu.VMEM)
 NN = (((1,), (0,)), ((), ()))
@@ -25,6 +26,10 @@
 def halves(a):
     high = a.astype(jnp.bfloat16)
     return high, (a - high.astype(jnp.float32)).astype(jnp.bfloat16)
+
+
+def in_hbm(array):
+    return pltpu.with_memory_space_constraint(array, pltpu.HBM)
 
 
 def place():
@@ -117,45 +122,88 @@
 
 
 def precondition(slot, query_grads, basis_in, basis_out, eigvals):
-    q_rows, _, width = query_grads.shape
+    q_rows, layers, width = query_grads.shape
+    space = pltpu.HBM if slot == 0 else pltpu.VMEM
+    operands = (query_grads, basis_in, basis_out, eigvals)
+    body, scratch = functools.partial(precond_kernel, slot), []
+    if slot == 0:
+        operands = [in_hbm(a) for a in operands]
+        body = functools.partial(fetched, len(operands), body)
+        scratch = [pltpu.VMEM(a.shape, a.dtype) for a in operands] + [pltpu.SemaphoreType.DMA((len(operands),))]
     return pl.pallas_call(
-        functools.partial(precond_kernel, slot),
+        body,
         out_shape=jax.ShapeDtypeStruct((q_rows, width), jnp.bfloat16),
-        in_specs=[VMEM] * 4,
+        in_specs=[pl.BlockSpec(memory_space=space)] * len(operands),
         out_specs=VMEM,
         scratch_shapes=[
             pltpu.VMEM((q_rows * width // LANES, LANES), jnp.float32),
             pltpu.VMEM((q_rows * width // LANES, LANES), jnp.float32),
             pltpu.VMEM((2 * width // LANES, LANES), jnp.float32),
-        ],
-        compiler_params=pltpu.CompilerParams(vmem_limit_bytes=12 * MIB),
+        ]
+        + scratch,
+        compiler_params=pltpu.CompilerParams(vmem_limit_bytes=8 * MIB),
         cost_estimate=pl.CostEstimate(flops=10**9, bytes_accessed=4 * MIB, transcendentals=0),
         name="precond",
-    )(query_grads, basis_in, basis_out, eigvals)
-
-
-def split_kernel(t_ref, flat_ref):
-    rows = 32
-    width = t_ref.shape[2]
-
-    @pl.loop(0, t_ref.shape[0] // rows)
-    def _(i):
-        at = pl.ds(pl.multiple_of(i * rows, rows), rows)
-        for layer in range(t_ref.shape[1]):
-            flat_ref[at, layer * width : (layer + 1) * width] = t_ref[at, layer, :]
+    )(*operands)
+
+
+def fetched(n, body, *refs):
+    operands, others = refs[:n], refs[n:]
+    others, here, sems = others[: -n - 1], others[-n - 1 : -1], others[-1]
+    copies = [pltpu.make_async_copy(a, b, sems.at[i]) for i, (a, b) in enumerate(zip(operands, here))]
+    for copy in copies:
+        copy.start()
+    for copy in copies:
+        copy.wait()
+    body(*here, *others)
+
+
+def split_kernel(layers, t_ref, flat_ref, here_ref, wide_ref, sems):
+    rows, chunks = BLOCK, sems.shape[0]
+    lines = t_ref.shape[1]
+    pitch = wide_ref.shape[0] // rows
+    chunk = t_ref.shape[0] // chunks
+    copies = [
+        pltpu.make_async_copy(
+            t_ref.at[pl.ds(i * chunk, chunk)], here_ref.at[pl.ds(i * chunk, chunk)], sems.at[i]
+        )
+        for i in range(chunks)
+    ]
+    for copy in copies:
+        copy.start()
+    for i in range(chunks):
+        copies[i].wait()
+
+        @pl.loop(i * chunk // rows, (i + 1) * chunk // rows)
+        def _(block):
+            at = pl.multiple_of(block * rows, rows)
+            for row in range(rows):
+                wide_ref[row * pitch : row * pitch + lines, :] = here_ref[at + row].astype(jnp.float32)
+            for line in range(lines):
+                column = ((line % layers) * (lines // layers) + line // layers) * LANES
+                out = wide_ref[pl.ds(line, rows, stride=pitch), :].astype(jnp.bfloat16)
+                flat_ref[pl.ds(at, rows), column : column + LANES] = out
 
 
 def split_layers(train_grads):
     tr_rows, layers, width = train_grads.shape
+    lines = layers * width // LANES
+    by_line = train_grads.reshape(tr_rows, layers, width // LANES, LANES)
+    by_line = by_line.transpose(0, 2, 1, 3).reshape(tr_rows, lines, LANES)
     return pl.pallas_call(
-        split_kernel,
+        functools.partial(split_kernel, layers),
         out_shape=jax.ShapeDtypeStruct((tr_rows, layers * width), jnp.bfloat16),
-        in_specs=[VMEM],
+        in_specs=[pl.BlockSpec(memory_space=pltpu.HBM)],
         out_specs=VMEM,
+        scratch_shapes=[
+            pltpu.VMEM((tr_rows, lines, LANES), jnp.bfloat16),
+            pltpu.VMEM((BLOCK * (lines + 8), LANES), jnp.float32),
+            pltpu.SemaphoreType.DMA((8,)),
+        ],
         compiler_params=pltpu.CompilerParams(vmem_limit_bytes=20 * MIB),
         cost_estimate=pl.CostEstimate(flops=10**9, bytes_accessed=16 * MIB, transcendentals=0),
         name="split",
-    )(train_grads)
+    )(in_hbm(by_line))
 
 
 def score_kernel(n_train, t_ref, *refs):
@@ -192,8 +240,12 @@
     zs = n_train // (XS * CORES)
     operands = (query_grads, basis_in, basis_out, eigvals)
     mine = precondition(0, *operands)
+    along_z = [hop(mine, n_train, dz=dz) for dz in range(zs - 1, 0, -1)]
+    first_x = hop(mine, n_train, dx=1)
+    mine, operands, train_grads = lax.optimization_barrier((mine, operands, train_grads))
     twin = precondition(1, *operands)
     flat_train = split_layers(train_grads)
+    along_z, first_x, twin, flat_train = lax.optimization_barrier((along_z, first_x, twin, flat_train))
     q_rows, width = mine.shape
 
     pieces = {}
@@ -203,8 +255,8 @@
         pieces[dg, dz, dx, 1] = hop(array, n_train, dc=1)
 
     for dz in range(zs):
-        own = hop(mine, n_train, dz=dz) if dz else mine
-        over_x = hop(own, n_train, dx=1)
+        own = along_z[zs - 1 - dz] if dz else mine
+        over_x = hop(own, n_train, dx=1) if dz else first_x
         over_g = hop(own, n_train, dg=1) if dz else twin
         corner = hop(over_g, n_train, dx=1) if dz % 2 else hop(over_x, n_train, dg=1)
         keep(own, dz, 0, 0)

time: 72.6 us -> 49.2 us (0.68)
  Pallas kernels: 25.4 us -> 13.4 us
  local copies, waits for them, and re-layouts: 6.77 us -> 0.02 us
  starting transfers between devices: 25.3 us -> 18.9 us
  waiting for transfers between devices: 14.8 us -> 16.5 us
    pallas_call x3, Pallas kernels: 21.4 us -> 9.54 us  [the longest x1 5.62 us: split_layers(): pl.pallas_call(functools.partial(split_kernel, layers), out_shape=jax.Sha...]
    unnamed x10 -> x8, local copies, waits for them, and re-layouts: 6.77 us -> 0.02 us
    ppermute x30, starting transfers between devices: 25.3 us -> 18.9 us  [hop(): return lax.ppermute(array, ('group', 'train'), perm)]
    ppermute x30, waiting for transfers between devices: 14.8 us -> 16.5 us  [hop(): return lax.ppermute(array, ('group', 'train'), perm)]
  transfers between devices with their start and end apart: 30 -> 30, of which waited for: 8 -> 10; matrix products, arithmetic and copies ran while one was open for 0% -> 0% of each run, Pallas kernels for 28% -> 14%
where the time goes in v3:
time: 49.2 us; the launch traced here: 49 us
  starting transfers between devices  18.9 us (38%)
  waiting for transfers between devices  16.5 us (34%)
  Pallas kernels  13.4 us (27%)
    ppermute x30, starting transfers between devices, hop(): return lax.ppermute(array, ('group', 'train'), perm)  18.9 us
    ppermute x30, waiting for transfers between devices, hop(): return lax.ppermute(array, ('group', 'train'), perm)  16.5 us
    pallas_call x1, Pallas kernels, split_layers(): pl.pallas_call(functools.partial(split_kernel, layers), out_shape=jax.Sha...  5.62 us
    pallas_call x2, Pallas kernels, precondition(): pl.pallas_call(body, out_shape=jax.ShapeDtypeStruct((q_rows, width), jnp....  3.92 us
    pallas_call x1, Pallas kernels, per_device(): pl.pallas_call(functools.partial(score_kernel, n_train), out_shape=jax.Sh...  3.87 us
  transfers between devices with their start and end apart: 30, of which 10 were waited for; matrix products, arithmetic and copies ran while one was open for 0% of the time, Pallas kernels for 14%

profile of v3, /device:TPU:0, one launch (start us, length us, event | category | flops | bytes accessed | tf_op | source)
XLA Modules:
  0.0 49.0 jit_solution(9364825489067054658)
XLA Ops:
  0.0 2.5 %precond.2.refs_0_ = bf16[16,4096]{1,0:T(8,128)(2,1)S(1)} custom-call(bf16[16,2,4096]{2,1,0:T(2,128)(2,1)} %q_ref, f32[2,64,64]{2,1,0:T(8,128)} %in_ref, f32[2,64,64]{2,1,0:T(8,128)} %out_ref, f32[2,4096]{1,0:T(2,128)} %eig_ref), custom_call_target="tpu_custom_call" | custom-call | flops 1000000000 | bytes 4194304 | tf_op jit(solution)/shard_map/precond/pallas_call | solution.py:133
  2.5 3.0 %collective-permute-start.3 = (bf16[16,4096]{1,0:T(8,128)(2,1)S(1)}, bf16[16,4096]{1,0:T(8,128)(2,1)S(1)}, u32[]{:S(2)}, u32[]{:S(2)}) collective-permute-start(bf16[16,4096]{1,0:T(8,128)(2,1)S(1)} %precond.2.refs_0_), channel_id=1, source_target_pairs={{0,2},{1,3},{2,0},{3,1},{4,6},{5,7},{6,4},{7,5},{8,10},{9,11},{10,... | collective-permute-start | bytes 393224 | tf_op jit(solution)/shard_map/ppermute | solution.py:48
  5.5 1.6 %collective-permute-start.2 = (bf16[16,4096]{1,0:T(8,128)(2,1)S(1)}, bf16[16,4096]{1,0:T(8,128)(2,1)S(1)}, u32[]{:S(2)}, u32[]{:S(2)}) collective-permute-start(bf16[16,4096]{1,0:T(8,128)(2,1)S(1)} %precond.2.refs_0_), channel_id=1, source_target_pairs={{0,4},{1,5},{2,6},{3,7},{4,8},{5,9},{6,10},{7,11},{8,12},{9,13},{1... | collective-permute-start | bytes 393224 | tf_op jit(solution)/shard_map/ppermute | solution.py:48
  7.0 2.6 %collective-permute-start.1 = (bf16[16,4096]{1,0:T(8,128)(2,1)S(1)}, bf16[16,4096]{1,0:T(8,128)(2,1)S(1)}, u32[]{:S(2)}, u32[]{:S(2)}) collective-permute-start(bf16[16,4096]{1,0:T(8,128)(2,1)S(1)} %precond.2.refs_0_), channel_id=1, source_target_pairs={{0,8},{1,9},{2,10},{3,11},{4,12},{5,13},{6,14},{7,15},{8,0},{9,1},... | collective-permute-start | bytes 393224 | tf_op jit(solution)/shard_map/ppermute | solution.py:48
  9.6 1.3 %collective-permute-start = (bf16[16,4096]{1,0:T(8,128)(2,1)S(1)}, bf16[16,4096]{1,0:T(8,128)(2,1)S(1)}, u32[]{:S(2)}, u32[]{:S(2)}) collective-permute-start(bf16[16,4096]{1,0:T(8,128)(2,1)S(1)} %precond.2.refs_0_), channel_id=1, source_target_pairs={{0,12},{1,13},{2,14},{3,15},{4,0},{5,1},{6,2},{7,3},{8,4},{9,5},{1... | collective-permute-start | bytes 393224 | tf_op jit(solution)/shard_map/ppermute | solution.py:48
  11.0 0.0 collective-permute-start.4
  11.0 0.0 copy-start.3
  11.0 5.6 %split.1.t_ref = bf16[512,8192]{1,0:T(8,128)(2,1)S(1)} custom-call(bf16[512,64,128]{2,1,0:T(8,128)(2,1)} %bitcast.5), custom_call_target="tpu_custom_call" | custom-call | flops 1000000000 | bytes 16777216 | tf_op jit(solution)/shard_map/split/pallas_call | solution.py:193
  16.7 1.5 %precond.3.refs_16_ = bf16[16,4096]{1,0:T(8,128)(2,1)S(1)} custom-call(bf16[16,2,4096]{2,1,0:T(2,128)(2,1)S(1)} %copy-done, f32[2,64,64]{2,1,0:T(8,128)S(1)} %copy-done.1, f32[2,64,64]{2,1,0:T(8,128)S(1)} %copy-done.2, f32[2,4096]{1,0:T(2,128)S(1)} %copy-done.3), custom_call_target="tpu_custom_call" | custom-call | flops 1000000000 | bytes 4194304 | tf_op jit(solution)/shard_map/precond/pallas_call | solution.py:133
  18.1 0.0 collective-permute-done.3.refs_2_
  18.2 0.0 collective-permute-done.2.refs_4_
  18.2 0.0 collective-permute-done.1.refs_8_
  18.2 0.0 collective-permute-done.refs_12_
  18.2 0.6 %collective-permute-start.15 = (bf16[16,4096]{1,0:T(8,128)(2,1)S(1)}, bf16[16,4096]{1,0:T(8,128)(2,1)S(1)}, u32[]{:S(2)}, u32[]{:S(2)}) collective-permute-start(bf16[16,4096]{1,0:T(8,128)(2,1)S(1)} %precond.3.refs_16_), channel_id=1, source_target_pairs={{0,1},{1,0},{2,3},{3,2},{4,5},{5,4},{6,7},{7,6},{8,9},{9,8},{10,11... | collective-permute-start | bytes 393224 | tf_op jit(solution)/shard_map/ppermute | solution.py:48
  18.8 1.5 %collective-permute-start.16 = (bf16[16,4096]{1,0:T(8,128)(2,1)S(1)}, bf16[16,4096]{1,0:T(8,128)(2,1)S(1)}, u32[]{:S(2)}, u32[]{:S(2)}) collective-permute-start(bf16[16,4096]{1,0:T(8,128)(2,1)S(1)} %collective-permute-done.3.refs_2_), channel_id=1, source_target_pairs={{0,16},{1,17},{2,18},{3,19},{4,20},{5,21},{6,22},{7,23},{8,24},{9,... | collective-permute-start | bytes 393224 | tf_op jit(solution)/shard_map/ppermute | solution.py:48
  20.3 0.0 collective-permute-start.5
  20.3 0.5 %collective-permute-start.18 = (bf16[16,4096]{1,0:T(8,128)(2,1)S(1)}, bf16[16,4096]{1,0:T(8,128)(2,1)S(1)}, u32[]{:S(2)}, u32[]{:S(2)}) collective-permute-start(bf16[16,4096]{1,0:T(8,128)(2,1)S(1)} %collective-permute-done.2.refs_4_), channel_id=1, source_target_pairs={{0,16},{1,17},{2,18},{3,19},{4,20},{5,21},{6,22},{7,23},{8,24},{9,... | collective-permute-start | bytes 393224 | tf_op jit(solution)/shard_map/ppermute | solution.py:48
  20.8 0.0 collective-permute-done.4.refs_1_
  20.8 0.5 %collective-permute-start.7 = (bf16[16,4096]{1,0:T(8,128)(2,1)S(1)}, bf16[16,4096]{1,0:T(8,128)(2,1)S(1)}, u32[]{:S(2)}, u32[]{:S(2)}) collective-permute-start(bf16[16,4096]{1,0:T(8,128)(2,1)S(1)} %collective-permute-done.2.refs_4_), channel_id=1, source_target_pairs={{0,2},{1,3},{2,0},{3,1},{4,6},{5,7},{6,4},{7,5},{8,10},{9,11},{10,... | collective-permute-start | bytes 393224 | tf_op jit(solution)/shard_map/ppermute | solution.py:48
  21.3 0.0 collective-permute-done.15.refs_17_
  21.3 0.0 collective-permute-start.6
  21.3 3.8 %collective-permute-done.16.refs_18_ = bf16[16,4096]{1,0:T(8,128)(2,1)S(1)} collective-permute-done((bf16[16,4096]{1,0:T(8,128)(2,1)S(1)}, bf16[16,4096]{1,0:T(8,128)(2,1)S(1)}, u32[]{:S(2)}, u32[]{:S(2)}) %collective-permute-start.16) | collective-permute-done | bytes 131104 | tf_op jit(solution)/shard_map/ppermute | solution.py:48
  25.1 1.5 %collective-permute-start.22 = (bf16[16,4096]{1,0:T(8,128)(2,1)S(1)}, bf16[16,4096]{1,0:T(8,128)(2,1)S(1)}, u32[]{:S(2)}, u32[]{:S(2)}) collective-permute-start(bf16[16,4096]{1,0:T(8,128)(2,1)S(1)} %collective-permute-done.1.refs_8_), channel_id=1, source_target_pairs={{0,16},{1,17},{2,18},{3,19},{4,20},{5,21},{6,22},{7,23},{8,24},{9,... | collective-permute-start | bytes 393224 | tf_op jit(solution)/shard_map/ppermute | solution.py:48
  26.6 0.0 collective-permute-done.5.refs_3_
  26.6 0.5 %collective-permute-start.10 = (bf16[16,4096]{1,0:T(8,128)(2,1)S(1)}, bf16[16,4096]{1,0:T(8,128)(2,1)S(1)}, u32[]{:S(2)}, u32[]{:S(2)}) collective-permute-start(bf16[16,4096]{1,0:T(8,128)(2,1)S(1)} %collective-permute-done.1.refs_8_), channel_id=1, source_target_pairs={{0,2},{1,3},{2,0},{3,1},{4,6},{5,7},{6,4},{7,5},{8,10},{9,11},{10,... | collective-permute-start | bytes 393224 | tf_op jit(solution)/shard_map/ppermute | solution.py:48
  27.2 0.7 %collective-permute-done.18.refs_20_ = bf16[16,4096]{1,0:T(8,128)(2,1)S(1)} collective-permute-done((bf16[16,4096]{1,0:T(8,128)(2,1)S(1)}, bf16[16,4096]{1,0:T(8,128)(2,1)S(1)}, u32[]{:S(2)}, u32[]{:S(2)}) %collective-permute-start.18) | collective-permute-done | bytes 131104 | tf_op jit(solution)/shard_map/ppermute | solution.py:48
  27.9 0.0 collective-permute-start.9
  27.9 0.0 collective-permute-done.7.refs_6_
  27.9 1.5 %collective-permute-start.26 = (bf16[16,4096]{1,0:T(8,128)(2,1)S(1)}, bf16[16,4096]{1,0:T(8,128)(2,1)S(1)}, u32[]{:S(2)}, u32[]{:S(2)}) collective-permute-start(bf16[16,4096]{1,0:T(8,128)(2,1)S(1)} %collective-permute-done.refs_12_), channel_id=1, source_target_pairs={{0,16},{1,17},{2,18},{3,19},{4,20},{5,21},{6,22},{7,23},{8,24},{9,... | collective-permute-start | bytes 393224 | tf_op jit(solution)/shard_map/ppermute | solution.py:48
  29.4 0.0 collective-permute-done.6.refs_5_
  29.4 0.5 %collective-permute-start.13 = (bf16[16,4096]{1,0:T(8,128)(2,1)S(1)}, bf16[16,4096]{1,0:T(8,128)(2,1)S(1)}, u32[]{:S(2)}, u32[]{:S(2)}) collective-permute-start(bf16[16,4096]{1,0:T(8,128)(2,1)S(1)} %collective-permute-done.refs_12_), channel_id=1, source_target_pairs={{0,2},{1,3},{2,0},{3,1},{4,6},{5,7},{6,4},{7,5},{8,10},{9,11},{10,... | collective-permute-start | bytes 393224 | tf_op jit(solution)/shard_map/ppermute | solution.py:48
  30.0 0.1 collective-permute-done.22.refs_24_
  30.1 0.0 collective-permute-start.12
  30.1 1.5 %collective-permute-done.10.refs_10_ = bf16[16,4096]{1,0:T(8,128)(2,1)S(1)} collective-permute-done((bf16[16,4096]{1,0:T(8,128)(2,1)S(1)}, bf16[16,4096]{1,0:T(8,128)(2,1)S(1)}, u32[]{:S(2)}, u32[]{:S(2)}) %collective-permute-start.10) | collective-permute-done | bytes 131104 | tf_op jit(solution)/shard_map/ppermute | solution.py:48
  31.6 0.0 collective-permute-start.17
  31.6 0.0 collective-permute-done.9.refs_9_
  31.6 0.5 %collective-permute-start.20 = (bf16[16,4096]{1,0:T(8,128)(2,1)S(1)}, bf16[16,4096]{1,0:T(8,128)(2,1)S(1)}, u32[]{:S(2)}, u32[]{:S(2)}) collective-permute-start(bf16[16,4096]{1,0:T(8,128)(2,1)S(1)} %collective-permute-done.18.refs_20_), channel_id=1, source_target_pairs={{0,2},{1,3},{2,0},{3,1},{4,6},{5,7},{6,4},{7,5},{8,10},{9,11},{10,... | collective-permute-start | bytes 393224 | tf_op jit(solution)/shard_map/ppermute | solution.py:48
  32.1 1.7 %collective-permute-done.26.refs_28_ = bf16[16,4096]{1,0:T(8,128)(2,1)S(1)} collective-permute-done((bf16[16,4096]{1,0:T(8,128)(2,1)S(1)}, bf16[16,4096]{1,0:T(8,128)(2,1)S(1)}, u32[]{:S(2)}, u32[]{:S(2)}) %collective-permute-start.26) | collective-permute-done | bytes 131104 | tf_op jit(solution)/shard_map/ppermute | solution.py:48
  33.8 0.0 collective-permute-start.19
  33.8 1.6 %collective-permute-done.13.refs_14_ = bf16[16,4096]{1,0:T(8,128)(2,1)S(1)} collective-permute-done((bf16[16,4096]{1,0:T(8,128)(2,1)S(1)}, bf16[16,4096]{1,0:T(8,128)(2,1)S(1)}, u32[]{:S(2)}, u32[]{:S(2)}) %collective-permute-start.13) | collective-permute-done | bytes 131104 | tf_op jit(solution)/shard_map/ppermute | solution.py:48
  35.4 0.0 collective-permute-start.8
  35.4 0.0 collective-permute-done.12.refs_13_
  35.4 0.5 %collective-permute-start.23 = (bf16[16,4096]{1,0:T(8,128)(2,1)S(1)}, bf16[16,4096]{1,0:T(8,128)(2,1)S(1)}, u32[]{:S(2)}, u32[]{:S(2)}) collective-permute-start(bf16[16,4096]{1,0:T(8,128)(2,1)S(1)} %collective-permute-done.22.refs_24_), channel_id=1, source_target_pairs={{0,1},{1,0},{2,3},{3,2},{4,5},{5,4},{6,7},{7,6},{8,9},{9,8},{10,11... | collective-permute-start | bytes 393224 | tf_op jit(solution)/shard_map/ppermute | solution.py:48
  35.9 0.0 collective-permute-done.17.refs_19_
  35.9 0.5 collective-permute-start.24
  36.4 1.5 %collective-permute-done.20.refs_22_ = bf16[16,4096]{1,0:T(8,128)(2,1)S(1)} collective-permute-done((bf16[16,4096]{1,0:T(8,128)(2,1)S(1)}, bf16[16,4096]{1,0:T(8,128)(2,1)S(1)}, u32[]{:S(2)}, u32[]{:S(2)}) %collective-permute-start.20) | collective-permute-done | bytes 131104 | tf_op jit(solution)/shard_map/ppermute | solution.py:48
  37.9 0.0 collective-permute-start.11
  37.9 0.0 collective-permute-done.19.refs_21_
  37.9 0.5 %collective-permute-start.28 = (bf16[16,4096]{1,0:T(8,128)(2,1)S(1)}, bf16[16,4096]{1,0:T(8,128)(2,1)S(1)}, u32[]{:S(2)}, u32[]{:S(2)}) collective-permute-start(bf16[16,4096]{1,0:T(8,128)(2,1)S(1)} %collective-permute-done.26.refs_28_), channel_id=1, source_target_pairs={{0,2},{1,3},{2,0},{3,1},{4,6},{5,7},{6,4},{7,5},{8,10},{9,11},{10,... | collective-permute-start | bytes 393224 | tf_op jit(solution)/shard_map/ppermute | solution.py:48
  38.4 0.0 collective-permute-done.8.refs_7_
  38.4 0.2 collective-permute-start.27
  38.7 0.0 collective-permute-done.23.refs_25_
  38.7 0.3 collective-permute-start.14
  38.9 2.4 %collective-permute-done.24.refs_26_ = bf16[16,4096]{1,0:T(8,128)(2,1)S(1)} collective-permute-done((bf16[16,4096]{1,0:T(8,128)(2,1)S(1)}, bf16[16,4096]{1,0:T(8,128)(2,1)S(1)}, u32[]{:S(2)}, u32[]{:S(2)}) %collective-permute-start.24) | collective-permute-done | bytes 131104 | tf_op jit(solution)/shard_map/ppermute | solution.py:48
  41.4 0.0 collective-permute-start.21
  41.4 0.0 collective-permute-done.11.refs_11_
  41.4 0.5 %collective-permute-start.25 = (bf16[16,4096]{1,0:T(8,128)(2,1)S(1)}, bf16[16,4096]{1,0:T(8,128)(2,1)S(1)}, u32[]{:S(2)}, u32[]{:S(2)}) collective-permute-start(bf16[16,4096]{1,0:T(8,128)(2,1)S(1)} %collective-permute-done.24.refs_26_), channel_id=1, source_target_pairs={{0,1},{1,0},{2,3},{3,2},{4,5},{5,4},{6,7},{7,6},{8,9},{9,8},{10,11... | collective-permute-start | bytes 393224 | tf_op jit(solution)/shard_map/ppermute | solution.py:48
  41.9 1.9 %collective-permute-done.28.refs_30_ = bf16[16,4096]{1,0:T(8,128)(2,1)S(1)} collective-permute-done((bf16[16,4096]{1,0:T(8,128)(2,1)S(1)}, bf16[16,4096]{1,0:T(8,128)(2,1)S(1)}, u32[]{:S(2)}, u32[]{:S(2)}) %collective-permute-start.28) | collective-permute-done | bytes 131104 | tf_op jit(solution)/shard_map/ppermute | solution.py:48
  43.8 0.0 collective-permute-start.29
  43.8 0.0 collective-permute-done.27.refs_29_
  43.8 0.0 collective-permute-done.14.refs_15_
  43.8 0.0 collective-permute-done.21.refs_23_
  43.8 1.3 %collective-permute-done.29.refs_31_ = bf16[16,4096]{1,0:T(8,128)(2,1)S(1)} collective-permute-done((bf16[16,4096]{1,0:T(8,128)(2,1)S(1)}, bf16[16,4096]{1,0:T(8,128)(2,1)S(1)}, u32[]{:S(2)}, u32[]{:S(2)}) %collective-permute-start.29) | collective-permute-done | bytes 131104 | tf_op jit(solution)/shard_map/ppermute | solution.py:48
  45.2 3.9 %scores.1 = f32[512,256]{1,0:T(8,128)} custom-call(bf16[512,8192]{1,0:T(8,128)(2,1)S(1)} %split.1.t_ref, bf16[16,4096]{1,0:T(8,128)(2,1)S(1)} %precond.2.refs_0_, bf16[16,4096]{1,0:T(8,128)(2,1)S(1)} %collective-permute-done.4.refs_1_, bf16[16,4096]{1,0:T(8,128)(2,1)S(1)} %collective-permute-done.3.refs_2_, ...), custom_call_target="tpu_custom_call" | custom-call | flops 2147483648 | bytes 6291456 | tf_op jit(solution)/shard_map/scores/pallas_call | solution.py:269
  (8 shorter events, 0.0 us)
Async XLA Ops:
  2.5 15.7 %collective-permute-start.3 = (bf16[16,4096]{1,0:T(8,128)(2,1)S(1)}, bf16[16,4096]{1,0:T(8,128)(2,1)S(1)}, u32[]{:S(2)}, u32[]{:S(2)}) collective-permute-start(bf16[16,4096]{1,0:T(8,128)(2,1)S(1)} %precond.2.refs_0_), channel_id=1, source_target_pairs={{0,2},{1,3},{2,0},{3,1},{4,6},{5,7},{6,4},{7,5},{8,10},{9,11},{10,... | collective-permute-start | bytes 393224 | tf_op jit(solution)/shard_map/ppermute | solution.py:48
  5.5 12.7 %collective-permute-start.2 = (bf16[16,4096]{1,0:T(8,128)(2,1)S(1)}, bf16[16,4096]{1,0:T(8,128)(2,1)S(1)}, u32[]{:S(2)}, u32[]{:S(2)}) collective-permute-start(bf16[16,4096]{1,0:T(8,128)(2,1)S(1)} %precond.2.refs_0_), channel_id=1, source_target_pairs={{0,4},{1,5},{2,6},{3,7},{4,8},{5,9},{6,10},{7,11},{8,12},{9,13},{1... | collective-permute-start | bytes 393224 | tf_op jit(solution)/shard_map/ppermute | solution.py:48
  7.0 11.1 %collective-permute-start.1 = (bf16[16,4096]{1,0:T(8,128)(2,1)S(1)}, bf16[16,4096]{1,0:T(8,128)(2,1)S(1)}, u32[]{:S(2)}, u32[]{:S(2)}) collective-permute-start(bf16[16,4096]{1,0:T(8,128)(2,1)S(1)} %precond.2.refs_0_), channel_id=1, source_target_pairs={{0,8},{1,9},{2,10},{3,11},{4,12},{5,13},{6,14},{7,15},{8,0},{9,1},... | collective-permute-start | bytes 393224 | tf_op jit(solution)/shard_map/ppermute | solution.py:48
  9.6 8.5 %collective-permute-start = (bf16[16,4096]{1,0:T(8,128)(2,1)S(1)}, bf16[16,4096]{1,0:T(8,128)(2,1)S(1)}, u32[]{:S(2)}, u32[]{:S(2)}) collective-permute-start(bf16[16,4096]{1,0:T(8,128)(2,1)S(1)} %precond.2.refs_0_), channel_id=1, source_target_pairs={{0,12},{1,13},{2,14},{3,15},{4,0},{5,1},{6,2},{7,3},{8,4},{9,5},{1... | collective-permute-start | bytes 393224 | tf_op jit(solution)/shard_map/ppermute | solution.py:48
  11.0 9.8 %collective-permute-start.4 = (bf16[16,4096]{1,0:T(8,128)(2,1)S(1)}, bf16[16,4096]{1,0:T(8,128)(2,1)S(1)}, u32[]{:S(2)}, u32[]{:S(2)}) collective-permute-start(bf16[16,4096]{1,0:T(8,128)(2,1)S(1)} %precond.2.refs_0_), channel_id=1, source_target_pairs={{0,1},{1,0},{2,3},{3,2},{4,5},{5,4},{6,7},{7,6},{8,9},{9,8},{10,11... | collective-permute-start | bytes 393224 | tf_op jit(solution)/shard_map/ppermute | solution.py:48
  11.0 5.7 %copy-start = (bf16[16,2,4096]{2,1,0:T(2,128)(2,1)S(1)}, bf16[16,2,4096]{2,1,0:T(2,128)(2,1)}, u32[]{:S(2)}) copy-start(bf16[16,2,4096]{2,1,0:T(2,128)(2,1)} %q_ref) | copy-start | bytes 786436
  11.0 5.7 %copy-start.1 = (f32[2,64,64]{2,1,0:T(8,128)S(1)}, f32[2,64,64]{2,1,0:T(8,128)}, u32[]{:S(2)}) copy-start(f32[2,64,64]{2,1,0:T(8,128)} %in_ref) | copy-start | bytes 98308
  11.0 5.7 %copy-start.2 = (f32[2,64,64]{2,1,0:T(8,128)S(1)}, f32[2,64,64]{2,1,0:T(8,128)}, u32[]{:S(2)}) copy-start(f32[2,64,64]{2,1,0:T(8,128)} %out_ref) | copy-start | bytes 98308
  11.0 5.7 %copy-start.3 = (f32[2,4096]{1,0:T(2,128)S(1)}, f32[2,4096]{1,0:T(2,128)}, u32[]{:S(2)}) copy-start(f32[2,4096]{1,0:T(2,128)} %eig_ref) | copy-start | bytes 98308
  18.2 3.1 %collective-permute-start.15 = (bf16[16,4096]{1,0:T(8,128)(2,1)S(1)}, bf16[16,4096]{1,0:T(8,128)(2,1)S(1)}, u32[]{:S(2)}, u32[]{:S(2)}) collective-permute-start(bf16[16,4096]{1,0:T(8,128)(2,1)S(1)} %precond.3.refs_16_), channel_id=1, source_target_pairs={{0,1},{1,0},{2,3},{3,2},{4,5},{5,4},{6,7},{7,6},{8,9},{9,8},{10,11... | collective-permute-start | bytes 393224 | tf_op jit(solution)/shard_map/ppermute | solution.py:48
  18.8 6.3 %collective-permute-start.16 = (bf16[16,4096]{1,0:T(8,128)(2,1)S(1)}, bf16[16,4096]{1,0:T(8,128)(2,1)S(1)}, u32[]{:S(2)}, u32[]{:S(2)}) collective-permute-start(bf16[16,4096]{1,0:T(8,128)(2,1)S(1)} %collective-permute-done.3.refs_2_), channel_id=1, source_target_pairs={{0,16},{1,17},{2,18},{3,19},{4,20},{5,21},{6,22},{7,23},{8,24},{9,... | collective-permute-start | bytes 393224 | tf_op jit(solution)/shard_map/ppermute | solution.py:48
  20.3 6.4 %collective-permute-start.5 = (bf16[16,4096]{1,0:T(8,128)(2,1)S(1)}, bf16[16,4096]{1,0:T(8,128)(2,1)S(1)}, u32[]{:S(2)}, u32[]{:S(2)}) collective-permute-start(bf16[16,4096]{1,0:T(8,128)(2,1)S(1)} %collective-permute-done.3.refs_2_), channel_id=1, source_target_pairs={{0,1},{1,0},{2,3},{3,2},{4,5},{5,4},{6,7},{7,6},{8,9},{9,8},{10,11... | collective-permute-start | bytes 393224 | tf_op jit(solution)/shard_map/ppermute | solution.py:48
  20.3 7.6 %collective-permute-start.18 = (bf16[16,4096]{1,0:T(8,128)(2,1)S(1)}, bf16[16,4096]{1,0:T(8,128)(2,1)S(1)}, u32[]{:S(2)}, u32[]{:S(2)}) collective-permute-start(bf16[16,4096]{1,0:T(8,128)(2,1)S(1)} %collective-permute-done.2.refs_4_), channel_id=1, source_target_pairs={{0,16},{1,17},{2,18},{3,19},{4,20},{5,21},{6,22},{7,23},{8,24},{9,... | collective-permute-start | bytes 393224 | tf_op jit(solution)/shard_map/ppermute | solution.py:48
  20.8 7.1 %collective-permute-start.7 = (bf16[16,4096]{1,0:T(8,128)(2,1)S(1)}, bf16[16,4096]{1,0:T(8,128)(2,1)S(1)}, u32[]{:S(2)}, u32[]{:S(2)}) collective-permute-start(bf16[16,4096]{1,0:T(8,128)(2,1)S(1)} %collective-permute-done.2.refs_4_), channel_id=1, source_target_pairs={{0,2},{1,3},{2,0},{3,1},{4,6},{5,7},{6,4},{7,5},{8,10},{9,11},{10,... | collective-permute-start | bytes 393224 | tf_op jit(solution)/shard_map/ppermute | solution.py:48
  21.3 8.1 %collective-permute-start.6 = (bf16[16,4096]{1,0:T(8,128)(2,1)S(1)}, bf16[16,4096]{1,0:T(8,128)(2,1)S(1)}, u32[]{:S(2)}, u32[]{:S(2)}) collective-permute-start(bf16[16,4096]{1,0:T(8,128)(2,1)S(1)} %collective-permute-done.2.refs_4_), channel_id=1, source_target_pairs={{0,1},{1,0},{2,3},{3,2},{4,5},{5,4},{6,7},{7,6},{8,9},{9,8},{10,11... | collective-permute-start | bytes 393224 | tf_op jit(solution)/shard_map/ppermute | solution.py:48
  25.1 5.0 %collective-permute-start.22 = (bf16[16,4096]{1,0:T(8,128)(2,1)S(1)}, bf16[16,4096]{1,0:T(8,128)(2,1)S(1)}, u32[]{:S(2)}, u32[]{:S(2)}) collective-permute-start(bf16[16,4096]{1,0:T(8,128)(2,1)S(1)} %collective-permute-done.1.refs_8_), channel_id=1, source_target_pairs={{0,16},{1,17},{2,18},{3,19},{4,20},{5,21},{6,22},{7,23},{8,24},{9,... | collective-permute-start | bytes 393224 | tf_op jit(solution)/shard_map/ppermute | solution.py:48
  26.6 5.0 %collective-permute-start.10 = (bf16[16,4096]{1,0:T(8,128)(2,1)S(1)}, bf16[16,4096]{1,0:T(8,128)(2,1)S(1)}, u32[]{:S(2)}, u32[]{:S(2)}) collective-permute-start(bf16[16,4096]{1,0:T(8,128)(2,1)S(1)} %collective-permute-done.1.refs_8_), channel_id=1, source_target_pairs={{0,2},{1,3},{2,0},{3,1},{4,6},{5,7},{6,4},{7,5},{8,10},{9,11},{10,... | collective-permute-start | bytes 393224 | tf_op jit(solution)/shard_map/ppermute | solution.py:48
  27.9 3.7 %collective-permute-start.9 = (bf16[16,4096]{1,0:T(8,128)(2,1)S(1)}, bf16[16,4096]{1,0:T(8,128)(2,1)S(1)}, u32[]{:S(2)}, u32[]{:S(2)}) collective-permute-start(bf16[16,4096]{1,0:T(8,128)(2,1)S(1)} %collective-permute-done.1.refs_8_), channel_id=1, source_target_pairs={{0,1},{1,0},{2,3},{3,2},{4,5},{5,4},{6,7},{7,6},{8,9},{9,8},{10,11... | collective-permute-start | bytes 393224 | tf_op jit(solution)/shard_map/ppermute | solution.py:48
  27.9 5.9 %collective-permute-start.26 = (bf16[16,4096]{1,0:T(8,128)(2,1)S(1)}, bf16[16,4096]{1,0:T(8,128)(2,1)S(1)}, u32[]{:S(2)}, u32[]{:S(2)}) collective-permute-start(bf16[16,4096]{1,0:T(8,128)(2,1)S(1)} %collective-permute-done.refs_12_), channel_id=1, source_target_pairs={{0,16},{1,17},{2,18},{3,19},{4,20},{5,21},{6,22},{7,23},{8,24},{9,... | collective-permute-start | bytes 393224 | tf_op jit(solution)/shard_map/ppermute | solution.py:48
  29.4 5.9 %collective-permute-start.13 = (bf16[16,4096]{1,0:T(8,128)(2,1)S(1)}, bf16[16,4096]{1,0:T(8,128)(2,1)S(1)}, u32[]{:S(2)}, u32[]{:S(2)}) collective-permute-start(bf16[16,4096]{1,0:T(8,128)(2,1)S(1)} %collective-permute-done.refs_12_), channel_id=1, source_target_pairs={{0,2},{1,3},{2,0},{3,1},{4,6},{5,7},{6,4},{7,5},{8,10},{9,11},{10,... | collective-permute-start | bytes 393224 | tf_op jit(solution)/shard_map/ppermute | solution.py:48
  30.1 5.3 %collective-permute-start.12 = (bf16[16,4096]{1,0:T(8,128)(2,1)S(1)}, bf16[16,4096]{1,0:T(8,128)(2,1)S(1)}, u32[]{:S(2)}, u32[]{:S(2)}) collective-permute-start(bf16[16,4096]{1,0:T(8,128)(2,1)S(1)} %collective-permute-done.refs_12_), channel_id=1, source_target_pairs={{0,1},{1,0},{2,3},{3,2},{4,5},{5,4},{6,7},{7,6},{8,9},{9,8},{10,11... | collective-permute-start | bytes 393224 | tf_op jit(solution)/shard_map/ppermute | solution.py:48
  31.6 4.3 %collective-permute-start.17 = (bf16[16,4096]{1,0:T(8,128)(2,1)S(1)}, bf16[16,4096]{1,0:T(8,128)(2,1)S(1)}, u32[]{:S(2)}, u32[]{:S(2)}) collective-permute-start(bf16[16,4096]{1,0:T(8,128)(2,1)S(1)} %collective-permute-done.16.refs_18_), channel_id=1, source_target_pairs={{0,1},{1,0},{2,3},{3,2},{4,5},{5,4},{6,7},{7,6},{8,9},{9,8},{10,11... | collective-permute-start | bytes 393224 | tf_op jit(solution)/shard_map/ppermute | solution.py:48
  31.6 6.3 %collective-permute-start.20 = (bf16[16,4096]{1,0:T(8,128)(2,1)S(1)}, bf16[16,4096]{1,0:T(8,128)(2,1)S(1)}, u32[]{:S(2)}, u32[]{:S(2)}) collective-permute-start(bf16[16,4096]{1,0:T(8,128)(2,1)S(1)} %collective-permute-done.18.refs_20_), channel_id=1, source_target_pairs={{0,2},{1,3},{2,0},{3,1},{4,6},{5,7},{6,4},{7,5},{8,10},{9,11},{10,... | collective-permute-start | bytes 393224 | tf_op jit(solution)/shard_map/ppermute | solution.py:48
  33.8 4.1 %collective-permute-start.19 = (bf16[16,4096]{1,0:T(8,128)(2,1)S(1)}, bf16[16,4096]{1,0:T(8,128)(2,1)S(1)}, u32[]{:S(2)}, u32[]{:S(2)}) collective-permute-start(bf16[16,4096]{1,0:T(8,128)(2,1)S(1)} %collective-permute-done.18.refs_20_), channel_id=1, source_target_pairs={{0,1},{1,0},{2,3},{3,2},{4,5},{5,4},{6,7},{7,6},{8,9},{9,8},{10,11... | collective-permute-start | bytes 393224 | tf_op jit(solution)/shard_map/ppermute | solution.py:48
  35.4 3.1 %collective-permute-start.8 = (bf16[16,4096]{1,0:T(8,128)(2,1)S(1)}, bf16[16,4096]{1,0:T(8,128)(2,1)S(1)}, u32[]{:S(2)}, u32[]{:S(2)}) collective-permute-start(bf16[16,4096]{1,0:T(8,128)(2,1)S(1)} %collective-permute-done.7.refs_6_), channel_id=1, source_target_pairs={{0,1},{1,0},{2,3},{3,2},{4,5},{5,4},{6,7},{7,6},{8,9},{9,8},{10,11... | collective-permute-start | bytes 393224 | tf_op jit(solution)/shard_map/ppermute | solution.py:48
  35.4 3.3 %collective-permute-start.23 = (bf16[16,4096]{1,0:T(8,128)(2,1)S(1)}, bf16[16,4096]{1,0:T(8,128)(2,1)S(1)}, u32[]{:S(2)}, u32[]{:S(2)}) collective-permute-start(bf16[16,4096]{1,0:T(8,128)(2,1)S(1)} %collective-permute-done.22.refs_24_), channel_id=1, source_target_pairs={{0,1},{1,0},{2,3},{3,2},{4,5},{5,4},{6,7},{7,6},{8,9},{9,8},{10,11... | collective-permute-start | bytes 393224 | tf_op jit(solution)/shard_map/ppermute | solution.py:48
  35.9 5.5 %collective-permute-start.24 = (bf16[16,4096]{1,0:T(8,128)(2,1)S(1)}, bf16[16,4096]{1,0:T(8,128)(2,1)S(1)}, u32[]{:S(2)}, u32[]{:S(2)}) collective-permute-start(bf16[16,4096]{1,0:T(8,128)(2,1)S(1)} %collective-permute-done.10.refs_10_), channel_id=1, source_target_pairs={{0,16},{1,17},{2,18},{3,19},{4,20},{5,21},{6,22},{7,23},{8,24},{9,... | collective-permute-start | bytes 393224 | tf_op jit(solution)/shard_map/ppermute | solution.py:48
  37.9 3.5 %collective-permute-start.11 = (bf16[16,4096]{1,0:T(8,128)(2,1)S(1)}, bf16[16,4096]{1,0:T(8,128)(2,1)S(1)}, u32[]{:S(2)}, u32[]{:S(2)}) collective-permute-start(bf16[16,4096]{1,0:T(8,128)(2,1)S(1)} %collective-permute-done.10.refs_10_), channel_id=1, source_target_pairs={{0,1},{1,0},{2,3},{3,2},{4,5},{5,4},{6,7},{7,6},{8,9},{9,8},{10,11... | collective-permute-start | bytes 393224 | tf_op jit(solution)/shard_map/ppermute | solution.py:48
  37.9 5.9 %collective-permute-start.28 = (bf16[16,4096]{1,0:T(8,128)(2,1)S(1)}, bf16[16,4096]{1,0:T(8,128)(2,1)S(1)}, u32[]{:S(2)}, u32[]{:S(2)}) collective-permute-start(bf16[16,4096]{1,0:T(8,128)(2,1)S(1)} %collective-permute-done.26.refs_28_), channel_id=1, source_target_pairs={{0,2},{1,3},{2,0},{3,1},{4,6},{5,7},{6,4},{7,5},{8,10},{9,11},{10,... | collective-permute-start | bytes 393224 | tf_op jit(solution)/shard_map/ppermute | solution.py:48
  38.4 5.4 %collective-permute-start.27 = (bf16[16,4096]{1,0:T(8,128)(2,1)S(1)}, bf16[16,4096]{1,0:T(8,128)(2,1)S(1)}, u32[]{:S(2)}, u32[]{:S(2)}) collective-permute-start(bf16[16,4096]{1,0:T(8,128)(2,1)S(1)} %collective-permute-done.26.refs_28_), channel_id=1, source_target_pairs={{0,1},{1,0},{2,3},{3,2},{4,5},{5,4},{6,7},{7,6},{8,9},{9,8},{10,11... | collective-permute-start | bytes 393224 | tf_op jit(solution)/shard_map/ppermute | solution.py:48
  38.7 5.2 %collective-permute-start.14 = (bf16[16,4096]{1,0:T(8,128)(2,1)S(1)}, bf16[16,4096]{1,0:T(8,128)(2,1)S(1)}, u32[]{:S(2)}, u32[]{:S(2)}) collective-permute-start(bf16[16,4096]{1,0:T(8,128)(2,1)S(1)} %collective-permute-done.13.refs_14_), channel_id=1, source_target_pairs={{0,1},{1,0},{2,3},{3,2},{4,5},{5,4},{6,7},{7,6},{8,9},{9,8},{10,11... | collective-permute-start | bytes 393224 | tf_op jit(solution)/shard_map/ppermute | solution.py:48
  41.4 2.4 %collective-permute-start.21 = (bf16[16,4096]{1,0:T(8,128)(2,1)S(1)}, bf16[16,4096]{1,0:T(8,128)(2,1)S(1)}, u32[]{:S(2)}, u32[]{:S(2)}) collective-permute-start(bf16[16,4096]{1,0:T(8,128)(2,1)S(1)} %collective-permute-done.20.refs_22_), channel_id=1, source_target_pairs={{0,1},{1,0},{2,3},{3,2},{4,5},{5,4},{6,7},{7,6},{8,9},{9,8},{10,11... | collective-permute-start | bytes 393224 | tf_op jit(solution)/shard_map/ppermute | solution.py:48
  41.4 2.5 %collective-permute-start.25 = (bf16[16,4096]{1,0:T(8,128)(2,1)S(1)}, bf16[16,4096]{1,0:T(8,128)(2,1)S(1)}, u32[]{:S(2)}, u32[]{:S(2)}) collective-permute-start(bf16[16,4096]{1,0:T(8,128)(2,1)S(1)} %collective-permute-done.24.refs_26_), channel_id=1, source_target_pairs={{0,1},{1,0},{2,3},{3,2},{4,5},{5,4},{6,7},{7,6},{8,9},{9,8},{10,11... | collective-permute-start | bytes 393224 | tf_op jit(solution)/shard_map/ppermute | solution.py:48
  43.8 1.3 %collective-permute-start.29 = (bf16[16,4096]{1,0:T(8,128)(2,1)S(1)}, bf16[16,4096]{1,0:T(8,128)(2,1)S(1)}, u32[]{:S(2)}, u32[]{:S(2)}) collective-permute-start(bf16[16,4096]{1,0:T(8,128)(2,1)S(1)} %collective-permute-done.28.refs_30_), channel_id=1, source_target_pairs={{0,1},{1,0},{2,3},{3,2},{4,5},{5,4},{6,7},{7,6},{8,9},{9,8},{10,11... | collective-permute-start | bytes 393224 | tf_op jit(solution)/shard_map/ppermute | solution.py:48

commit v4 on v3

--- a/solution.py
+++ b/solution.py
@@ -2,6 +2,7 @@
 
 import jax
 import jax.numpy as jnp
+import numpy as np
 from jax import lax
 from jax.experimental import pallas as pl
 from jax.experimental.pallas import tpu as pltpu
@@ -32,30 +33,59 @@
     return pltpu.with_memory_space_constraint(array, pltpu.HBM)
 
 
-def place():
-    t = lax.axis_index("train")
-    return t // (XS * CORES), (t // CORES) % XS, t % CORES, lax.axis_index("group")
-
-
-def hop(array, n_train, dz=0, dx=0, dc=0, dg=0):
-    zs = n_train // (XS * CORES)
-    perm = []
-    for g in range(GROUPS):
-        for t in range(n_train):
-            z, x, c = t // (XS * CORES), (t // CORES) % XS, t % CORES
-            to = (((z + dz) % zs) * XS + (x ^ dx)) * CORES + (c ^ dc)
-            perm.append((g * n_train + t, (g ^ dg) * n_train + to))
-    return lax.ppermute(array, ("group", "train"), perm)
-
-
-def precond_kernel(slot, q_ref, in_ref, out_ref, eig_ref, piece_ref, wide_ref, tall_ref, even_ref):
-    layer = (lax.axis_index("group") + slot) % GROUPS
-    q_rows, width = piece_ref.shape
+class Blocks:
+    def __init__(self, array, came):
+        self.array, self.came = array, came
+
+    def hop(self, turn):
+        groups, n_train = self.came.shape
+        perm, came = [], np.zeros_like(self.came)
+        for g in range(groups):
+            for t in range(n_train):
+                z, x, c = t // (XS * CORES), t // CORES % XS, t % CORES
+                to_g, z, x, c = turn(g, z, x, c)
+                to_t = (z * XS + x) * CORES + c
+                perm.append((g * n_train + t, to_g * n_train + to_t))
+                came[to_g, to_t] = self.came[g, t]
+        return Blocks(lax.ppermute(self.array, ("group", "train"), perm), came)
+
+
+def over_core(g, z, x, c):
+    return g, z, x, c ^ 1
+
+
+def over_x(g, z, x, c):
+    return g, z, x ^ 1, c
+
+
+def over_z(g, z, x, c):
+    return g, z ^ 1, x, c
+
+
+def far_z(pair):
+    return lambda g, z, x, c: (g, z ^ (2 * pair + 1 - g), x, c)
+
+
+def x_or_group(g, z, x, c):
+    return (g, z, x ^ 1, c) if c == 0 else (g ^ 1, z, x, c)
+
+
+def group_or_x(g, z, x, c):
+    return (g, z, x ^ 1, c) if c == 1 else (g ^ 1, z, x, c)
+
+
+def precond_kernel(q_ref, in_ref, out_ref, eig_ref, block_ref, *scratch):
+    for layer in range(in_ref.shape[0]):
+        precond_layer(layer, q_ref, in_ref, out_ref, eig_ref, block_ref, *(ref.at[layer] for ref in scratch))
+
+
+def precond_layer(layer, q_ref, in_ref, out_ref, eig_ref, block_ref, wide_ref, tall_ref, even_ref):
+    q_rows, _, width = q_ref.shape
     rows = width // LANES
     p_in, p_out = in_ref.shape[1:]
     left = lax.broadcasted_iota(jnp.int32, (1, LANES), 1) < p_out
 
-    eig = eig_ref[pl.ds(layer, 1), :]
+    eig = eig_ref[layer : layer + 1, :]
     damping = 0.1 / width * jnp.sum(eig, axis=1, keepdims=True)
     for j in range(rows):
         pair = eig[:, j * LANES : (j + 1) * LANES]
@@ -92,8 +122,7 @@
         axis=0,
     )
 
-    flat = jnp.where(layer == 0, q_ref[:, 0, :].astype(jnp.float32), q_ref[:, 1, :].astype(jnp.float32))
-    flat = flat.astype(jnp.bfloat16)
+    flat = q_ref[:, layer, :]
     stacked = jnp.concatenate([flat[:, j * LANES : (j + 1) * LANES] for j in range(rows)], axis=0)
     both = mxu(stacked, fore_right)
     wide_ref[...] = both[:, :LANES] + both[:, LANES:]
@@ -118,30 +147,27 @@
     tall_ref[...] = both[:, :LANES] + both[:, LANES:]
     for j in range(rows):
         block = tall_ref[pl.ds(j, q_rows, stride=rows), :]
-        piece_ref[:, j * LANES : (j + 1) * LANES] = block.astype(jnp.bfloat16)
-
-
-def precondition(slot, query_grads, basis_in, basis_out, eigvals):
+        column = layer * width + j * LANES
+        block_ref[:, column : column + LANES] = block.astype(jnp.bfloat16)
+
+
+def precondition(query_grads, basis_in, basis_out, eigvals):
     q_rows, layers, width = query_grads.shape
-    space = pltpu.HBM if slot == 0 else pltpu.VMEM
-    operands = (query_grads, basis_in, basis_out, eigvals)
-    body, scratch = functools.partial(precond_kernel, slot), []
-    if slot == 0:
-        operands = [in_hbm(a) for a in operands]
-        body = functools.partial(fetched, len(operands), body)
-        scratch = [pltpu.VMEM(a.shape, a.dtype) for a in operands] + [pltpu.SemaphoreType.DMA((len(operands),))]
+    lines = q_rows * width // LANES
+    operands = [in_hbm(a) for a in (query_grads, basis_in, basis_out, eigvals)]
     return pl.pallas_call(
-        body,
-        out_shape=jax.ShapeDtypeStruct((q_rows, width), jnp.bfloat16),
-        in_specs=[pl.BlockSpec(memory_space=space)] * len(operands),
+        functools.partial(fetched, len(operands), precond_kernel),
+        out_shape=jax.ShapeDtypeStruct((q_rows, layers * width), jnp.bfloat16),
+        in_specs=[pl.BlockSpec(memory_space=pltpu.HBM)] * len(operands),
         out_specs=VMEM,
         scratch_shapes=[
-            pltpu.VMEM((q_rows * width // LANES, LANES), jnp.float32),
-            pltpu.VMEM((q_rows * width // LANES, LANES), jnp.float32),
-            pltpu.VMEM((2 * width // LANES, LANES), jnp.float32),
+            pltpu.VMEM((layers, lines, LANES), jnp.float32),
+            pltpu.VMEM((layers, lines, LANES), jnp.float32),
+            pltpu.VMEM((layers, 2 * width // LANES, LANES), jnp.float32),
         ]
-        + scratch,
-        compiler_params=pltpu.CompilerParams(vmem_limit_bytes=8 * MIB),
+        + [pltpu.VMEM(a.shape, a.dtype) for a in operands]
+        + [pltpu.SemaphoreType.DMA((len(operands),))],
+        compiler_params=pltpu.CompilerParams(vmem_limit_bytes=16 * MIB),
         cost_estimate=pl.CostEstimate(flops=10**9, bytes_accessed=4 * MIB, transcendentals=0),
         name="precond",
     )(*operands)
@@ -206,77 +232,77 @@
     )(in_hbm(by_line))
 
 
-def score_kernel(n_train, t_ref, *refs):
-    pieces, out_ref = refs[:-1], refs[-1]
-    zs = n_train // (XS * CORES)
-    q_rows, width = pieces[0].shape
-    n_query = n_train * q_rows
-    z, x, c, g = place()
+def score_kernel(masks, t_ref, *refs):
+    blocks, out_ref = refs[:-1], refs[-1]
+    q_rows, width = blocks[0].shape
+    n_query = len(blocks) * q_rows
     depth = min(width, 1024)
     total = None
-    for part in range(GROUPS):
-        mine = pieces[part * n_train : (part + 1) * n_train]
-        for at in range(0, width, depth):
-            columns = pl.ds(pl.multiple_of((g + part) % GROUPS * width + at, depth), depth)
-            block = jnp.concatenate([piece[:, at : at + depth] for piece in mine], axis=0)
-            term = mxu(t_ref[:, columns], block, NT)
-            total = term if total is None else total + term
-
-    came = lax.broadcasted_iota(jnp.int32, (n_query, n_query), 0)
-    query = lax.broadcasted_iota(jnp.int32, (n_query, n_query), 1)
-    block = came // q_rows
-    to_z = (z - block // (XS * CORES) + zs) % zs
-    to_x = (x + block // CORES) % XS
-    to_c = (c + block) % CORES
-    goes = ((to_z * XS + to_x) * CORES + to_c) * q_rows + came % q_rows
-    order = jnp.where(goes == query, 1.0, 0.0).astype(jnp.bfloat16)
+    for at in range(0, width, depth):
+        block = jnp.concatenate([ref[:, at : at + depth] for ref in blocks], axis=0)
+        term = mxu(t_ref[:, at : at + depth], block, NT)
+        total = term if total is None else total + term
+
+    me, g = lax.axis_index("train"), lax.axis_index("group")
+    row = lax.broadcasted_iota(jnp.int32, (q_rows, n_query), 0)
+    query = lax.broadcasted_iota(jnp.int32, (q_rows, n_query), 1)
+    order = []
+    for mask in masks:
+        c0, c1 = (jnp.where(g == 0, mask[0][c], mask[1][c]) for c in range(CORES))
+        source = me ^ jnp.where(me % CORES == 0, c0, c1)
+        order.append(jnp.where(query == source * q_rows + row, 1.0, 0.0))
+    order = jnp.concatenate(order, axis=0).astype(jnp.bfloat16)
     high, low = halves(total)
     lowest = (total - high.astype(jnp.float32) - low.astype(jnp.float32)).astype(jnp.bfloat16)
     out_ref[...] = mxu(high, order) + mxu(low, order) + mxu(lowest, order)
 
 
+def came_masks(blocks, n_train):
+    xors = blocks.came ^ np.arange(n_train)[None]
+    masks = [[int(xors[g, c]) for c in range(CORES)] for g in range(GROUPS)]
+    assert all((xors[g, c::CORES] == masks[g][c]).all() for g in range(GROUPS) for c in range(CORES))
+    return masks
+
+
 def per_device(n_train, train_grads, query_grads, basis_in, basis_out, eigvals):
     tr_rows = train_grads.shape[0]
     zs = n_train // (XS * CORES)
-    operands = (query_grads, basis_in, basis_out, eigvals)
-    mine = precondition(0, *operands)
-    along_z = [hop(mine, n_train, dz=dz) for dz in range(zs - 1, 0, -1)]
-    first_x = hop(mine, n_train, dx=1)
-    mine, operands, train_grads = lax.optimization_barrier((mine, operands, train_grads))
-    twin = precondition(1, *operands)
+    block = precondition(query_grads, basis_in, basis_out, eigvals)
+    q_rows, width = block.shape
+    own = Blocks(block, np.tile(np.arange(n_train), (GROUPS, 1)))
+
+    far = [own.hop(far_z(pair)) for pair in range(1, zs // 2)]
+    at_x = own.hop(over_x)
+    at_z = own.hop(over_z)
+    twins = [own.hop(over_core)]
+    own.array, train_grads = lax.optimization_barrier((own.array, train_grads))
     flat_train = split_layers(train_grads)
-    along_z, first_x, twin, flat_train = lax.optimization_barrier((along_z, first_x, twin, flat_train))
-    q_rows, width = mine.shape
-
-    pieces = {}
-
-    def keep(array, dz, dx, dg):
-        pieces[dg, dz, dx, 0] = array
-        pieces[dg, dz, dx, 1] = hop(array, n_train, dc=1)
-
-    for dz in range(zs):
-        own = along_z[zs - 1 - dz] if dz else mine
-        over_x = hop(own, n_train, dx=1) if dz else first_x
-        over_g = hop(own, n_train, dg=1) if dz else twin
-        corner = hop(over_g, n_train, dx=1) if dz % 2 else hop(over_x, n_train, dg=1)
-        keep(own, dz, 0, 0)
-        keep(over_x, dz, 1, 0)
-        keep(over_g, dz, 0, 1)
-        keep(corner, dz, 1, 1)
+    at_x.array, flat_train = lax.optimization_barrier((at_x.array, flat_train))
+    at_xz = at_x.hop(over_z)
+    twins.append(at_x.hop(over_core))
+    here = [own, at_x, at_z, at_xz]
+    for fetched_far in far:
+        fetched_far.array, flat_train = lax.optimization_barrier((fetched_far.array, flat_train))
+        first = fetched_far.hop(x_or_group)
+        second = fetched_far.hop(group_or_x)
+        corner = first.hop(group_or_x)
+        twins += [a.hop(over_core) for a in (fetched_far, first, second, corner)]
+        here += [fetched_far, first, second, corner]
+    twins += [a.hop(over_core) for a in (at_z, at_xz)]
+    everything = here + twins
 
     n_query = n_train * q_rows
-    ordered = [pieces[key] for key in sorted(pieces)]
     partial_scores = pl.pallas_call(
-        functools.partial(score_kernel, n_train),
+        functools.partial(score_kernel, [came_masks(a, n_train) for a in everything]),
         out_shape=jax.ShapeDtypeStruct((tr_rows, n_query), jnp.float32),
-        in_specs=[VMEM] * (1 + len(ordered)),
+        in_specs=[VMEM] * (1 + len(everything)),
         out_specs=VMEM,
         compiler_params=pltpu.CompilerParams(vmem_limit_bytes=36 * MIB),
         cost_estimate=pl.CostEstimate(
-            flops=4 * tr_rows * n_query * width, bytes_accessed=2 * width * (tr_rows + n_query), transcendentals=0
+            flops=2 * tr_rows * n_query * width, bytes_accessed=2 * width * (tr_rows + n_query), transcendentals=0
         ),
         name="scores",
-    )(flat_train, *ordered)
+    )(flat_train, *(a.array for a in everything))
     return lax.psum_scatter(partial_scores, "layer", scatter_dimension=1, tiled=True)
 
 

time: 49.2 us -> 40.5 us (0.82)
  waiting for transfers between devices: 16.5 us -> 10.7 us
  starting transfers between devices: 18.9 us -> 16.7 us
  Pallas kernels: 13.4 us -> 12.8 us
    ppermute x30 -> x15, waiting for transfers between devices: 16.5 us -> 10.7 us  [hop(): return Blocks(lax.ppermute(self.array, ('group', 'train'), perm), came)]
    ppermute x30 -> x15, starting transfers between devices: 18.9 us -> 16.7 us  [hop(): return Blocks(lax.ppermute(self.array, ('group', 'train'), perm), came)]
    pallas_call x3 -> x2, Pallas kernels: 7.79 us -> 7.24 us  [the longest x1 3.77 us: per_device(): pl.pallas_call(functools.partial(score_kernel, [came_masks(a, n_train) fo...]
  transfers between devices with their start and end apart: 30 -> 15, of which waited for: 10 -> 4; matrix products, arithmetic and copies ran while one was open for 0% -> 0% of each run, Pallas kernels for 14% -> 14%
where the time goes in v4:
time: 40.5 us; the launch traced here: 40.3 us
  starting transfers between devices  16.7 us (41%)
  Pallas kernels  12.8 us (32%)
  waiting for transfers between devices  10.7 us (26%)
    ppermute x15, starting transfers between devices, hop(): return Blocks(lax.ppermute(self.array, ('group', 'train'), perm), came)  16.7 us
    ppermute x15, waiting for transfers between devices, hop(): return Blocks(lax.ppermute(self.array, ('group', 'train'), perm), came)  10.7 us
    pallas_call x1, Pallas kernels, split_layers(): pl.pallas_call(functools.partial(split_kernel, layers), out_shape=jax.Sha...  5.57 us
    pallas_call x1, Pallas kernels, per_device(): pl.pallas_call(functools.partial(score_kernel, [came_masks(a, n_train) fo...  3.77 us
    pallas_call x1, Pallas kernels, precondition(): pl.pallas_call(functools.partial(fetched, len(operands), precond_kernel),...  3.47 us
  transfers between devices with their start and end apart: 15, of which 4 were waited for; matrix products, arithmetic and copies ran while one was open for 0% of the time, Pallas kernels for 14%

profile of v4, /device:TPU:0, one launch (start us, length us, event | category | flops | bytes accessed | tf_op | source)
XLA Modules:
  0.0 40.3 jit_solution(8090138476536428984)
XLA Ops:
  0.0 3.5 %precond.1.refs_0_ = bf16[16,8192]{1,0:T(8,128)(2,1)S(1)} custom-call(bf16[16,2,4096]{2,1,0:T(2,128)(2,1)} %refs_0_.1, f32[2,64,64]{2,1,0:T(8,128)} %refs_1_.1, f32[2,64,64]{2,1,0:T(8,128)} %refs_2_.1, f32[2,4096]{1,0:T(2,128)} %refs_3_.1), custom_call_target="tpu_custom_call" | custom-call | flops 1000000000 | bytes 4194304 | tf_op jit(solution)/shard_map/precond/pallas_call | solution.py:158
  3.5 3.0 %collective-permute-start.1 = (bf16[16,8192]{1,0:T(8,128)(2,1)S(1)}, bf16[16,8192]{1,0:T(8,128)(2,1)S(1)}, u32[]{:S(2)}, u32[]{:S(2)}) collective-permute-start(bf16[16,8192]{1,0:T(8,128)(2,1)S(1)} %precond.1.refs_0_), channel_id=1, source_target_pairs={{0,2},{1,3},{2,0},{3,1},{4,6},{5,7},{6,4},{7,5},{8,10},{9,11},{10,... | collective-permute-start | bytes 786440 | tf_op jit(solution)/shard_map/ppermute | solution.py:50
  6.5 3.6 %collective-permute-start = (bf16[16,8192]{1,0:T(8,128)(2,1)S(1)}, bf16[16,8192]{1,0:T(8,128)(2,1)S(1)}, u32[]{:S(2)}, u32[]{:S(2)}) collective-permute-start(bf16[16,8192]{1,0:T(8,128)(2,1)S(1)} %precond.1.refs_0_), channel_id=1, source_target_pairs={{0,12},{1,13},{2,14},{3,15},{4,8},{5,9},{6,10},{7,11},{8,4},{9,5},... | collective-permute-start | bytes 786440 | tf_op jit(solution)/shard_map/ppermute | solution.py:50
  10.1 0.0 collective-permute-start.7
  10.1 0.0 collective-permute-start.2
  10.1 5.6 %split.1.t_ref = bf16[512,8192]{1,0:T(8,128)(2,1)S(1)} custom-call(bf16[512,64,128]{2,1,0:T(8,128)(2,1)} %bitcast.5), custom_call_target="tpu_custom_call" | custom-call | flops 1000000000 | bytes 16777216 | tf_op jit(solution)/shard_map/split/pallas_call | solution.py:219
  15.7 0.0 collective-permute-done.1.refs_1_
  15.7 1.8 %collective-permute-done.refs_4_ = bf16[16,8192]{1,0:T(8,128)(2,1)S(1)} collective-permute-done((bf16[16,8192]{1,0:T(8,128)(2,1)S(1)}, bf16[16,8192]{1,0:T(8,128)(2,1)S(1)}, u32[]{:S(2)}, u32[]{:S(2)}) %collective-permute-start) | collective-permute-done | bytes 262176 | tf_op jit(solution)/shard_map/ppermute | solution.py:50
  17.5 0.3 collective-permute-start.4
  17.8 4.0 %collective-permute-done.2.refs_2_ = bf16[16,8192]{1,0:T(8,128)(2,1)S(1)} collective-permute-done((bf16[16,8192]{1,0:T(8,128)(2,1)S(1)}, bf16[16,8192]{1,0:T(8,128)(2,1)S(1)}, u32[]{:S(2)}, u32[]{:S(2)}) %collective-permute-start.2) | collective-permute-done | bytes 262176 | tf_op jit(solution)/shard_map/ppermute | solution.py:50
  21.8 0.1 collective-permute-start.13
  21.9 0.4 %collective-permute-start.9 = (bf16[16,8192]{1,0:T(8,128)(2,1)S(1)}, bf16[16,8192]{1,0:T(8,128)(2,1)S(1)}, u32[]{:S(2)}, u32[]{:S(2)}) collective-permute-start(bf16[16,8192]{1,0:T(8,128)(2,1)S(1)} %collective-permute-done.refs_4_), channel_id=1, source_target_pairs={{0,1},{1,0},{2,3},{3,2},{4,5},{5,4},{6,7},{7,6},{8,9},{9,8},{10,11... | collective-permute-start | bytes 786440 | tf_op jit(solution)/shard_map/ppermute | solution.py:50
  22.3 2.0 %collective-permute-start.5 = (bf16[16,8192]{1,0:T(8,128)(2,1)S(1)}, bf16[16,8192]{1,0:T(8,128)(2,1)S(1)}, u32[]{:S(2)}, u32[]{:S(2)}) collective-permute-start(bf16[16,8192]{1,0:T(8,128)(2,1)S(1)} %collective-permute-done.refs_4_), channel_id=1, source_target_pairs={{0,16},{1,3},{2,18},{3,1},{4,20},{5,7},{6,22},{7,5},{8,24},{9,11},... | collective-permute-start | bytes 786440 | tf_op jit(solution)/shard_map/ppermute | solution.py:50
  24.3 0.0 collective-permute-done.7.refs_8_
  24.3 0.2 collective-permute-start.3
  24.5 0.0 collective-permute-done.4.refs_5_
  24.5 6.1 %collective-permute-start.6 = (bf16[16,8192]{1,0:T(8,128)(2,1)S(1)}, bf16[16,8192]{1,0:T(8,128)(2,1)S(1)}, u32[]{:S(2)}, u32[]{:S(2)}) collective-permute-start(bf16[16,8192]{1,0:T(8,128)(2,1)S(1)} %collective-permute-done.4.refs_5_), channel_id=1, source_target_pairs={{0,16},{1,3},{2,18},{3,1},{4,20},{5,7},{6,22},{7,5},{8,24},{9,11},... | collective-permute-start | bytes 786440 | tf_op jit(solution)/shard_map/ppermute | solution.py:50
  30.6 0.0 collective-permute-done.13.refs_14_
  30.6 0.0 collective-permute-start.8
  30.6 0.0 collective-permute-done.9.refs_10_
  30.6 0.5 %collective-permute-start.10 = (bf16[16,8192]{1,0:T(8,128)(2,1)S(1)}, bf16[16,8192]{1,0:T(8,128)(2,1)S(1)}, u32[]{:S(2)}, u32[]{:S(2)}) collective-permute-start(bf16[16,8192]{1,0:T(8,128)(2,1)S(1)} %collective-permute-done.4.refs_5_), channel_id=1, source_target_pairs={{0,1},{1,0},{2,3},{3,2},{4,5},{5,4},{6,7},{7,6},{8,9},{9,8},{10,11... | collective-permute-start | bytes 786440 | tf_op jit(solution)/shard_map/ppermute | solution.py:50
  31.1 0.0 collective-permute-done.5.refs_6_
  31.1 0.1 collective-permute-start.11
  31.2 0.0 collective-permute-done.3.refs_3_
  31.2 0.4 %collective-permute-start.14 = (bf16[16,8192]{1,0:T(8,128)(2,1)S(1)}, bf16[16,8192]{1,0:T(8,128)(2,1)S(1)}, u32[]{:S(2)}, u32[]{:S(2)}) collective-permute-start(bf16[16,8192]{1,0:T(8,128)(2,1)S(1)} %collective-permute-done.3.refs_3_), channel_id=1, source_target_pairs={{0,1},{1,0},{2,3},{3,2},{4,5},{5,4},{6,7},{7,6},{8,9},{9,8},{10,11... | collective-permute-start | bytes 786440 | tf_op jit(solution)/shard_map/ppermute | solution.py:50
  31.6 3.3 %collective-permute-done.6.refs_7_ = bf16[16,8192]{1,0:T(8,128)(2,1)S(1)} collective-permute-done((bf16[16,8192]{1,0:T(8,128)(2,1)S(1)}, bf16[16,8192]{1,0:T(8,128)(2,1)S(1)}, u32[]{:S(2)}, u32[]{:S(2)}) %collective-permute-start.6) | collective-permute-done | bytes 262176 | tf_op jit(solution)/shard_map/ppermute | solution.py:50
  35.0 0.0 collective-permute-start.12
  35.0 0.0 collective-permute-done.8.refs_9_
  35.0 0.0 collective-permute-done.11.refs_12_
  35.0 0.0 collective-permute-done.10.refs_11_
  35.0 0.0 collective-permute-done.14.refs_15_
  35.0 1.5 %collective-permute-done.12.refs_13_ = bf16[16,8192]{1,0:T(8,128)(2,1)S(1)} collective-permute-done((bf16[16,8192]{1,0:T(8,128)(2,1)S(1)}, bf16[16,8192]{1,0:T(8,128)(2,1)S(1)}, u32[]{:S(2)}, u32[]{:S(2)}) %collective-permute-start.12) | collective-permute-done | bytes 262176 | tf_op jit(solution)/shard_map/ppermute | solution.py:50
  36.5 3.8 %scores.1 = f32[512,256]{1,0:T(8,128)} custom-call(bf16[512,8192]{1,0:T(8,128)(2,1)S(1)} %split.1.t_ref, bf16[16,8192]{1,0:T(8,128)(2,1)S(1)} %precond.1.refs_0_, bf16[16,8192]{1,0:T(8,128)(2,1)S(1)} %collective-permute-done.1.refs_1_, bf16[16,8192]{1,0:T(8,128)(2,1)S(1)} %collective-permute-done.2.refs_2_, ...), custom_call_target="tpu_custom_call" | custom-call | flops 2147483648 | bytes 12582912 | tf_op jit(solution)/shard_map/scores/pallas_call | solution.py:295
Async XLA Ops:
  3.5 12.2 %collective-permute-start.1 = (bf16[16,8192]{1,0:T(8,128)(2,1)S(1)}, bf16[16,8192]{1,0:T(8,128)(2,1)S(1)}, u32[]{:S(2)}, u32[]{:S(2)}) collective-permute-start(bf16[16,8192]{1,0:T(8,128)(2,1)S(1)} %precond.1.refs_0_), channel_id=1, source_target_pairs={{0,2},{1,3},{2,0},{3,1},{4,6},{5,7},{6,4},{7,5},{8,10},{9,11},{10,... | collective-permute-start | bytes 786440 | tf_op jit(solution)/shard_map/ppermute | solution.py:50
  6.5 11.0 %collective-permute-start = (bf16[16,8192]{1,0:T(8,128)(2,1)S(1)}, bf16[16,8192]{1,0:T(8,128)(2,1)S(1)}, u32[]{:S(2)}, u32[]{:S(2)}) collective-permute-start(bf16[16,8192]{1,0:T(8,128)(2,1)S(1)} %precond.1.refs_0_), channel_id=1, source_target_pairs={{0,12},{1,13},{2,14},{3,15},{4,8},{5,9},{6,10},{7,11},{8,4},{9,5},... | collective-permute-start | bytes 786440 | tf_op jit(solution)/shard_map/ppermute | solution.py:50
  10.1 14.3 %collective-permute-start.7 = (bf16[16,8192]{1,0:T(8,128)(2,1)S(1)}, bf16[16,8192]{1,0:T(8,128)(2,1)S(1)}, u32[]{:S(2)}, u32[]{:S(2)}) collective-permute-start(bf16[16,8192]{1,0:T(8,128)(2,1)S(1)} %precond.1.refs_0_), channel_id=1, source_target_pairs={{0,1},{1,0},{2,3},{3,2},{4,5},{5,4},{6,7},{7,6},{8,9},{9,8},{10,11... | collective-permute-start | bytes 786440 | tf_op jit(solution)/shard_map/ppermute | solution.py:50
  10.1 11.7 %collective-permute-start.2 = (bf16[16,8192]{1,0:T(8,128)(2,1)S(1)}, bf16[16,8192]{1,0:T(8,128)(2,1)S(1)}, u32[]{:S(2)}, u32[]{:S(2)}) collective-permute-start(bf16[16,8192]{1,0:T(8,128)(2,1)S(1)} %precond.1.refs_0_), channel_id=1, source_target_pairs={{0,4},{1,5},{2,6},{3,7},{4,0},{5,1},{6,2},{7,3},{8,12},{9,13},{10,... | collective-permute-start | bytes 786440 | tf_op jit(solution)/shard_map/ppermute | solution.py:50
  17.5 7.0 %collective-permute-start.4 = (bf16[16,8192]{1,0:T(8,128)(2,1)S(1)}, bf16[16,8192]{1,0:T(8,128)(2,1)S(1)}, u32[]{:S(2)}, u32[]{:S(2)}) collective-permute-start(bf16[16,8192]{1,0:T(8,128)(2,1)S(1)} %collective-permute-done.refs_4_), channel_id=1, source_target_pairs={{0,2},{1,17},{2,0},{3,19},{4,6},{5,21},{6,4},{7,23},{8,10},{9,25},... | collective-permute-start | bytes 786440 | tf_op jit(solution)/shard_map/ppermute | solution.py:50
  21.8 8.8 %collective-permute-start.13 = (bf16[16,8192]{1,0:T(8,128)(2,1)S(1)}, bf16[16,8192]{1,0:T(8,128)(2,1)S(1)}, u32[]{:S(2)}, u32[]{:S(2)}) collective-permute-start(bf16[16,8192]{1,0:T(8,128)(2,1)S(1)} %collective-permute-done.2.refs_2_), channel_id=1, source_target_pairs={{0,1},{1,0},{2,3},{3,2},{4,5},{5,4},{6,7},{7,6},{8,9},{9,8},{10,11... | collective-permute-start | bytes 786440 | tf_op jit(solution)/shard_map/ppermute | solution.py:50
  21.9 8.7 %collective-permute-start.9 = (bf16[16,8192]{1,0:T(8,128)(2,1)S(1)}, bf16[16,8192]{1,0:T(8,128)(2,1)S(1)}, u32[]{:S(2)}, u32[]{:S(2)}) collective-permute-start(bf16[16,8192]{1,0:T(8,128)(2,1)S(1)} %collective-permute-done.refs_4_), channel_id=1, source_target_pairs={{0,1},{1,0},{2,3},{3,2},{4,5},{5,4},{6,7},{7,6},{8,9},{9,8},{10,11... | collective-permute-start | bytes 786440 | tf_op jit(solution)/shard_map/ppermute | solution.py:50
  22.3 8.8 %collective-permute-start.5 = (bf16[16,8192]{1,0:T(8,128)(2,1)S(1)}, bf16[16,8192]{1,0:T(8,128)(2,1)S(1)}, u32[]{:S(2)}, u32[]{:S(2)}) collective-permute-start(bf16[16,8192]{1,0:T(8,128)(2,1)S(1)} %collective-permute-done.refs_4_), channel_id=1, source_target_pairs={{0,16},{1,3},{2,18},{3,1},{4,20},{5,7},{6,22},{7,5},{8,24},{9,11},... | collective-permute-start | bytes 786440 | tf_op jit(solution)/shard_map/ppermute | solution.py:50
  24.3 6.9 %collective-permute-start.3 = (bf16[16,8192]{1,0:T(8,128)(2,1)S(1)}, bf16[16,8192]{1,0:T(8,128)(2,1)S(1)}, u32[]{:S(2)}, u32[]{:S(2)}) collective-permute-start(bf16[16,8192]{1,0:T(8,128)(2,1)S(1)} %collective-permute-done.1.refs_1_), channel_id=1, source_target_pairs={{0,4},{1,5},{2,6},{3,7},{4,0},{5,1},{6,2},{7,3},{8,12},{9,13},{10,... | collective-permute-start | bytes 786440 | tf_op jit(solution)/shard_map/ppermute | solution.py:50
  24.5 10.4 %collective-permute-start.6 = (bf16[16,8192]{1,0:T(8,128)(2,1)S(1)}, bf16[16,8192]{1,0:T(8,128)(2,1)S(1)}, u32[]{:S(2)}, u32[]{:S(2)}) collective-permute-start(bf16[16,8192]{1,0:T(8,128)(2,1)S(1)} %collective-permute-done.4.refs_5_), channel_id=1, source_target_pairs={{0,16},{1,3},{2,18},{3,1},{4,20},{5,7},{6,22},{7,5},{8,24},{9,11},... | collective-permute-start | bytes 786440 | tf_op jit(solution)/shard_map/ppermute | solution.py:50
  30.6 4.4 %collective-permute-start.8 = (bf16[16,8192]{1,0:T(8,128)(2,1)S(1)}, bf16[16,8192]{1,0:T(8,128)(2,1)S(1)}, u32[]{:S(2)}, u32[]{:S(2)}) collective-permute-start(bf16[16,8192]{1,0:T(8,128)(2,1)S(1)} %collective-permute-done.1.refs_1_), channel_id=1, source_target_pairs={{0,1},{1,0},{2,3},{3,2},{4,5},{5,4},{6,7},{7,6},{8,9},{9,8},{10,11... | collective-permute-start | bytes 786440 | tf_op jit(solution)/shard_map/ppermute | solution.py:50
  30.6 4.4 %collective-permute-start.10 = (bf16[16,8192]{1,0:T(8,128)(2,1)S(1)}, bf16[16,8192]{1,0:T(8,128)(2,1)S(1)}, u32[]{:S(2)}, u32[]{:S(2)}) collective-permute-start(bf16[16,8192]{1,0:T(8,128)(2,1)S(1)} %collective-permute-done.4.refs_5_), channel_id=1, source_target_pairs={{0,1},{1,0},{2,3},{3,2},{4,5},{5,4},{6,7},{7,6},{8,9},{9,8},{10,11... | collective-permute-start | bytes 786440 | tf_op jit(solution)/shard_map/ppermute | solution.py:50
  31.1 3.8 %collective-permute-start.11 = (bf16[16,8192]{1,0:T(8,128)(2,1)S(1)}, bf16[16,8192]{1,0:T(8,128)(2,1)S(1)}, u32[]{:S(2)}, u32[]{:S(2)}) collective-permute-start(bf16[16,8192]{1,0:T(8,128)(2,1)S(1)} %collective-permute-done.5.refs_6_), channel_id=1, source_target_pairs={{0,1},{1,0},{2,3},{3,2},{4,5},{5,4},{6,7},{7,6},{8,9},{9,8},{10,11... | collective-permute-start | bytes 786440 | tf_op jit(solution)/shard_map/ppermute | solution.py:50
  31.2 3.8 %collective-permute-start.14 = (bf16[16,8192]{1,0:T(8,128)(2,1)S(1)}, bf16[16,8192]{1,0:T(8,128)(2,1)S(1)}, u32[]{:S(2)}, u32[]{:S(2)}) collective-permute-start(bf16[16,8192]{1,0:T(8,128)(2,1)S(1)} %collective-permute-done.3.refs_3_), channel_id=1, source_target_pairs={{0,1},{1,0},{2,3},{3,2},{4,5},{5,4},{6,7},{7,6},{8,9},{9,8},{10,11... | collective-permute-start | bytes 786440 | tf_op jit(solution)/shard_map/ppermute | solution.py:50
  35.0 1.5 %collective-permute-start.12 = (bf16[16,8192]{1,0:T(8,128)(2,1)S(1)}, bf16[16,8192]{1,0:T(8,128)(2,1)S(1)}, u32[]{:S(2)}, u32[]{:S(2)}) collective-permute-start(bf16[16,8192]{1,0:T(8,128)(2,1)S(1)} %collective-permute-done.6.refs_7_), channel_id=1, source_target_pairs={{0,1},{1,0},{2,3},{3,2},{4,5},{5,4},{6,7},{7,6},{8,9},{9,8},{10,11... | collective-permute-start | bytes 786440 | tf_op jit(solution)/shard_map/ppermute | solution.py:50

commit v5 on v4

--- a/solution.py
+++ b/solution.py
@@ -38,16 +38,34 @@
         self.array, self.came = array, came
 
     def hop(self, turn):
-        groups, n_train = self.came.shape
-        perm, came = [], np.zeros_like(self.came)
+        groups, n_train = self.came[0].shape
+        perm, came = [], [np.zeros_like(a) for a in self.came]
         for g in range(groups):
             for t in range(n_train):
                 z, x, c = t // (XS * CORES), t // CORES % XS, t % CORES
                 to_g, z, x, c = turn(g, z, x, c)
                 to_t = (z * XS + x) * CORES + c
                 perm.append((g * n_train + t, to_g * n_train + to_t))
-                came[to_g, to_t] = self.came[g, t]
+                for here, there in zip(self.came, came):
+                    there[to_g, to_t] = here[g, t]
         return Blocks(lax.ppermute(self.array, ("group", "train"), perm), came)
+
+    def columns(self, start, stop):
+        return Blocks(self.array[:, start:stop], self.came)
+
+
+def stack(*parts):
+    return Blocks(jnp.concatenate([a.array for a in parts], axis=0), sum((a.came for a in parts), []))
+
+
+def beside(left, right):
+    assert all((a == b).all() for a, b in zip(left.came, right.came))
+    return Blocks(jnp.concatenate([left.array, right.array], axis=1), left.came)
+
+
+def after(kernel_result, *parts):
+    arrays, kernel_result = lax.optimization_barrier(([a.array for a in parts], kernel_result))
+    return kernel_result, *(Blocks(array, a.came) for array, a in zip(arrays, parts))
 
 
 def over_core(g, z, x, c):
@@ -66,12 +84,8 @@
     return lambda g, z, x, c: (g, z ^ (2 * pair + 1 - g), x, c)
 
 
-def x_or_group(g, z, x, c):
-    return (g, z, x ^ 1, c) if c == 0 else (g ^ 1, z, x, c)
-
-
-def group_or_x(g, z, x, c):
-    return (g, z, x ^ 1, c) if c == 1 else (g ^ 1, z, x, c)
+def over_group(g, z, x, c):
+    return g ^ 1, z, x, c
 
 
 def precond_kernel(q_ref, in_ref, out_ref, eig_ref, block_ref, *scratch):
@@ -235,7 +249,7 @@
 def score_kernel(masks, t_ref, *refs):
     blocks, out_ref = refs[:-1], refs[-1]
     q_rows, width = blocks[0].shape
-    n_query = len(blocks) * q_rows
+    n_query = len(masks) * q_rows
     depth = min(width, 1024)
     total = None
     for at in range(0, width, depth):
@@ -257,8 +271,8 @@
     out_ref[...] = mxu(high, order) + mxu(low, order) + mxu(lowest, order)
 
 
-def came_masks(blocks, n_train):
-    xors = blocks.came ^ np.arange(n_train)[None]
+def came_masks(came):
+    xors = came ^ np.arange(came.shape[1])[None]
     masks = [[int(xors[g, c]) for c in range(CORES)] for g in range(GROUPS)]
     assert all((xors[g, c::CORES] == masks[g][c]).all() for g in range(GROUPS) for c in range(CORES))
     return masks
@@ -269,31 +283,38 @@
     zs = n_train // (XS * CORES)
     block = precondition(query_grads, basis_in, basis_out, eigvals)
     q_rows, width = block.shape
-    own = Blocks(block, np.tile(np.arange(n_train), (GROUPS, 1)))
+    own = Blocks(block, [np.tile(np.arange(n_train), (GROUPS, 1))])
 
     far = [own.hop(far_z(pair)) for pair in range(1, zs // 2)]
     at_x = own.hop(over_x)
     at_z = own.hop(over_z)
     twins = [own.hop(over_core)]
-    own.array, train_grads = lax.optimization_barrier((own.array, train_grads))
+    train_grads, own = after(train_grads, own)
     flat_train = split_layers(train_grads)
-    at_x.array, flat_train = lax.optimization_barrier((at_x.array, flat_train))
-    at_xz = at_x.hop(over_z)
-    twins.append(at_x.hop(over_core))
-    here = [own, at_x, at_z, at_xz]
-    for fetched_far in far:
-        fetched_far.array, flat_train = lax.optimization_barrier((fetched_far.array, flat_train))
-        first = fetched_far.hop(x_or_group)
-        second = fetched_far.hop(group_or_x)
-        corner = first.hop(group_or_x)
-        twins += [a.hop(over_core) for a in (fetched_far, first, second, corner)]
-        here += [fetched_far, first, second, corner]
-    twins += [a.hop(over_core) for a in (at_z, at_xz)]
+    here = [own, at_x, at_z]
+    for pair, one in enumerate(far):
+        flat_train, one = after(flat_train, one)
+        by_x, by_group = one.hop(over_x), one.hop(over_group)
+        if pair == 0:
+            one.array, at_x = after(one.array, at_x)
+            at_xz = at_x.hop(over_z)
+            twins.append(stack(at_x, one).hop(over_core))
+            twins.append(stack(at_z, at_xz).hop(over_core))
+            here.append(at_xz)
+        else:
+            twins.append(one.hop(over_core))
+        twins.append(stack(by_x, by_group).hop(over_core))
+        corner = beside(
+            by_x.columns(0, width // 2).hop(over_group), by_group.columns(width // 2, width).hop(over_x)
+        )
+        twins.append(corner.hop(over_core))
+        here += [one, by_x, by_group, corner]
     everything = here + twins
+    masks = [came_masks(came) for a in everything for came in a.came]
 
     n_query = n_train * q_rows
     partial_scores = pl.pallas_call(
-        functools.partial(score_kernel, [came_masks(a, n_train) for a in everything]),
+        functools.partial(score_kernel, masks),
         out_shape=jax.ShapeDtypeStruct((tr_rows, n_query), jnp.float32),
         in_specs=[VMEM] * (1 + len(everything)),
         out_specs=VMEM,

time: 40.5 us -> 40.2 us (level)
    ppermute x15 -> x13, waiting for transfers between devices: 10.7 us -> 10.5 us  [hop(): return Blocks(lax.ppermute(self.array, ('group', 'train'), perm), came)]
    ppermute x15 -> x13, starting transfers between devices: 16.7 us -> 16.5 us  [hop(): return Blocks(lax.ppermute(self.array, ('group', 'train'), perm), came)]
  transfers between devices with their start and end apart: 15 -> 13, of which waited for: 4 -> 6; matrix products, arithmetic and copies ran while one was open for 0% -> 0% of each run, Pallas kernels for 14% -> 14%
where the time goes in v5:
time: 40.2 us; the launch traced here: 40 us
  starting transfers between devices  16.5 us (41%)
  Pallas kernels  12.8 us (32%)
  waiting for transfers between devices  10.5 us (26%)
    ppermute x13, starting transfers between devices, hop(): return Blocks(lax.ppermute(self.array, ('group', 'train'), perm), came)  16.5 us
    ppermute x13, waiting for transfers between devices, hop(): return Blocks(lax.ppermute(self.array, ('group', 'train'), perm), came)  10.5 us
    pallas_call x1, Pallas kernels, split_layers(): pl.pallas_call(functools.partial(split_kernel, layers), out_shape=jax.Sha...  5.57 us
    pallas_call x1, Pallas kernels, per_device(): pl.pallas_call(functools.partial(score_kernel, masks), out_shape=jax.Shap...  3.76 us
    pallas_call x1, Pallas kernels, precondition(): pl.pallas_call(functools.partial(fetched, len(operands), precond_kernel),...  3.47 us
  transfers between devices with their start and end apart: 13, of which 6 were waited for; matrix products, arithmetic and copies ran while one was open for 0% of the time, Pallas kernels for 14%

profile of v5, /device:TPU:0, one launch (start us, length us, event | category | flops | bytes accessed | tf_op | source)
XLA Modules:
  0.0 40.0 jit_solution(5686809255691418540)
XLA Ops:
  0.0 3.5 %precond.1.refs_0_ = bf16[16,8192]{1,0:T(8,128)(2,1)S(1)} custom-call(bf16[16,2,4096]{2,1,0:T(2,128)(2,1)} %refs_0_.1, f32[2,64,64]{2,1,0:T(8,128)} %refs_1_.1, f32[2,64,64]{2,1,0:T(8,128)} %refs_2_.1, f32[2,4096]{1,0:T(2,128)} %refs_3_.1), custom_call_target="tpu_custom_call" | custom-call | flops 1000000000 | bytes 4194304 | tf_op jit(solution)/shard_map/precond/pallas_call | solution.py:172
  3.5 5.1 %collective-permute-start = (bf16[16,8192]{1,0:T(8,128)(2,1)S(1)}, bf16[16,8192]{1,0:T(8,128)(2,1)S(1)}, u32[]{:S(2)}, u32[]{:S(2)}) collective-permute-start(bf16[16,8192]{1,0:T(8,128)(2,1)S(1)} %precond.1.refs_0_), channel_id=1, source_target_pairs={{0,12},{1,13},{2,14},{3,15},{4,8},{5,9},{6,10},{7,11},{8,4},{9,5},... | collective-permute-start | bytes 786440 | tf_op jit(solution)/shard_map/ppermute | solution.py:51
  8.6 1.5 %collective-permute-start.1 = (bf16[16,8192]{1,0:T(8,128)(2,1)S(1)}, bf16[16,8192]{1,0:T(8,128)(2,1)S(1)}, u32[]{:S(2)}, u32[]{:S(2)}) collective-permute-start(bf16[16,8192]{1,0:T(8,128)(2,1)S(1)} %precond.1.refs_0_), channel_id=1, source_target_pairs={{0,2},{1,3},{2,0},{3,1},{4,6},{5,7},{6,4},{7,5},{8,10},{9,11},{10,... | collective-permute-start | bytes 786440 | tf_op jit(solution)/shard_map/ppermute | solution.py:51
  10.1 0.0 collective-permute-start.2
  10.1 0.0 collective-permute-start.8
  10.1 5.6 %split.1.t_ref = bf16[512,8192]{1,0:T(8,128)(2,1)S(1)} custom-call(bf16[512,64,128]{2,1,0:T(8,128)(2,1)} %bitcast.5), custom_call_target="tpu_custom_call" | custom-call | flops 1000000000 | bytes 16777216 | tf_op jit(solution)/shard_map/split/pallas_call | solution.py:233
  15.7 0.1 collective-permute-done.refs_4_
  15.8 1.7 %collective-permute-start.4 = (bf16[16,8192]{1,0:T(8,128)(2,1)S(1)}, bf16[16,8192]{1,0:T(8,128)(2,1)S(1)}, u32[]{:S(2)}, u32[]{:S(2)}) collective-permute-start(bf16[16,8192]{1,0:T(8,128)(2,1)S(1)} %collective-permute-done.refs_4_), channel_id=1, source_target_pairs={{0,2},{1,3},{2,0},{3,1},{4,6},{5,7},{6,4},{7,5},{8,10},{9,11},{10,... | collective-permute-start | bytes 786440 | tf_op jit(solution)/shard_map/ppermute | solution.py:51
  17.5 5.2 %collective-permute-start.5 = (bf16[16,8192]{1,0:T(8,128)(2,1)S(1)}, bf16[16,8192]{1,0:T(8,128)(2,1)S(1)}, u32[]{:S(2)}, u32[]{:S(2)}) collective-permute-start(bf16[16,8192]{1,0:T(8,128)(2,1)S(1)} %collective-permute-done.refs_4_), channel_id=1, source_target_pairs={{0,16},{1,17},{2,18},{3,19},{4,20},{5,21},{6,22},{7,23},{8,24},{9,... | collective-permute-start | bytes 786440 | tf_op jit(solution)/shard_map/ppermute | solution.py:51
  22.7 0.0 collective-permute-done.1.refs_1_
  22.7 0.6 %collective-permute-start.3 = (bf16[16,8192]{1,0:T(8,128)(2,1)S(1)}, bf16[16,8192]{1,0:T(8,128)(2,1)S(1)}, u32[]{:S(2)}, u32[]{:S(2)}) collective-permute-start(bf16[16,8192]{1,0:T(8,128)(2,1)S(1)} %collective-permute-done.1.refs_1_), channel_id=1, source_target_pairs={{0,4},{1,5},{2,6},{3,7},{4,0},{5,1},{6,2},{7,3},{8,12},{9,13},{10,... | collective-permute-start | bytes 786440 | tf_op jit(solution)/shard_map/ppermute | solution.py:51
  23.3 1.2 %collective-permute-done.4.refs_5_ = bf16[16,8192]{1,0:T(8,128)(2,1)S(1)} collective-permute-done((bf16[16,8192]{1,0:T(8,128)(2,1)S(1)}, bf16[16,8192]{1,0:T(8,128)(2,1)S(1)}, u32[]{:S(2)}, u32[]{:S(2)}) %collective-permute-start.4) | collective-permute-done | bytes 262176 | tf_op jit(solution)/shard_map/ppermute | solution.py:51
  24.5 0.0 collective-permute-start.9
  24.5 3.3 %collective-permute-done.5.refs_6_ = bf16[16,8192]{1,0:T(8,128)(2,1)S(1)} collective-permute-done((bf16[16,8192]{1,0:T(8,128)(2,1)S(1)}, bf16[16,8192]{1,0:T(8,128)(2,1)S(1)}, u32[]{:S(2)}, u32[]{:S(2)}) %collective-permute-start.5) | collective-permute-done | bytes 262176 | tf_op jit(solution)/shard_map/ppermute | solution.py:51
  27.8 1.7 %collective-permute-start.6 = (bf16[16,4096]{1,0:T(8,128)(2,1)S(1)}, bf16[16,4096]{1,0:T(8,128)(2,1)S(1)}, u32[]{:S(2)}, u32[]{:S(2)}) collective-permute-start(bf16[16,4096]{1,0:T(8,128)(2,1)S(1)} %slice.8), channel_id=1, source_target_pairs={{0,16},{1,17},{2,18},{3,19},{4,20},{5,21},{6,22},{7,23},{8,24},{9,... | collective-permute-start | bytes 393224 | tf_op jit(solution)/shard_map/ppermute | solution.py:51
  29.6 0.0 collective-permute-done.2.refs_2_
  29.6 0.6 %collective-permute-start.7 = (bf16[16,4096]{1,0:T(8,128)(2,1)S(1)}, bf16[16,4096]{1,0:T(8,128)(2,1)S(1)}, u32[]{:S(2)}, u32[]{:S(2)}) collective-permute-start(bf16[16,4096]{1,0:T(8,128)(2,1)S(1)} %slice.9), channel_id=1, source_target_pairs={{0,2},{1,3},{2,0},{3,1},{4,6},{5,7},{6,4},{7,5},{8,10},{9,11},{10,... | collective-permute-start | bytes 393224 | tf_op jit(solution)/shard_map/ppermute | solution.py:51
  30.2 0.0 collective-permute-done.3.refs_3_
  30.2 0.0 collective-permute-start.11
  30.2 2.5 %collective-permute-done.6 = bf16[16,4096]{1,0:T(8,128)(2,1)S(1)} collective-permute-done((bf16[16,4096]{1,0:T(8,128)(2,1)S(1)}, bf16[16,4096]{1,0:T(8,128)(2,1)S(1)}, u32[]{:S(2)}, u32[]{:S(2)}) %collective-permute-start.6) | collective-permute-done | bytes 131104 | tf_op jit(solution)/shard_map/ppermute | solution.py:51
  32.8 0.0 collective-permute-start.10
  32.8 1.9 %collective-permute-done.7 = bf16[16,4096]{1,0:T(8,128)(2,1)S(1)} collective-permute-done((bf16[16,4096]{1,0:T(8,128)(2,1)S(1)}, bf16[16,4096]{1,0:T(8,128)(2,1)S(1)}, u32[]{:S(2)}, u32[]{:S(2)}) %collective-permute-start.7) | collective-permute-done | bytes 131104 | tf_op jit(solution)/shard_map/ppermute | solution.py:51
  34.6 0.1 collective-permute-start.12
  34.7 0.0 collective-permute-done.8.refs_8_
  34.7 0.0 collective-permute-done.9.refs_9_
  34.7 1.5 %collective-permute-done.12.refs_12_ = bf16[16,8192]{1,0:T(8,128)(2,1)S(1)} collective-permute-done((bf16[16,8192]{1,0:T(8,128)(2,1)S(1)}, bf16[16,8192]{1,0:T(8,128)(2,1)S(1)}, u32[]{:S(2)}, u32[]{:S(2)}) %collective-permute-start.12) | collective-permute-done | bytes 262176 | tf_op jit(solution)/shard_map/ppermute | solution.py:51
  36.3 0.0 collective-permute-done.11.refs_11_
  36.3 0.0 collective-permute-done.10.refs_10_
  36.3 3.8 %scores.1 = f32[512,256]{1,0:T(8,128)} custom-call(bf16[512,8192]{1,0:T(8,128)(2,1)S(1)} %split.1.t_ref, bf16[16,8192]{1,0:T(8,128)(2,1)S(1)} %precond.1.refs_0_, bf16[16,8192]{1,0:T(8,128)(2,1)S(1)} %collective-permute-done.1.refs_1_, bf16[16,8192]{1,0:T(8,128)(2,1)S(1)} %collective-permute-done.2.refs_2_, ...), custom_call_target="tpu_custom_call" | custom-call | flops 2147483648 | bytes 12582912 | tf_op jit(solution)/shard_map/scores/pallas_call | solution.py:316
  (7 shorter events, 0.1 us)
Async XLA Ops:
  3.5 12.3 %collective-permute-start = (bf16[16,8192]{1,0:T(8,128)(2,1)S(1)}, bf16[16,8192]{1,0:T(8,128)(2,1)S(1)}, u32[]{:S(2)}, u32[]{:S(2)}) collective-permute-start(bf16[16,8192]{1,0:T(8,128)(2,1)S(1)} %precond.1.refs_0_), channel_id=1, source_target_pairs={{0,12},{1,13},{2,14},{3,15},{4,8},{5,9},{6,10},{7,11},{8,4},{9,5},... | collective-permute-start | bytes 786440 | tf_op jit(solution)/shard_map/ppermute | solution.py:51
  8.6 14.1 %collective-permute-start.1 = (bf16[16,8192]{1,0:T(8,128)(2,1)S(1)}, bf16[16,8192]{1,0:T(8,128)(2,1)S(1)}, u32[]{:S(2)}, u32[]{:S(2)}) collective-permute-start(bf16[16,8192]{1,0:T(8,128)(2,1)S(1)} %precond.1.refs_0_), channel_id=1, source_target_pairs={{0,2},{1,3},{2,0},{3,1},{4,6},{5,7},{6,4},{7,5},{8,10},{9,11},{10,... | collective-permute-start | bytes 786440 | tf_op jit(solution)/shard_map/ppermute | solution.py:51
  10.1 19.5 %collective-permute-start.2 = (bf16[16,8192]{1,0:T(8,128)(2,1)S(1)}, bf16[16,8192]{1,0:T(8,128)(2,1)S(1)}, u32[]{:S(2)}, u32[]{:S(2)}) collective-permute-start(bf16[16,8192]{1,0:T(8,128)(2,1)S(1)} %precond.1.refs_0_), channel_id=1, source_target_pairs={{0,4},{1,5},{2,6},{3,7},{4,0},{5,1},{6,2},{7,3},{8,12},{9,13},{10,... | collective-permute-start | bytes 786440 | tf_op jit(solution)/shard_map/ppermute | solution.py:51
  10.1 24.6 %collective-permute-start.8 = (bf16[16,8192]{1,0:T(8,128)(2,1)S(1)}, bf16[16,8192]{1,0:T(8,128)(2,1)S(1)}, u32[]{:S(2)}, u32[]{:S(2)}) collective-permute-start(bf16[16,8192]{1,0:T(8,128)(2,1)S(1)} %precond.1.refs_0_), channel_id=1, source_target_pairs={{0,1},{1,0},{2,3},{3,2},{4,5},{5,4},{6,7},{7,6},{8,9},{9,8},{10,11... | collective-permute-start | bytes 786440 | tf_op jit(solution)/shard_map/ppermute | solution.py:51
  15.8 8.7 %collective-permute-start.4 = (bf16[16,8192]{1,0:T(8,128)(2,1)S(1)}, bf16[16,8192]{1,0:T(8,128)(2,1)S(1)}, u32[]{:S(2)}, u32[]{:S(2)}) collective-permute-start(bf16[16,8192]{1,0:T(8,128)(2,1)S(1)} %collective-permute-done.refs_4_), channel_id=1, source_target_pairs={{0,2},{1,3},{2,0},{3,1},{4,6},{5,7},{6,4},{7,5},{8,10},{9,11},{10,... | collective-permute-start | bytes 786440 | tf_op jit(solution)/shard_map/ppermute | solution.py:51
  17.5 10.3 %collective-permute-start.5 = (bf16[16,8192]{1,0:T(8,128)(2,1)S(1)}, bf16[16,8192]{1,0:T(8,128)(2,1)S(1)}, u32[]{:S(2)}, u32[]{:S(2)}) collective-permute-start(bf16[16,8192]{1,0:T(8,128)(2,1)S(1)} %collective-permute-done.refs_4_), channel_id=1, source_target_pairs={{0,16},{1,17},{2,18},{3,19},{4,20},{5,21},{6,22},{7,23},{8,24},{9,... | collective-permute-start | bytes 786440 | tf_op jit(solution)/shard_map/ppermute | solution.py:51
  22.7 7.5 %collective-permute-start.3 = (bf16[16,8192]{1,0:T(8,128)(2,1)S(1)}, bf16[16,8192]{1,0:T(8,128)(2,1)S(1)}, u32[]{:S(2)}, u32[]{:S(2)}) collective-permute-start(bf16[16,8192]{1,0:T(8,128)(2,1)S(1)} %collective-permute-done.1.refs_1_), channel_id=1, source_target_pairs={{0,4},{1,5},{2,6},{3,7},{4,0},{5,1},{6,2},{7,3},{8,12},{9,13},{10,... | collective-permute-start | bytes 786440 | tf_op jit(solution)/shard_map/ppermute | solution.py:51
  24.5 10.3 %collective-permute-start.9 = (bf16[32,8192]{1,0:T(8,128)(2,1)S(1)}, bf16[32,8192]{1,0:T(8,128)(2,1)S(1)}, u32[]{:S(2)}, u32[]{:S(2)}) collective-permute-start(bf16[32,8192]{1,0:T(8,128)(2,1)S(1)} %pad_maximum_fusion), channel_id=1, source_target_pairs={{0,1},{1,0},{2,3},{3,2},{4,5},{5,4},{6,7},{7,6},{8,9},{9,8},{10,11... | collective-permute-start | bytes 1572872 | tf_op jit(solution)/shard_map/ppermute | solution.py:51
  27.8 5.0 %collective-permute-start.6 = (bf16[16,4096]{1,0:T(8,128)(2,1)S(1)}, bf16[16,4096]{1,0:T(8,128)(2,1)S(1)}, u32[]{:S(2)}, u32[]{:S(2)}) collective-permute-start(bf16[16,4096]{1,0:T(8,128)(2,1)S(1)} %slice.8), channel_id=1, source_target_pairs={{0,16},{1,17},{2,18},{3,19},{4,20},{5,21},{6,22},{7,23},{8,24},{9,... | collective-permute-start | bytes 393224 | tf_op jit(solution)/shard_map/ppermute | solution.py:51
  29.6 5.0 %collective-permute-start.7 = (bf16[16,4096]{1,0:T(8,128)(2,1)S(1)}, bf16[16,4096]{1,0:T(8,128)(2,1)S(1)}, u32[]{:S(2)}, u32[]{:S(2)}) collective-permute-start(bf16[16,4096]{1,0:T(8,128)(2,1)S(1)} %slice.9), channel_id=1, source_target_pairs={{0,2},{1,3},{2,0},{3,1},{4,6},{5,7},{6,4},{7,5},{8,10},{9,11},{10,... | collective-permute-start | bytes 393224 | tf_op jit(solution)/shard_map/ppermute | solution.py:51
  30.2 6.1 %collective-permute-start.11 = (bf16[32,8192]{1,0:T(8,128)(2,1)S(1)}, bf16[32,8192]{1,0:T(8,128)(2,1)S(1)}, u32[]{:S(2)}, u32[]{:S(2)}) collective-permute-start(bf16[32,8192]{1,0:T(8,128)(2,1)S(1)} %pad_maximum_fusion.2), channel_id=1, source_target_pairs={{0,1},{1,0},{2,3},{3,2},{4,5},{5,4},{6,7},{7,6},{8,9},{9,8},{10,11... | collective-permute-start | bytes 1572872 | tf_op jit(solution)/shard_map/ppermute | solution.py:51
  32.8 3.5 %collective-permute-start.10 = (bf16[32,8192]{1,0:T(8,128)(2,1)S(1)}, bf16[32,8192]{1,0:T(8,128)(2,1)S(1)}, u32[]{:S(2)}, u32[]{:S(2)}) collective-permute-start(bf16[32,8192]{1,0:T(8,128)(2,1)S(1)} %pad_maximum_fusion.1), channel_id=1, source_target_pairs={{0,1},{1,0},{2,3},{3,2},{4,5},{5,4},{6,7},{7,6},{8,9},{9,8},{10,11... | collective-permute-start | bytes 1572872 | tf_op jit(solution)/shard_map/ppermute | solution.py:51
  34.6 1.6 %collective-permute-start.12 = (bf16[16,8192]{1,0:T(8,128)(2,1)S(1)}, bf16[16,8192]{1,0:T(8,128)(2,1)S(1)}, u32[]{:S(2)}, u32[]{:S(2)}) collective-permute-start(bf16[16,8192]{1,0:T(8,128)(2,1)S(1)} %constant_dynamic-update-slice_fusion.refs_7_), channel_id=1, source_target_pairs={{0,1},{1,0},{2,3},{3,2},{4,5},{5,4},{6,7},{7,6},{8,9},{9,8},{10,11... | collective-permute-start | bytes 786440 | tf_op jit(solution)/shard_map/ppermute | solution.py:51

commit v6 on v5

--- a/solution.py
+++ b/solution.py
@@ -88,14 +88,20 @@
     return g ^ 1, z, x, c
 
 
-def precond_kernel(q_ref, in_ref, out_ref, eig_ref, block_ref, *scratch):
+def precond_kernel(q_ref, in_ref, out_ref, eig_ref, block_ref, lines_ref, *scratch):
+    q_rows, lines, _ = q_ref.shape
+    pitch = lines_ref.shape[0] // q_rows
+    for q in range(q_rows):
+        lines_ref[q * pitch : q * pitch + lines, :] = q_ref[q].astype(jnp.float32)
     for layer in range(in_ref.shape[0]):
-        precond_layer(layer, q_ref, in_ref, out_ref, eig_ref, block_ref, *(ref.at[layer] for ref in scratch))
-
-
-def precond_layer(layer, q_ref, in_ref, out_ref, eig_ref, block_ref, wide_ref, tall_ref, even_ref):
-    q_rows, _, width = q_ref.shape
+        precond_layer(layer, lines_ref, in_ref, out_ref, eig_ref, block_ref, *(ref.at[layer] for ref in scratch))
+
+
+def precond_layer(layer, lines_ref, in_ref, out_ref, eig_ref, block_ref, wide_ref, tall_ref, even_ref):
+    q_rows = block_ref.shape[0]
+    layers, width = eig_ref.shape
     rows = width // LANES
+    pitch = lines_ref.shape[0] // q_rows
     p_in, p_out = in_ref.shape[1:]
     left = lax.broadcasted_iota(jnp.int32, (1, LANES), 1) < p_out
 
@@ -136,8 +142,9 @@
         axis=0,
     )
 
-    flat = q_ref[:, layer, :]
-    stacked = jnp.concatenate([flat[:, j * LANES : (j + 1) * LANES] for j in range(rows)], axis=0)
+    stacked = jnp.concatenate(
+        [lines_ref[pl.ds(layers * j + layer, q_rows, stride=pitch), :] for j in range(rows)], axis=0
+    ).astype(jnp.bfloat16)
     both = mxu(stacked, fore_right)
     wide_ref[...] = both[:, :LANES] + both[:, LANES:]
     by_query = jnp.concatenate([wide_ref[pl.ds(q, rows, stride=q_rows), :] for q in range(q_rows)], axis=1)
@@ -165,22 +172,33 @@
         block_ref[:, column : column + LANES] = block.astype(jnp.bfloat16)
 
 
-def precondition(query_grads, basis_in, basis_out, eigvals):
-    q_rows, layers, width = query_grads.shape
-    lines = q_rows * width // LANES
-    operands = [in_hbm(a) for a in (query_grads, basis_in, basis_out, eigvals)]
+def by_lines(array):
+    rows, layers, width = array.shape
+    array = array.reshape(rows, layers, width // LANES, LANES)
+    return array.transpose(0, 2, 1, 3).reshape(rows, -1, LANES)
+
+
+def precondition(queries, basis_in, basis_out, eigvals, here=False):
+    q_rows, lines, _ = queries.shape
+    layers, width = eigvals.shape
+    operands, body, scratch = [queries, basis_in, basis_out, eigvals], precond_kernel, []
+    if not here:
+        operands = [in_hbm(a) for a in operands]
+        body = functools.partial(fetched, len(operands), body)
+        scratch = [pltpu.VMEM(a.shape, a.dtype) for a in operands] + [pltpu.SemaphoreType.DMA((len(operands),))]
+    space = pltpu.VMEM if here else pltpu.HBM
     return pl.pallas_call(
-        functools.partial(fetched, len(operands), precond_kernel),
+        body,
         out_shape=jax.ShapeDtypeStruct((q_rows, layers * width), jnp.bfloat16),
-        in_specs=[pl.BlockSpec(memory_space=pltpu.HBM)] * len(operands),
+        in_specs=[pl.BlockSpec(memory_space=space)] * len(operands),
         out_specs=VMEM,
         scratch_shapes=[
-            pltpu.VMEM((layers, lines, LANES), jnp.float32),
-            pltpu.VMEM((layers, lines, LANES), jnp.float32),
+            pltpu.VMEM((q_rows * (lines + 8), LANES), jnp.float32),
+            pltpu.VMEM((layers, q_rows * width // LANES, LANES), jnp.float32),
+            pltpu.VMEM((layers, q_rows * width // LANES, LANES), jnp.float32),
             pltpu.VMEM((layers, 2 * width // LANES, LANES), jnp.float32),
         ]
-        + [pltpu.VMEM(a.shape, a.dtype) for a in operands]
-        + [pltpu.SemaphoreType.DMA((len(operands),))],
+        + scratch,
         compiler_params=pltpu.CompilerParams(vmem_limit_bytes=16 * MIB),
         cost_estimate=pl.CostEstimate(flops=10**9, bytes_accessed=4 * MIB, transcendentals=0),
         name="precond",
@@ -228,8 +246,6 @@
 def split_layers(train_grads):
     tr_rows, layers, width = train_grads.shape
     lines = layers * width // LANES
-    by_line = train_grads.reshape(tr_rows, layers, width // LANES, LANES)
-    by_line = by_line.transpose(0, 2, 1, 3).reshape(tr_rows, lines, LANES)
     return pl.pallas_call(
         functools.partial(split_kernel, layers),
         out_shape=jax.ShapeDtypeStruct((tr_rows, layers * width), jnp.bfloat16),
@@ -243,7 +259,7 @@
         compiler_params=pltpu.CompilerParams(vmem_limit_bytes=20 * MIB),
         cost_estimate=pl.CostEstimate(flops=10**9, bytes_accessed=16 * MIB, transcendentals=0),
         name="split",
-    )(in_hbm(by_line))
+    )(in_hbm(by_lines(train_grads)))
 
 
 def score_kernel(masks, t_ref, *refs):
@@ -281,11 +297,12 @@
 def per_device(n_train, train_grads, query_grads, basis_in, basis_out, eigvals):
     tr_rows = train_grads.shape[0]
     zs = n_train // (XS * CORES)
-    block = precondition(query_grads, basis_in, basis_out, eigvals)
-    q_rows, width = block.shape
-    own = Blocks(block, [np.tile(np.arange(n_train), (GROUPS, 1))])
-
-    far = [own.hop(far_z(pair)) for pair in range(1, zs // 2)]
+    rest = basis_in, basis_out, eigvals
+    queries = by_lines(query_grads)
+    places = [np.tile(np.arange(n_train), (GROUPS, 1))]
+    far = [Blocks(queries, places).hop(far_z(pair)) for pair in range(1, zs // 2)]
+    own = Blocks(precondition(queries, *rest), places)
+    q_rows, width = own.array.shape
     at_x = own.hop(over_x)
     at_z = own.hop(over_z)
     twins = [own.hop(over_core)]
@@ -294,6 +311,7 @@
     here = [own, at_x, at_z]
     for pair, one in enumerate(far):
         flat_train, one = after(flat_train, one)
+        one = Blocks(precondition(one.array, *rest, here=True), one.came)
         by_x, by_group = one.hop(over_x), one.hop(over_group)
         if pair == 0:
             one.array, at_x = after(one.array, at_x)

time: 40.2 us -> 39.6 us (0.985)
  starting transfers between devices: 16.5 us -> 14.7 us
  Pallas kernels: 12.8 us -> 14.5 us
  waiting for transfers between devices: 10.5 us -> 9.97 us
    ppermute x13, starting transfers between devices: 16.5 us -> 14.7 us  [hop(): return Blocks(lax.ppermute(self.array, ('group', 'train'), perm), came)]
    pallas_call x1 -> x2, Pallas kernels: 3.47 us -> 5.1 us  [precondition(): pl.pallas_call(body, out_shape=jax.ShapeDtypeStruct((q_rows, layers * wid...]
    ppermute x13, waiting for transfers between devices: 10.5 us -> 9.97 us  [hop(): return Blocks(lax.ppermute(self.array, ('group', 'train'), perm), came)]
  transfers between devices with their start and end apart: 13 -> 13, of which waited for: 6 -> 5; matrix products, arithmetic and copies ran while one was open for 0% -> 0% of each run, Pallas kernels for 14% -> 27%
where the time goes in v6:
time: 39.6 us; the launch traced here: 39.5 us
  starting transfers between devices  14.7 us (37%)
  Pallas kernels  14.5 us (37%)
  waiting for transfers between devices  9.97 us (25%)
    ppermute x13, starting transfers between devices, hop(): return Blocks(lax.ppermute(self.array, ('group', 'train'), perm), came)  14.7 us
    ppermute x13, waiting for transfers between devices, hop(): return Blocks(lax.ppermute(self.array, ('group', 'train'), perm), came)  9.97 us
    pallas_call x1, Pallas kernels, split_layers(): pl.pallas_call(functools.partial(split_kernel, layers), out_shape=jax.Sha...  5.62 us
    pallas_call x2, Pallas kernels, precondition(): pl.pallas_call(body, out_shape=jax.ShapeDtypeStruct((q_rows, layers * wid...  5.1 us
    pallas_call x1, Pallas kernels, per_device(): pl.pallas_call(functools.partial(score_kernel, masks), out_shape=jax.Shap...  3.76 us
  transfers between devices with their start and end apart: 13, of which 5 were waited for; matrix products, arithmetic and copies ran while one was open for 0% of the time, Pallas kernels for 27%

profile of v6, /device:TPU:0, one launch (start us, length us, event | category | flops | bytes accessed | tf_op | source)
XLA Modules:
  0.0 39.5 jit_solution(6431945571819037021)
XLA Ops:
  0.0 5.0 %collective-permute-start = (bf16[16,64,128]{2,1,0:T(8,128)(2,1)}, bf16[16,64,128]{2,1,0:T(8,128)(2,1)S(1)}, u32[]{:S(2)}, u32[]{:S(2)}) collective-permute-start(bf16[16,64,128]{2,1,0:T(8,128)(2,1)} %bitcast.11), channel_id=1, source_target_pairs={{0,12},{1,13},{2,14},{3,15},{4,8},{5,9},{6,10},{7,11},{8,4},{9,5},... | collective-permute-start | bytes 786440 | tf_op jit(solution)/shard_map/ppermute | solution.py:51
  5.0 3.1 %precond.2.refs_0_ = bf16[16,8192]{1,0:T(8,128)(2,1)S(1)} custom-call(bf16[16,64,128]{2,1,0:T(8,128)(2,1)} %bitcast.12, f32[2,64,64]{2,1,0:T(8,128)} %in_ref.1, f32[2,64,64]{2,1,0:T(8,128)} %out_ref.1, f32[2,4096]{1,0:T(2,128)} %eig_ref.1), custom_call_target="tpu_custom_call" | custom-call | flops 1000000000 | bytes 4194304 | tf_op jit(solution)/shard_map/precond/pallas_call | solution.py:190
  8.1 1.6 %collective-permute-start.1 = (bf16[16,8192]{1,0:T(8,128)(2,1)S(1)}, bf16[16,8192]{1,0:T(8,128)(2,1)S(1)}, u32[]{:S(2)}, u32[]{:S(2)}) collective-permute-start(bf16[16,8192]{1,0:T(8,128)(2,1)S(1)} %precond.2.refs_0_), channel_id=1, source_target_pairs={{0,2},{1,3},{2,0},{3,1},{4,6},{5,7},{6,4},{7,5},{8,10},{9,11},{10,... | collective-permute-start | bytes 786440 | tf_op jit(solution)/shard_map/ppermute | solution.py:51
  9.7 0.0 collective-permute-start.2
  9.7 0.0 collective-permute-start.8
  9.7 0.0 copy-start
  9.7 0.0 copy-start.1
  9.7 0.0 copy-start.2
  9.7 5.6 %split.1.t_ref = bf16[512,8192]{1,0:T(8,128)(2,1)S(1)} custom-call(bf16[512,64,128]{2,1,0:T(8,128)(2,1)} %bitcast.10), custom_call_target="tpu_custom_call" | custom-call | flops 1000000000 | bytes 16777216 | tf_op jit(solution)/shard_map/split/pallas_call | solution.py:249
  15.3 0.0 collective-permute-done.q_ref
  15.3 0.0 copy-done
  15.4 0.0 copy-done.1
  15.4 0.0 copy-done.2
  15.4 2.0 %precond.3.refs_4_ = bf16[16,8192]{1,0:T(8,128)(2,1)S(1)} custom-call(bf16[16,64,128]{2,1,0:T(8,128)(2,1)S(1)} %collective-permute-done.q_ref, f32[2,64,64]{2,1,0:T(8,128)S(1)} %copy-done, f32[2,64,64]{2,1,0:T(8,128)S(1)} %copy-done.1, f32[2,4096]{1,0:T(2,128)S(1)} %copy-done.2), custom_call_target="tpu_custom_call" | custom-call | flops 1000000000 | bytes 4194304 | tf_op jit(solution)/shard_map/precond/pallas_call | solution.py:190
  17.4 0.6 %collective-permute-start.4 = (bf16[16,8192]{1,0:T(8,128)(2,1)S(1)}, bf16[16,8192]{1,0:T(8,128)(2,1)S(1)}, u32[]{:S(2)}, u32[]{:S(2)}) collective-permute-start(bf16[16,8192]{1,0:T(8,128)(2,1)S(1)} %precond.3.refs_4_), channel_id=1, source_target_pairs={{0,2},{1,3},{2,0},{3,1},{4,6},{5,7},{6,4},{7,5},{8,10},{9,11},{10,... | collective-permute-start | bytes 786440 | tf_op jit(solution)/shard_map/ppermute | solution.py:51
  18.0 3.4 %collective-permute-start.5 = (bf16[16,8192]{1,0:T(8,128)(2,1)S(1)}, bf16[16,8192]{1,0:T(8,128)(2,1)S(1)}, u32[]{:S(2)}, u32[]{:S(2)}) collective-permute-start(bf16[16,8192]{1,0:T(8,128)(2,1)S(1)} %precond.3.refs_4_), channel_id=1, source_target_pairs={{0,16},{1,17},{2,18},{3,19},{4,20},{5,21},{6,22},{7,23},{8,24},{9,... | collective-permute-start | bytes 786440 | tf_op jit(solution)/shard_map/ppermute | solution.py:51
  21.5 0.0 collective-permute-done.1.refs_1_
  21.5 0.7 %collective-permute-start.3 = (bf16[16,8192]{1,0:T(8,128)(2,1)S(1)}, bf16[16,8192]{1,0:T(8,128)(2,1)S(1)}, u32[]{:S(2)}, u32[]{:S(2)}) collective-permute-start(bf16[16,8192]{1,0:T(8,128)(2,1)S(1)} %collective-permute-done.1.refs_1_), channel_id=1, source_target_pairs={{0,4},{1,5},{2,6},{3,7},{4,0},{5,1},{6,2},{7,3},{8,12},{9,13},{10,... | collective-permute-start | bytes 786440 | tf_op jit(solution)/shard_map/ppermute | solution.py:51
  22.2 4.0 %collective-permute-done.4.refs_5_ = bf16[16,8192]{1,0:T(8,128)(2,1)S(1)} collective-permute-done((bf16[16,8192]{1,0:T(8,128)(2,1)S(1)}, bf16[16,8192]{1,0:T(8,128)(2,1)S(1)}, u32[]{:S(2)}, u32[]{:S(2)}) %collective-permute-start.4) | collective-permute-done | bytes 262176 | tf_op jit(solution)/shard_map/ppermute | solution.py:51
  26.2 0.0 collective-permute-start.9
  26.2 0.6 %collective-permute-done.5.refs_6_ = bf16[16,8192]{1,0:T(8,128)(2,1)S(1)} collective-permute-done((bf16[16,8192]{1,0:T(8,128)(2,1)S(1)}, bf16[16,8192]{1,0:T(8,128)(2,1)S(1)}, u32[]{:S(2)}, u32[]{:S(2)}) %collective-permute-start.5) | collective-permute-done | bytes 262176 | tf_op jit(solution)/shard_map/ppermute | solution.py:51
  26.8 1.7 %collective-permute-start.6 = (bf16[16,4096]{1,0:T(8,128)(2,1)S(1)}, bf16[16,4096]{1,0:T(8,128)(2,1)S(1)}, u32[]{:S(2)}, u32[]{:S(2)}) collective-permute-start(bf16[16,4096]{1,0:T(8,128)(2,1)S(1)} %slice.8), channel_id=1, source_target_pairs={{0,16},{1,17},{2,18},{3,19},{4,20},{5,21},{6,22},{7,23},{8,24},{9,... | collective-permute-start | bytes 393224 | tf_op jit(solution)/shard_map/ppermute | solution.py:51
  28.6 0.0 collective-permute-done.2.refs_2_
  28.6 1.6 %collective-permute-start.7 = (bf16[16,4096]{1,0:T(8,128)(2,1)S(1)}, bf16[16,4096]{1,0:T(8,128)(2,1)S(1)}, u32[]{:S(2)}, u32[]{:S(2)}) collective-permute-start(bf16[16,4096]{1,0:T(8,128)(2,1)S(1)} %slice.9), channel_id=1, source_target_pairs={{0,2},{1,3},{2,0},{3,1},{4,6},{5,7},{6,4},{7,5},{8,10},{9,11},{10,... | collective-permute-start | bytes 393224 | tf_op jit(solution)/shard_map/ppermute | solution.py:51
  30.1 0.0 collective-permute-done.3.refs_3_
  30.1 0.0 collective-permute-start.11
  30.2 2.3 %collective-permute-done.6 = bf16[16,4096]{1,0:T(8,128)(2,1)S(1)} collective-permute-done((bf16[16,4096]{1,0:T(8,128)(2,1)S(1)}, bf16[16,4096]{1,0:T(8,128)(2,1)S(1)}, u32[]{:S(2)}, u32[]{:S(2)}) %collective-permute-start.6) | collective-permute-done | bytes 131104 | tf_op jit(solution)/shard_map/ppermute | solution.py:51
  32.5 0.0 collective-permute-start.10
  32.5 1.6 %collective-permute-done.7 = bf16[16,4096]{1,0:T(8,128)(2,1)S(1)} collective-permute-done((bf16[16,4096]{1,0:T(8,128)(2,1)S(1)}, bf16[16,4096]{1,0:T(8,128)(2,1)S(1)}, u32[]{:S(2)}, u32[]{:S(2)}) %collective-permute-start.7) | collective-permute-done | bytes 131104 | tf_op jit(solution)/shard_map/ppermute | solution.py:51
  34.1 0.1 collective-permute-start.12
  34.2 0.0 collective-permute-done.8.refs_8_
  34.2 0.0 collective-permute-done.9.refs_9_
  34.2 1.5 %collective-permute-done.12.refs_12_ = bf16[16,8192]{1,0:T(8,128)(2,1)S(1)} collective-permute-done((bf16[16,8192]{1,0:T(8,128)(2,1)S(1)}, bf16[16,8192]{1,0:T(8,128)(2,1)S(1)}, u32[]{:S(2)}, u32[]{:S(2)}) %collective-permute-start.12) | collective-permute-done | bytes 262176 | tf_op jit(solution)/shard_map/ppermute | solution.py:51
  35.7 0.0 collective-permute-done.11.refs_11_
  35.7 0.0 collective-permute-done.10.refs_10_
  35.7 3.8 %scores.1 = f32[512,256]{1,0:T(8,128)} custom-call(bf16[512,8192]{1,0:T(8,128)(2,1)S(1)} %split.1.t_ref, bf16[16,8192]{1,0:T(8,128)(2,1)S(1)} %precond.2.refs_0_, bf16[16,8192]{1,0:T(8,128)(2,1)S(1)} %collective-permute-done.1.refs_1_, bf16[16,8192]{1,0:T(8,128)(2,1)S(1)} %collective-permute-done.2.refs_2_, ...), custom_call_target="tpu_custom_call" | custom-call | flops 2147483648 | bytes 12582912 | tf_op jit(solution)/shard_map/scores/pallas_call | solution.py:334
  (7 shorter events, 0.1 us)
Async XLA Ops:
  0.0 15.3 %collective-permute-start = (bf16[16,64,128]{2,1,0:T(8,128)(2,1)}, bf16[16,64,128]{2,1,0:T(8,128)(2,1)S(1)}, u32[]{:S(2)}, u32[]{:S(2)}) collective-permute-start(bf16[16,64,128]{2,1,0:T(8,128)(2,1)} %bitcast.11), channel_id=1, source_target_pairs={{0,12},{1,13},{2,14},{3,15},{4,8},{5,9},{6,10},{7,11},{8,4},{9,5},... | collective-permute-start | bytes 786440 | tf_op jit(solution)/shard_map/ppermute | solution.py:51
  8.1 13.3 %collective-permute-start.1 = (bf16[16,8192]{1,0:T(8,128)(2,1)S(1)}, bf16[16,8192]{1,0:T(8,128)(2,1)S(1)}, u32[]{:S(2)}, u32[]{:S(2)}) collective-permute-start(bf16[16,8192]{1,0:T(8,128)(2,1)S(1)} %precond.2.refs_0_), channel_id=1, source_target_pairs={{0,2},{1,3},{2,0},{3,1},{4,6},{5,7},{6,4},{7,5},{8,10},{9,11},{10,... | collective-permute-start | bytes 786440 | tf_op jit(solution)/shard_map/ppermute | solution.py:51
  9.7 18.9 %collective-permute-start.2 = (bf16[16,8192]{1,0:T(8,128)(2,1)S(1)}, bf16[16,8192]{1,0:T(8,128)(2,1)S(1)}, u32[]{:S(2)}, u32[]{:S(2)}) collective-permute-start(bf16[16,8192]{1,0:T(8,128)(2,1)S(1)} %precond.2.refs_0_), channel_id=1, source_target_pairs={{0,4},{1,5},{2,6},{3,7},{4,0},{5,1},{6,2},{7,3},{8,12},{9,13},{10,... | collective-permute-start | bytes 786440 | tf_op jit(solution)/shard_map/ppermute | solution.py:51
  9.7 24.5 %collective-permute-start.8 = (bf16[16,8192]{1,0:T(8,128)(2,1)S(1)}, bf16[16,8192]{1,0:T(8,128)(2,1)S(1)}, u32[]{:S(2)}, u32[]{:S(2)}) collective-permute-start(bf16[16,8192]{1,0:T(8,128)(2,1)S(1)} %precond.2.refs_0_), channel_id=1, source_target_pairs={{0,1},{1,0},{2,3},{3,2},{4,5},{5,4},{6,7},{7,6},{8,9},{9,8},{10,11... | collective-permute-start | bytes 786440 | tf_op jit(solution)/shard_map/ppermute | solution.py:51
  9.7 5.7 %copy-start = (f32[2,64,64]{2,1,0:T(8,128)S(1)}, f32[2,64,64]{2,1,0:T(8,128)}, u32[]{:S(2)}) copy-start(f32[2,64,64]{2,1,0:T(8,128)} %in_ref.1) | copy-start | bytes 98308
  9.7 5.7 %copy-start.1 = (f32[2,64,64]{2,1,0:T(8,128)S(1)}, f32[2,64,64]{2,1,0:T(8,128)}, u32[]{:S(2)}) copy-start(f32[2,64,64]{2,1,0:T(8,128)} %out_ref.1) | copy-start | bytes 98308
  9.7 5.7 %copy-start.2 = (f32[2,4096]{1,0:T(2,128)S(1)}, f32[2,4096]{1,0:T(2,128)}, u32[]{:S(2)}) copy-start(f32[2,4096]{1,0:T(2,128)} %eig_ref.1) | copy-start | bytes 98308
  17.4 8.8 %collective-permute-start.4 = (bf16[16,8192]{1,0:T(8,128)(2,1)S(1)}, bf16[16,8192]{1,0:T(8,128)(2,1)S(1)}, u32[]{:S(2)}, u32[]{:S(2)}) collective-permute-start(bf16[16,8192]{1,0:T(8,128)(2,1)S(1)} %precond.3.refs_4_), channel_id=1, source_target_pairs={{0,2},{1,3},{2,0},{3,1},{4,6},{5,7},{6,4},{7,5},{8,10},{9,11},{10,... | collective-permute-start | bytes 786440 | tf_op jit(solution)/shard_map/ppermute | solution.py:51
  18.0 8.7 %collective-permute-start.5 = (bf16[16,8192]{1,0:T(8,128)(2,1)S(1)}, bf16[16,8192]{1,0:T(8,128)(2,1)S(1)}, u32[]{:S(2)}, u32[]{:S(2)}) collective-permute-start(bf16[16,8192]{1,0:T(8,128)(2,1)S(1)} %precond.3.refs_4_), channel_id=1, source_target_pairs={{0,16},{1,17},{2,18},{3,19},{4,20},{5,21},{6,22},{7,23},{8,24},{9,... | collective-permute-start | bytes 786440 | tf_op jit(solution)/shard_map/ppermute | solution.py:51
  21.5 8.7 %collective-permute-start.3 = (bf16[16,8192]{1,0:T(8,128)(2,1)S(1)}, bf16[16,8192]{1,0:T(8,128)(2,1)S(1)}, u32[]{:S(2)}, u32[]{:S(2)}) collective-permute-start(bf16[16,8192]{1,0:T(8,128)(2,1)S(1)} %collective-permute-done.1.refs_1_), channel_id=1, source_target_pairs={{0,4},{1,5},{2,6},{3,7},{4,0},{5,1},{6,2},{7,3},{8,12},{9,13},{10,... | collective-permute-start | bytes 786440 | tf_op jit(solution)/shard_map/ppermute | solution.py:51
  26.2 8.0 %collective-permute-start.9 = (bf16[32,8192]{1,0:T(8,128)(2,1)S(1)}, bf16[32,8192]{1,0:T(8,128)(2,1)S(1)}, u32[]{:S(2)}, u32[]{:S(2)}) collective-permute-start(bf16[32,8192]{1,0:T(8,128)(2,1)S(1)} %pad_maximum_fusion), channel_id=1, source_target_pairs={{0,1},{1,0},{2,3},{3,2},{4,5},{5,4},{6,7},{7,6},{8,9},{9,8},{10,11... | collective-permute-start | bytes 1572872 | tf_op jit(solution)/shard_map/ppermute | solution.py:51
  26.8 5.7 %collective-permute-start.6 = (bf16[16,4096]{1,0:T(8,128)(2,1)S(1)}, bf16[16,4096]{1,0:T(8,128)(2,1)S(1)}, u32[]{:S(2)}, u32[]{:S(2)}) collective-permute-start(bf16[16,4096]{1,0:T(8,128)(2,1)S(1)} %slice.8), channel_id=1, source_target_pairs={{0,16},{1,17},{2,18},{3,19},{4,20},{5,21},{6,22},{7,23},{8,24},{9,... | collective-permute-start | bytes 393224 | tf_op jit(solution)/shard_map/ppermute | solution.py:51
  28.6 5.5 %collective-permute-start.7 = (bf16[16,4096]{1,0:T(8,128)(2,1)S(1)}, bf16[16,4096]{1,0:T(8,128)(2,1)S(1)}, u32[]{:S(2)}, u32[]{:S(2)}) collective-permute-start(bf16[16,4096]{1,0:T(8,128)(2,1)S(1)} %slice.9), channel_id=1, source_target_pairs={{0,2},{1,3},{2,0},{3,1},{4,6},{5,7},{6,4},{7,5},{8,10},{9,11},{10,... | collective-permute-start | bytes 393224 | tf_op jit(solution)/shard_map/ppermute | solution.py:51
  30.1 5.6 %collective-permute-start.11 = (bf16[32,8192]{1,0:T(8,128)(2,1)S(1)}, bf16[32,8192]{1,0:T(8,128)(2,1)S(1)}, u32[]{:S(2)}, u32[]{:S(2)}) collective-permute-start(bf16[32,8192]{1,0:T(8,128)(2,1)S(1)} %pad_maximum_fusion.2), channel_id=1, source_target_pairs={{0,1},{1,0},{2,3},{3,2},{4,5},{5,4},{6,7},{7,6},{8,9},{9,8},{10,11... | collective-permute-start | bytes 1572872 | tf_op jit(solution)/shard_map/ppermute | solution.py:51
  32.5 3.2 %collective-permute-start.10 = (bf16[32,8192]{1,0:T(8,128)(2,1)S(1)}, bf16[32,8192]{1,0:T(8,128)(2,1)S(1)}, u32[]{:S(2)}, u32[]{:S(2)}) collective-permute-start(bf16[32,8192]{1,0:T(8,128)(2,1)S(1)} %pad_maximum_fusion.1), channel_id=1, source_target_pairs={{0,1},{1,0},{2,3},{3,2},{4,5},{5,4},{6,7},{7,6},{8,9},{9,8},{10,11... | collective-permute-start | bytes 1572872 | tf_op jit(solution)/shard_map/ppermute | solution.py:51
  34.1 1.6 %collective-permute-start.12 = (bf16[16,8192]{1,0:T(8,128)(2,1)S(1)}, bf16[16,8192]{1,0:T(8,128)(2,1)S(1)}, u32[]{:S(2)}, u32[]{:S(2)}) collective-permute-start(bf16[16,8192]{1,0:T(8,128)(2,1)S(1)} %constant_dynamic-update-slice_fusion.refs_7_), channel_id=1, source_target_pairs={{0,1},{1,0},{2,3},{3,2},{4,5},{5,4},{6,7},{7,6},{8,9},{9,8},{10,11... | collective-permute-start | bytes 786440 | tf_op jit(solution)/shard_map/ppermute | solution.py:51

commit v7 on v6

--- a/solution.py
+++ b/solution.py
@@ -262,10 +262,10 @@
     )(in_hbm(by_lines(train_grads)))
 
 
-def score_kernel(masks, t_ref, *refs):
-    blocks, out_ref = refs[:-1], refs[-1]
-    q_rows, width = blocks[0].shape
-    n_query = len(masks) * q_rows
+def score_kernel(masks, added, t_ref, *refs):
+    blocks, out_ref = refs[added:-1], refs[-1]
+    q_rows, width = sum(ref.shape[0] for ref in blocks) // len(masks), t_ref.shape[1]
+    n_query = out_ref.shape[1]
     depth = min(width, 1024)
     total = None
     for at in range(0, width, depth):
@@ -284,7 +284,26 @@
     order = jnp.concatenate(order, axis=0).astype(jnp.bfloat16)
     high, low = halves(total)
     lowest = (total - high.astype(jnp.float32) - low.astype(jnp.float32)).astype(jnp.bfloat16)
-    out_ref[...] = mxu(high, order) + mxu(low, order) + mxu(lowest, order)
+    placed = mxu(high, order) + mxu(low, order) + mxu(lowest, order)
+    out_ref[...] = refs[0][...] + placed if added else placed
+
+
+def scores(flat_train, parts, n_query, earlier=None):
+    tr_rows, width = flat_train.shape
+    masks = [came_masks(came) for a in parts for came in a.came]
+    operands = [flat_train] + ([] if earlier is None else [earlier]) + [a.array for a in parts]
+    rows = sum(a.array.shape[0] for a in parts)
+    return pl.pallas_call(
+        functools.partial(score_kernel, masks, 0 if earlier is None else 1),
+        out_shape=jax.ShapeDtypeStruct((tr_rows, n_query), jnp.float32),
+        in_specs=[VMEM] * len(operands),
+        out_specs=VMEM,
+        compiler_params=pltpu.CompilerParams(vmem_limit_bytes=32 * MIB),
+        cost_estimate=pl.CostEstimate(
+            flops=2 * tr_rows * n_query * width, bytes_accessed=2 * width * (tr_rows + rows), transcendentals=0
+        ),
+        name="scores",
+    )(*operands)
 
 
 def came_masks(came):
@@ -295,7 +314,6 @@
 
 
 def per_device(n_train, train_grads, query_grads, basis_in, basis_out, eigvals):
-    tr_rows = train_grads.shape[0]
     zs = n_train // (XS * CORES)
     rest = basis_in, basis_out, eigvals
     queries = by_lines(query_grads)
@@ -303,12 +321,14 @@
     far = [Blocks(queries, places).hop(far_z(pair)) for pair in range(1, zs // 2)]
     own = Blocks(precondition(queries, *rest), places)
     q_rows, width = own.array.shape
+    n_query = n_train * q_rows
     at_x = own.hop(over_x)
-    at_z = own.hop(over_z)
-    twins = [own.hop(over_core)]
+    twin = own.hop(over_core)
     train_grads, own = after(train_grads, own)
     flat_train = split_layers(train_grads)
-    here = [own, at_x, at_z]
+    flat_train, own = after(flat_train, own)
+    at_z = own.hop(over_z)
+    early, parts = [own, twin], [at_z]
     for pair, one in enumerate(far):
         flat_train, one = after(flat_train, one)
         one = Blocks(precondition(one.array, *rest, here=True), one.came)
@@ -316,32 +336,21 @@
         if pair == 0:
             one.array, at_x = after(one.array, at_x)
             at_xz = at_x.hop(over_z)
-            twins.append(stack(at_x, one).hop(over_core))
-            twins.append(stack(at_z, at_xz).hop(over_core))
-            here.append(at_xz)
+            early += [at_x, one]
+            first_scores = scores(flat_train, early, n_query)
+            first_scores, by_x = after(first_scores, by_x)
+            parts.append(stack(at_x, one).hop(over_core))
+            parts.append(at_xz)
         else:
-            twins.append(one.hop(over_core))
-        twins.append(stack(by_x, by_group).hop(over_core))
-        corner = beside(
-            by_x.columns(0, width // 2).hop(over_group), by_group.columns(width // 2, width).hop(over_x)
-        )
-        twins.append(corner.hop(over_core))
-        here += [one, by_x, by_group, corner]
-    everything = here + twins
-    masks = [came_masks(came) for a in everything for came in a.came]
-
-    n_query = n_train * q_rows
-    partial_scores = pl.pallas_call(
-        functools.partial(score_kernel, masks),
-        out_shape=jax.ShapeDtypeStruct((tr_rows, n_query), jnp.float32),
-        in_specs=[VMEM] * (1 + len(everything)),
-        out_specs=VMEM,
-        compiler_params=pltpu.CompilerParams(vmem_limit_bytes=36 * MIB),
-        cost_estimate=pl.CostEstimate(
-            flops=2 * tr_rows * n_query * width, bytes_accessed=2 * width * (tr_rows + n_query), transcendentals=0
-        ),
-        name="scores",
-    )(flat_train, *(a.array for a in everything))
+            parts += [one, one.hop(over_core)]
+        parts.append(stack(by_x, by_group).hop(over_core))
+        half = by_x.columns(0, width // 2).hop(over_group)
+        if pair == 0:
+            half.array, near, near_x = after(half.array, at_z, at_xz)
+            parts.append(stack(near, near_x).hop(over_core))
+        corner = beside(half, by_group.columns(width // 2, width).hop(over_x))
+        parts += [by_x, by_group, corner, corner.hop(over_core)]
+    partial_scores = scores(flat_train, parts, n_query, first_scores)
     return lax.psum_scatter(partial_scores, "layer", scatter_dimension=1, tiled=True)
 
 

time: 39.6 us -> 39.7 us (level)
  Pallas kernels: 14.5 us -> 17.4 us
  waiting for transfers between devices: 9.97 us -> 7.79 us
  starting transfers between devices: 14.7 us -> 14.1 us
    pallas_call x1 -> x2, Pallas kernels: 3.76 us -> 6.66 us  [scores(): pl.pallas_call(functools.partial(score_kernel, masks, 0 if earlier is Non...]
    ppermute x13, waiting for transfers between devices: 9.97 us -> 7.79 us  [hop(): return Blocks(lax.ppermute(self.array, ('group', 'train'), perm), came)]
    ppermute x13, starting transfers between devices: 14.7 us -> 14.1 us  [hop(): return Blocks(lax.ppermute(self.array, ('group', 'train'), perm), came)]
  transfers between devices with their start and end apart: 13 -> 13, of which waited for: 5 -> 5; matrix products, arithmetic and copies ran while one was open for 0% -> 0% of each run, Pallas kernels for 27% -> 34%
where the time goes in v7:
time: 39.7 us; the launch traced here: 39.6 us
  Pallas kernels  17.4 us (44%)
  starting transfers between devices  14.1 us (36%)
  waiting for transfers between devices  7.79 us (20%)
    ppermute x13, starting transfers between devices, hop(): return Blocks(lax.ppermute(self.array, ('group', 'train'), perm), came)  14.1 us
    ppermute x13, waiting for transfers between devices, hop(): return Blocks(lax.ppermute(self.array, ('group', 'train'), perm), came)  7.79 us
    pallas_call x2, Pallas kernels, scores(): pl.pallas_call(functools.partial(score_kernel, masks, 0 if earlier is Non...  6.66 us
    pallas_call x1, Pallas kernels, split_layers(): pl.pallas_call(functools.partial(split_kernel, layers), out_shape=jax.Sha...  5.61 us
    pallas_call x2, Pallas kernels, precondition(): pl.pallas_call(body, out_shape=jax.ShapeDtypeStruct((q_rows, layers * wid...  5.11 us
  transfers between devices with their start and end apart: 13, of which 5 were waited for; matrix products, arithmetic and copies ran while one was open for 0% of the time, Pallas kernels for 34%

profile of v7, /device:TPU:0, one launch (start us, length us, event | category | flops | bytes accessed | tf_op | source)
XLA Modules:
  0.0 39.6 jit_solution(4202044757579577498)
XLA Ops:
  0.0 5.0 %collective-permute-start = (bf16[16,64,128]{2,1,0:T(8,128)(2,1)}, bf16[16,64,128]{2,1,0:T(8,128)(2,1)S(1)}, u32[]{:S(2)}, u32[]{:S(2)}) collective-permute-start(bf16[16,64,128]{2,1,0:T(8,128)(2,1)} %bitcast.11), channel_id=1, source_target_pairs={{0,12},{1,13},{2,14},{3,15},{4,8},{5,9},{6,10},{7,11},{8,4},{9,5},... | collective-permute-start | bytes 786440 | tf_op jit(solution)/shard_map/ppermute | solution.py:51
  5.0 3.1 %precond.2.refs_0_ = bf16[16,8192]{1,0:T(8,128)(2,1)S(1)} custom-call(bf16[16,64,128]{2,1,0:T(8,128)(2,1)} %bitcast.12, f32[2,64,64]{2,1,0:T(8,128)} %in_ref.1, f32[2,64,64]{2,1,0:T(8,128)} %out_ref.1, f32[2,4096]{1,0:T(2,128)} %eig_ref.1), custom_call_target="tpu_custom_call" | custom-call | flops 1000000000 | bytes 4194304 | tf_op jit(solution)/shard_map/precond/pallas_call | solution.py:190
  8.1 1.6 %collective-permute-start.3 = (bf16[16,8192]{1,0:T(8,128)(2,1)S(1)}, bf16[16,8192]{1,0:T(8,128)(2,1)S(1)}, u32[]{:S(2)}, u32[]{:S(2)}) collective-permute-start(bf16[16,8192]{1,0:T(8,128)(2,1)S(1)} %precond.2.refs_0_), channel_id=1, source_target_pairs={{0,2},{1,3},{2,0},{3,1},{4,6},{5,7},{6,4},{7,5},{8,10},{9,11},{10,... | collective-permute-start | bytes 786440 | tf_op jit(solution)/shard_map/ppermute | solution.py:51
  9.7 0.0 collective-permute-start.2
  9.7 0.0 copy-start
  9.7 0.0 copy-start.1
  9.7 0.0 copy-start.2
  9.7 5.6 %split.1.t_ref = bf16[512,8192]{1,0:T(8,128)(2,1)S(1)} custom-call(bf16[512,64,128]{2,1,0:T(8,128)(2,1)} %bitcast.10), custom_call_target="tpu_custom_call" | custom-call | flops 1000000000 | bytes 16777216 | tf_op jit(solution)/shard_map/split/pallas_call | solution.py:249
  15.3 0.1 collective-permute-start.4
  15.4 0.0 collective-permute-done.q_ref
  15.4 0.0 copy-done
  15.4 0.0 copy-done.1
  15.4 0.0 copy-done.2
  15.4 2.0 %precond.3.refs_3_ = bf16[16,8192]{1,0:T(8,128)(2,1)S(1)} custom-call(bf16[16,64,128]{2,1,0:T(8,128)(2,1)S(1)} %collective-permute-done.q_ref, f32[2,64,64]{2,1,0:T(8,128)S(1)} %copy-done, f32[2,64,64]{2,1,0:T(8,128)S(1)} %copy-done.1, f32[2,4096]{1,0:T(2,128)S(1)} %copy-done.2), custom_call_target="tpu_custom_call" | custom-call | flops 1000000000 | bytes 4194304 | tf_op jit(solution)/shard_map/precond/pallas_call | solution.py:190
  17.5 0.6 %collective-permute-start.1 = (bf16[16,8192]{1,0:T(8,128)(2,1)S(1)}, bf16[16,8192]{1,0:T(8,128)(2,1)S(1)}, u32[]{:S(2)}, u32[]{:S(2)}) collective-permute-start(bf16[16,8192]{1,0:T(8,128)(2,1)S(1)} %precond.3.refs_3_), channel_id=1, source_target_pairs={{0,2},{1,3},{2,0},{3,1},{4,6},{5,7},{6,4},{7,5},{8,10},{9,11},{10,... | collective-permute-start | bytes 786440 | tf_op jit(solution)/shard_map/ppermute | solution.py:51
  18.1 3.3 %collective-permute-start.7 = (bf16[16,8192]{1,0:T(8,128)(2,1)S(1)}, bf16[16,8192]{1,0:T(8,128)(2,1)S(1)}, u32[]{:S(2)}, u32[]{:S(2)}) collective-permute-start(bf16[16,8192]{1,0:T(8,128)(2,1)S(1)} %precond.3.refs_3_), channel_id=1, source_target_pairs={{0,16},{1,17},{2,18},{3,19},{4,20},{5,21},{6,22},{7,23},{8,24},{9,... | collective-permute-start | bytes 786440 | tf_op jit(solution)/shard_map/ppermute | solution.py:51
  21.4 0.0 collective-permute-done.3.refs_2_
  21.4 0.8 %collective-permute-start.6 = (bf16[16,8192]{1,0:T(8,128)(2,1)S(1)}, bf16[16,8192]{1,0:T(8,128)(2,1)S(1)}, u32[]{:S(2)}, u32[]{:S(2)}) collective-permute-start(bf16[16,8192]{1,0:T(8,128)(2,1)S(1)} %collective-permute-done.3.refs_2_), channel_id=1, source_target_pairs={{0,4},{1,5},{2,6},{3,7},{4,0},{5,1},{6,2},{7,3},{8,12},{9,13},{10,... | collective-permute-start | bytes 786440 | tf_op jit(solution)/shard_map/ppermute | solution.py:51
  22.2 0.0 collective-permute-done.2.refs_1_
  22.2 0.1 collective-permute-start.5
  22.3 2.9 %scores.2.refs_0_ = f32[512,256]{1,0:T(8,128)S(1)} custom-call(bf16[512,8192]{1,0:T(8,128)(2,1)S(1)} %split.1.t_ref, bf16[16,8192]{1,0:T(8,128)(2,1)S(1)} %precond.2.refs_0_, bf16[16,8192]{1,0:T(8,128)(2,1)S(1)} %collective-permute-done.2.refs_1_, bf16[16,8192]{1,0:T(8,128)(2,1)S(1)} %collective-permute-done.3.refs_2_, bf16[16,8192]{1,0:T(8,128)(2,1)S(1)} %precond.3.refs_3_), custom_call_target="tpu_custom_call" | custom-call | flops 2147483648 | bytes 9437184 | tf_op jit(solution)/shard_map/scores/pallas_call | solution.py:296
  25.2 1.0 %collective-permute-done.1.refs_6_ = bf16[16,8192]{1,0:T(8,128)(2,1)S(1)} collective-permute-done((bf16[16,8192]{1,0:T(8,128)(2,1)S(1)}, bf16[16,8192]{1,0:T(8,128)(2,1)S(1)}, u32[]{:S(2)}, u32[]{:S(2)}) %collective-permute-start.1) | collective-permute-done | bytes 262176 | tf_op jit(solution)/shard_map/ppermute | solution.py:51
  26.3 1.8 %collective-permute-start.9 = (bf16[16,4096]{1,0:T(8,128)(2,1)S(1)}, bf16[16,4096]{1,0:T(8,128)(2,1)S(1)}, u32[]{:S(2)}, u32[]{:S(2)}) collective-permute-start(bf16[16,4096]{1,0:T(8,128)(2,1)S(1)} %slice.6), channel_id=1, source_target_pairs={{0,16},{1,17},{2,18},{3,19},{4,20},{5,21},{6,22},{7,23},{8,24},{9,... | collective-permute-start | bytes 393224 | tf_op jit(solution)/shard_map/ppermute | solution.py:51
  28.1 0.0 collective-permute-done.7.refs_7_
  28.1 0.1 collective-permute-start.8
  28.2 0.0 collective-permute-done.4.refs_1_
  28.2 0.6 %collective-permute-start.11 = (bf16[16,4096]{1,0:T(8,128)(2,1)S(1)}, bf16[16,4096]{1,0:T(8,128)(2,1)S(1)}, u32[]{:S(2)}, u32[]{:S(2)}) collective-permute-start(bf16[16,4096]{1,0:T(8,128)(2,1)S(1)} %slice.8), channel_id=1, source_target_pairs={{0,2},{1,3},{2,0},{3,1},{4,6},{5,7},{6,4},{7,5},{8,10},{9,11},{10,... | collective-permute-start | bytes 393224 | tf_op jit(solution)/shard_map/ppermute | solution.py:51
  28.8 0.9 %collective-permute-done.6.refs_3_ = bf16[16,8192]{1,0:T(8,128)(2,1)S(1)} collective-permute-done((bf16[16,8192]{1,0:T(8,128)(2,1)S(1)}, bf16[16,8192]{1,0:T(8,128)(2,1)S(1)}, u32[]{:S(2)}, u32[]{:S(2)}) %collective-permute-start.6) | collective-permute-done | bytes 262176 | tf_op jit(solution)/shard_map/ppermute | solution.py:51
  29.7 1.7 %collective-permute-done.9 = bf16[16,4096]{1,0:T(8,128)(2,1)S(1)} collective-permute-done((bf16[16,4096]{1,0:T(8,128)(2,1)S(1)}, bf16[16,4096]{1,0:T(8,128)(2,1)S(1)}, u32[]{:S(2)}, u32[]{:S(2)}) %collective-permute-start.9) | collective-permute-done | bytes 131104 | tf_op jit(solution)/shard_map/ppermute | solution.py:51
  31.5 0.1 collective-permute-start.10
  31.6 2.6 %collective-permute-done.11 = bf16[16,4096]{1,0:T(8,128)(2,1)S(1)} collective-permute-done((bf16[16,4096]{1,0:T(8,128)(2,1)S(1)}, bf16[16,4096]{1,0:T(8,128)(2,1)S(1)}, u32[]{:S(2)}, u32[]{:S(2)}) %collective-permute-start.11) | collective-permute-done | bytes 131104 | tf_op jit(solution)/shard_map/ppermute | solution.py:51
  34.2 0.1 collective-permute-start.12
  34.3 0.0 collective-permute-done.5.refs_2_
  34.3 1.5 %collective-permute-done.12.refs_9_ = bf16[16,8192]{1,0:T(8,128)(2,1)S(1)} collective-permute-done((bf16[16,8192]{1,0:T(8,128)(2,1)S(1)}, bf16[16,8192]{1,0:T(8,128)(2,1)S(1)}, u32[]{:S(2)}, u32[]{:S(2)}) %collective-permute-start.12) | collective-permute-done | bytes 262176 | tf_op jit(solution)/shard_map/ppermute | solution.py:51
  35.8 0.0 collective-permute-done.8.refs_4_
  35.8 0.0 collective-permute-done.10.refs_5_
  35.8 3.8 %scores.3 = f32[512,256]{1,0:T(8,128)} custom-call(bf16[512,8192]{1,0:T(8,128)(2,1)S(1)} %split.1.t_ref, f32[512,256]{1,0:T(8,128)S(1)} %scores.2.refs_0_, bf16[16,8192]{1,0:T(8,128)(2,1)S(1)} %collective-permute-done.4.refs_1_, bf16[32,8192]{1,0:T(8,128)(2,1)S(1)} %collective-permute-done.5.refs_2_, bf16[16,8192]{1,0:T(8,128)(2,1)S(1)} %collective-permute-done.6.refs_3_, ...), custom_call_target="tpu_custom_call" | custom-call | flops 2147483648 | bytes 11534336 | tf_op jit(solution)/shard_map/scores/pallas_call | solution.py:296
  (7 shorter events, 0.1 us)
Async XLA Ops:
  0.0 15.4 %collective-permute-start = (bf16[16,64,128]{2,1,0:T(8,128)(2,1)}, bf16[16,64,128]{2,1,0:T(8,128)(2,1)S(1)}, u32[]{:S(2)}, u32[]{:S(2)}) collective-permute-start(bf16[16,64,128]{2,1,0:T(8,128)(2,1)} %bitcast.11), channel_id=1, source_target_pairs={{0,12},{1,13},{2,14},{3,15},{4,8},{5,9},{6,10},{7,11},{8,4},{9,5},... | collective-permute-start | bytes 786440 | tf_op jit(solution)/shard_map/ppermute | solution.py:51
  8.1 13.2 %collective-permute-start.3 = (bf16[16,8192]{1,0:T(8,128)(2,1)S(1)}, bf16[16,8192]{1,0:T(8,128)(2,1)S(1)}, u32[]{:S(2)}, u32[]{:S(2)}) collective-permute-start(bf16[16,8192]{1,0:T(8,128)(2,1)S(1)} %precond.2.refs_0_), channel_id=1, source_target_pairs={{0,2},{1,3},{2,0},{3,1},{4,6},{5,7},{6,4},{7,5},{8,10},{9,11},{10,... | collective-permute-start | bytes 786440 | tf_op jit(solution)/shard_map/ppermute | solution.py:51
  9.7 12.5 %collective-permute-start.2 = (bf16[16,8192]{1,0:T(8,128)(2,1)S(1)}, bf16[16,8192]{1,0:T(8,128)(2,1)S(1)}, u32[]{:S(2)}, u32[]{:S(2)}) collective-permute-start(bf16[16,8192]{1,0:T(8,128)(2,1)S(1)} %precond.2.refs_0_), channel_id=1, source_target_pairs={{0,1},{1,0},{2,3},{3,2},{4,5},{5,4},{6,7},{7,6},{8,9},{9,8},{10,11... | collective-permute-start | bytes 786440 | tf_op jit(solution)/shard_map/ppermute | solution.py:51
  9.7 5.7 %copy-start = (f32[2,64,64]{2,1,0:T(8,128)S(1)}, f32[2,64,64]{2,1,0:T(8,128)}, u32[]{:S(2)}) copy-start(f32[2,64,64]{2,1,0:T(8,128)} %in_ref.1) | copy-start | bytes 98308
  9.7 5.7 %copy-start.1 = (f32[2,64,64]{2,1,0:T(8,128)S(1)}, f32[2,64,64]{2,1,0:T(8,128)}, u32[]{:S(2)}) copy-start(f32[2,64,64]{2,1,0:T(8,128)} %out_ref.1) | copy-start | bytes 98308
  9.7 5.7 %copy-start.2 = (f32[2,4096]{1,0:T(2,128)S(1)}, f32[2,4096]{1,0:T(2,128)}, u32[]{:S(2)}) copy-start(f32[2,4096]{1,0:T(2,128)} %eig_ref.1) | copy-start | bytes 98308
  15.3 12.9 %collective-permute-start.4 = (bf16[16,8192]{1,0:T(8,128)(2,1)S(1)}, bf16[16,8192]{1,0:T(8,128)(2,1)S(1)}, u32[]{:S(2)}, u32[]{:S(2)}) collective-permute-start(bf16[16,8192]{1,0:T(8,128)(2,1)S(1)} %precond.2.refs_0_), channel_id=1, source_target_pairs={{0,4},{1,5},{2,6},{3,7},{4,0},{5,1},{6,2},{7,3},{8,12},{9,13},{10,... | collective-permute-start | bytes 786440 | tf_op jit(solution)/shard_map/ppermute | solution.py:51
  17.5 8.8 %collective-permute-start.1 = (bf16[16,8192]{1,0:T(8,128)(2,1)S(1)}, bf16[16,8192]{1,0:T(8,128)(2,1)S(1)}, u32[]{:S(2)}, u32[]{:S(2)}) collective-permute-start(bf16[16,8192]{1,0:T(8,128)(2,1)S(1)} %precond.3.refs_3_), channel_id=1, source_target_pairs={{0,2},{1,3},{2,0},{3,1},{4,6},{5,7},{6,4},{7,5},{8,10},{9,11},{10,... | collective-permute-start | bytes 786440 | tf_op jit(solution)/shard_map/ppermute | solution.py:51
  18.1 10.0 %collective-permute-start.7 = (bf16[16,8192]{1,0:T(8,128)(2,1)S(1)}, bf16[16,8192]{1,0:T(8,128)(2,1)S(1)}, u32[]{:S(2)}, u32[]{:S(2)}) collective-permute-start(bf16[16,8192]{1,0:T(8,128)(2,1)S(1)} %precond.3.refs_3_), channel_id=1, source_target_pairs={{0,16},{1,17},{2,18},{3,19},{4,20},{5,21},{6,22},{7,23},{8,24},{9,... | collective-permute-start | bytes 786440 | tf_op jit(solution)/shard_map/ppermute | solution.py:51
  21.4 8.3 %collective-permute-start.6 = (bf16[16,8192]{1,0:T(8,128)(2,1)S(1)}, bf16[16,8192]{1,0:T(8,128)(2,1)S(1)}, u32[]{:S(2)}, u32[]{:S(2)}) collective-permute-start(bf16[16,8192]{1,0:T(8,128)(2,1)S(1)} %collective-permute-done.3.refs_2_), channel_id=1, source_target_pairs={{0,4},{1,5},{2,6},{3,7},{4,0},{5,1},{6,2},{7,3},{8,12},{9,13},{10,... | collective-permute-start | bytes 786440 | tf_op jit(solution)/shard_map/ppermute | solution.py:51
  22.2 12.1 %collective-permute-start.5 = (bf16[32,8192]{1,0:T(8,128)(2,1)S(1)}, bf16[32,8192]{1,0:T(8,128)(2,1)S(1)}, u32[]{:S(2)}, u32[]{:S(2)}) collective-permute-start(bf16[32,8192]{1,0:T(8,128)(2,1)S(1)} %pad_maximum_fusion), channel_id=1, source_target_pairs={{0,1},{1,0},{2,3},{3,2},{4,5},{5,4},{6,7},{7,6},{8,9},{9,8},{10,11... | collective-permute-start | bytes 1572872 | tf_op jit(solution)/shard_map/ppermute | solution.py:51
  26.3 5.2 %collective-permute-start.9 = (bf16[16,4096]{1,0:T(8,128)(2,1)S(1)}, bf16[16,4096]{1,0:T(8,128)(2,1)S(1)}, u32[]{:S(2)}, u32[]{:S(2)}) collective-permute-start(bf16[16,4096]{1,0:T(8,128)(2,1)S(1)} %slice.6), channel_id=1, source_target_pairs={{0,16},{1,17},{2,18},{3,19},{4,20},{5,21},{6,22},{7,23},{8,24},{9,... | collective-permute-start | bytes 393224 | tf_op jit(solution)/shard_map/ppermute | solution.py:51
  28.1 7.7 %collective-permute-start.8 = (bf16[32,8192]{1,0:T(8,128)(2,1)S(1)}, bf16[32,8192]{1,0:T(8,128)(2,1)S(1)}, u32[]{:S(2)}, u32[]{:S(2)}) collective-permute-start(bf16[32,8192]{1,0:T(8,128)(2,1)S(1)} %pad_maximum_fusion.1), channel_id=1, source_target_pairs={{0,1},{1,0},{2,3},{3,2},{4,5},{5,4},{6,7},{7,6},{8,9},{9,8},{10,11... | collective-permute-start | bytes 1572872 | tf_op jit(solution)/shard_map/ppermute | solution.py:51
  28.2 6.0 %collective-permute-start.11 = (bf16[16,4096]{1,0:T(8,128)(2,1)S(1)}, bf16[16,4096]{1,0:T(8,128)(2,1)S(1)}, u32[]{:S(2)}, u32[]{:S(2)}) collective-permute-start(bf16[16,4096]{1,0:T(8,128)(2,1)S(1)} %slice.8), channel_id=1, source_target_pairs={{0,2},{1,3},{2,0},{3,1},{4,6},{5,7},{6,4},{7,5},{8,10},{9,11},{10,... | collective-permute-start | bytes 393224 | tf_op jit(solution)/shard_map/ppermute | solution.py:51
  31.5 4.3 %collective-permute-start.10 = (bf16[32,8192]{1,0:T(8,128)(2,1)S(1)}, bf16[32,8192]{1,0:T(8,128)(2,1)S(1)}, u32[]{:S(2)}, u32[]{:S(2)}) collective-permute-start(bf16[32,8192]{1,0:T(8,128)(2,1)S(1)} %pad_maximum_fusion.2), channel_id=1, source_target_pairs={{0,1},{1,0},{2,3},{3,2},{4,5},{5,4},{6,7},{7,6},{8,9},{9,8},{10,11... | collective-permute-start | bytes 1572872 | tf_op jit(solution)/shard_map/ppermute | solution.py:51
  34.2 1.6 %collective-permute-start.12 = (bf16[16,8192]{1,0:T(8,128)(2,1)S(1)}, bf16[16,8192]{1,0:T(8,128)(2,1)S(1)}, u32[]{:S(2)}, u32[]{:S(2)}) collective-permute-start(bf16[16,8192]{1,0:T(8,128)(2,1)S(1)} %constant_dynamic-update-slice_fusion.refs_8_), channel_id=1, source_target_pairs={{0,1},{1,0},{2,3},{3,2},{4,5},{5,4},{6,7},{7,6},{8,9},{9,8},{10,11... | collective-permute-start | bytes 786440 | tf_op jit(solution)/shard_map/ppermute | solution.py:51

commit v8 on v7

--- a/solution.py
+++ b/solution.py
@@ -81,7 +81,7 @@
 
 
 def far_z(pair):
-    return lambda g, z, x, c: (g, z ^ (2 * pair + 1 - g), x, c)
+    return lambda g, z, x, c: (g, z ^ (2 * pair + (g == c)), x, c)
 
 
 def over_group(g, z, x, c):
@@ -270,7 +270,8 @@
     total = None
     for at in range(0, width, depth):
         block = jnp.concatenate([ref[:, at : at + depth] for ref in blocks], axis=0)
-        term = mxu(t_ref[:, at : at + depth], block, NT)
+        sides = t_ref[:, at : at + depth], block
+        term = mxu(*(sides[::-1] if added else sides), NT)
         total = term if total is None else total + term
 
     me, g = lax.axis_index("train"), lax.axis_index("group")
@@ -284,7 +285,7 @@
     order = jnp.concatenate(order, axis=0).astype(jnp.bfloat16)
     high, low = halves(total)
     lowest = (total - high.astype(jnp.float32) - low.astype(jnp.float32)).astype(jnp.bfloat16)
-    placed = mxu(high, order) + mxu(low, order) + mxu(lowest, order)
+    placed = sum(mxu(part, order, TN if added else NN) for part in (high, low, lowest))
     out_ref[...] = refs[0][...] + placed if added else placed
 
 
@@ -328,7 +329,7 @@
     flat_train = split_layers(train_grads)
     flat_train, own = after(flat_train, own)
     at_z = own.hop(over_z)
-    early, parts = [own, twin], [at_z]
+    early, parts = [own, twin, at_x, at_z], []
     for pair, one in enumerate(far):
         flat_train, one = after(flat_train, one)
         one = Blocks(precondition(one.array, *rest, here=True), one.came)
@@ -336,20 +337,19 @@
         if pair == 0:
             one.array, at_x = after(one.array, at_x)
             at_xz = at_x.hop(over_z)
-            early += [at_x, one]
-            first_scores = scores(flat_train, early, n_query)
-            first_scores, by_x = after(first_scores, by_x)
-            parts.append(stack(at_x, one).hop(over_core))
-            parts.append(at_xz)
+            early += [at_xz, one, stack(at_x, one).hop(over_core), by_x, by_group]
         else:
-            parts += [one, one.hop(over_core)]
+            parts += [one, one.hop(over_core), by_x, by_group]
         parts.append(stack(by_x, by_group).hop(over_core))
         half = by_x.columns(0, width // 2).hop(over_group)
+        other_half = by_group.columns(width // 2, width).hop(over_x)
         if pair == 0:
+            first_scores = scores(flat_train, early, n_query)
+            first_scores, half = after(first_scores, half)
             half.array, near, near_x = after(half.array, at_z, at_xz)
             parts.append(stack(near, near_x).hop(over_core))
-        corner = beside(half, by_group.columns(width // 2, width).hop(over_x))
-        parts += [by_x, by_group, corner, corner.hop(over_core)]
+        corner = beside(half, other_half)
+        parts += [corner, corner.hop(over_core)]
     partial_scores = scores(flat_train, parts, n_query, first_scores)
     return lax.psum_scatter(partial_scores, "layer", scatter_dimension=1, tiled=True)
 

time: 39.7 us -> 39.5 us (level)
  waiting for transfers between devices: 7.79 us -> 6.92 us
  starting transfers between devices: 14.1 us -> 14.6 us
    ppermute x13, waiting for transfers between devices: 7.79 us -> 6.92 us  [hop(): return Blocks(lax.ppermute(self.array, ('group', 'train'), perm), came)]
    ppermute x13, starting transfers between devices: 14.1 us -> 14.6 us  [hop(): return Blocks(lax.ppermute(self.array, ('group', 'train'), perm), came)]
  transfers between devices with their start and end apart: 13 -> 13, of which waited for: 5 -> 4; matrix products, arithmetic and copies ran while one was open for 0% -> 0% of each run, Pallas kernels for 34% -> 35%
where the time goes in v8:
time: 39.5 us; the launch traced here: 39.4 us
  Pallas kernels  17.5 us (44%)
  starting transfers between devices  14.6 us (37%)
  waiting for transfers between devices  6.92 us (18%)
    ppermute x13, starting transfers between devices, hop(): return Blocks(lax.ppermute(self.array, ('group', 'train'), perm), came)  14.6 us
    ppermute x13, waiting for transfers between devices, hop(): return Blocks(lax.ppermute(self.array, ('group', 'train'), perm), came)  6.92 us
    pallas_call x2, Pallas kernels, scores(): pl.pallas_call(functools.partial(score_kernel, masks, 0 if earlier is Non...  6.81 us
    pallas_call x1, Pallas kernels, split_layers(): pl.pallas_call(functools.partial(split_kernel, layers), out_shape=jax.Sha...  5.61 us
    pallas_call x2, Pallas kernels, precondition(): pl.pallas_call(body, out_shape=jax.ShapeDtypeStruct((q_rows, layers * wid...  5.11 us
  transfers between devices with their start and end apart: 13, of which 4 were waited for; matrix products, arithmetic and copies ran while one was open for 0% of the time, Pallas kernels for 35%

profile of v8, /device:TPU:0, one launch (start us, length us, event | category | flops | bytes accessed | tf_op | source)
XLA Modules:
  0.0 39.4 jit_solution(2497312219480868584)
XLA Ops:
  0.0 5.0 %collective-permute-start = (bf16[16,64,128]{2,1,0:T(8,128)(2,1)}, bf16[16,64,128]{2,1,0:T(8,128)(2,1)S(1)}, u32[]{:S(2)}, u32[]{:S(2)}) collective-permute-start(bf16[16,64,128]{2,1,0:T(8,128)(2,1)} %bitcast.11), channel_id=1, source_target_pairs={{0,12},{1,9},{2,14},{3,11},{4,8},{5,13},{6,10},{7,15},{8,4},{9,1},... | collective-permute-start | bytes 786440 | tf_op jit(solution)/shard_map/ppermute | solution.py:51
  5.0 3.1 %precond.2.refs_0_ = bf16[16,8192]{1,0:T(8,128)(2,1)S(1)} custom-call(bf16[16,64,128]{2,1,0:T(8,128)(2,1)} %bitcast.12, f32[2,64,64]{2,1,0:T(8,128)} %in_ref.1, f32[2,64,64]{2,1,0:T(8,128)} %out_ref.1, f32[2,4096]{1,0:T(2,128)} %eig_ref.1), custom_call_target="tpu_custom_call" | custom-call | flops 1000000000 | bytes 4194304 | tf_op jit(solution)/shard_map/precond/pallas_call | solution.py:190
  8.1 1.6 %collective-permute-start.4 = (bf16[16,8192]{1,0:T(8,128)(2,1)S(1)}, bf16[16,8192]{1,0:T(8,128)(2,1)S(1)}, u32[]{:S(2)}, u32[]{:S(2)}) collective-permute-start(bf16[16,8192]{1,0:T(8,128)(2,1)S(1)} %precond.2.refs_0_), channel_id=1, source_target_pairs={{0,2},{1,3},{2,0},{3,1},{4,6},{5,7},{6,4},{7,5},{8,10},{9,11},{10,... | collective-permute-start | bytes 786440 | tf_op jit(solution)/shard_map/ppermute | solution.py:51
  9.7 0.0 collective-permute-start.3
  9.7 0.0 copy-start
  9.7 0.0 copy-start.1
  9.7 0.0 copy-start.2
  9.7 5.6 %split.1.t_ref = bf16[512,8192]{1,0:T(8,128)(2,1)S(1)} custom-call(bf16[512,64,128]{2,1,0:T(8,128)(2,1)} %bitcast.10), custom_call_target="tpu_custom_call" | custom-call | flops 1000000000 | bytes 16777216 | tf_op jit(solution)/shard_map/split/pallas_call | solution.py:249
  15.3 0.1 collective-permute-start.5
  15.4 0.0 collective-permute-done.q_ref
  15.4 0.0 copy-done
  15.4 0.0 copy-done.1
  15.4 0.0 copy-done.2
  15.4 2.0 %precond.3.refs_5_ = bf16[16,8192]{1,0:T(8,128)(2,1)S(1)} custom-call(bf16[16,64,128]{2,1,0:T(8,128)(2,1)S(1)} %collective-permute-done.q_ref, f32[2,64,64]{2,1,0:T(8,128)S(1)} %copy-done, f32[2,64,64]{2,1,0:T(8,128)S(1)} %copy-done.1, f32[2,4096]{1,0:T(2,128)S(1)} %copy-done.2), custom_call_target="tpu_custom_call" | custom-call | flops 1000000000 | bytes 4194304 | tf_op jit(solution)/shard_map/precond/pallas_call | solution.py:190
  17.5 0.6 %collective-permute-start.1 = (bf16[16,8192]{1,0:T(8,128)(2,1)S(1)}, bf16[16,8192]{1,0:T(8,128)(2,1)S(1)}, u32[]{:S(2)}, u32[]{:S(2)}) collective-permute-start(bf16[16,8192]{1,0:T(8,128)(2,1)S(1)} %precond.3.refs_5_), channel_id=1, source_target_pairs={{0,2},{1,3},{2,0},{3,1},{4,6},{5,7},{6,4},{7,5},{8,10},{9,11},{10,... | collective-permute-start | bytes 786440 | tf_op jit(solution)/shard_map/ppermute | solution.py:51
  18.1 3.4 %collective-permute-start.8 = (bf16[16,8192]{1,0:T(8,128)(2,1)S(1)}, bf16[16,8192]{1,0:T(8,128)(2,1)S(1)}, u32[]{:S(2)}, u32[]{:S(2)}) collective-permute-start(bf16[16,8192]{1,0:T(8,128)(2,1)S(1)} %precond.3.refs_5_), channel_id=1, source_target_pairs={{0,16},{1,17},{2,18},{3,19},{4,20},{5,21},{6,22},{7,23},{8,24},{9,... | collective-permute-start | bytes 786440 | tf_op jit(solution)/shard_map/ppermute | solution.py:51
  21.5 0.0 collective-permute-done.4.refs_2_
  21.5 0.0 collective-permute-start.6
  21.5 4.7 %collective-permute-done.1.refs_7_ = bf16[16,8192]{1,0:T(8,128)(2,1)S(1)} collective-permute-done((bf16[16,8192]{1,0:T(8,128)(2,1)S(1)}, bf16[16,8192]{1,0:T(8,128)(2,1)S(1)}, u32[]{:S(2)}, u32[]{:S(2)}) %collective-permute-start.1) | collective-permute-done | bytes 262176 | tf_op jit(solution)/shard_map/ppermute | solution.py:51
  26.2 0.0 collective-permute-start.7
  26.3 0.3 collective-permute-done.8.refs_8_
  26.5 1.7 %collective-permute-start.2 = (bf16[16,4096]{1,0:T(8,128)(2,1)S(1)}, bf16[16,4096]{1,0:T(8,128)(2,1)S(1)}, u32[]{:S(2)}, u32[]{:S(2)}) collective-permute-start(bf16[16,4096]{1,0:T(8,128)(2,1)S(1)} %slice.8), channel_id=1, source_target_pairs={{0,16},{1,17},{2,18},{3,19},{4,20},{5,21},{6,22},{7,23},{8,24},{9,... | collective-permute-start | bytes 393224 | tf_op jit(solution)/shard_map/ppermute | solution.py:51
  28.3 0.0 collective-permute-done.5.refs_3_
  28.3 1.6 %collective-permute-start.11 = (bf16[16,4096]{1,0:T(8,128)(2,1)S(1)}, bf16[16,4096]{1,0:T(8,128)(2,1)S(1)}, u32[]{:S(2)}, u32[]{:S(2)}) collective-permute-start(bf16[16,4096]{1,0:T(8,128)(2,1)S(1)} %slice.9), channel_id=1, source_target_pairs={{0,2},{1,3},{2,0},{3,1},{4,6},{5,7},{6,4},{7,5},{8,10},{9,11},{10,... | collective-permute-start | bytes 393224 | tf_op jit(solution)/shard_map/ppermute | solution.py:51
  29.9 0.0 collective-permute-done.3.refs_1_
  29.9 0.0 collective-permute-start.9
  29.9 0.0 collective-permute-done.6.refs_4_
  29.9 0.0 collective-permute-done.7.refs_6_
  29.9 2.9 %scores.2.refs_0_ = f32[512,256]{1,0:T(8,128)S(1)} custom-call(bf16[512,8192]{1,0:T(8,128)(2,1)S(1)} %split.1.t_ref, bf16[16,8192]{1,0:T(8,128)(2,1)S(1)} %precond.2.refs_0_, bf16[16,8192]{1,0:T(8,128)(2,1)S(1)} %collective-permute-done.3.refs_1_, bf16[16,8192]{1,0:T(8,128)(2,1)S(1)} %collective-permute-done.4.refs_2_, ...), custom_call_target="tpu_custom_call" | custom-call | flops 2147483648 | bytes 11010048 | tf_op jit(solution)/shard_map/scores/pallas_call | solution.py:297
  32.9 0.0 collective-permute-done.2
  32.9 0.6 %collective-permute-start.10 = (bf16[32,8192]{1,0:T(8,128)(2,1)S(1)}, bf16[32,8192]{1,0:T(8,128)(2,1)S(1)}, u32[]{:S(2)}, u32[]{:S(2)}) collective-permute-start(bf16[32,8192]{1,0:T(8,128)(2,1)S(1)} %pad_maximum_fusion.2), channel_id=1, source_target_pairs={{0,1},{1,0},{2,3},{3,2},{4,5},{5,4},{6,7},{7,6},{8,9},{9,8},{10,11... | collective-permute-start | bytes 1572872 | tf_op jit(solution)/shard_map/ppermute | solution.py:51
  33.5 0.4 collective-permute-done.11
  33.9 0.1 collective-permute-start.12
  34.0 1.5 %collective-permute-done.12.refs_4_ = bf16[16,8192]{1,0:T(8,128)(2,1)S(1)} collective-permute-done((bf16[16,8192]{1,0:T(8,128)(2,1)S(1)}, bf16[16,8192]{1,0:T(8,128)(2,1)S(1)}, u32[]{:S(2)}, u32[]{:S(2)}) %collective-permute-start.12) | collective-permute-done | bytes 262176 | tf_op jit(solution)/shard_map/ppermute | solution.py:51
  35.5 0.0 collective-permute-done.9.refs_1_
  35.5 0.0 collective-permute-done.10.refs_2_
  35.5 3.9 %scores.3 = f32[512,256]{1,0:T(8,128)} custom-call(bf16[512,8192]{1,0:T(8,128)(2,1)S(1)} %split.1.t_ref, f32[512,256]{1,0:T(8,128)S(1)} %scores.2.refs_0_, bf16[32,8192]{1,0:T(8,128)(2,1)S(1)} %collective-permute-done.9.refs_1_, bf16[32,8192]{1,0:T(8,128)(2,1)S(1)} %collective-permute-done.10.refs_2_, ...), custom_call_target="tpu_custom_call" | custom-call | flops 2147483648 | bytes 9961472 | tf_op jit(solution)/shard_map/scores/pallas_call | solution.py:297
  (7 shorter events, 0.1 us)
Async XLA Ops:
  0.0 15.4 %collective-permute-start = (bf16[16,64,128]{2,1,0:T(8,128)(2,1)}, bf16[16,64,128]{2,1,0:T(8,128)(2,1)S(1)}, u32[]{:S(2)}, u32[]{:S(2)}) collective-permute-start(bf16[16,64,128]{2,1,0:T(8,128)(2,1)} %bitcast.11), channel_id=1, source_target_pairs={{0,12},{1,9},{2,14},{3,11},{4,8},{5,13},{6,10},{7,15},{8,4},{9,1},... | collective-permute-start | bytes 786440 | tf_op jit(solution)/shard_map/ppermute | solution.py:51
  8.1 13.3 %collective-permute-start.4 = (bf16[16,8192]{1,0:T(8,128)(2,1)S(1)}, bf16[16,8192]{1,0:T(8,128)(2,1)S(1)}, u32[]{:S(2)}, u32[]{:S(2)}) collective-permute-start(bf16[16,8192]{1,0:T(8,128)(2,1)S(1)} %precond.2.refs_0_), channel_id=1, source_target_pairs={{0,2},{1,3},{2,0},{3,1},{4,6},{5,7},{6,4},{7,5},{8,10},{9,11},{10,... | collective-permute-start | bytes 786440 | tf_op jit(solution)/shard_map/ppermute | solution.py:51
  9.7 20.2 %collective-permute-start.3 = (bf16[16,8192]{1,0:T(8,128)(2,1)S(1)}, bf16[16,8192]{1,0:T(8,128)(2,1)S(1)}, u32[]{:S(2)}, u32[]{:S(2)}) collective-permute-start(bf16[16,8192]{1,0:T(8,128)(2,1)S(1)} %precond.2.refs_0_), channel_id=1, source_target_pairs={{0,1},{1,0},{2,3},{3,2},{4,5},{5,4},{6,7},{7,6},{8,9},{9,8},{10,11... | collective-permute-start | bytes 786440 | tf_op jit(solution)/shard_map/ppermute | solution.py:51
  9.7 5.7 %copy-start = (f32[2,64,64]{2,1,0:T(8,128)S(1)}, f32[2,64,64]{2,1,0:T(8,128)}, u32[]{:S(2)}) copy-start(f32[2,64,64]{2,1,0:T(8,128)} %in_ref.1) | copy-start | bytes 98308
  9.7 5.7 %copy-start.1 = (f32[2,64,64]{2,1,0:T(8,128)S(1)}, f32[2,64,64]{2,1,0:T(8,128)}, u32[]{:S(2)}) copy-start(f32[2,64,64]{2,1,0:T(8,128)} %out_ref.1) | copy-start | bytes 98308
  9.7 5.7 %copy-start.2 = (f32[2,4096]{1,0:T(2,128)S(1)}, f32[2,4096]{1,0:T(2,128)}, u32[]{:S(2)}) copy-start(f32[2,4096]{1,0:T(2,128)} %eig_ref.1) | copy-start | bytes 98308
  15.3 13.0 %collective-permute-start.5 = (bf16[16,8192]{1,0:T(8,128)(2,1)S(1)}, bf16[16,8192]{1,0:T(8,128)(2,1)S(1)}, u32[]{:S(2)}, u32[]{:S(2)}) collective-permute-start(bf16[16,8192]{1,0:T(8,128)(2,1)S(1)} %precond.2.refs_0_), channel_id=1, source_target_pairs={{0,4},{1,5},{2,6},{3,7},{4,0},{5,1},{6,2},{7,3},{8,12},{9,13},{10,... | collective-permute-start | bytes 786440 | tf_op jit(solution)/shard_map/ppermute | solution.py:51
  17.5 8.8 %collective-permute-start.1 = (bf16[16,8192]{1,0:T(8,128)(2,1)S(1)}, bf16[16,8192]{1,0:T(8,128)(2,1)S(1)}, u32[]{:S(2)}, u32[]{:S(2)}) collective-permute-start(bf16[16,8192]{1,0:T(8,128)(2,1)S(1)} %precond.3.refs_5_), channel_id=1, source_target_pairs={{0,2},{1,3},{2,0},{3,1},{4,6},{5,7},{6,4},{7,5},{8,10},{9,11},{10,... | collective-permute-start | bytes 786440 | tf_op jit(solution)/shard_map/ppermute | solution.py:51
  18.1 8.5 %collective-permute-start.8 = (bf16[16,8192]{1,0:T(8,128)(2,1)S(1)}, bf16[16,8192]{1,0:T(8,128)(2,1)S(1)}, u32[]{:S(2)}, u32[]{:S(2)}) collective-permute-start(bf16[16,8192]{1,0:T(8,128)(2,1)S(1)} %precond.3.refs_5_), channel_id=1, source_target_pairs={{0,16},{1,17},{2,18},{3,19},{4,20},{5,21},{6,22},{7,23},{8,24},{9,... | collective-permute-start | bytes 786440 | tf_op jit(solution)/shard_map/ppermute | solution.py:51
  21.5 8.4 %collective-permute-start.6 = (bf16[16,8192]{1,0:T(8,128)(2,1)S(1)}, bf16[16,8192]{1,0:T(8,128)(2,1)S(1)}, u32[]{:S(2)}, u32[]{:S(2)}) collective-permute-start(bf16[16,8192]{1,0:T(8,128)(2,1)S(1)} %collective-permute-done.4.refs_2_), channel_id=1, source_target_pairs={{0,4},{1,5},{2,6},{3,7},{4,0},{5,1},{6,2},{7,3},{8,12},{9,13},{10,... | collective-permute-start | bytes 786440 | tf_op jit(solution)/shard_map/ppermute | solution.py:51
  26.2 3.7 %collective-permute-start.7 = (bf16[32,8192]{1,0:T(8,128)(2,1)S(1)}, bf16[32,8192]{1,0:T(8,128)(2,1)S(1)}, u32[]{:S(2)}, u32[]{:S(2)}) collective-permute-start(bf16[32,8192]{1,0:T(8,128)(2,1)S(1)} %pad_maximum_fusion), channel_id=1, source_target_pairs={{0,1},{1,0},{2,3},{3,2},{4,5},{5,4},{6,7},{7,6},{8,9},{9,8},{10,11... | collective-permute-start | bytes 1572872 | tf_op jit(solution)/shard_map/ppermute | solution.py:51
  26.5 6.3 %collective-permute-start.2 = (bf16[16,4096]{1,0:T(8,128)(2,1)S(1)}, bf16[16,4096]{1,0:T(8,128)(2,1)S(1)}, u32[]{:S(2)}, u32[]{:S(2)}) collective-permute-start(bf16[16,4096]{1,0:T(8,128)(2,1)S(1)} %slice.8), channel_id=1, source_target_pairs={{0,16},{1,17},{2,18},{3,19},{4,20},{5,21},{6,22},{7,23},{8,24},{9,... | collective-permute-start | bytes 393224 | tf_op jit(solution)/shard_map/ppermute | solution.py:51
  28.3 5.5 %collective-permute-start.11 = (bf16[16,4096]{1,0:T(8,128)(2,1)S(1)}, bf16[16,4096]{1,0:T(8,128)(2,1)S(1)}, u32[]{:S(2)}, u32[]{:S(2)}) collective-permute-start(bf16[16,4096]{1,0:T(8,128)(2,1)S(1)} %slice.9), channel_id=1, source_target_pairs={{0,2},{1,3},{2,0},{3,1},{4,6},{5,7},{6,4},{7,5},{8,10},{9,11},{10,... | collective-permute-start | bytes 393224 | tf_op jit(solution)/shard_map/ppermute | solution.py:51
  29.9 5.6 %collective-permute-start.9 = (bf16[32,8192]{1,0:T(8,128)(2,1)S(1)}, bf16[32,8192]{1,0:T(8,128)(2,1)S(1)}, u32[]{:S(2)}, u32[]{:S(2)}) collective-permute-start(bf16[32,8192]{1,0:T(8,128)(2,1)S(1)} %pad_maximum_fusion.1), channel_id=1, source_target_pairs={{0,1},{1,0},{2,3},{3,2},{4,5},{5,4},{6,7},{7,6},{8,9},{9,8},{10,11... | collective-permute-start | bytes 1572872 | tf_op jit(solution)/shard_map/ppermute | solution.py:51
  32.9 2.6 %collective-permute-start.10 = (bf16[32,8192]{1,0:T(8,128)(2,1)S(1)}, bf16[32,8192]{1,0:T(8,128)(2,1)S(1)}, u32[]{:S(2)}, u32[]{:S(2)}) collective-permute-start(bf16[32,8192]{1,0:T(8,128)(2,1)S(1)} %pad_maximum_fusion.2), channel_id=1, source_target_pairs={{0,1},{1,0},{2,3},{3,2},{4,5},{5,4},{6,7},{7,6},{8,9},{9,8},{10,11... | collective-permute-start | bytes 1572872 | tf_op jit(solution)/shard_map/ppermute | solution.py:51
  33.9 1.6 %collective-permute-start.12 = (bf16[16,8192]{1,0:T(8,128)(2,1)S(1)}, bf16[16,8192]{1,0:T(8,128)(2,1)S(1)}, u32[]{:S(2)}, u32[]{:S(2)}) collective-permute-start(bf16[16,8192]{1,0:T(8,128)(2,1)S(1)} %constant_dynamic-update-slice_fusion.refs_3_), channel_id=1, source_target_pairs={{0,1},{1,0},{2,3},{3,2},{4,5},{5,4},{6,7},{7,6},{8,9},{9,8},{10,11... | collective-permute-start | bytes 786440 | tf_op jit(solution)/shard_map/ppermute | solution.py:51

commit v9 on v6

--- a/solution.py
+++ b/solution.py
@@ -81,7 +81,7 @@
 
 
 def far_z(pair):
-    return lambda g, z, x, c: (g, z ^ (2 * pair + 1 - g), x, c)
+    return lambda g, z, x, c: (g, z ^ (2 * pair + (g == c)), x, c)
 
 
 def over_group(g, z, x, c):
@@ -216,7 +216,7 @@
     body(*here, *others)
 
 
-def split_kernel(layers, t_ref, flat_ref, here_ref, wide_ref, sems):
+def split_kernel(layers, t_ref, slabs_ref, here_ref, wide_ref, sems):
     rows, chunks = BLOCK, sems.shape[0]
     lines = t_ref.shape[1]
     pitch = wide_ref.shape[0] // rows
@@ -238,9 +238,8 @@
             for row in range(rows):
                 wide_ref[row * pitch : row * pitch + lines, :] = here_ref[at + row].astype(jnp.float32)
             for line in range(lines):
-                column = ((line % layers) * (lines // layers) + line // layers) * LANES
-                out = wide_ref[pl.ds(line, rows, stride=pitch), :].astype(jnp.bfloat16)
-                flat_ref[pl.ds(at, rows), column : column + LANES] = out
+                slab = (line % layers) * (lines // layers) + line // layers
+                slabs_ref[slab, pl.ds(at, rows), :] = wide_ref[pl.ds(line, rows, stride=pitch), :].astype(jnp.bfloat16)
 
 
 def split_layers(train_grads):
@@ -248,7 +247,7 @@
     lines = layers * width // LANES
     return pl.pallas_call(
         functools.partial(split_kernel, layers),
-        out_shape=jax.ShapeDtypeStruct((tr_rows, layers * width), jnp.bfloat16),
+        out_shape=jax.ShapeDtypeStruct((lines, tr_rows, LANES), jnp.bfloat16),
         in_specs=[pl.BlockSpec(memory_space=pltpu.HBM)],
         out_specs=VMEM,
         scratch_shapes=[
@@ -262,15 +261,18 @@
     )(in_hbm(by_lines(train_grads)))
 
 
-def score_kernel(masks, t_ref, *refs):
+def score_kernel(masks, slabs_ref, *refs):
     blocks, out_ref = refs[:-1], refs[-1]
-    q_rows, width = blocks[0].shape
-    n_query = len(masks) * q_rows
-    depth = min(width, 1024)
+    slabs = slabs_ref.shape[0]
+    q_rows = out_ref.shape[1] // len(masks)
+    n_query = out_ref.shape[1]
+    step = min(slabs, 8)
     total = None
-    for at in range(0, width, depth):
-        block = jnp.concatenate([ref[:, at : at + depth] for ref in blocks], axis=0)
-        term = mxu(t_ref[:, at : at + depth], block, NT)
+    for at in range(0, slabs, step):
+        train = jnp.concatenate([slabs_ref[at + i] for i in range(step)], axis=1)
+        columns = slice(at * LANES, (at + step) * LANES)
+        block = jnp.concatenate([ref[:, columns] for ref in blocks], axis=0)
+        term = mxu(train, block, NT)
         total = term if total is None else total + term
 
     me, g = lax.axis_index("train"), lax.axis_index("group")
@@ -295,7 +297,6 @@
 
 
 def per_device(n_train, train_grads, query_grads, basis_in, basis_out, eigvals):
-    tr_rows = train_grads.shape[0]
     zs = n_train // (XS * CORES)
     rest = basis_in, basis_out, eigvals
     queries = by_lines(query_grads)
@@ -303,45 +304,48 @@
     far = [Blocks(queries, places).hop(far_z(pair)) for pair in range(1, zs // 2)]
     own = Blocks(precondition(queries, *rest), places)
     q_rows, width = own.array.shape
+    n_query = n_train * q_rows
     at_x = own.hop(over_x)
+    twin = own.hop(over_core)
+    train_grads, own = after(train_grads, own)
+    slabs = split_layers(train_grads)
+    slabs, own = after(slabs, own)
     at_z = own.hop(over_z)
-    twins = [own.hop(over_core)]
-    train_grads, own = after(train_grads, own)
-    flat_train = split_layers(train_grads)
-    here = [own, at_x, at_z]
+    parts = [own, twin, at_x, at_z]
     for pair, one in enumerate(far):
-        flat_train, one = after(flat_train, one)
+        slabs, one = after(slabs, one)
         one = Blocks(precondition(one.array, *rest, here=True), one.came)
         by_x, by_group = one.hop(over_x), one.hop(over_group)
+        parts.append(one)
         if pair == 0:
             one.array, at_x = after(one.array, at_x)
             at_xz = at_x.hop(over_z)
-            twins.append(stack(at_x, one).hop(over_core))
-            twins.append(stack(at_z, at_xz).hop(over_core))
-            here.append(at_xz)
+            stacked = stack(at_x, one)
+            stacked.array, by_x = after(stacked.array, by_x)
+            parts += [at_xz, stacked.hop(over_core)]
         else:
-            twins.append(one.hop(over_core))
-        twins.append(stack(by_x, by_group).hop(over_core))
-        corner = beside(
-            by_x.columns(0, width // 2).hop(over_group), by_group.columns(width // 2, width).hop(over_x)
-        )
-        twins.append(corner.hop(over_core))
-        here += [one, by_x, by_group, corner]
-    everything = here + twins
-    masks = [came_masks(came) for a in everything for came in a.came]
-
-    n_query = n_train * q_rows
+            parts.append(one.hop(over_core))
+        parts += [by_x, by_group, stack(by_x, by_group).hop(over_core)]
+        half = by_x.columns(0, width // 2).hop(over_group)
+        if pair == 0:
+            half.array, near, near_x = after(half.array, at_z, at_xz)
+            parts.append(stack(near, near_x).hop(over_core))
+        corner = beside(half, by_group.columns(width // 2, width).hop(over_x))
+        parts += [corner, corner.hop(over_core)]
+
+    tr_rows = train_grads.shape[0]
+    operands = [slabs] + [a.array for a in parts]
     partial_scores = pl.pallas_call(
-        functools.partial(score_kernel, masks),
+        functools.partial(score_kernel, [came_masks(came) for a in parts for came in a.came]),
         out_shape=jax.ShapeDtypeStruct((tr_rows, n_query), jnp.float32),
-        in_specs=[VMEM] * (1 + len(everything)),
+        in_specs=[VMEM] * len(operands),
         out_specs=VMEM,
-        compiler_params=pltpu.CompilerParams(vmem_limit_bytes=36 * MIB),
+        compiler_params=pltpu.CompilerParams(vmem_limit_bytes=32 * MIB),
         cost_estimate=pl.CostEstimate(
             flops=2 * tr_rows * n_query * width, bytes_accessed=2 * width * (tr_rows + n_query), transcendentals=0
         ),
         name="scores",
-    )(flat_train, *(a.array for a in everything))
+    )(*operands)
     return lax.psum_scatter(partial_scores, "layer", scatter_dimension=1, tiled=True)
 
 

time: 39.6 us -> 38.2 us (0.965)
  starting transfers between devices: 14.7 us -> 13.9 us
  Pallas kernels: 14.5 us -> 14 us
    ppermute x13, starting transfers between devices: 14.7 us -> 13.9 us  [hop(): return Blocks(lax.ppermute(self.array, ('group', 'train'), perm), came)]
    pallas_call x1, Pallas kernels: 5.62 us -> 5.1 us  [split_layers(): pl.pallas_call(functools.partial(split_kernel, layers), out_shape=jax.Sha...]
where the time goes in v9:
time: 38.2 us; the launch traced here: 38 us
  Pallas kernels  14 us (37%)
  starting transfers between devices  13.9 us (36%)
  waiting for transfers between devices  9.89 us (26%)
    ppermute x13, starting transfers between devices, hop(): return Blocks(lax.ppermute(self.array, ('group', 'train'), perm), came)  13.9 us
    ppermute x13, waiting for transfers between devices, hop(): return Blocks(lax.ppermute(self.array, ('group', 'train'), perm), came)  9.89 us
    pallas_call x2, Pallas kernels, precondition(): pl.pallas_call(body, out_shape=jax.ShapeDtypeStruct((q_rows, layers * wid...  5.11 us
    pallas_call x1, Pallas kernels, split_layers(): pl.pallas_call(functools.partial(split_kernel, layers), out_shape=jax.Sha...  5.1 us
    pallas_call x1, Pallas kernels, per_device(): pl.pallas_call(functools.partial(score_kernel, [came_masks(came) for a in...  3.76 us
  transfers between devices with their start and end apart: 13, of which 5 were waited for; matrix products, arithmetic and copies ran while one was open for 0% of the time, Pallas kernels for 27%

profile of v9, /device:TPU:0, one launch (start us, length us, event | category | flops | bytes accessed | tf_op | source)
XLA Modules:
  0.0 38.0 jit_solution(5628578683732385756)
XLA Ops:
  0.0 5.0 %collective-permute-start = (bf16[16,64,128]{2,1,0:T(8,128)(2,1)}, bf16[16,64,128]{2,1,0:T(8,128)(2,1)S(1)}, u32[]{:S(2)}, u32[]{:S(2)}) collective-permute-start(bf16[16,64,128]{2,1,0:T(8,128)(2,1)} %bitcast.11), channel_id=1, source_target_pairs={{0,12},{1,9},{2,14},{3,11},{4,8},{5,13},{6,10},{7,15},{8,4},{9,1},... | collective-permute-start | bytes 786440 | tf_op jit(solution)/shard_map/ppermute | solution.py:51
  5.0 3.1 %precond.2.refs_0_ = bf16[16,8192]{1,0:T(8,128)(2,1)S(1)} custom-call(bf16[16,64,128]{2,1,0:T(8,128)(2,1)} %bitcast.12, f32[2,64,64]{2,1,0:T(8,128)} %in_ref.1, f32[2,64,64]{2,1,0:T(8,128)} %out_ref.1, f32[2,4096]{1,0:T(2,128)} %eig_ref.1), custom_call_target="tpu_custom_call" | custom-call | flops 1000000000 | bytes 4194304 | tf_op jit(solution)/shard_map/precond/pallas_call | solution.py:190
  8.1 1.6 %collective-permute-start.2 = (bf16[16,8192]{1,0:T(8,128)(2,1)S(1)}, bf16[16,8192]{1,0:T(8,128)(2,1)S(1)}, u32[]{:S(2)}, u32[]{:S(2)}) collective-permute-start(bf16[16,8192]{1,0:T(8,128)(2,1)S(1)} %precond.2.refs_0_), channel_id=1, source_target_pairs={{0,2},{1,3},{2,0},{3,1},{4,6},{5,7},{6,4},{7,5},{8,10},{9,11},{10,... | collective-permute-start | bytes 786440 | tf_op jit(solution)/shard_map/ppermute | solution.py:51
  9.7 0.0 collective-permute-start.1
  9.7 0.0 copy-start
  9.7 0.0 copy-start.1
  9.7 0.0 copy-start.2
  9.7 5.1 %split.1.slabs_ref = bf16[64,512,128]{2,1,0:T(8,128)(2,1)S(1)} custom-call(bf16[512,64,128]{2,1,0:T(8,128)(2,1)} %bitcast.10), custom_call_target="tpu_custom_call" | custom-call | flops 1000000000 | bytes 16777216 | tf_op jit(solution)/shard_map/split/pallas_call | solution.py:248
  14.8 0.1 collective-permute-start.3
  14.9 0.0 collective-permute-done.q_ref
  14.9 0.0 copy-done
  14.9 0.0 copy-done.1
  14.9 0.0 copy-done.2
  14.9 2.0 %precond.3.refs_4_ = bf16[16,8192]{1,0:T(8,128)(2,1)S(1)} custom-call(bf16[16,64,128]{2,1,0:T(8,128)(2,1)S(1)} %collective-permute-done.q_ref, f32[2,64,64]{2,1,0:T(8,128)S(1)} %copy-done, f32[2,64,64]{2,1,0:T(8,128)S(1)} %copy-done.1, f32[2,4096]{1,0:T(2,128)S(1)} %copy-done.2), custom_call_target="tpu_custom_call" | custom-call | flops 1000000000 | bytes 4194304 | tf_op jit(solution)/shard_map/precond/pallas_call | solution.py:190
  17.0 0.6 %collective-permute-start.5 = (bf16[16,8192]{1,0:T(8,128)(2,1)S(1)}, bf16[16,8192]{1,0:T(8,128)(2,1)S(1)}, u32[]{:S(2)}, u32[]{:S(2)}) collective-permute-start(bf16[16,8192]{1,0:T(8,128)(2,1)S(1)} %precond.3.refs_4_), channel_id=1, source_target_pairs={{0,2},{1,3},{2,0},{3,1},{4,6},{5,7},{6,4},{7,5},{8,10},{9,11},{10,... | collective-permute-start | bytes 786440 | tf_op jit(solution)/shard_map/ppermute | solution.py:51
  17.6 3.9 %collective-permute-start.7 = (bf16[16,8192]{1,0:T(8,128)(2,1)S(1)}, bf16[16,8192]{1,0:T(8,128)(2,1)S(1)}, u32[]{:S(2)}, u32[]{:S(2)}) collective-permute-start(bf16[16,8192]{1,0:T(8,128)(2,1)S(1)} %precond.3.refs_4_), channel_id=1, source_target_pairs={{0,16},{1,17},{2,18},{3,19},{4,20},{5,21},{6,22},{7,23},{8,24},{9,... | collective-permute-start | bytes 786440 | tf_op jit(solution)/shard_map/ppermute | solution.py:51
  21.5 0.0 collective-permute-done.2.refs_2_
  21.5 0.0 collective-permute-start.4
  21.5 4.2 %collective-permute-done.5.refs_7_ = bf16[16,8192]{1,0:T(8,128)(2,1)S(1)} collective-permute-done((bf16[16,8192]{1,0:T(8,128)(2,1)S(1)}, bf16[16,8192]{1,0:T(8,128)(2,1)S(1)}, u32[]{:S(2)}, u32[]{:S(2)}) %collective-permute-start.5) | collective-permute-done | bytes 262176 | tf_op jit(solution)/shard_map/ppermute | solution.py:51
  25.8 1.8 %collective-permute-start.9 = (bf16[16,4096]{1,0:T(8,128)(2,1)S(1)}, bf16[16,4096]{1,0:T(8,128)(2,1)S(1)}, u32[]{:S(2)}, u32[]{:S(2)}) collective-permute-start(bf16[16,4096]{1,0:T(8,128)(2,1)S(1)} %slice.6), channel_id=1, source_target_pairs={{0,16},{1,17},{2,18},{3,19},{4,20},{5,21},{6,22},{7,23},{8,24},{9,... | collective-permute-start | bytes 393224 | tf_op jit(solution)/shard_map/ppermute | solution.py:51
  27.6 0.0 collective-permute-done.7.refs_8_
  27.6 0.6 %collective-permute-start.11 = (bf16[16,4096]{1,0:T(8,128)(2,1)S(1)}, bf16[16,4096]{1,0:T(8,128)(2,1)S(1)}, u32[]{:S(2)}, u32[]{:S(2)}) collective-permute-start(bf16[16,4096]{1,0:T(8,128)(2,1)S(1)} %slice.8), channel_id=1, source_target_pairs={{0,2},{1,3},{2,0},{3,1},{4,6},{5,7},{6,4},{7,5},{8,10},{9,11},{10,... | collective-permute-start | bytes 393224 | tf_op jit(solution)/shard_map/ppermute | solution.py:51
  28.2 0.0 collective-permute-done.3.refs_3_
  28.3 0.1 collective-permute-start.8
  28.3 0.9 %collective-permute-done.4.refs_5_ = bf16[16,8192]{1,0:T(8,128)(2,1)S(1)} collective-permute-done((bf16[16,8192]{1,0:T(8,128)(2,1)S(1)}, bf16[16,8192]{1,0:T(8,128)(2,1)S(1)}, u32[]{:S(2)}, u32[]{:S(2)}) %collective-permute-start.4) | collective-permute-done | bytes 262176 | tf_op jit(solution)/shard_map/ppermute | solution.py:51
  29.2 0.0 collective-permute-start.6
  29.2 1.7 %collective-permute-done.9 = bf16[16,4096]{1,0:T(8,128)(2,1)S(1)} collective-permute-done((bf16[16,4096]{1,0:T(8,128)(2,1)S(1)}, bf16[16,4096]{1,0:T(8,128)(2,1)S(1)}, u32[]{:S(2)}, u32[]{:S(2)}) %collective-permute-start.9) | collective-permute-done | bytes 131104 | tf_op jit(solution)/shard_map/ppermute | solution.py:51
  31.0 0.1 collective-permute-start.10
  31.1 1.6 %collective-permute-done.11 = bf16[16,4096]{1,0:T(8,128)(2,1)S(1)} collective-permute-done((bf16[16,4096]{1,0:T(8,128)(2,1)S(1)}, bf16[16,4096]{1,0:T(8,128)(2,1)S(1)}, u32[]{:S(2)}, u32[]{:S(2)}) %collective-permute-start.11) | collective-permute-done | bytes 131104 | tf_op jit(solution)/shard_map/ppermute | solution.py:51
  32.7 0.1 collective-permute-start.12
  32.7 0.0 collective-permute-done.1.refs_1_
  32.7 1.5 %collective-permute-done.12.refs_12_ = bf16[16,8192]{1,0:T(8,128)(2,1)S(1)} collective-permute-done((bf16[16,8192]{1,0:T(8,128)(2,1)S(1)}, bf16[16,8192]{1,0:T(8,128)(2,1)S(1)}, u32[]{:S(2)}, u32[]{:S(2)}) %collective-permute-start.12) | collective-permute-done | bytes 262176 | tf_op jit(solution)/shard_map/ppermute | solution.py:51
  34.3 0.0 collective-permute-done.8.refs_9_
  34.3 0.0 collective-permute-done.6.refs_6_
  34.3 0.0 collective-permute-done.10.refs_10_
  34.3 3.8 %scores.1 = f32[512,256]{1,0:T(8,128)} custom-call(bf16[64,512,128]{2,1,0:T(8,128)(2,1)S(1)} %split.1.slabs_ref, bf16[16,8192]{1,0:T(8,128)(2,1)S(1)} %precond.2.refs_0_, bf16[16,8192]{1,0:T(8,128)(2,1)S(1)} %collective-permute-done.1.refs_1_, bf16[16,8192]{1,0:T(8,128)(2,1)S(1)} %collective-permute-done.2.refs_2_, ...), custom_call_target="tpu_custom_call" | custom-call | flops 2147483648 | bytes 12582912 | tf_op jit(solution)/shard_map/scores/pallas_call | solution.py:338
  (7 shorter events, 0.1 us)
Async XLA Ops:
  0.0 14.9 %collective-permute-start = (bf16[16,64,128]{2,1,0:T(8,128)(2,1)}, bf16[16,64,128]{2,1,0:T(8,128)(2,1)S(1)}, u32[]{:S(2)}, u32[]{:S(2)}) collective-permute-start(bf16[16,64,128]{2,1,0:T(8,128)(2,1)} %bitcast.11), channel_id=1, source_target_pairs={{0,12},{1,9},{2,14},{3,11},{4,8},{5,13},{6,10},{7,15},{8,4},{9,1},... | collective-permute-start | bytes 786440 | tf_op jit(solution)/shard_map/ppermute | solution.py:51
  8.1 13.4 %collective-permute-start.2 = (bf16[16,8192]{1,0:T(8,128)(2,1)S(1)}, bf16[16,8192]{1,0:T(8,128)(2,1)S(1)}, u32[]{:S(2)}, u32[]{:S(2)}) collective-permute-start(bf16[16,8192]{1,0:T(8,128)(2,1)S(1)} %precond.2.refs_0_), channel_id=1, source_target_pairs={{0,2},{1,3},{2,0},{3,1},{4,6},{5,7},{6,4},{7,5},{8,10},{9,11},{10,... | collective-permute-start | bytes 786440 | tf_op jit(solution)/shard_map/ppermute | solution.py:51
  9.7 23.1 %collective-permute-start.1 = (bf16[16,8192]{1,0:T(8,128)(2,1)S(1)}, bf16[16,8192]{1,0:T(8,128)(2,1)S(1)}, u32[]{:S(2)}, u32[]{:S(2)}) collective-permute-start(bf16[16,8192]{1,0:T(8,128)(2,1)S(1)} %precond.2.refs_0_), channel_id=1, source_target_pairs={{0,1},{1,0},{2,3},{3,2},{4,5},{5,4},{6,7},{7,6},{8,9},{9,8},{10,11... | collective-permute-start | bytes 786440 | tf_op jit(solution)/shard_map/ppermute | solution.py:51
  9.7 5.2 %copy-start = (f32[2,64,64]{2,1,0:T(8,128)S(1)}, f32[2,64,64]{2,1,0:T(8,128)}, u32[]{:S(2)}) copy-start(f32[2,64,64]{2,1,0:T(8,128)} %in_ref.1) | copy-start | bytes 98308
  9.7 5.2 %copy-start.1 = (f32[2,64,64]{2,1,0:T(8,128)S(1)}, f32[2,64,64]{2,1,0:T(8,128)}, u32[]{:S(2)}) copy-start(f32[2,64,64]{2,1,0:T(8,128)} %out_ref.1) | copy-start | bytes 98308
  9.7 5.2 %copy-start.2 = (f32[2,4096]{1,0:T(2,128)S(1)}, f32[2,4096]{1,0:T(2,128)}, u32[]{:S(2)}) copy-start(f32[2,4096]{1,0:T(2,128)} %eig_ref.1) | copy-start | bytes 98308
  14.8 13.4 %collective-permute-start.3 = (bf16[16,8192]{1,0:T(8,128)(2,1)S(1)}, bf16[16,8192]{1,0:T(8,128)(2,1)S(1)}, u32[]{:S(2)}, u32[]{:S(2)}) collective-permute-start(bf16[16,8192]{1,0:T(8,128)(2,1)S(1)} %precond.2.refs_0_), channel_id=1, source_target_pairs={{0,4},{1,5},{2,6},{3,7},{4,0},{5,1},{6,2},{7,3},{8,12},{9,13},{10,... | collective-permute-start | bytes 786440 | tf_op jit(solution)/shard_map/ppermute | solution.py:51
  17.0 8.8 %collective-permute-start.5 = (bf16[16,8192]{1,0:T(8,128)(2,1)S(1)}, bf16[16,8192]{1,0:T(8,128)(2,1)S(1)}, u32[]{:S(2)}, u32[]{:S(2)}) collective-permute-start(bf16[16,8192]{1,0:T(8,128)(2,1)S(1)} %precond.3.refs_4_), channel_id=1, source_target_pairs={{0,2},{1,3},{2,0},{3,1},{4,6},{5,7},{6,4},{7,5},{8,10},{9,11},{10,... | collective-permute-start | bytes 786440 | tf_op jit(solution)/shard_map/ppermute | solution.py:51
  17.6 10.0 %collective-permute-start.7 = (bf16[16,8192]{1,0:T(8,128)(2,1)S(1)}, bf16[16,8192]{1,0:T(8,128)(2,1)S(1)}, u32[]{:S(2)}, u32[]{:S(2)}) collective-permute-start(bf16[16,8192]{1,0:T(8,128)(2,1)S(1)} %precond.3.refs_4_), channel_id=1, source_target_pairs={{0,16},{1,17},{2,18},{3,19},{4,20},{5,21},{6,22},{7,23},{8,24},{9,... | collective-permute-start | bytes 786440 | tf_op jit(solution)/shard_map/ppermute | solution.py:51
  21.5 7.7 %collective-permute-start.4 = (bf16[16,8192]{1,0:T(8,128)(2,1)S(1)}, bf16[16,8192]{1,0:T(8,128)(2,1)S(1)}, u32[]{:S(2)}, u32[]{:S(2)}) collective-permute-start(bf16[16,8192]{1,0:T(8,128)(2,1)S(1)} %collective-permute-done.2.refs_2_), channel_id=1, source_target_pairs={{0,4},{1,5},{2,6},{3,7},{4,0},{5,1},{6,2},{7,3},{8,12},{9,13},{10,... | collective-permute-start | bytes 786440 | tf_op jit(solution)/shard_map/ppermute | solution.py:51
  25.8 5.2 %collective-permute-start.9 = (bf16[16,4096]{1,0:T(8,128)(2,1)S(1)}, bf16[16,4096]{1,0:T(8,128)(2,1)S(1)}, u32[]{:S(2)}, u32[]{:S(2)}) collective-permute-start(bf16[16,4096]{1,0:T(8,128)(2,1)S(1)} %slice.6), channel_id=1, source_target_pairs={{0,16},{1,17},{2,18},{3,19},{4,20},{5,21},{6,22},{7,23},{8,24},{9,... | collective-permute-start | bytes 393224 | tf_op jit(solution)/shard_map/ppermute | solution.py:51
  27.6 5.0 %collective-permute-start.11 = (bf16[16,4096]{1,0:T(8,128)(2,1)S(1)}, bf16[16,4096]{1,0:T(8,128)(2,1)S(1)}, u32[]{:S(2)}, u32[]{:S(2)}) collective-permute-start(bf16[16,4096]{1,0:T(8,128)(2,1)S(1)} %slice.8), channel_id=1, source_target_pairs={{0,2},{1,3},{2,0},{3,1},{4,6},{5,7},{6,4},{7,5},{8,10},{9,11},{10,... | collective-permute-start | bytes 393224 | tf_op jit(solution)/shard_map/ppermute | solution.py:51
  28.3 6.0 %collective-permute-start.8 = (bf16[32,8192]{1,0:T(8,128)(2,1)S(1)}, bf16[32,8192]{1,0:T(8,128)(2,1)S(1)}, u32[]{:S(2)}, u32[]{:S(2)}) collective-permute-start(bf16[32,8192]{1,0:T(8,128)(2,1)S(1)} %pad_maximum_fusion.1), channel_id=1, source_target_pairs={{0,1},{1,0},{2,3},{3,2},{4,5},{5,4},{6,7},{7,6},{8,9},{9,8},{10,11... | collective-permute-start | bytes 1572872 | tf_op jit(solution)/shard_map/ppermute | solution.py:51
  29.2 5.1 %collective-permute-start.6 = (bf16[32,8192]{1,0:T(8,128)(2,1)S(1)}, bf16[32,8192]{1,0:T(8,128)(2,1)S(1)}, u32[]{:S(2)}, u32[]{:S(2)}) collective-permute-start(bf16[32,8192]{1,0:T(8,128)(2,1)S(1)} %pad_maximum_fusion), channel_id=1, source_target_pairs={{0,1},{1,0},{2,3},{3,2},{4,5},{5,4},{6,7},{7,6},{8,9},{9,8},{10,11... | collective-permute-start | bytes 1572872 | tf_op jit(solution)/shard_map/ppermute | solution.py:51
  31.0 3.3 %collective-permute-start.10 = (bf16[32,8192]{1,0:T(8,128)(2,1)S(1)}, bf16[32,8192]{1,0:T(8,128)(2,1)S(1)}, u32[]{:S(2)}, u32[]{:S(2)}) collective-permute-start(bf16[32,8192]{1,0:T(8,128)(2,1)S(1)} %pad_maximum_fusion.2), channel_id=1, source_target_pairs={{0,1},{1,0},{2,3},{3,2},{4,5},{5,4},{6,7},{7,6},{8,9},{9,8},{10,11... | collective-permute-start | bytes 1572872 | tf_op jit(solution)/shard_map/ppermute | solution.py:51
  32.7 1.6 %collective-permute-start.12 = (bf16[16,8192]{1,0:T(8,128)(2,1)S(1)}, bf16[16,8192]{1,0:T(8,128)(2,1)S(1)}, u32[]{:S(2)}, u32[]{:S(2)}) collective-permute-start(bf16[16,8192]{1,0:T(8,128)(2,1)S(1)} %constant_dynamic-update-slice_fusion.refs_11_), channel_id=1, source_target_pairs={{0,1},{1,0},{2,3},{3,2},{4,5},{5,4},{6,7},{7,6},{8,9},{9,8},{10,11... | collective-permute-start | bytes 786440 | tf_op jit(solution)/shard_map/ppermute | solution.py:51

commit v10 on v9

--- a/solution.py
+++ b/solution.py
@@ -261,10 +261,39 @@
     )(in_hbm(by_lines(train_grads)))
 
 
-def score_kernel(masks, slabs_ref, *refs):
+def order_rows(masks, q_rows, n_query):
+    me, g = lax.axis_index("train"), lax.axis_index("group")
+    row = lax.broadcasted_iota(jnp.int32, (q_rows, n_query), 0)
+    query = lax.broadcasted_iota(jnp.int32, (q_rows, n_query), 1)
+    order = []
+    for mask in masks:
+        c0, c1 = (jnp.where(g == 0, mask[0][c], mask[1][c]) for c in range(CORES))
+        source = me ^ jnp.where(me % CORES == 0, c0, c1)
+        order.append(jnp.where(query == source * q_rows + row, 1.0, 0.0))
+    return jnp.concatenate(order, axis=0).astype(jnp.bfloat16)
+
+
+def order_kernel(masks, q_rows, *refs):
+    order_ref = refs[-1]
+    order_ref[...] = order_rows(masks, q_rows, order_ref.shape[1])
+
+
+def first_order(parts, stands_after, q_rows, n_query):
+    masks = [came_masks(came) for a in parts for came in a.came]
+    return pl.pallas_call(
+        functools.partial(order_kernel, masks, q_rows),
+        out_shape=jax.ShapeDtypeStruct((len(masks) * q_rows, n_query), jnp.bfloat16),
+        in_specs=[pl.BlockSpec(memory_space=pl.ANY)] * len(stands_after),
+        out_specs=VMEM,
+        compiler_params=pltpu.CompilerParams(vmem_limit_bytes=16 * MIB),
+        cost_estimate=pl.CostEstimate(flops=4 * 10**9, bytes_accessed=16 * MIB, transcendentals=0),
+        name="order",
+    )(*(a.array for a in stands_after))
+
+
+def score_kernel(q_rows, masks, slabs_ref, first_ref, *refs):
     blocks, out_ref = refs[:-1], refs[-1]
     slabs = slabs_ref.shape[0]
-    q_rows = out_ref.shape[1] // len(masks)
     n_query = out_ref.shape[1]
     step = min(slabs, 8)
     total = None
@@ -275,15 +304,7 @@
         term = mxu(train, block, NT)
         total = term if total is None else total + term
 
-    me, g = lax.axis_index("train"), lax.axis_index("group")
-    row = lax.broadcasted_iota(jnp.int32, (q_rows, n_query), 0)
-    query = lax.broadcasted_iota(jnp.int32, (q_rows, n_query), 1)
-    order = []
-    for mask in masks:
-        c0, c1 = (jnp.where(g == 0, mask[0][c], mask[1][c]) for c in range(CORES))
-        source = me ^ jnp.where(me % CORES == 0, c0, c1)
-        order.append(jnp.where(query == source * q_rows + row, 1.0, 0.0))
-    order = jnp.concatenate(order, axis=0).astype(jnp.bfloat16)
+    order = jnp.concatenate([first_ref[...], order_rows(masks, q_rows, n_query)], axis=0)
     high, low = halves(total)
     lowest = (total - high.astype(jnp.float32) - low.astype(jnp.float32)).astype(jnp.bfloat16)
     out_ref[...] = mxu(high, order) + mxu(low, order) + mxu(lowest, order)
@@ -321,8 +342,10 @@
             one.array, at_x = after(one.array, at_x)
             at_xz = at_x.hop(over_z)
             stacked = stack(at_x, one)
-            stacked.array, by_x = after(stacked.array, by_x)
             parts += [at_xz, stacked.hop(over_core)]
+            n_first = sum(len(a.came) for a in parts)
+            order = first_order(parts, [twin, at_x], q_rows, n_query)
+            order, by_x = after(order, by_x)
         else:
             parts.append(one.hop(over_core))
         parts += [by_x, by_group, stack(by_x, by_group).hop(over_core)]
@@ -334,9 +357,10 @@
         parts += [corner, corner.hop(over_core)]
 
     tr_rows = train_grads.shape[0]
-    operands = [slabs] + [a.array for a in parts]
+    operands = [slabs, order] + [a.array for a in parts]
+    masks = [came_masks(came) for a in parts for came in a.came]
     partial_scores = pl.pallas_call(
-        functools.partial(score_kernel, [came_masks(came) for a in parts for came in a.came]),
+        functools.partial(score_kernel, q_rows, masks[n_first:]),
         out_shape=jax.ShapeDtypeStruct((tr_rows, n_query), jnp.float32),
         in_specs=[VMEM] * len(operands),
         out_specs=VMEM,

time: 38.2 us -> 39.2 us (1.026)
  waiting for transfers between devices: 9.89 us -> 10.8 us
    ppermute x13, waiting for transfers between devices: 9.89 us -> 10.8 us  [hop(): return Blocks(lax.ppermute(self.array, ('group', 'train'), perm), came)]
    pallas_call x1 -> x2, Pallas kernels: 3.76 us -> 3.79 us  [the longest x1 3.77 us: per_device(): pl.pallas_call(functools.partial(score_kernel, q_rows, masks[n_first:]),...]
  transfers between devices with their start and end apart: 13 -> 13, of which waited for: 5 -> 5; matrix products, arithmetic and copies ran while one was open for 0% -> 0% of each run, Pallas kernels for 27% -> 26%
where the time goes in v10:
time: 39.2 us; the launch traced here: 39.1 us
  Pallas kernels  14 us (36%)
  starting transfers between devices  13.9 us (35%)
  waiting for transfers between devices  10.8 us (28%)
    ppermute x13, starting transfers between devices, hop(): return Blocks(lax.ppermute(self.array, ('group', 'train'), perm), came)  13.9 us
    ppermute x13, waiting for transfers between devices, hop(): return Blocks(lax.ppermute(self.array, ('group', 'train'), perm), came)  10.8 us
    pallas_call x2, Pallas kernels, precondition(): pl.pallas_call(body, out_shape=jax.ShapeDtypeStruct((q_rows, layers * wid...  5.11 us
    pallas_call x1, Pallas kernels, split_layers(): pl.pallas_call(functools.partial(split_kernel, layers), out_shape=jax.Sha...  5.1 us
    pallas_call x1, Pallas kernels, per_device(): pl.pallas_call(functools.partial(score_kernel, q_rows, masks[n_first:]),...  3.77 us
  transfers between devices with their start and end apart: 13, of which 5 were waited for; matrix products, arithmetic and copies ran while one was open for 0% of the time, Pallas kernels for 26%

profile of v10, /device:TPU:0, one launch (start us, length us, event | category | flops | bytes accessed | tf_op | source)
XLA Modules:
  0.0 39.1 jit_solution(5335434782627900701)
XLA Ops:
  0.0 5.0 %collective-permute-start = (bf16[16,64,128]{2,1,0:T(8,128)(2,1)}, bf16[16,64,128]{2,1,0:T(8,128)(2,1)S(1)}, u32[]{:S(2)}, u32[]{:S(2)}) collective-permute-start(bf16[16,64,128]{2,1,0:T(8,128)(2,1)} %bitcast.11), channel_id=1, source_target_pairs={{0,12},{1,9},{2,14},{3,11},{4,8},{5,13},{6,10},{7,15},{8,4},{9,1},... | collective-permute-start | bytes 786440 | tf_op jit(solution)/shard_map/ppermute | solution.py:51
  5.0 3.1 %precond.2.refs_0_ = bf16[16,8192]{1,0:T(8,128)(2,1)S(1)} custom-call(bf16[16,64,128]{2,1,0:T(8,128)(2,1)} %bitcast.12, f32[2,64,64]{2,1,0:T(8,128)} %in_ref.1, f32[2,64,64]{2,1,0:T(8,128)} %out_ref.1, f32[2,4096]{1,0:T(2,128)} %eig_ref.1), custom_call_target="tpu_custom_call" | custom-call | flops 1000000000 | bytes 4194304 | tf_op jit(solution)/shard_map/precond/pallas_call | solution.py:190
  8.1 1.6 %collective-permute-start.3 = (bf16[16,8192]{1,0:T(8,128)(2,1)S(1)}, bf16[16,8192]{1,0:T(8,128)(2,1)S(1)}, u32[]{:S(2)}, u32[]{:S(2)}) collective-permute-start(bf16[16,8192]{1,0:T(8,128)(2,1)S(1)} %precond.2.refs_0_), channel_id=1, source_target_pairs={{0,2},{1,3},{2,0},{3,1},{4,6},{5,7},{6,4},{7,5},{8,10},{9,11},{10,... | collective-permute-start | bytes 786440 | tf_op jit(solution)/shard_map/ppermute | solution.py:51
  9.7 0.0 collective-permute-start.2
  9.7 0.0 copy-start
  9.7 0.0 copy-start.1
  9.7 0.0 copy-start.2
  9.7 5.1 %split.1.slabs_ref = bf16[64,512,128]{2,1,0:T(8,128)(2,1)S(1)} custom-call(bf16[512,64,128]{2,1,0:T(8,128)(2,1)} %bitcast.10), custom_call_target="tpu_custom_call" | custom-call | flops 1000000000 | bytes 16777216 | tf_op jit(solution)/shard_map/split/pallas_call | solution.py:248
  14.8 0.1 collective-permute-start.4
  14.9 0.0 collective-permute-done.q_ref
  14.9 0.0 copy-done
  14.9 0.0 copy-done.1
  14.9 0.0 copy-done.2
  14.9 2.0 %precond.3.refs_4_ = bf16[16,8192]{1,0:T(8,128)(2,1)S(1)} custom-call(bf16[16,64,128]{2,1,0:T(8,128)(2,1)S(1)} %collective-permute-done.q_ref, f32[2,64,64]{2,1,0:T(8,128)S(1)} %copy-done, f32[2,64,64]{2,1,0:T(8,128)S(1)} %copy-done.1, f32[2,4096]{1,0:T(2,128)S(1)} %copy-done.2), custom_call_target="tpu_custom_call" | custom-call | flops 1000000000 | bytes 4194304 | tf_op jit(solution)/shard_map/precond/pallas_call | solution.py:190
  17.0 0.6 %collective-permute-start.1 = (bf16[16,8192]{1,0:T(8,128)(2,1)S(1)}, bf16[16,8192]{1,0:T(8,128)(2,1)S(1)}, u32[]{:S(2)}, u32[]{:S(2)}) collective-permute-start(bf16[16,8192]{1,0:T(8,128)(2,1)S(1)} %precond.3.refs_4_), channel_id=1, source_target_pairs={{0,2},{1,3},{2,0},{3,1},{4,6},{5,7},{6,4},{7,5},{8,10},{9,11},{10,... | collective-permute-start | bytes 786440 | tf_op jit(solution)/shard_map/ppermute | solution.py:51
  17.6 3.9 %collective-permute-start.7 = (bf16[16,8192]{1,0:T(8,128)(2,1)S(1)}, bf16[16,8192]{1,0:T(8,128)(2,1)S(1)}, u32[]{:S(2)}, u32[]{:S(2)}) collective-permute-start(bf16[16,8192]{1,0:T(8,128)(2,1)S(1)} %precond.3.refs_4_), channel_id=1, source_target_pairs={{0,16},{1,17},{2,18},{3,19},{4,20},{5,21},{6,22},{7,23},{8,24},{9,... | collective-permute-start | bytes 786440 | tf_op jit(solution)/shard_map/ppermute | solution.py:51
  21.5 0.0 collective-permute-done.3.refs_1_.refs_2_
  21.5 0.0 collective-permute-start.5
  21.5 0.0 collective-permute-done.2.refs_0_.refs_1_
  21.6 0.1 collective-permute-start.6
  21.7 4.1 %collective-permute-done.1.refs_7_ = bf16[16,8192]{1,0:T(8,128)(2,1)S(1)} collective-permute-done((bf16[16,8192]{1,0:T(8,128)(2,1)S(1)}, bf16[16,8192]{1,0:T(8,128)(2,1)S(1)}, u32[]{:S(2)}, u32[]{:S(2)}) %collective-permute-start.1) | collective-permute-done | bytes 262176 | tf_op jit(solution)/shard_map/ppermute | solution.py:51
  25.8 1.8 %collective-permute-start.9 = (bf16[16,4096]{1,0:T(8,128)(2,1)S(1)}, bf16[16,4096]{1,0:T(8,128)(2,1)S(1)}, u32[]{:S(2)}, u32[]{:S(2)}) collective-permute-start(bf16[16,4096]{1,0:T(8,128)(2,1)S(1)} %slice.6), channel_id=1, source_target_pairs={{0,16},{1,17},{2,18},{3,19},{4,20},{5,21},{6,22},{7,23},{8,24},{9,... | collective-permute-start | bytes 393224 | tf_op jit(solution)/shard_map/ppermute | solution.py:51
  27.6 0.0 collective-permute-done.7.refs_8_
  27.6 0.1 collective-permute-start.8
  27.7 0.0 collective-permute-done.4.refs_3_
  27.7 0.6 %collective-permute-start.11 = (bf16[16,4096]{1,0:T(8,128)(2,1)S(1)}, bf16[16,4096]{1,0:T(8,128)(2,1)S(1)}, u32[]{:S(2)}, u32[]{:S(2)}) collective-permute-start(bf16[16,4096]{1,0:T(8,128)(2,1)S(1)} %slice.8), channel_id=1, source_target_pairs={{0,2},{1,3},{2,0},{3,1},{4,6},{5,7},{6,4},{7,5},{8,10},{9,11},{10,... | collective-permute-start | bytes 393224 | tf_op jit(solution)/shard_map/ppermute | solution.py:51
  28.3 0.9 %collective-permute-done.5.refs_5_ = bf16[16,8192]{1,0:T(8,128)(2,1)S(1)} collective-permute-done((bf16[16,8192]{1,0:T(8,128)(2,1)S(1)}, bf16[16,8192]{1,0:T(8,128)(2,1)S(1)}, u32[]{:S(2)}, u32[]{:S(2)}) %collective-permute-start.5) | collective-permute-done | bytes 262176 | tf_op jit(solution)/shard_map/ppermute | solution.py:51
  29.2 1.7 %collective-permute-done.9 = bf16[16,4096]{1,0:T(8,128)(2,1)S(1)} collective-permute-done((bf16[16,4096]{1,0:T(8,128)(2,1)S(1)}, bf16[16,4096]{1,0:T(8,128)(2,1)S(1)}, u32[]{:S(2)}, u32[]{:S(2)}) %collective-permute-start.9) | collective-permute-done | bytes 131104 | tf_op jit(solution)/shard_map/ppermute | solution.py:51
  31.0 0.1 collective-permute-start.10
  31.1 2.6 %collective-permute-done.11 = bf16[16,4096]{1,0:T(8,128)(2,1)S(1)} collective-permute-done((bf16[16,4096]{1,0:T(8,128)(2,1)S(1)}, bf16[16,4096]{1,0:T(8,128)(2,1)S(1)}, u32[]{:S(2)}, u32[]{:S(2)}) %collective-permute-start.11) | collective-permute-done | bytes 131104 | tf_op jit(solution)/shard_map/ppermute | solution.py:51
  33.7 0.1 collective-permute-start.12
  33.8 0.0 collective-permute-done.6.refs_6_
  33.8 1.5 %collective-permute-done.12.refs_12_ = bf16[16,8192]{1,0:T(8,128)(2,1)S(1)} collective-permute-done((bf16[16,8192]{1,0:T(8,128)(2,1)S(1)}, bf16[16,8192]{1,0:T(8,128)(2,1)S(1)}, u32[]{:S(2)}, u32[]{:S(2)}) %collective-permute-start.12) | collective-permute-done | bytes 262176 | tf_op jit(solution)/shard_map/ppermute | solution.py:51
  35.3 0.0 collective-permute-done.8.refs_9_
  35.3 0.0 collective-permute-done.10.refs_10_
  35.3 3.8 %scores.1 = f32[512,256]{1,0:T(8,128)} custom-call(bf16[64,512,128]{2,1,0:T(8,128)(2,1)S(1)} %split.1.slabs_ref, bf16[128,256]{1,0:T(8,128)(2,1)S(1)} %order.1.first_ref, bf16[16,8192]{1,0:T(8,128)(2,1)S(1)} %precond.2.refs_0_, bf16[16,8192]{1,0:T(8,128)(2,1)S(1)} %collective-permute-done.2.refs_0_.refs_1_, ...), custom_call_target="tpu_custom_call" | custom-call | flops 2147483648 | bytes 12582912 | tf_op jit(solution)/shard_map/scores/pallas_call | solution.py:362
  (8 shorter events, 0.2 us)
Async XLA Ops:
  0.0 14.9 %collective-permute-start = (bf16[16,64,128]{2,1,0:T(8,128)(2,1)}, bf16[16,64,128]{2,1,0:T(8,128)(2,1)S(1)}, u32[]{:S(2)}, u32[]{:S(2)}) collective-permute-start(bf16[16,64,128]{2,1,0:T(8,128)(2,1)} %bitcast.11), channel_id=1, source_target_pairs={{0,12},{1,9},{2,14},{3,11},{4,8},{5,13},{6,10},{7,15},{8,4},{9,1},... | collective-permute-start | bytes 786440 | tf_op jit(solution)/shard_map/ppermute | solution.py:51
  8.1 13.4 %collective-permute-start.3 = (bf16[16,8192]{1,0:T(8,128)(2,1)S(1)}, bf16[16,8192]{1,0:T(8,128)(2,1)S(1)}, u32[]{:S(2)}, u32[]{:S(2)}) collective-permute-start(bf16[16,8192]{1,0:T(8,128)(2,1)S(1)} %precond.2.refs_0_), channel_id=1, source_target_pairs={{0,2},{1,3},{2,0},{3,1},{4,6},{5,7},{6,4},{7,5},{8,10},{9,11},{10,... | collective-permute-start | bytes 786440 | tf_op jit(solution)/shard_map/ppermute | solution.py:51
  9.7 11.9 %collective-permute-start.2 = (bf16[16,8192]{1,0:T(8,128)(2,1)S(1)}, bf16[16,8192]{1,0:T(8,128)(2,1)S(1)}, u32[]{:S(2)}, u32[]{:S(2)}) collective-permute-start(bf16[16,8192]{1,0:T(8,128)(2,1)S(1)} %precond.2.refs_0_), channel_id=1, source_target_pairs={{0,1},{1,0},{2,3},{3,2},{4,5},{5,4},{6,7},{7,6},{8,9},{9,8},{10,11... | collective-permute-start | bytes 786440 | tf_op jit(solution)/shard_map/ppermute | solution.py:51
  9.7 5.2 %copy-start = (f32[2,64,64]{2,1,0:T(8,128)S(1)}, f32[2,64,64]{2,1,0:T(8,128)}, u32[]{:S(2)}) copy-start(f32[2,64,64]{2,1,0:T(8,128)} %in_ref.1) | copy-start | bytes 98308
  9.7 5.2 %copy-start.1 = (f32[2,64,64]{2,1,0:T(8,128)S(1)}, f32[2,64,64]{2,1,0:T(8,128)}, u32[]{:S(2)}) copy-start(f32[2,64,64]{2,1,0:T(8,128)} %out_ref.1) | copy-start | bytes 98308
  9.7 5.2 %copy-start.2 = (f32[2,4096]{1,0:T(2,128)S(1)}, f32[2,4096]{1,0:T(2,128)}, u32[]{:S(2)}) copy-start(f32[2,4096]{1,0:T(2,128)} %eig_ref.1) | copy-start | bytes 98308
  14.8 12.9 %collective-permute-start.4 = (bf16[16,8192]{1,0:T(8,128)(2,1)S(1)}, bf16[16,8192]{1,0:T(8,128)(2,1)S(1)}, u32[]{:S(2)}, u32[]{:S(2)}) collective-permute-start(bf16[16,8192]{1,0:T(8,128)(2,1)S(1)} %precond.2.refs_0_), channel_id=1, source_target_pairs={{0,4},{1,5},{2,6},{3,7},{4,0},{5,1},{6,2},{7,3},{8,12},{9,13},{10,... | collective-permute-start | bytes 786440 | tf_op jit(solution)/shard_map/ppermute | solution.py:51
  17.0 8.8 %collective-permute-start.1 = (bf16[16,8192]{1,0:T(8,128)(2,1)S(1)}, bf16[16,8192]{1,0:T(8,128)(2,1)S(1)}, u32[]{:S(2)}, u32[]{:S(2)}) collective-permute-start(bf16[16,8192]{1,0:T(8,128)(2,1)S(1)} %precond.3.refs_4_), channel_id=1, source_target_pairs={{0,2},{1,3},{2,0},{3,1},{4,6},{5,7},{6,4},{7,5},{8,10},{9,11},{10,... | collective-permute-start | bytes 786440 | tf_op jit(solution)/shard_map/ppermute | solution.py:51
  17.6 10.0 %collective-permute-start.7 = (bf16[16,8192]{1,0:T(8,128)(2,1)S(1)}, bf16[16,8192]{1,0:T(8,128)(2,1)S(1)}, u32[]{:S(2)}, u32[]{:S(2)}) collective-permute-start(bf16[16,8192]{1,0:T(8,128)(2,1)S(1)} %precond.3.refs_4_), channel_id=1, source_target_pairs={{0,16},{1,17},{2,18},{3,19},{4,20},{5,21},{6,22},{7,23},{8,24},{9,... | collective-permute-start | bytes 786440 | tf_op jit(solution)/shard_map/ppermute | solution.py:51
  21.5 7.7 %collective-permute-start.5 = (bf16[16,8192]{1,0:T(8,128)(2,1)S(1)}, bf16[16,8192]{1,0:T(8,128)(2,1)S(1)}, u32[]{:S(2)}, u32[]{:S(2)}) collective-permute-start(bf16[16,8192]{1,0:T(8,128)(2,1)S(1)} %collective-permute-done.3.refs_1_.refs_2_), channel_id=1, source_target_pairs={{0,4},{1,5},{2,6},{3,7},{4,0},{5,1},{6,2},{7,3},{8,12},{9,13},{10,... | collective-permute-start | bytes 786440 | tf_op jit(solution)/shard_map/ppermute | solution.py:51
  21.6 12.2 %collective-permute-start.6 = (bf16[32,8192]{1,0:T(8,128)(2,1)S(1)}, bf16[32,8192]{1,0:T(8,128)(2,1)S(1)}, u32[]{:S(2)}, u32[]{:S(2)}) collective-permute-start(bf16[32,8192]{1,0:T(8,128)(2,1)S(1)} %pad_maximum_fusion), channel_id=1, source_target_pairs={{0,1},{1,0},{2,3},{3,2},{4,5},{5,4},{6,7},{7,6},{8,9},{9,8},{10,11... | collective-permute-start | bytes 1572872 | tf_op jit(solution)/shard_map/ppermute | solution.py:51
  25.8 5.2 %collective-permute-start.9 = (bf16[16,4096]{1,0:T(8,128)(2,1)S(1)}, bf16[16,4096]{1,0:T(8,128)(2,1)S(1)}, u32[]{:S(2)}, u32[]{:S(2)}) collective-permute-start(bf16[16,4096]{1,0:T(8,128)(2,1)S(1)} %slice.6), channel_id=1, source_target_pairs={{0,16},{1,17},{2,18},{3,19},{4,20},{5,21},{6,22},{7,23},{8,24},{9,... | collective-permute-start | bytes 393224 | tf_op jit(solution)/shard_map/ppermute | solution.py:51
  27.6 7.7 %collective-permute-start.8 = (bf16[32,8192]{1,0:T(8,128)(2,1)S(1)}, bf16[32,8192]{1,0:T(8,128)(2,1)S(1)}, u32[]{:S(2)}, u32[]{:S(2)}) collective-permute-start(bf16[32,8192]{1,0:T(8,128)(2,1)S(1)} %pad_maximum_fusion.1), channel_id=1, source_target_pairs={{0,1},{1,0},{2,3},{3,2},{4,5},{5,4},{6,7},{7,6},{8,9},{9,8},{10,11... | collective-permute-start | bytes 1572872 | tf_op jit(solution)/shard_map/ppermute | solution.py:51
  27.7 6.0 %collective-permute-start.11 = (bf16[16,4096]{1,0:T(8,128)(2,1)S(1)}, bf16[16,4096]{1,0:T(8,128)(2,1)S(1)}, u32[]{:S(2)}, u32[]{:S(2)}) collective-permute-start(bf16[16,4096]{1,0:T(8,128)(2,1)S(1)} %slice.8), channel_id=1, source_target_pairs={{0,2},{1,3},{2,0},{3,1},{4,6},{5,7},{6,4},{7,5},{8,10},{9,11},{10,... | collective-permute-start | bytes 393224 | tf_op jit(solution)/shard_map/ppermute | solution.py:51
  31.0 4.3 %collective-permute-start.10 = (bf16[32,8192]{1,0:T(8,128)(2,1)S(1)}, bf16[32,8192]{1,0:T(8,128)(2,1)S(1)}, u32[]{:S(2)}, u32[]{:S(2)}) collective-permute-start(bf16[32,8192]{1,0:T(8,128)(2,1)S(1)} %pad_maximum_fusion.2), channel_id=1, source_target_pairs={{0,1},{1,0},{2,3},{3,2},{4,5},{5,4},{6,7},{7,6},{8,9},{9,8},{10,11... | collective-permute-start | bytes 1572872 | tf_op jit(solution)/shard_map/ppermute | solution.py:51
  33.7 1.6 %collective-permute-start.12 = (bf16[16,8192]{1,0:T(8,128)(2,1)S(1)}, bf16[16,8192]{1,0:T(8,128)(2,1)S(1)}, u32[]{:S(2)}, u32[]{:S(2)}) collective-permute-start(bf16[16,8192]{1,0:T(8,128)(2,1)S(1)} %constant_dynamic-update-slice_fusion.refs_11_), channel_id=1, source_target_pairs={{0,1},{1,0},{2,3},{3,2},{4,5},{5,4},{6,7},{7,6},{8,9},{9,8},{10,11... | collective-permute-start | bytes 786440 | tf_op jit(solution)/shard_map/ppermute | solution.py:51

commit v11 on v10

--- a/solution.py
+++ b/solution.py
@@ -348,11 +348,10 @@
             order, by_x = after(order, by_x)
         else:
             parts.append(one.hop(over_core))
-        parts += [by_x, by_group, stack(by_x, by_group).hop(over_core)]
         half = by_x.columns(0, width // 2).hop(over_group)
-        if pair == 0:
-            half.array, near, near_x = after(half.array, at_z, at_xz)
-            parts.append(stack(near, near_x).hop(over_core))
+        swapped = [by_x, by_group] + ([at_z, at_xz] if pair == 0 else [])
+        half.array, *swapped = after(half.array, *swapped)
+        parts += [by_x, by_group, stack(*swapped).hop(over_core)]
         corner = beside(half, by_group.columns(width // 2, width).hop(over_x))
         parts += [corner, corner.hop(over_core)]
 

time: 39.2 us -> 39.2 us (level)
    ppermute x13 -> x12, waiting for transfers between devices: 10.8 us -> 10.9 us  [hop(): return Blocks(lax.ppermute(self.array, ('group', 'train'), perm), came)]
    ppermute x13 -> x12, starting transfers between devices: 13.9 us -> 13.9 us  [hop(): return Blocks(lax.ppermute(self.array, ('group', 'train'), perm), came)]
  transfers between devices with their start and end apart: 13 -> 12, of which waited for: 5 -> 5; matrix products, arithmetic and copies ran while one was open for 0% -> 0% of each run, Pallas kernels for 26% -> 26%
where the time goes in v11:
time: 39.2 us; the launch traced here: 39.1 us
  Pallas kernels  14 us (36%)
  starting transfers between devices  13.9 us (35%)
  waiting for transfers between devices  10.9 us (28%)
    ppermute x12, starting transfers between devices, hop(): return Blocks(lax.ppermute(self.array, ('group', 'train'), perm), came)  13.9 us
    ppermute x12, waiting for transfers between devices, hop(): return Blocks(lax.ppermute(self.array, ('group', 'train'), perm), came)  10.9 us
    pallas_call x2, Pallas kernels, precondition(): pl.pallas_call(body, out_shape=jax.ShapeDtypeStruct((q_rows, layers * wid...  5.11 us
    pallas_call x1, Pallas kernels, split_layers(): pl.pallas_call(functools.partial(split_kernel, layers), out_shape=jax.Sha...  5.1 us
    pallas_call x1, Pallas kernels, per_device(): pl.pallas_call(functools.partial(score_kernel, q_rows, masks[n_first:]),...  3.77 us
  transfers between devices with their start and end apart: 12, of which 5 were waited for; matrix products, arithmetic and copies ran while one was open for 0% of the time, Pallas kernels for 26%

profile of v11, /device:TPU:0, one launch (start us, length us, event | category | flops | bytes accessed | tf_op | source)
XLA Modules:
  0.0 39.1 jit_solution(7348196721469297860)
XLA Ops:
  0.0 5.0 %collective-permute-start = (bf16[16,64,128]{2,1,0:T(8,128)(2,1)}, bf16[16,64,128]{2,1,0:T(8,128)(2,1)S(1)}, u32[]{:S(2)}, u32[]{:S(2)}) collective-permute-start(bf16[16,64,128]{2,1,0:T(8,128)(2,1)} %bitcast.11), channel_id=1, source_target_pairs={{0,12},{1,9},{2,14},{3,11},{4,8},{5,13},{6,10},{7,15},{8,4},{9,1},... | collective-permute-start | bytes 786440 | tf_op jit(solution)/shard_map/ppermute | solution.py:51
  5.0 3.1 %precond.2.refs_0_ = bf16[16,8192]{1,0:T(8,128)(2,1)S(1)} custom-call(bf16[16,64,128]{2,1,0:T(8,128)(2,1)} %bitcast.12, f32[2,64,64]{2,1,0:T(8,128)} %in_ref.1, f32[2,64,64]{2,1,0:T(8,128)} %out_ref.1, f32[2,4096]{1,0:T(2,128)} %eig_ref.1), custom_call_target="tpu_custom_call" | custom-call | flops 1000000000 | bytes 4194304 | tf_op jit(solution)/shard_map/precond/pallas_call | solution.py:190
  8.1 1.6 %collective-permute-start.3 = (bf16[16,8192]{1,0:T(8,128)(2,1)S(1)}, bf16[16,8192]{1,0:T(8,128)(2,1)S(1)}, u32[]{:S(2)}, u32[]{:S(2)}) collective-permute-start(bf16[16,8192]{1,0:T(8,128)(2,1)S(1)} %precond.2.refs_0_), channel_id=1, source_target_pairs={{0,2},{1,3},{2,0},{3,1},{4,6},{5,7},{6,4},{7,5},{8,10},{9,11},{10,... | collective-permute-start | bytes 786440 | tf_op jit(solution)/shard_map/ppermute | solution.py:51
  9.7 0.0 collective-permute-start.2
  9.7 0.0 copy-start
  9.7 0.0 copy-start.1
  9.7 0.0 copy-start.2
  9.7 5.1 %split.1.slabs_ref = bf16[64,512,128]{2,1,0:T(8,128)(2,1)S(1)} custom-call(bf16[512,64,128]{2,1,0:T(8,128)(2,1)} %bitcast.10), custom_call_target="tpu_custom_call" | custom-call | flops 1000000000 | bytes 16777216 | tf_op jit(solution)/shard_map/split/pallas_call | solution.py:248
  14.8 0.1 collective-permute-start.4
  14.9 0.0 collective-permute-done.q_ref
  14.9 0.0 copy-done
  14.9 0.0 copy-done.1
  14.9 0.0 copy-done.2
  14.9 2.0 %precond.3.refs_4_ = bf16[16,8192]{1,0:T(8,128)(2,1)S(1)} custom-call(bf16[16,64,128]{2,1,0:T(8,128)(2,1)S(1)} %collective-permute-done.q_ref, f32[2,64,64]{2,1,0:T(8,128)S(1)} %copy-done, f32[2,64,64]{2,1,0:T(8,128)S(1)} %copy-done.1, f32[2,4096]{1,0:T(2,128)S(1)} %copy-done.2), custom_call_target="tpu_custom_call" | custom-call | flops 1000000000 | bytes 4194304 | tf_op jit(solution)/shard_map/precond/pallas_call | solution.py:190
  17.0 0.6 %collective-permute-start.1 = (bf16[16,8192]{1,0:T(8,128)(2,1)S(1)}, bf16[16,8192]{1,0:T(8,128)(2,1)S(1)}, u32[]{:S(2)}, u32[]{:S(2)}) collective-permute-start(bf16[16,8192]{1,0:T(8,128)(2,1)S(1)} %precond.3.refs_4_), channel_id=1, source_target_pairs={{0,2},{1,3},{2,0},{3,1},{4,6},{5,7},{6,4},{7,5},{8,10},{9,11},{10,... | collective-permute-start | bytes 786440 | tf_op jit(solution)/shard_map/ppermute | solution.py:51
  17.6 3.9 %collective-permute-start.7 = (bf16[16,8192]{1,0:T(8,128)(2,1)S(1)}, bf16[16,8192]{1,0:T(8,128)(2,1)S(1)}, u32[]{:S(2)}, u32[]{:S(2)}) collective-permute-start(bf16[16,8192]{1,0:T(8,128)(2,1)S(1)} %precond.3.refs_4_), channel_id=1, source_target_pairs={{0,16},{1,17},{2,18},{3,19},{4,20},{5,21},{6,22},{7,23},{8,24},{9,... | collective-permute-start | bytes 786440 | tf_op jit(solution)/shard_map/ppermute | solution.py:51
  21.5 0.0 collective-permute-done.3.refs_1_.refs_2_
  21.5 0.0 collective-permute-start.5
  21.5 0.0 collective-permute-done.2.refs_0_.refs_1_
  21.5 4.2 %collective-permute-done.1.refs_7_ = bf16[16,8192]{1,0:T(8,128)(2,1)S(1)} collective-permute-done((bf16[16,8192]{1,0:T(8,128)(2,1)S(1)}, bf16[16,8192]{1,0:T(8,128)(2,1)S(1)}, u32[]{:S(2)}, u32[]{:S(2)}) %collective-permute-start.1) | collective-permute-done | bytes 262176 | tf_op jit(solution)/shard_map/ppermute | solution.py:51
  25.8 1.8 %collective-permute-start.8 = (bf16[16,4096]{1,0:T(8,128)(2,1)S(1)}, bf16[16,4096]{1,0:T(8,128)(2,1)S(1)}, u32[]{:S(2)}, u32[]{:S(2)}) collective-permute-start(bf16[16,4096]{1,0:T(8,128)(2,1)S(1)} %slice.6), channel_id=1, source_target_pairs={{0,16},{1,17},{2,18},{3,19},{4,20},{5,21},{6,22},{7,23},{8,24},{9,... | collective-permute-start | bytes 393224 | tf_op jit(solution)/shard_map/ppermute | solution.py:51
  27.6 0.1 collective-permute-start.6
  27.7 0.0 collective-permute-done.7.refs_8_
  27.7 0.6 %collective-permute-start.10 = (bf16[16,4096]{1,0:T(8,128)(2,1)S(1)}, bf16[16,4096]{1,0:T(8,128)(2,1)S(1)}, u32[]{:S(2)}, u32[]{:S(2)}) collective-permute-start(bf16[16,4096]{1,0:T(8,128)(2,1)S(1)} %slice.8), channel_id=1, source_target_pairs={{0,2},{1,3},{2,0},{3,1},{4,6},{5,7},{6,4},{7,5},{8,10},{9,11},{10,... | collective-permute-start | bytes 393224 | tf_op jit(solution)/shard_map/ppermute | solution.py:51
  28.3 0.0 collective-permute-done.4.refs_3_
  28.3 0.9 %collective-permute-done.5.refs_5_ = bf16[16,8192]{1,0:T(8,128)(2,1)S(1)} collective-permute-done((bf16[16,8192]{1,0:T(8,128)(2,1)S(1)}, bf16[16,8192]{1,0:T(8,128)(2,1)S(1)}, u32[]{:S(2)}, u32[]{:S(2)}) %collective-permute-start.5) | collective-permute-done | bytes 262176 | tf_op jit(solution)/shard_map/ppermute | solution.py:51
  29.2 1.7 %collective-permute-done.8 = bf16[16,4096]{1,0:T(8,128)(2,1)S(1)} collective-permute-done((bf16[16,4096]{1,0:T(8,128)(2,1)S(1)}, bf16[16,4096]{1,0:T(8,128)(2,1)S(1)}, u32[]{:S(2)}, u32[]{:S(2)}) %collective-permute-start.8) | collective-permute-done | bytes 131104 | tf_op jit(solution)/shard_map/ppermute | solution.py:51
  30.9 0.1 pad_maximum_fusion
  31.0 0.1 collective-permute-start.9
  31.1 2.6 %collective-permute-done.10 = bf16[16,4096]{1,0:T(8,128)(2,1)S(1)} collective-permute-done((bf16[16,4096]{1,0:T(8,128)(2,1)S(1)}, bf16[16,4096]{1,0:T(8,128)(2,1)S(1)}, u32[]{:S(2)}, u32[]{:S(2)}) %collective-permute-start.10) | collective-permute-done | bytes 131104 | tf_op jit(solution)/shard_map/ppermute | solution.py:51
  33.7 0.1 collective-permute-start.11
  33.8 0.0 collective-permute-done.6.refs_6_
  33.8 1.5 %collective-permute-done.11.refs_11_ = bf16[16,8192]{1,0:T(8,128)(2,1)S(1)} collective-permute-done((bf16[16,8192]{1,0:T(8,128)(2,1)S(1)}, bf16[16,8192]{1,0:T(8,128)(2,1)S(1)}, u32[]{:S(2)}, u32[]{:S(2)}) %collective-permute-start.11) | collective-permute-done | bytes 262176 | tf_op jit(solution)/shard_map/ppermute | solution.py:51
  35.3 0.0 collective-permute-done.9.refs_9_
  35.3 3.8 %scores.1 = f32[512,256]{1,0:T(8,128)} custom-call(bf16[64,512,128]{2,1,0:T(8,128)(2,1)S(1)} %split.1.slabs_ref, bf16[128,256]{1,0:T(8,128)(2,1)S(1)} %order.1.first_ref, bf16[16,8192]{1,0:T(8,128)(2,1)S(1)} %precond.2.refs_0_, bf16[16,8192]{1,0:T(8,128)(2,1)S(1)} %collective-permute-done.2.refs_0_.refs_1_, ...), custom_call_target="tpu_custom_call" | custom-call | flops 2147483648 | bytes 12582912 | tf_op jit(solution)/shard_map/scores/pallas_call | solution.py:361
  (6 shorter events, 0.1 us)
Async XLA Ops:
  0.0 14.9 %collective-permute-start = (bf16[16,64,128]{2,1,0:T(8,128)(2,1)}, bf16[16,64,128]{2,1,0:T(8,128)(2,1)S(1)}, u32[]{:S(2)}, u32[]{:S(2)}) collective-permute-start(bf16[16,64,128]{2,1,0:T(8,128)(2,1)} %bitcast.11), channel_id=1, source_target_pairs={{0,12},{1,9},{2,14},{3,11},{4,8},{5,13},{6,10},{7,15},{8,4},{9,1},... | collective-permute-start | bytes 786440 | tf_op jit(solution)/shard_map/ppermute | solution.py:51
  8.1 13.4 %collective-permute-start.3 = (bf16[16,8192]{1,0:T(8,128)(2,1)S(1)}, bf16[16,8192]{1,0:T(8,128)(2,1)S(1)}, u32[]{:S(2)}, u32[]{:S(2)}) collective-permute-start(bf16[16,8192]{1,0:T(8,128)(2,1)S(1)} %precond.2.refs_0_), channel_id=1, source_target_pairs={{0,2},{1,3},{2,0},{3,1},{4,6},{5,7},{6,4},{7,5},{8,10},{9,11},{10,... | collective-permute-start | bytes 786440 | tf_op jit(solution)/shard_map/ppermute | solution.py:51
  9.7 11.8 %collective-permute-start.2 = (bf16[16,8192]{1,0:T(8,128)(2,1)S(1)}, bf16[16,8192]{1,0:T(8,128)(2,1)S(1)}, u32[]{:S(2)}, u32[]{:S(2)}) collective-permute-start(bf16[16,8192]{1,0:T(8,128)(2,1)S(1)} %precond.2.refs_0_), channel_id=1, source_target_pairs={{0,1},{1,0},{2,3},{3,2},{4,5},{5,4},{6,7},{7,6},{8,9},{9,8},{10,11... | collective-permute-start | bytes 786440 | tf_op jit(solution)/shard_map/ppermute | solution.py:51
  9.7 5.2 %copy-start = (f32[2,64,64]{2,1,0:T(8,128)S(1)}, f32[2,64,64]{2,1,0:T(8,128)}, u32[]{:S(2)}) copy-start(f32[2,64,64]{2,1,0:T(8,128)} %in_ref.1) | copy-start | bytes 98308
  9.7 5.2 %copy-start.1 = (f32[2,64,64]{2,1,0:T(8,128)S(1)}, f32[2,64,64]{2,1,0:T(8,128)}, u32[]{:S(2)}) copy-start(f32[2,64,64]{2,1,0:T(8,128)} %out_ref.1) | copy-start | bytes 98308
  9.7 5.2 %copy-start.2 = (f32[2,4096]{1,0:T(2,128)S(1)}, f32[2,4096]{1,0:T(2,128)}, u32[]{:S(2)}) copy-start(f32[2,4096]{1,0:T(2,128)} %eig_ref.1) | copy-start | bytes 98308
  14.8 13.5 %collective-permute-start.4 = (bf16[16,8192]{1,0:T(8,128)(2,1)S(1)}, bf16[16,8192]{1,0:T(8,128)(2,1)S(1)}, u32[]{:S(2)}, u32[]{:S(2)}) collective-permute-start(bf16[16,8192]{1,0:T(8,128)(2,1)S(1)} %precond.2.refs_0_), channel_id=1, source_target_pairs={{0,4},{1,5},{2,6},{3,7},{4,0},{5,1},{6,2},{7,3},{8,12},{9,13},{10,... | collective-permute-start | bytes 786440 | tf_op jit(solution)/shard_map/ppermute | solution.py:51
  17.0 8.8 %collective-permute-start.1 = (bf16[16,8192]{1,0:T(8,128)(2,1)S(1)}, bf16[16,8192]{1,0:T(8,128)(2,1)S(1)}, u32[]{:S(2)}, u32[]{:S(2)}) collective-permute-start(bf16[16,8192]{1,0:T(8,128)(2,1)S(1)} %precond.3.refs_4_), channel_id=1, source_target_pairs={{0,2},{1,3},{2,0},{3,1},{4,6},{5,7},{6,4},{7,5},{8,10},{9,11},{10,... | collective-permute-start | bytes 786440 | tf_op jit(solution)/shard_map/ppermute | solution.py:51
  17.6 10.1 %collective-permute-start.7 = (bf16[16,8192]{1,0:T(8,128)(2,1)S(1)}, bf16[16,8192]{1,0:T(8,128)(2,1)S(1)}, u32[]{:S(2)}, u32[]{:S(2)}) collective-permute-start(bf16[16,8192]{1,0:T(8,128)(2,1)S(1)} %precond.3.refs_4_), channel_id=1, source_target_pairs={{0,16},{1,17},{2,18},{3,19},{4,20},{5,21},{6,22},{7,23},{8,24},{9,... | collective-permute-start | bytes 786440 | tf_op jit(solution)/shard_map/ppermute | solution.py:51
  21.5 7.7 %collective-permute-start.5 = (bf16[16,8192]{1,0:T(8,128)(2,1)S(1)}, bf16[16,8192]{1,0:T(8,128)(2,1)S(1)}, u32[]{:S(2)}, u32[]{:S(2)}) collective-permute-start(bf16[16,8192]{1,0:T(8,128)(2,1)S(1)} %collective-permute-done.3.refs_1_.refs_2_), channel_id=1, source_target_pairs={{0,4},{1,5},{2,6},{3,7},{4,0},{5,1},{6,2},{7,3},{8,12},{9,13},{10,... | collective-permute-start | bytes 786440 | tf_op jit(solution)/shard_map/ppermute | solution.py:51
  25.8 5.2 %collective-permute-start.8 = (bf16[16,4096]{1,0:T(8,128)(2,1)S(1)}, bf16[16,4096]{1,0:T(8,128)(2,1)S(1)}, u32[]{:S(2)}, u32[]{:S(2)}) collective-permute-start(bf16[16,4096]{1,0:T(8,128)(2,1)S(1)} %slice.6), channel_id=1, source_target_pairs={{0,16},{1,17},{2,18},{3,19},{4,20},{5,21},{6,22},{7,23},{8,24},{9,... | collective-permute-start | bytes 393224 | tf_op jit(solution)/shard_map/ppermute | solution.py:51
  27.6 6.2 %collective-permute-start.6 = (bf16[32,8192]{1,0:T(8,128)(2,1)S(1)}, bf16[32,8192]{1,0:T(8,128)(2,1)S(1)}, u32[]{:S(2)}, u32[]{:S(2)}) collective-permute-start(bf16[32,8192]{1,0:T(8,128)(2,1)S(1)} %pad_maximum_fusion.1), channel_id=1, source_target_pairs={{0,1},{1,0},{2,3},{3,2},{4,5},{5,4},{6,7},{7,6},{8,9},{9,8},{10,11... | collective-permute-start | bytes 1572872 | tf_op jit(solution)/shard_map/ppermute | solution.py:51
  27.7 6.0 %collective-permute-start.10 = (bf16[16,4096]{1,0:T(8,128)(2,1)S(1)}, bf16[16,4096]{1,0:T(8,128)(2,1)S(1)}, u32[]{:S(2)}, u32[]{:S(2)}) collective-permute-start(bf16[16,4096]{1,0:T(8,128)(2,1)S(1)} %slice.8), channel_id=1, source_target_pairs={{0,2},{1,3},{2,0},{3,1},{4,6},{5,7},{6,4},{7,5},{8,10},{9,11},{10,... | collective-permute-start | bytes 393224 | tf_op jit(solution)/shard_map/ppermute | solution.py:51
  31.0 4.3 %collective-permute-start.9 = (bf16[64,8192]{1,0:T(8,128)(2,1)S(1)}, bf16[64,8192]{1,0:T(8,128)(2,1)S(1)}, u32[]{:S(2)}, u32[]{:S(2)}) collective-permute-start(bf16[64,8192]{1,0:T(8,128)(2,1)S(1)} %pad_maximum_fusion), channel_id=1, source_target_pairs={{0,1},{1,0},{2,3},{3,2},{4,5},{5,4},{6,7},{7,6},{8,9},{9,8},{10,11... | collective-permute-start | bytes 3145736 | tf_op jit(solution)/shard_map/ppermute | solution.py:51
  33.7 1.6 %collective-permute-start.11 = (bf16[16,8192]{1,0:T(8,128)(2,1)S(1)}, bf16[16,8192]{1,0:T(8,128)(2,1)S(1)}, u32[]{:S(2)}, u32[]{:S(2)}) collective-permute-start(bf16[16,8192]{1,0:T(8,128)(2,1)S(1)} %constant_dynamic-update-slice_fusion.refs_10_), channel_id=1, source_target_pairs={{0,1},{1,0},{2,3},{3,2},{4,5},{5,4},{6,7},{7,6},{8,9},{9,8},{10,11... | collective-permute-start | bytes 786440 | tf_op jit(solution)/shard_map/ppermute | solution.py:51

commit v12 on v9

--- a/solution.py
+++ b/solution.py
@@ -88,21 +88,35 @@
     return g ^ 1, z, x, c
 
 
-def precond_kernel(q_ref, in_ref, out_ref, eig_ref, block_ref, lines_ref, *scratch):
+def spread_lines(q_ref, lines_ref):
     q_rows, lines, _ = q_ref.shape
     pitch = lines_ref.shape[0] // q_rows
     for q in range(q_rows):
         lines_ref[q * pitch : q * pitch + lines, :] = q_ref[q].astype(jnp.float32)
+
+
+def precond_kernel(q_ref, in_ref, out_ref, eig_ref, block_ref, *refs):
+    made, (lines_ref, wide_ref, tall_ref, even_ref) = refs[:-4], refs[-4:]
+    spread_lines(q_ref, lines_ref)
     for layer in range(in_ref.shape[0]):
-        precond_layer(layer, lines_ref, in_ref, out_ref, eig_ref, block_ref, *(ref.at[layer] for ref in scratch))
-
-
-def precond_layer(layer, lines_ref, in_ref, out_ref, eig_ref, block_ref, wide_ref, tall_ref, even_ref):
-    q_rows = block_ref.shape[0]
-    layers, width = eig_ref.shape
+        factors = prepare_layer(layer, in_ref, out_ref, eig_ref, even_ref.at[layer])
+        for ref, factor in zip(made, factors):
+            ref[layer] = factor
+        precond_layer(layer, factors, lines_ref, block_ref, wide_ref.at[layer], tall_ref.at[layer])
+
+
+def later_kernel(q_ref, *refs):
+    made, (block_ref, lines_ref, wide_ref, tall_ref) = refs[:-4], refs[-4:]
+    spread_lines(q_ref, lines_ref)
+    for layer in range(wide_ref.shape[0]):
+        factors = [ref[layer] for ref in made]
+        precond_layer(layer, factors, lines_ref, block_ref, wide_ref.at[layer], tall_ref.at[layer])
+
+
+def prepare_layer(layer, in_ref, out_ref, eig_ref, even_ref):
+    width = eig_ref.shape[1]
     rows = width // LANES
-    pitch = lines_ref.shape[0] // q_rows
-    p_in, p_out = in_ref.shape[1:]
+    p_out = out_ref.shape[2]
     left = lax.broadcasted_iota(jnp.int32, (1, LANES), 1) < p_out
 
     eig = eig_ref[layer : layer + 1, :]
@@ -141,6 +155,19 @@
         ],
         axis=0,
     )
+    return scale, fore, back, fore_right, back_right
+
+
+def precond_layer(layer, factors, lines_ref, block_ref, wide_ref, tall_ref):
+    scale, fore, back, fore_right, back_right = factors
+    q_rows = block_ref.shape[0]
+    width = wide_ref.shape[0] * LANES // q_rows
+    layers = block_ref.shape[1] // width
+    rows = width // LANES
+    pitch = lines_ref.shape[0] // q_rows
+    p_in = scale.shape[0]
+    p_out = width // p_in
+    left = lax.broadcasted_iota(jnp.int32, (1, LANES), 1) < p_out
 
     stacked = jnp.concatenate(
         [lines_ref[pl.ds(layers * j + layer, q_rows, stride=pitch), :] for j in range(rows)], axis=0
@@ -178,27 +205,47 @@
     return array.transpose(0, 2, 1, 3).reshape(rows, -1, LANES)
 
 
-def precondition(queries, basis_in, basis_out, eigvals, here=False):
+def block_scratch(q_rows, layers, width):
+    lines = layers * width // LANES
+    return [pltpu.VMEM((q_rows * (lines + 8), LANES), jnp.float32)] + [
+        pltpu.VMEM((layers, q_rows * width // LANES, LANES), jnp.float32)
+    ] * 2
+
+
+def precondition(queries, basis_in, basis_out, eigvals):
+    q_rows = queries.shape[0]
+    layers, width = eigvals.shape
+    p_in, rows = basis_in.shape[1], width // LANES
+    operands = [in_hbm(a) for a in (queries, basis_in, basis_out, eigvals)]
+    shapes = [(p_in, LANES), (3 * rows, 2 * p_in), (2 * rows, 3 * p_in), (LANES, 2 * LANES), (2 * LANES, 2 * LANES)]
+    types = [jnp.float32] + [jnp.bfloat16] * 4
+    block, *factors = pl.pallas_call(
+        functools.partial(fetched, len(operands), precond_kernel),
+        out_shape=[jax.ShapeDtypeStruct((q_rows, layers * width), jnp.bfloat16)]
+        + [jax.ShapeDtypeStruct((layers, *shape), dtype) for shape, dtype in zip(shapes, types)],
+        in_specs=[pl.BlockSpec(memory_space=pltpu.HBM)] * len(operands),
+        out_specs=[VMEM] * 6,
+        scratch_shapes=block_scratch(q_rows, layers, width)
+        + [pltpu.VMEM((layers, 2 * rows, LANES), jnp.float32)]
+        + [pltpu.VMEM(a.shape, a.dtype) for a in operands]
+        + [pltpu.SemaphoreType.DMA((len(operands),))],
+        compiler_params=pltpu.CompilerParams(vmem_limit_bytes=16 * MIB),
+        cost_estimate=pl.CostEstimate(flops=10**9, bytes_accessed=4 * MIB, transcendentals=0),
+        name="precond",
+    )(*operands)
+    return block, factors
+
+
+def precondition_more(queries, factors):
     q_rows, lines, _ = queries.shape
-    layers, width = eigvals.shape
-    operands, body, scratch = [queries, basis_in, basis_out, eigvals], precond_kernel, []
-    if not here:
-        operands = [in_hbm(a) for a in operands]
-        body = functools.partial(fetched, len(operands), body)
-        scratch = [pltpu.VMEM(a.shape, a.dtype) for a in operands] + [pltpu.SemaphoreType.DMA((len(operands),))]
-    space = pltpu.VMEM if here else pltpu.HBM
+    layers = factors[0].shape[0]
+    operands = [queries, *factors]
     return pl.pallas_call(
-        body,
-        out_shape=jax.ShapeDtypeStruct((q_rows, layers * width), jnp.bfloat16),
-        in_specs=[pl.BlockSpec(memory_space=space)] * len(operands),
+        later_kernel,
+        out_shape=jax.ShapeDtypeStruct((q_rows, lines * LANES), jnp.bfloat16),
+        in_specs=[VMEM] * len(operands),
         out_specs=VMEM,
-        scratch_shapes=[
-            pltpu.VMEM((q_rows * (lines + 8), LANES), jnp.float32),
-            pltpu.VMEM((layers, q_rows * width // LANES, LANES), jnp.float32),
-            pltpu.VMEM((layers, q_rows * width // LANES, LANES), jnp.float32),
-            pltpu.VMEM((layers, 2 * width // LANES, LANES), jnp.float32),
-        ]
-        + scratch,
+        scratch_shapes=block_scratch(q_rows, layers, lines * LANES // layers),
         compiler_params=pltpu.CompilerParams(vmem_limit_bytes=16 * MIB),
         cost_estimate=pl.CostEstimate(flops=10**9, bytes_accessed=4 * MIB, transcendentals=0),
         name="precond",
@@ -302,7 +349,8 @@
     queries = by_lines(query_grads)
     places = [np.tile(np.arange(n_train), (GROUPS, 1))]
     far = [Blocks(queries, places).hop(far_z(pair)) for pair in range(1, zs // 2)]
-    own = Blocks(precondition(queries, *rest), places)
+    block, factors = precondition(queries, *rest)
+    own = Blocks(block, places)
     q_rows, width = own.array.shape
     n_query = n_train * q_rows
     at_x = own.hop(over_x)
@@ -314,7 +362,7 @@
     parts = [own, twin, at_x, at_z]
     for pair, one in enumerate(far):
         slabs, one = after(slabs, one)
-        one = Blocks(precondition(one.array, *rest, here=True), one.came)
+        one = Blocks(precondition_more(one.array, factors), one.came)
         by_x, by_group = one.hop(over_x), one.hop(over_group)
         parts.append(one)
         if pair == 0:

time: 38.2 us -> 38 us (level)
  no operation moved by 1% of the time
where the time goes in v12:
time: 38 us; the launch traced here: 37.8 us
  starting transfers between devices  14 us (37%)
  Pallas kernels  13.8 us (36%)
  waiting for transfers between devices  9.83 us (26%)
    ppermute x13, starting transfers between devices, hop(): return Blocks(lax.ppermute(self.array, ('group', 'train'), perm), came)  14 us
    ppermute x13, waiting for transfers between devices, hop(): return Blocks(lax.ppermute(self.array, ('group', 'train'), perm), came)  9.83 us
    pallas_call x1, Pallas kernels, split_layers(): pl.pallas_call(functools.partial(split_kernel, layers), out_shape=jax.Sha...  5.06 us
    pallas_call x1, Pallas kernels, per_device(): pl.pallas_call(functools.partial(score_kernel, [came_masks(came) for a in...  3.76 us
    pallas_call x1, Pallas kernels, precondition(): pl.pallas_call(functools.partial(fetched, len(operands), precond_kernel),...  3.07 us
    pallas_call x1, Pallas kernels, precondition_more(): pl.pallas_call(later_kernel, out_shape=jax.ShapeDtypeStruct((q_rows, line...  1.89 us
  transfers between devices with their start and end apart: 13, of which 5 were waited for; matrix products, arithmetic and copies ran while one was open for 0% of the time, Pallas kernels for 27%

profile of v12, /device:TPU:0, one launch (start us, length us, event | category | flops | bytes accessed | tf_op | source)
XLA Modules:
  0.0 37.8 jit_solution(1043199373609346636)
XLA Ops:
  0.0 5.0 %collective-permute-start = (bf16[16,64,128]{2,1,0:T(8,128)(2,1)}, bf16[16,64,128]{2,1,0:T(8,128)(2,1)S(1)}, u32[]{:S(2)}, u32[]{:S(2)}) collective-permute-start(bf16[16,64,128]{2,1,0:T(8,128)(2,1)} %bitcast.11), channel_id=1, source_target_pairs={{0,12},{1,9},{2,14},{3,11},{4,8},{5,13},{6,10},{7,15},{8,4},{9,1},... | collective-permute-start | bytes 786440 | tf_op jit(solution)/shard_map/ppermute | solution.py:51
  5.0 3.1 %precond.2 = (bf16[16,8192]{1,0:T(8,128)(2,1)S(1)}, f32[2,64,128]{2,1,0:T(8,128)S(1)}, bf16[2,96,128]{2,1,0:T(8,128)(2,1)S(1)}, bf16[2,64,192]{2,1,0:T(8,128)(2,...) custom-call(bf16[16,64,128]{2,1,0:T(8,128)(2,1)} %bitcast.12, f32[2,64,64]{2,1,0:T(8,128)} %refs_1_.1, ...), custom_call_target="tpu_custom_call" | custom-call | flops 1000000000 | bytes 4194304 | tf_op jit(solution)/shard_map/precond/pallas_call | solution.py:222
  8.1 1.6 %collective-permute-start.2 = (bf16[16,8192]{1,0:T(8,128)(2,1)S(1)}, bf16[16,8192]{1,0:T(8,128)(2,1)S(1)}, u32[]{:S(2)}, u32[]{:S(2)}) collective-permute-start(bf16[16,8192]{1,0:T(8,128)(2,1)S(1)} %get-tuple-element.29.refs_0_), channel_id=1, source_target_pairs={{0,2},{1,3},{2,0},{3,1},{4,6},{5,7},{6,4},{7,5},{8,10},{9,11},{10,... | collective-permute-start | bytes 786440 | tf_op jit(solution)/shard_map/ppermute | solution.py:51
  9.7 0.0 collective-permute-start.1
  9.7 5.1 %split.1.slabs_ref = bf16[64,512,128]{2,1,0:T(8,128)(2,1)S(1)} custom-call(bf16[512,64,128]{2,1,0:T(8,128)(2,1)} %bitcast.10), custom_call_target="tpu_custom_call" | custom-call | flops 1000000000 | bytes 16777216 | tf_op jit(solution)/shard_map/split/pallas_call | solution.py:295
  14.8 0.1 collective-permute-start.3
  14.8 0.0 collective-permute-done.q_ref
  14.8 1.9 %precond.3.refs_4_ = bf16[16,8192]{1,0:T(8,128)(2,1)S(1)} custom-call(bf16[16,64,128]{2,1,0:T(8,128)(2,1)S(1)} %collective-permute-done.q_ref, f32[2,64,128]{2,1,0:T(8,128)S(1)} %get-tuple-element.31.refs_0_, bf16[2,96,128]{2,1,0:T(8,128)(2,1)S(1)} %get-tuple-element.32.refs_1_, bf16[2,64,192]{2,1,0:T(8,128)(2,1)S(1)} %get-tuple-element.33.refs_2_, ...), custom_call_target="tpu_custom_call" | custom-call | flops 1000000000 | bytes 4194304 | tf_op jit(solution)/shard_map/precond/pallas_call | solution.py:243
  16.7 0.6 %collective-permute-start.5 = (bf16[16,8192]{1,0:T(8,128)(2,1)S(1)}, bf16[16,8192]{1,0:T(8,128)(2,1)S(1)}, u32[]{:S(2)}, u32[]{:S(2)}) collective-permute-start(bf16[16,8192]{1,0:T(8,128)(2,1)S(1)} %precond.3.refs_4_), channel_id=1, source_target_pairs={{0,2},{1,3},{2,0},{3,1},{4,6},{5,7},{6,4},{7,5},{8,10},{9,11},{10,... | collective-permute-start | bytes 786440 | tf_op jit(solution)/shard_map/ppermute | solution.py:51
  17.3 4.0 %collective-permute-start.7 = (bf16[16,8192]{1,0:T(8,128)(2,1)S(1)}, bf16[16,8192]{1,0:T(8,128)(2,1)S(1)}, u32[]{:S(2)}, u32[]{:S(2)}) collective-permute-start(bf16[16,8192]{1,0:T(8,128)(2,1)S(1)} %precond.3.refs_4_), channel_id=1, source_target_pairs={{0,16},{1,17},{2,18},{3,19},{4,20},{5,21},{6,22},{7,23},{8,24},{9,... | collective-permute-start | bytes 786440 | tf_op jit(solution)/shard_map/ppermute | solution.py:51
  21.3 0.0 collective-permute-done.2.refs_2_
  21.3 0.0 collective-permute-start.4
  21.4 4.1 %collective-permute-done.5.refs_7_ = bf16[16,8192]{1,0:T(8,128)(2,1)S(1)} collective-permute-done((bf16[16,8192]{1,0:T(8,128)(2,1)S(1)}, bf16[16,8192]{1,0:T(8,128)(2,1)S(1)}, u32[]{:S(2)}, u32[]{:S(2)}) %collective-permute-start.5) | collective-permute-done | bytes 262176 | tf_op jit(solution)/shard_map/ppermute | solution.py:51
  25.5 1.9 %collective-permute-start.9 = (bf16[16,4096]{1,0:T(8,128)(2,1)S(1)}, bf16[16,4096]{1,0:T(8,128)(2,1)S(1)}, u32[]{:S(2)}, u32[]{:S(2)}) collective-permute-start(bf16[16,4096]{1,0:T(8,128)(2,1)S(1)} %slice.6), channel_id=1, source_target_pairs={{0,16},{1,17},{2,18},{3,19},{4,20},{5,21},{6,22},{7,23},{8,24},{9,... | collective-permute-start | bytes 393224 | tf_op jit(solution)/shard_map/ppermute | solution.py:51
  27.4 0.0 collective-permute-done.7.refs_8_
  27.4 0.6 %collective-permute-start.11 = (bf16[16,4096]{1,0:T(8,128)(2,1)S(1)}, bf16[16,4096]{1,0:T(8,128)(2,1)S(1)}, u32[]{:S(2)}, u32[]{:S(2)}) collective-permute-start(bf16[16,4096]{1,0:T(8,128)(2,1)S(1)} %slice.8), channel_id=1, source_target_pairs={{0,2},{1,3},{2,0},{3,1},{4,6},{5,7},{6,4},{7,5},{8,10},{9,11},{10,... | collective-permute-start | bytes 393224 | tf_op jit(solution)/shard_map/ppermute | solution.py:51
  28.1 0.0 collective-permute-done.3.refs_3_
  28.1 0.1 collective-permute-start.8
  28.1 1.0 %collective-permute-done.4.refs_5_ = bf16[16,8192]{1,0:T(8,128)(2,1)S(1)} collective-permute-done((bf16[16,8192]{1,0:T(8,128)(2,1)S(1)}, bf16[16,8192]{1,0:T(8,128)(2,1)S(1)}, u32[]{:S(2)}, u32[]{:S(2)}) %collective-permute-start.4) | collective-permute-done | bytes 262176 | tf_op jit(solution)/shard_map/ppermute | solution.py:51
  29.2 0.0 collective-permute-start.6
  29.2 1.6 %collective-permute-done.9 = bf16[16,4096]{1,0:T(8,128)(2,1)S(1)} collective-permute-done((bf16[16,4096]{1,0:T(8,128)(2,1)S(1)}, bf16[16,4096]{1,0:T(8,128)(2,1)S(1)}, u32[]{:S(2)}, u32[]{:S(2)}) %collective-permute-start.9) | collective-permute-done | bytes 131104 | tf_op jit(solution)/shard_map/ppermute | solution.py:51
  30.8 0.1 collective-permute-start.10
  30.9 1.6 %collective-permute-done.11 = bf16[16,4096]{1,0:T(8,128)(2,1)S(1)} collective-permute-done((bf16[16,4096]{1,0:T(8,128)(2,1)S(1)}, bf16[16,4096]{1,0:T(8,128)(2,1)S(1)}, u32[]{:S(2)}, u32[]{:S(2)}) %collective-permute-start.11) | collective-permute-done | bytes 131104 | tf_op jit(solution)/shard_map/ppermute | solution.py:51
  32.5 0.1 collective-permute-start.12
  32.5 0.0 collective-permute-done.1.refs_1_
  32.5 1.5 %collective-permute-done.12.refs_12_ = bf16[16,8192]{1,0:T(8,128)(2,1)S(1)} collective-permute-done((bf16[16,8192]{1,0:T(8,128)(2,1)S(1)}, bf16[16,8192]{1,0:T(8,128)(2,1)S(1)}, u32[]{:S(2)}, u32[]{:S(2)}) %collective-permute-start.12) | collective-permute-done | bytes 262176 | tf_op jit(solution)/shard_map/ppermute | solution.py:51
  34.1 0.0 collective-permute-done.8.refs_9_
  34.1 0.0 collective-permute-done.6.refs_6_
  34.1 0.0 collective-permute-done.10.refs_10_
  34.1 3.8 %scores.1 = f32[512,256]{1,0:T(8,128)} custom-call(bf16[64,512,128]{2,1,0:T(8,128)(2,1)S(1)} %split.1.slabs_ref, bf16[16,8192]{1,0:T(8,128)(2,1)S(1)} %get-tuple-element.29.refs_0_, bf16[16,8192]{1,0:T(8,128)(2,1)S(1)} %collective-permute-done.1.refs_1_, bf16[16,8192]{1,0:T(8,128)(2,1)S(1)} %collective-permute-done.2.refs_2_, ...), custom_call_target="tpu_custom_call" | custom-call | flops 2147483648 | bytes 12582912 | tf_op jit(solution)/shard_map/scores/pallas_call | solution.py:386
  (7 shorter events, 0.1 us)
Async XLA Ops:
  0.0 14.8 %collective-permute-start = (bf16[16,64,128]{2,1,0:T(8,128)(2,1)}, bf16[16,64,128]{2,1,0:T(8,128)(2,1)S(1)}, u32[]{:S(2)}, u32[]{:S(2)}) collective-permute-start(bf16[16,64,128]{2,1,0:T(8,128)(2,1)} %bitcast.11), channel_id=1, source_target_pairs={{0,12},{1,9},{2,14},{3,11},{4,8},{5,13},{6,10},{7,15},{8,4},{9,1},... | collective-permute-start | bytes 786440 | tf_op jit(solution)/shard_map/ppermute | solution.py:51
  8.1 13.2 %collective-permute-start.2 = (bf16[16,8192]{1,0:T(8,128)(2,1)S(1)}, bf16[16,8192]{1,0:T(8,128)(2,1)S(1)}, u32[]{:S(2)}, u32[]{:S(2)}) collective-permute-start(bf16[16,8192]{1,0:T(8,128)(2,1)S(1)} %get-tuple-element.29.refs_0_), channel_id=1, source_target_pairs={{0,2},{1,3},{2,0},{3,1},{4,6},{5,7},{6,4},{7,5},{8,10},{9,11},{10,... | collective-permute-start | bytes 786440 | tf_op jit(solution)/shard_map/ppermute | solution.py:51
  9.7 22.8 %collective-permute-start.1 = (bf16[16,8192]{1,0:T(8,128)(2,1)S(1)}, bf16[16,8192]{1,0:T(8,128)(2,1)S(1)}, u32[]{:S(2)}, u32[]{:S(2)}) collective-permute-start(bf16[16,8192]{1,0:T(8,128)(2,1)S(1)} %get-tuple-element.29.refs_0_), channel_id=1, source_target_pairs={{0,1},{1,0},{2,3},{3,2},{4,5},{5,4},{6,7},{7,6},{8,9},{9,8},{10,11... | collective-permute-start | bytes 786440 | tf_op jit(solution)/shard_map/ppermute | solution.py:51
  14.8 13.3 %collective-permute-start.3 = (bf16[16,8192]{1,0:T(8,128)(2,1)S(1)}, bf16[16,8192]{1,0:T(8,128)(2,1)S(1)}, u32[]{:S(2)}, u32[]{:S(2)}) collective-permute-start(bf16[16,8192]{1,0:T(8,128)(2,1)S(1)} %get-tuple-element.29.refs_0_), channel_id=1, source_target_pairs={{0,4},{1,5},{2,6},{3,7},{4,0},{5,1},{6,2},{7,3},{8,12},{9,13},{10,... | collective-permute-start | bytes 786440 | tf_op jit(solution)/shard_map/ppermute | solution.py:51
  16.7 8.8 %collective-permute-start.5 = (bf16[16,8192]{1,0:T(8,128)(2,1)S(1)}, bf16[16,8192]{1,0:T(8,128)(2,1)S(1)}, u32[]{:S(2)}, u32[]{:S(2)}) collective-permute-start(bf16[16,8192]{1,0:T(8,128)(2,1)S(1)} %precond.3.refs_4_), channel_id=1, source_target_pairs={{0,2},{1,3},{2,0},{3,1},{4,6},{5,7},{6,4},{7,5},{8,10},{9,11},{10,... | collective-permute-start | bytes 786440 | tf_op jit(solution)/shard_map/ppermute | solution.py:51
  17.3 10.0 %collective-permute-start.7 = (bf16[16,8192]{1,0:T(8,128)(2,1)S(1)}, bf16[16,8192]{1,0:T(8,128)(2,1)S(1)}, u32[]{:S(2)}, u32[]{:S(2)}) collective-permute-start(bf16[16,8192]{1,0:T(8,128)(2,1)S(1)} %precond.3.refs_4_), channel_id=1, source_target_pairs={{0,16},{1,17},{2,18},{3,19},{4,20},{5,21},{6,22},{7,23},{8,24},{9,... | collective-permute-start | bytes 786440 | tf_op jit(solution)/shard_map/ppermute | solution.py:51
  21.3 7.8 %collective-permute-start.4 = (bf16[16,8192]{1,0:T(8,128)(2,1)S(1)}, bf16[16,8192]{1,0:T(8,128)(2,1)S(1)}, u32[]{:S(2)}, u32[]{:S(2)}) collective-permute-start(bf16[16,8192]{1,0:T(8,128)(2,1)S(1)} %collective-permute-done.2.refs_2_), channel_id=1, source_target_pairs={{0,4},{1,5},{2,6},{3,7},{4,0},{5,1},{6,2},{7,3},{8,12},{9,13},{10,... | collective-permute-start | bytes 786440 | tf_op jit(solution)/shard_map/ppermute | solution.py:51
  25.5 5.2 %collective-permute-start.9 = (bf16[16,4096]{1,0:T(8,128)(2,1)S(1)}, bf16[16,4096]{1,0:T(8,128)(2,1)S(1)}, u32[]{:S(2)}, u32[]{:S(2)}) collective-permute-start(bf16[16,4096]{1,0:T(8,128)(2,1)S(1)} %slice.6), channel_id=1, source_target_pairs={{0,16},{1,17},{2,18},{3,19},{4,20},{5,21},{6,22},{7,23},{8,24},{9,... | collective-permute-start | bytes 393224 | tf_op jit(solution)/shard_map/ppermute | solution.py:51
  27.4 5.0 %collective-permute-start.11 = (bf16[16,4096]{1,0:T(8,128)(2,1)S(1)}, bf16[16,4096]{1,0:T(8,128)(2,1)S(1)}, u32[]{:S(2)}, u32[]{:S(2)}) collective-permute-start(bf16[16,4096]{1,0:T(8,128)(2,1)S(1)} %slice.8), channel_id=1, source_target_pairs={{0,2},{1,3},{2,0},{3,1},{4,6},{5,7},{6,4},{7,5},{8,10},{9,11},{10,... | collective-permute-start | bytes 393224 | tf_op jit(solution)/shard_map/ppermute | solution.py:51
  28.1 6.0 %collective-permute-start.8 = (bf16[32,8192]{1,0:T(8,128)(2,1)S(1)}, bf16[32,8192]{1,0:T(8,128)(2,1)S(1)}, u32[]{:S(2)}, u32[]{:S(2)}) collective-permute-start(bf16[32,8192]{1,0:T(8,128)(2,1)S(1)} %pad_maximum_fusion.1), channel_id=1, source_target_pairs={{0,1},{1,0},{2,3},{3,2},{4,5},{5,4},{6,7},{7,6},{8,9},{9,8},{10,11... | collective-permute-start | bytes 1572872 | tf_op jit(solution)/shard_map/ppermute | solution.py:51
  29.2 4.9 %collective-permute-start.6 = (bf16[32,8192]{1,0:T(8,128)(2,1)S(1)}, bf16[32,8192]{1,0:T(8,128)(2,1)S(1)}, u32[]{:S(2)}, u32[]{:S(2)}) collective-permute-start(bf16[32,8192]{1,0:T(8,128)(2,1)S(1)} %pad_maximum_fusion), channel_id=1, source_target_pairs={{0,1},{1,0},{2,3},{3,2},{4,5},{5,4},{6,7},{7,6},{8,9},{9,8},{10,11... | collective-permute-start | bytes 1572872 | tf_op jit(solution)/shard_map/ppermute | solution.py:51
  30.8 3.3 %collective-permute-start.10 = (bf16[32,8192]{1,0:T(8,128)(2,1)S(1)}, bf16[32,8192]{1,0:T(8,128)(2,1)S(1)}, u32[]{:S(2)}, u32[]{:S(2)}) collective-permute-start(bf16[32,8192]{1,0:T(8,128)(2,1)S(1)} %pad_maximum_fusion.2), channel_id=1, source_target_pairs={{0,1},{1,0},{2,3},{3,2},{4,5},{5,4},{6,7},{7,6},{8,9},{9,8},{10,11... | collective-permute-start | bytes 1572872 | tf_op jit(solution)/shard_map/ppermute | solution.py:51
  32.5 1.6 %collective-permute-start.12 = (bf16[16,8192]{1,0:T(8,128)(2,1)S(1)}, bf16[16,8192]{1,0:T(8,128)(2,1)S(1)}, u32[]{:S(2)}, u32[]{:S(2)}) collective-permute-start(bf16[16,8192]{1,0:T(8,128)(2,1)S(1)} %constant_dynamic-update-slice_fusion.refs_11_), channel_id=1, source_target_pairs={{0,1},{1,0},{2,3},{3,2},{4,5},{5,4},{6,7},{7,6},{8,9},{9,8},{10,11... | collective-permute-start | bytes 786440 | tf_op jit(solution)/shard_map/ppermute | solution.py:51

commit v13 on v12

--- a/solution.py
+++ b/solution.py
@@ -353,6 +353,7 @@
     own = Blocks(block, places)
     q_rows, width = own.array.shape
     n_query = n_train * q_rows
+    cut = 3 * width // 4
     at_x = own.hop(over_x)
     twin = own.hop(over_core)
     train_grads, own = after(train_grads, own)
@@ -374,11 +375,11 @@
         else:
             parts.append(one.hop(over_core))
         parts += [by_x, by_group, stack(by_x, by_group).hop(over_core)]
-        half = by_x.columns(0, width // 2).hop(over_group)
+        half = by_x.columns(0, cut).hop(over_group)
         if pair == 0:
             half.array, near, near_x = after(half.array, at_z, at_xz)
             parts.append(stack(near, near_x).hop(over_core))
-        corner = beside(half, by_group.columns(width // 2, width).hop(over_x))
+        corner = beside(half, by_group.columns(cut, width).hop(over_x))
         parts += [corner, corner.hop(over_core)]
 
     tr_rows = train_grads.shape[0]

time: 38 us -> 38.4 us (1.011)
  starting transfers between devices: 14 us -> 14.4 us
    ppermute x13, starting transfers between devices: 14 us -> 14.4 us  [hop(): return Blocks(lax.ppermute(self.array, ('group', 'train'), perm), came)]
  transfers between devices with their start and end apart: 13 -> 13, of which waited for: 5 -> 4; matrix products, arithmetic and copies ran while one was open for 0% -> 0% of each run, Pallas kernels for 27% -> 26%
where the time goes in v13:
time: 38.4 us; the launch traced here: 38.3 us
  starting transfers between devices  14.4 us (38%)
  Pallas kernels  13.8 us (36%)
  waiting for transfers between devices  9.81 us (26%)
    ppermute x13, starting transfers between devices, hop(): return Blocks(lax.ppermute(self.array, ('group', 'train'), perm), came)  14.4 us
    ppermute x13, waiting for transfers between devices, hop(): return Blocks(lax.ppermute(self.array, ('group', 'train'), perm), came)  9.81 us
    pallas_call x1, Pallas kernels, split_layers(): pl.pallas_call(functools.partial(split_kernel, layers), out_shape=jax.Sha...  5.06 us
    pallas_call x1, Pallas kernels, per_device(): pl.pallas_call(functools.partial(score_kernel, [came_masks(came) for a in...  3.76 us
    pallas_call x1, Pallas kernels, precondition(): pl.pallas_call(functools.partial(fetched, len(operands), precond_kernel),...  3.07 us
    pallas_call x1, Pallas kernels, precondition_more(): pl.pallas_call(later_kernel, out_shape=jax.ShapeDtypeStruct((q_rows, line...  1.89 us
  transfers between devices with their start and end apart: 13, of which 4 were waited for; matrix products, arithmetic and copies ran while one was open for 0% of the time, Pallas kernels for 26%

profile of v13, /device:TPU:0, one launch (start us, length us, event | category | flops | bytes accessed | tf_op | source)
XLA Modules:
  0.0 38.3 jit_solution(1055782837101934671)
XLA Ops:
  0.0 5.0 %collective-permute-start = (bf16[16,64,128]{2,1,0:T(8,128)(2,1)}, bf16[16,64,128]{2,1,0:T(8,128)(2,1)S(1)}, u32[]{:S(2)}, u32[]{:S(2)}) collective-permute-start(bf16[16,64,128]{2,1,0:T(8,128)(2,1)} %bitcast.11), channel_id=1, source_target_pairs={{0,12},{1,9},{2,14},{3,11},{4,8},{5,13},{6,10},{7,15},{8,4},{9,1},... | collective-permute-start | bytes 786440 | tf_op jit(solution)/shard_map/ppermute | solution.py:51
  5.0 3.1 %precond.2 = (bf16[16,8192]{1,0:T(8,128)(2,1)S(1)}, f32[2,64,128]{2,1,0:T(8,128)S(1)}, bf16[2,96,128]{2,1,0:T(8,128)(2,1)S(1)}, bf16[2,64,192]{2,1,0:T(8,128)(2,...) custom-call(bf16[16,64,128]{2,1,0:T(8,128)(2,1)} %bitcast.12, f32[2,64,64]{2,1,0:T(8,128)} %refs_1_.1, ...), custom_call_target="tpu_custom_call" | custom-call | flops 1000000000 | bytes 4194304 | tf_op jit(solution)/shard_map/precond/pallas_call | solution.py:222
  8.1 1.6 %collective-permute-start.2 = (bf16[16,8192]{1,0:T(8,128)(2,1)S(1)}, bf16[16,8192]{1,0:T(8,128)(2,1)S(1)}, u32[]{:S(2)}, u32[]{:S(2)}) collective-permute-start(bf16[16,8192]{1,0:T(8,128)(2,1)S(1)} %get-tuple-element.29.refs_0_), channel_id=1, source_target_pairs={{0,2},{1,3},{2,0},{3,1},{4,6},{5,7},{6,4},{7,5},{8,10},{9,11},{10,... | collective-permute-start | bytes 786440 | tf_op jit(solution)/shard_map/ppermute | solution.py:51
  9.7 0.0 collective-permute-start.1
  9.7 5.1 %split.1.slabs_ref = bf16[64,512,128]{2,1,0:T(8,128)(2,1)S(1)} custom-call(bf16[512,64,128]{2,1,0:T(8,128)(2,1)} %bitcast.10), custom_call_target="tpu_custom_call" | custom-call | flops 1000000000 | bytes 16777216 | tf_op jit(solution)/shard_map/split/pallas_call | solution.py:295
  14.8 0.1 collective-permute-start.3
  14.8 0.0 collective-permute-done.q_ref
  14.8 1.9 %precond.3.refs_4_ = bf16[16,8192]{1,0:T(8,128)(2,1)S(1)} custom-call(bf16[16,64,128]{2,1,0:T(8,128)(2,1)S(1)} %collective-permute-done.q_ref, f32[2,64,128]{2,1,0:T(8,128)S(1)} %get-tuple-element.31.refs_0_, bf16[2,96,128]{2,1,0:T(8,128)(2,1)S(1)} %get-tuple-element.32.refs_1_, bf16[2,64,192]{2,1,0:T(8,128)(2,1)S(1)} %get-tuple-element.33.refs_2_, ...), custom_call_target="tpu_custom_call" | custom-call | flops 1000000000 | bytes 4194304 | tf_op jit(solution)/shard_map/precond/pallas_call | solution.py:243
  16.7 0.6 %collective-permute-start.5 = (bf16[16,8192]{1,0:T(8,128)(2,1)S(1)}, bf16[16,8192]{1,0:T(8,128)(2,1)S(1)}, u32[]{:S(2)}, u32[]{:S(2)}) collective-permute-start(bf16[16,8192]{1,0:T(8,128)(2,1)S(1)} %precond.3.refs_4_), channel_id=1, source_target_pairs={{0,2},{1,3},{2,0},{3,1},{4,6},{5,7},{6,4},{7,5},{8,10},{9,11},{10,... | collective-permute-start | bytes 786440 | tf_op jit(solution)/shard_map/ppermute | solution.py:51
  17.3 4.0 %collective-permute-start.7 = (bf16[16,8192]{1,0:T(8,128)(2,1)S(1)}, bf16[16,8192]{1,0:T(8,128)(2,1)S(1)}, u32[]{:S(2)}, u32[]{:S(2)}) collective-permute-start(bf16[16,8192]{1,0:T(8,128)(2,1)S(1)} %precond.3.refs_4_), channel_id=1, source_target_pairs={{0,16},{1,17},{2,18},{3,19},{4,20},{5,21},{6,22},{7,23},{8,24},{9,... | collective-permute-start | bytes 786440 | tf_op jit(solution)/shard_map/ppermute | solution.py:51
  21.3 0.0 collective-permute-done.2.refs_2_
  21.3 0.0 collective-permute-start.4
  21.4 4.1 %collective-permute-done.5.refs_7_ = bf16[16,8192]{1,0:T(8,128)(2,1)S(1)} collective-permute-done((bf16[16,8192]{1,0:T(8,128)(2,1)S(1)}, bf16[16,8192]{1,0:T(8,128)(2,1)S(1)}, u32[]{:S(2)}, u32[]{:S(2)}) %collective-permute-start.5) | collective-permute-done | bytes 262176 | tf_op jit(solution)/shard_map/ppermute | solution.py:51
  25.5 1.9 %collective-permute-start.9 = (bf16[16,6144]{1,0:T(8,128)(2,1)S(1)}, bf16[16,6144]{1,0:T(8,128)(2,1)S(1)}, u32[]{:S(2)}, u32[]{:S(2)}) collective-permute-start(bf16[16,6144]{1,0:T(8,128)(2,1)S(1)} %slice.6), channel_id=1, source_target_pairs={{0,16},{1,17},{2,18},{3,19},{4,20},{5,21},{6,22},{7,23},{8,24},{9,... | collective-permute-start | bytes 589832 | tf_op jit(solution)/shard_map/ppermute | solution.py:51
  27.4 0.0 collective-permute-done.7.refs_8_
  27.4 0.6 %collective-permute-start.11 = (bf16[16,2048]{1,0:T(8,128)(2,1)S(1)}, bf16[16,2048]{1,0:T(8,128)(2,1)S(1)}, u32[]{:S(2)}, u32[]{:S(2)}) collective-permute-start(bf16[16,2048]{1,0:T(8,128)(2,1)S(1)} %slice.8), channel_id=1, source_target_pairs={{0,2},{1,3},{2,0},{3,1},{4,6},{5,7},{6,4},{7,5},{8,10},{9,11},{10,... | collective-permute-start | bytes 196616 | tf_op jit(solution)/shard_map/ppermute | solution.py:51
  28.1 0.0 collective-permute-done.3.refs_3_
  28.1 0.1 collective-permute-start.8
  28.1 1.0 %collective-permute-done.4.refs_5_ = bf16[16,8192]{1,0:T(8,128)(2,1)S(1)} collective-permute-done((bf16[16,8192]{1,0:T(8,128)(2,1)S(1)}, bf16[16,8192]{1,0:T(8,128)(2,1)S(1)}, u32[]{:S(2)}, u32[]{:S(2)}) %collective-permute-start.4) | collective-permute-done | bytes 262176 | tf_op jit(solution)/shard_map/ppermute | solution.py:51
  29.2 0.0 collective-permute-start.6
  29.2 3.0 %collective-permute-done.9 = bf16[16,6144]{1,0:T(8,128)(2,1)S(1)} collective-permute-done((bf16[16,6144]{1,0:T(8,128)(2,1)S(1)}, bf16[16,6144]{1,0:T(8,128)(2,1)S(1)}, u32[]{:S(2)}, u32[]{:S(2)}) %collective-permute-start.9) | collective-permute-done | bytes 196640 | tf_op jit(solution)/shard_map/ppermute | solution.py:51
  32.2 0.1 collective-permute-start.10
  32.3 0.0 collective-permute-done.11
  32.3 0.6 %collective-permute-start.12 = (bf16[16,8192]{1,0:T(8,128)(2,1)S(1)}, bf16[16,8192]{1,0:T(8,128)(2,1)S(1)}, u32[]{:S(2)}, u32[]{:S(2)}) collective-permute-start(bf16[16,8192]{1,0:T(8,128)(2,1)S(1)} %constant_dynamic-update-slice_fusion.refs_11_), channel_id=1, source_target_pairs={{0,1},{1,0},{2,3},{3,2},{4,5},{5,4},{6,7},{7,6},{8,9},{9,8},{10,11... | collective-permute-start | bytes 786440 | tf_op jit(solution)/shard_map/ppermute | solution.py:51
  32.9 0.0 collective-permute-done.1.refs_1_
  32.9 1.7 %collective-permute-done.12.refs_12_ = bf16[16,8192]{1,0:T(8,128)(2,1)S(1)} collective-permute-done((bf16[16,8192]{1,0:T(8,128)(2,1)S(1)}, bf16[16,8192]{1,0:T(8,128)(2,1)S(1)}, u32[]{:S(2)}, u32[]{:S(2)}) %collective-permute-start.12) | collective-permute-done | bytes 262176 | tf_op jit(solution)/shard_map/ppermute | solution.py:51
  34.5 0.0 collective-permute-done.8.refs_9_
  34.5 0.0 collective-permute-done.6.refs_6_
  34.5 0.0 collective-permute-done.10.refs_10_
  34.5 3.8 %scores.1 = f32[512,256]{1,0:T(8,128)} custom-call(bf16[64,512,128]{2,1,0:T(8,128)(2,1)S(1)} %split.1.slabs_ref, bf16[16,8192]{1,0:T(8,128)(2,1)S(1)} %get-tuple-element.29.refs_0_, bf16[16,8192]{1,0:T(8,128)(2,1)S(1)} %collective-permute-done.1.refs_1_, bf16[16,8192]{1,0:T(8,128)(2,1)S(1)} %collective-permute-done.2.refs_2_, ...), custom_call_target="tpu_custom_call" | custom-call | flops 2147483648 | bytes 12582912 | tf_op jit(solution)/shard_map/scores/pallas_call | solution.py:387
  (7 shorter events, 0.1 us)
Async XLA Ops:
  0.0 14.8 %collective-permute-start = (bf16[16,64,128]{2,1,0:T(8,128)(2,1)}, bf16[16,64,128]{2,1,0:T(8,128)(2,1)S(1)}, u32[]{:S(2)}, u32[]{:S(2)}) collective-permute-start(bf16[16,64,128]{2,1,0:T(8,128)(2,1)} %bitcast.11), channel_id=1, source_target_pairs={{0,12},{1,9},{2,14},{3,11},{4,8},{5,13},{6,10},{7,15},{8,4},{9,1},... | collective-permute-start | bytes 786440 | tf_op jit(solution)/shard_map/ppermute | solution.py:51
  8.1 13.2 %collective-permute-start.2 = (bf16[16,8192]{1,0:T(8,128)(2,1)S(1)}, bf16[16,8192]{1,0:T(8,128)(2,1)S(1)}, u32[]{:S(2)}, u32[]{:S(2)}) collective-permute-start(bf16[16,8192]{1,0:T(8,128)(2,1)S(1)} %get-tuple-element.29.refs_0_), channel_id=1, source_target_pairs={{0,2},{1,3},{2,0},{3,1},{4,6},{5,7},{6,4},{7,5},{8,10},{9,11},{10,... | collective-permute-start | bytes 786440 | tf_op jit(solution)/shard_map/ppermute | solution.py:51
  9.7 23.2 %collective-permute-start.1 = (bf16[16,8192]{1,0:T(8,128)(2,1)S(1)}, bf16[16,8192]{1,0:T(8,128)(2,1)S(1)}, u32[]{:S(2)}, u32[]{:S(2)}) collective-permute-start(bf16[16,8192]{1,0:T(8,128)(2,1)S(1)} %get-tuple-element.29.refs_0_), channel_id=1, source_target_pairs={{0,1},{1,0},{2,3},{3,2},{4,5},{5,4},{6,7},{7,6},{8,9},{9,8},{10,11... | collective-permute-start | bytes 786440 | tf_op jit(solution)/shard_map/ppermute | solution.py:51
  14.8 13.3 %collective-permute-start.3 = (bf16[16,8192]{1,0:T(8,128)(2,1)S(1)}, bf16[16,8192]{1,0:T(8,128)(2,1)S(1)}, u32[]{:S(2)}, u32[]{:S(2)}) collective-permute-start(bf16[16,8192]{1,0:T(8,128)(2,1)S(1)} %get-tuple-element.29.refs_0_), channel_id=1, source_target_pairs={{0,4},{1,5},{2,6},{3,7},{4,0},{5,1},{6,2},{7,3},{8,12},{9,13},{10,... | collective-permute-start | bytes 786440 | tf_op jit(solution)/shard_map/ppermute | solution.py:51
  16.7 8.8 %collective-permute-start.5 = (bf16[16,8192]{1,0:T(8,128)(2,1)S(1)}, bf16[16,8192]{1,0:T(8,128)(2,1)S(1)}, u32[]{:S(2)}, u32[]{:S(2)}) collective-permute-start(bf16[16,8192]{1,0:T(8,128)(2,1)S(1)} %precond.3.refs_4_), channel_id=1, source_target_pairs={{0,2},{1,3},{2,0},{3,1},{4,6},{5,7},{6,4},{7,5},{8,10},{9,11},{10,... | collective-permute-start | bytes 786440 | tf_op jit(solution)/shard_map/ppermute | solution.py:51
  17.3 10.1 %collective-permute-start.7 = (bf16[16,8192]{1,0:T(8,128)(2,1)S(1)}, bf16[16,8192]{1,0:T(8,128)(2,1)S(1)}, u32[]{:S(2)}, u32[]{:S(2)}) collective-permute-start(bf16[16,8192]{1,0:T(8,128)(2,1)S(1)} %precond.3.refs_4_), channel_id=1, source_target_pairs={{0,16},{1,17},{2,18},{3,19},{4,20},{5,21},{6,22},{7,23},{8,24},{9,... | collective-permute-start | bytes 786440 | tf_op jit(solution)/shard_map/ppermute | solution.py:51
  21.3 7.8 %collective-permute-start.4 = (bf16[16,8192]{1,0:T(8,128)(2,1)S(1)}, bf16[16,8192]{1,0:T(8,128)(2,1)S(1)}, u32[]{:S(2)}, u32[]{:S(2)}) collective-permute-start(bf16[16,8192]{1,0:T(8,128)(2,1)S(1)} %collective-permute-done.2.refs_2_), channel_id=1, source_target_pairs={{0,4},{1,5},{2,6},{3,7},{4,0},{5,1},{6,2},{7,3},{8,12},{9,13},{10,... | collective-permute-start | bytes 786440 | tf_op jit(solution)/shard_map/ppermute | solution.py:51
  25.5 6.6 %collective-permute-start.9 = (bf16[16,6144]{1,0:T(8,128)(2,1)S(1)}, bf16[16,6144]{1,0:T(8,128)(2,1)S(1)}, u32[]{:S(2)}, u32[]{:S(2)}) collective-permute-start(bf16[16,6144]{1,0:T(8,128)(2,1)S(1)} %slice.6), channel_id=1, source_target_pairs={{0,16},{1,17},{2,18},{3,19},{4,20},{5,21},{6,22},{7,23},{8,24},{9,... | collective-permute-start | bytes 589832 | tf_op jit(solution)/shard_map/ppermute | solution.py:51
  27.4 4.9 %collective-permute-start.11 = (bf16[16,2048]{1,0:T(8,128)(2,1)S(1)}, bf16[16,2048]{1,0:T(8,128)(2,1)S(1)}, u32[]{:S(2)}, u32[]{:S(2)}) collective-permute-start(bf16[16,2048]{1,0:T(8,128)(2,1)S(1)} %slice.8), channel_id=1, source_target_pairs={{0,2},{1,3},{2,0},{3,1},{4,6},{5,7},{6,4},{7,5},{8,10},{9,11},{10,... | collective-permute-start | bytes 196616 | tf_op jit(solution)/shard_map/ppermute | solution.py:51
  28.1 6.5 %collective-permute-start.8 = (bf16[32,8192]{1,0:T(8,128)(2,1)S(1)}, bf16[32,8192]{1,0:T(8,128)(2,1)S(1)}, u32[]{:S(2)}, u32[]{:S(2)}) collective-permute-start(bf16[32,8192]{1,0:T(8,128)(2,1)S(1)} %pad_maximum_fusion.1), channel_id=1, source_target_pairs={{0,1},{1,0},{2,3},{3,2},{4,5},{5,4},{6,7},{7,6},{8,9},{9,8},{10,11... | collective-permute-start | bytes 1572872 | tf_op jit(solution)/shard_map/ppermute | solution.py:51
  29.2 5.4 %collective-permute-start.6 = (bf16[32,8192]{1,0:T(8,128)(2,1)S(1)}, bf16[32,8192]{1,0:T(8,128)(2,1)S(1)}, u32[]{:S(2)}, u32[]{:S(2)}) collective-permute-start(bf16[32,8192]{1,0:T(8,128)(2,1)S(1)} %pad_maximum_fusion), channel_id=1, source_target_pairs={{0,1},{1,0},{2,3},{3,2},{4,5},{5,4},{6,7},{7,6},{8,9},{9,8},{10,11... | collective-permute-start | bytes 1572872 | tf_op jit(solution)/shard_map/ppermute | solution.py:51
  32.2 2.4 %collective-permute-start.10 = (bf16[32,8192]{1,0:T(8,128)(2,1)S(1)}, bf16[32,8192]{1,0:T(8,128)(2,1)S(1)}, u32[]{:S(2)}, u32[]{:S(2)}) collective-permute-start(bf16[32,8192]{1,0:T(8,128)(2,1)S(1)} %pad_maximum_fusion.2), channel_id=1, source_target_pairs={{0,1},{1,0},{2,3},{3,2},{4,5},{5,4},{6,7},{7,6},{8,9},{9,8},{10,11... | collective-permute-start | bytes 1572872 | tf_op jit(solution)/shard_map/ppermute | solution.py:51
  32.3 2.2 %collective-permute-start.12 = (bf16[16,8192]{1,0:T(8,128)(2,1)S(1)}, bf16[16,8192]{1,0:T(8,128)(2,1)S(1)}, u32[]{:S(2)}, u32[]{:S(2)}) collective-permute-start(bf16[16,8192]{1,0:T(8,128)(2,1)S(1)} %constant_dynamic-update-slice_fusion.refs_11_), channel_id=1, source_target_pairs={{0,1},{1,0},{2,3},{3,2},{4,5},{5,4},{6,7},{7,6},{8,9},{9,8},{10,11... | collective-permute-start | bytes 786440 | tf_op jit(solution)/shard_map/ppermute | solution.py:51

commit v14 on v13

--- a/solution.py
+++ b/solution.py
@@ -353,7 +353,7 @@
     own = Blocks(block, places)
     q_rows, width = own.array.shape
     n_query = n_train * q_rows
-    cut = 3 * width // 4
+    cut = 5 * width // 8
     at_x = own.hop(over_x)
     twin = own.hop(over_core)
     train_grads, own = after(train_grads, own)

time: 38.4 us -> 37.8 us (0.984)
  starting transfers between devices: 14.4 us -> 14 us
    ppermute x13, starting transfers between devices: 14.4 us -> 14 us  [hop(): return Blocks(lax.ppermute(self.array, ('group', 'train'), perm), came)]
  transfers between devices with their start and end apart: 13 -> 13, of which waited for: 4 -> 5; matrix products, arithmetic and copies ran while one was open for 0% -> 0% of each run, Pallas kernels for 26% -> 27%
where the time goes in v14:
time: 37.8 us; the launch traced here: 37.6 us
  starting transfers between devices  14 us (37%)
  Pallas kernels  13.8 us (37%)
  waiting for transfers between devices  9.61 us (25%)
    ppermute x13, starting transfers between devices, hop(): return Blocks(lax.ppermute(self.array, ('group', 'train'), perm), came)  14 us
    ppermute x13, waiting for transfers between devices, hop(): return Blocks(lax.ppermute(self.array, ('group', 'train'), perm), came)  9.61 us
    pallas_call x1, Pallas kernels, split_layers(): pl.pallas_call(functools.partial(split_kernel, layers), out_shape=jax.Sha...  5.06 us
    pallas_call x1, Pallas kernels, per_device(): pl.pallas_call(functools.partial(score_kernel, [came_masks(came) for a in...  3.77 us
    pallas_call x1, Pallas kernels, precondition(): pl.pallas_call(functools.partial(fetched, len(operands), precond_kernel),...  3.07 us
    pallas_call x1, Pallas kernels, precondition_more(): pl.pallas_call(later_kernel, out_shape=jax.ShapeDtypeStruct((q_rows, line...  1.89 us
  transfers between devices with their start and end apart: 13, of which 5 were waited for; matrix products, arithmetic and copies ran while one was open for 0% of the time, Pallas kernels for 27%

profile of v14, /device:TPU:0, one launch (start us, length us, event | category | flops | bytes accessed | tf_op | source)
XLA Modules:
  0.0 37.6 jit_solution(2079988440212396470)
XLA Ops:
  0.0 5.0 %collective-permute-start = (bf16[16,64,128]{2,1,0:T(8,128)(2,1)}, bf16[16,64,128]{2,1,0:T(8,128)(2,1)S(1)}, u32[]{:S(2)}, u32[]{:S(2)}) collective-permute-start(bf16[16,64,128]{2,1,0:T(8,128)(2,1)} %bitcast.11), channel_id=1, source_target_pairs={{0,12},{1,9},{2,14},{3,11},{4,8},{5,13},{6,10},{7,15},{8,4},{9,1},... | collective-permute-start | bytes 786440 | tf_op jit(solution)/shard_map/ppermute | solution.py:51
  5.0 3.1 %precond.2 = (bf16[16,8192]{1,0:T(8,128)(2,1)S(1)}, f32[2,64,128]{2,1,0:T(8,128)S(1)}, bf16[2,96,128]{2,1,0:T(8,128)(2,1)S(1)}, bf16[2,64,192]{2,1,0:T(8,128)(2,...) custom-call(bf16[16,64,128]{2,1,0:T(8,128)(2,1)} %bitcast.12, f32[2,64,64]{2,1,0:T(8,128)} %refs_1_.1, ...), custom_call_target="tpu_custom_call" | custom-call | flops 1000000000 | bytes 4194304 | tf_op jit(solution)/shard_map/precond/pallas_call | solution.py:222
  8.1 1.6 %collective-permute-start.2 = (bf16[16,8192]{1,0:T(8,128)(2,1)S(1)}, bf16[16,8192]{1,0:T(8,128)(2,1)S(1)}, u32[]{:S(2)}, u32[]{:S(2)}) collective-permute-start(bf16[16,8192]{1,0:T(8,128)(2,1)S(1)} %get-tuple-element.29.refs_0_), channel_id=1, source_target_pairs={{0,2},{1,3},{2,0},{3,1},{4,6},{5,7},{6,4},{7,5},{8,10},{9,11},{10,... | collective-permute-start | bytes 786440 | tf_op jit(solution)/shard_map/ppermute | solution.py:51
  9.7 0.0 collective-permute-start.1
  9.7 5.1 %split.1.slabs_ref = bf16[64,512,128]{2,1,0:T(8,128)(2,1)S(1)} custom-call(bf16[512,64,128]{2,1,0:T(8,128)(2,1)} %bitcast.10), custom_call_target="tpu_custom_call" | custom-call | flops 1000000000 | bytes 16777216 | tf_op jit(solution)/shard_map/split/pallas_call | solution.py:295
  14.8 0.1 collective-permute-start.3
  14.8 0.0 collective-permute-done.q_ref
  14.8 1.9 %precond.3.refs_4_ = bf16[16,8192]{1,0:T(8,128)(2,1)S(1)} custom-call(bf16[16,64,128]{2,1,0:T(8,128)(2,1)S(1)} %collective-permute-done.q_ref, f32[2,64,128]{2,1,0:T(8,128)S(1)} %get-tuple-element.31.refs_0_, bf16[2,96,128]{2,1,0:T(8,128)(2,1)S(1)} %get-tuple-element.32.refs_1_, bf16[2,64,192]{2,1,0:T(8,128)(2,1)S(1)} %get-tuple-element.33.refs_2_, ...), custom_call_target="tpu_custom_call" | custom-call | flops 1000000000 | bytes 4194304 | tf_op jit(solution)/shard_map/precond/pallas_call | solution.py:243
  16.7 0.6 %collective-permute-start.5 = (bf16[16,8192]{1,0:T(8,128)(2,1)S(1)}, bf16[16,8192]{1,0:T(8,128)(2,1)S(1)}, u32[]{:S(2)}, u32[]{:S(2)}) collective-permute-start(bf16[16,8192]{1,0:T(8,128)(2,1)S(1)} %precond.3.refs_4_), channel_id=1, source_target_pairs={{0,2},{1,3},{2,0},{3,1},{4,6},{5,7},{6,4},{7,5},{8,10},{9,11},{10,... | collective-permute-start | bytes 786440 | tf_op jit(solution)/shard_map/ppermute | solution.py:51
  17.3 4.0 %collective-permute-start.7 = (bf16[16,8192]{1,0:T(8,128)(2,1)S(1)}, bf16[16,8192]{1,0:T(8,128)(2,1)S(1)}, u32[]{:S(2)}, u32[]{:S(2)}) collective-permute-start(bf16[16,8192]{1,0:T(8,128)(2,1)S(1)} %precond.3.refs_4_), channel_id=1, source_target_pairs={{0,16},{1,17},{2,18},{3,19},{4,20},{5,21},{6,22},{7,23},{8,24},{9,... | collective-permute-start | bytes 786440 | tf_op jit(solution)/shard_map/ppermute | solution.py:51
  21.3 0.0 collective-permute-done.2.refs_2_
  21.3 0.0 collective-permute-start.4
  21.4 4.1 %collective-permute-done.5.refs_7_ = bf16[16,8192]{1,0:T(8,128)(2,1)S(1)} collective-permute-done((bf16[16,8192]{1,0:T(8,128)(2,1)S(1)}, bf16[16,8192]{1,0:T(8,128)(2,1)S(1)}, u32[]{:S(2)}, u32[]{:S(2)}) %collective-permute-start.5) | collective-permute-done | bytes 262176 | tf_op jit(solution)/shard_map/ppermute | solution.py:51
  25.5 1.9 %collective-permute-start.9 = (bf16[16,5120]{1,0:T(8,128)(2,1)S(1)}, bf16[16,5120]{1,0:T(8,128)(2,1)S(1)}, u32[]{:S(2)}, u32[]{:S(2)}) collective-permute-start(bf16[16,5120]{1,0:T(8,128)(2,1)S(1)} %slice.6), channel_id=1, source_target_pairs={{0,16},{1,17},{2,18},{3,19},{4,20},{5,21},{6,22},{7,23},{8,24},{9,... | collective-permute-start | bytes 491528 | tf_op jit(solution)/shard_map/ppermute | solution.py:51
  27.4 0.0 collective-permute-done.7.refs_8_
  27.4 0.6 %collective-permute-start.11 = (bf16[16,3072]{1,0:T(8,128)(2,1)S(1)}, bf16[16,3072]{1,0:T(8,128)(2,1)S(1)}, u32[]{:S(2)}, u32[]{:S(2)}) collective-permute-start(bf16[16,3072]{1,0:T(8,128)(2,1)S(1)} %slice.8), channel_id=1, source_target_pairs={{0,2},{1,3},{2,0},{3,1},{4,6},{5,7},{6,4},{7,5},{8,10},{9,11},{10,... | collective-permute-start | bytes 294920 | tf_op jit(solution)/shard_map/ppermute | solution.py:51
  28.1 0.0 collective-permute-done.3.refs_3_
  28.1 0.1 collective-permute-start.8
  28.1 1.0 %collective-permute-done.4.refs_5_ = bf16[16,8192]{1,0:T(8,128)(2,1)S(1)} collective-permute-done((bf16[16,8192]{1,0:T(8,128)(2,1)S(1)}, bf16[16,8192]{1,0:T(8,128)(2,1)S(1)}, u32[]{:S(2)}, u32[]{:S(2)}) %collective-permute-start.4) | collective-permute-done | bytes 262176 | tf_op jit(solution)/shard_map/ppermute | solution.py:51
  29.2 0.0 collective-permute-start.6
  29.2 2.3 %collective-permute-done.9 = bf16[16,5120]{1,0:T(8,128)(2,1)S(1)} collective-permute-done((bf16[16,5120]{1,0:T(8,128)(2,1)S(1)}, bf16[16,5120]{1,0:T(8,128)(2,1)S(1)}, u32[]{:S(2)}, u32[]{:S(2)}) %collective-permute-start.9) | collective-permute-done | bytes 163872 | tf_op jit(solution)/shard_map/ppermute | solution.py:51
  31.5 0.1 collective-permute-start.10
  31.6 0.5 %collective-permute-done.11 = bf16[16,3072]{1,0:T(8,128)(2,1)S(1)} collective-permute-done((bf16[16,3072]{1,0:T(8,128)(2,1)S(1)}, bf16[16,3072]{1,0:T(8,128)(2,1)S(1)}, u32[]{:S(2)}, u32[]{:S(2)}) %collective-permute-start.11) | collective-permute-done | bytes 98336 | tf_op jit(solution)/shard_map/ppermute | solution.py:51
  32.1 0.1 collective-permute-start.12
  32.2 0.0 collective-permute-done.1.refs_1_
  32.2 1.7 %collective-permute-done.12.refs_12_ = bf16[16,8192]{1,0:T(8,128)(2,1)S(1)} collective-permute-done((bf16[16,8192]{1,0:T(8,128)(2,1)S(1)}, bf16[16,8192]{1,0:T(8,128)(2,1)S(1)}, u32[]{:S(2)}, u32[]{:S(2)}) %collective-permute-start.12) | collective-permute-done | bytes 262176 | tf_op jit(solution)/shard_map/ppermute | solution.py:51
  33.8 0.0 collective-permute-done.8.refs_9_
  33.8 0.0 collective-permute-done.6.refs_6_
  33.8 0.0 collective-permute-done.10.refs_10_
  33.9 3.8 %scores.1 = f32[512,256]{1,0:T(8,128)} custom-call(bf16[64,512,128]{2,1,0:T(8,128)(2,1)S(1)} %split.1.slabs_ref, bf16[16,8192]{1,0:T(8,128)(2,1)S(1)} %get-tuple-element.29.refs_0_, bf16[16,8192]{1,0:T(8,128)(2,1)S(1)} %collective-permute-done.1.refs_1_, bf16[16,8192]{1,0:T(8,128)(2,1)S(1)} %collective-permute-done.2.refs_2_, ...), custom_call_target="tpu_custom_call" | custom-call | flops 2147483648 | bytes 12582912 | tf_op jit(solution)/shard_map/scores/pallas_call | solution.py:387
  (7 shorter events, 0.1 us)
Async XLA Ops:
  0.0 14.8 %collective-permute-start = (bf16[16,64,128]{2,1,0:T(8,128)(2,1)}, bf16[16,64,128]{2,1,0:T(8,128)(2,1)S(1)}, u32[]{:S(2)}, u32[]{:S(2)}) collective-permute-start(bf16[16,64,128]{2,1,0:T(8,128)(2,1)} %bitcast.11), channel_id=1, source_target_pairs={{0,12},{1,9},{2,14},{3,11},{4,8},{5,13},{6,10},{7,15},{8,4},{9,1},... | collective-permute-start | bytes 786440 | tf_op jit(solution)/shard_map/ppermute | solution.py:51
  8.1 13.2 %collective-permute-start.2 = (bf16[16,8192]{1,0:T(8,128)(2,1)S(1)}, bf16[16,8192]{1,0:T(8,128)(2,1)S(1)}, u32[]{:S(2)}, u32[]{:S(2)}) collective-permute-start(bf16[16,8192]{1,0:T(8,128)(2,1)S(1)} %get-tuple-element.29.refs_0_), channel_id=1, source_target_pairs={{0,2},{1,3},{2,0},{3,1},{4,6},{5,7},{6,4},{7,5},{8,10},{9,11},{10,... | collective-permute-start | bytes 786440 | tf_op jit(solution)/shard_map/ppermute | solution.py:51
  9.7 22.5 %collective-permute-start.1 = (bf16[16,8192]{1,0:T(8,128)(2,1)S(1)}, bf16[16,8192]{1,0:T(8,128)(2,1)S(1)}, u32[]{:S(2)}, u32[]{:S(2)}) collective-permute-start(bf16[16,8192]{1,0:T(8,128)(2,1)S(1)} %get-tuple-element.29.refs_0_), channel_id=1, source_target_pairs={{0,1},{1,0},{2,3},{3,2},{4,5},{5,4},{6,7},{7,6},{8,9},{9,8},{10,11... | collective-permute-start | bytes 786440 | tf_op jit(solution)/shard_map/ppermute | solution.py:51
  14.8 13.3 %collective-permute-start.3 = (bf16[16,8192]{1,0:T(8,128)(2,1)S(1)}, bf16[16,8192]{1,0:T(8,128)(2,1)S(1)}, u32[]{:S(2)}, u32[]{:S(2)}) collective-permute-start(bf16[16,8192]{1,0:T(8,128)(2,1)S(1)} %get-tuple-element.29.refs_0_), channel_id=1, source_target_pairs={{0,4},{1,5},{2,6},{3,7},{4,0},{5,1},{6,2},{7,3},{8,12},{9,13},{10,... | collective-permute-start | bytes 786440 | tf_op jit(solution)/shard_map/ppermute | solution.py:51
  16.7 8.8 %collective-permute-start.5 = (bf16[16,8192]{1,0:T(8,128)(2,1)S(1)}, bf16[16,8192]{1,0:T(8,128)(2,1)S(1)}, u32[]{:S(2)}, u32[]{:S(2)}) collective-permute-start(bf16[16,8192]{1,0:T(8,128)(2,1)S(1)} %precond.3.refs_4_), channel_id=1, source_target_pairs={{0,2},{1,3},{2,0},{3,1},{4,6},{5,7},{6,4},{7,5},{8,10},{9,11},{10,... | collective-permute-start | bytes 786440 | tf_op jit(solution)/shard_map/ppermute | solution.py:51
  17.3 10.1 %collective-permute-start.7 = (bf16[16,8192]{1,0:T(8,128)(2,1)S(1)}, bf16[16,8192]{1,0:T(8,128)(2,1)S(1)}, u32[]{:S(2)}, u32[]{:S(2)}) collective-permute-start(bf16[16,8192]{1,0:T(8,128)(2,1)S(1)} %precond.3.refs_4_), channel_id=1, source_target_pairs={{0,16},{1,17},{2,18},{3,19},{4,20},{5,21},{6,22},{7,23},{8,24},{9,... | collective-permute-start | bytes 786440 | tf_op jit(solution)/shard_map/ppermute | solution.py:51
  21.3 7.8 %collective-permute-start.4 = (bf16[16,8192]{1,0:T(8,128)(2,1)S(1)}, bf16[16,8192]{1,0:T(8,128)(2,1)S(1)}, u32[]{:S(2)}, u32[]{:S(2)}) collective-permute-start(bf16[16,8192]{1,0:T(8,128)(2,1)S(1)} %collective-permute-done.2.refs_2_), channel_id=1, source_target_pairs={{0,4},{1,5},{2,6},{3,7},{4,0},{5,1},{6,2},{7,3},{8,12},{9,13},{10,... | collective-permute-start | bytes 786440 | tf_op jit(solution)/shard_map/ppermute | solution.py:51
  25.5 5.9 %collective-permute-start.9 = (bf16[16,5120]{1,0:T(8,128)(2,1)S(1)}, bf16[16,5120]{1,0:T(8,128)(2,1)S(1)}, u32[]{:S(2)}, u32[]{:S(2)}) collective-permute-start(bf16[16,5120]{1,0:T(8,128)(2,1)S(1)} %slice.6), channel_id=1, source_target_pairs={{0,16},{1,17},{2,18},{3,19},{4,20},{5,21},{6,22},{7,23},{8,24},{9,... | collective-permute-start | bytes 491528 | tf_op jit(solution)/shard_map/ppermute | solution.py:51
  27.4 4.7 %collective-permute-start.11 = (bf16[16,3072]{1,0:T(8,128)(2,1)S(1)}, bf16[16,3072]{1,0:T(8,128)(2,1)S(1)}, u32[]{:S(2)}, u32[]{:S(2)}) collective-permute-start(bf16[16,3072]{1,0:T(8,128)(2,1)S(1)} %slice.8), channel_id=1, source_target_pairs={{0,2},{1,3},{2,0},{3,1},{4,6},{5,7},{6,4},{7,5},{8,10},{9,11},{10,... | collective-permute-start | bytes 294920 | tf_op jit(solution)/shard_map/ppermute | solution.py:51
  28.1 5.8 %collective-permute-start.8 = (bf16[32,8192]{1,0:T(8,128)(2,1)S(1)}, bf16[32,8192]{1,0:T(8,128)(2,1)S(1)}, u32[]{:S(2)}, u32[]{:S(2)}) collective-permute-start(bf16[32,8192]{1,0:T(8,128)(2,1)S(1)} %pad_maximum_fusion.1), channel_id=1, source_target_pairs={{0,1},{1,0},{2,3},{3,2},{4,5},{5,4},{6,7},{7,6},{8,9},{9,8},{10,11... | collective-permute-start | bytes 1572872 | tf_op jit(solution)/shard_map/ppermute | solution.py:51
  29.2 4.7 %collective-permute-start.6 = (bf16[32,8192]{1,0:T(8,128)(2,1)S(1)}, bf16[32,8192]{1,0:T(8,128)(2,1)S(1)}, u32[]{:S(2)}, u32[]{:S(2)}) collective-permute-start(bf16[32,8192]{1,0:T(8,128)(2,1)S(1)} %pad_maximum_fusion), channel_id=1, source_target_pairs={{0,1},{1,0},{2,3},{3,2},{4,5},{5,4},{6,7},{7,6},{8,9},{9,8},{10,11... | collective-permute-start | bytes 1572872 | tf_op jit(solution)/shard_map/ppermute | solution.py:51
  31.5 2.4 %collective-permute-start.10 = (bf16[32,8192]{1,0:T(8,128)(2,1)S(1)}, bf16[32,8192]{1,0:T(8,128)(2,1)S(1)}, u32[]{:S(2)}, u32[]{:S(2)}) collective-permute-start(bf16[32,8192]{1,0:T(8,128)(2,1)S(1)} %pad_maximum_fusion.2), channel_id=1, source_target_pairs={{0,1},{1,0},{2,3},{3,2},{4,5},{5,4},{6,7},{7,6},{8,9},{9,8},{10,11... | collective-permute-start | bytes 1572872 | tf_op jit(solution)/shard_map/ppermute | solution.py:51
  32.1 1.7 %collective-permute-start.12 = (bf16[16,8192]{1,0:T(8,128)(2,1)S(1)}, bf16[16,8192]{1,0:T(8,128)(2,1)S(1)}, u32[]{:S(2)}, u32[]{:S(2)}) collective-permute-start(bf16[16,8192]{1,0:T(8,128)(2,1)S(1)} %constant_dynamic-update-slice_fusion.refs_11_), channel_id=1, source_target_pairs={{0,1},{1,0},{2,3},{3,2},{4,5},{5,4},{6,7},{7,6},{8,9},{9,8},{10,11... | collective-permute-start | bytes 786440 | tf_op jit(solution)/shard_map/ppermute | solution.py:51

commit v15 on v14

--- a/solution.py
+++ b/solution.py
@@ -313,7 +313,7 @@
     slabs = slabs_ref.shape[0]
     q_rows = out_ref.shape[1] // len(masks)
     n_query = out_ref.shape[1]
-    step = min(slabs, 8)
+    step = min(slabs, 32)
     total = None
     for at in range(0, slabs, step):
         train = jnp.concatenate([slabs_ref[at + i] for i in range(step)], axis=1)

time: 37.8 us -> 37.8 us (level)
  no operation moved by 1% of the time
where the time goes in v15:
time: 37.8 us; the launch traced here: 37.6 us
  starting transfers between devices  14 us (37%)
  Pallas kernels  13.8 us (37%)
  waiting for transfers between devices  9.61 us (25%)
    ppermute x13, starting transfers between devices, hop(): return Blocks(lax.ppermute(self.array, ('group', 'train'), perm), came)  14 us
    ppermute x13, waiting for transfers between devices, hop(): return Blocks(lax.ppermute(self.array, ('group', 'train'), perm), came)  9.61 us
    pallas_call x1, Pallas kernels, split_layers(): pl.pallas_call(functools.partial(split_kernel, layers), out_shape=jax.Sha...  5.06 us
    pallas_call x1, Pallas kernels, per_device(): pl.pallas_call(functools.partial(score_kernel, [came_masks(came) for a in...  3.77 us
    pallas_call x1, Pallas kernels, precondition(): pl.pallas_call(functools.partial(fetched, len(operands), precond_kernel),...  3.07 us
    pallas_call x1, Pallas kernels, precondition_more(): pl.pallas_call(later_kernel, out_shape=jax.ShapeDtypeStruct((q_rows, line...  1.89 us
  transfers between devices with their start and end apart: 13, of which 5 were waited for; matrix products, arithmetic and copies ran while one was open for 0% of the time, Pallas kernels for 27%

profile of v15, /device:TPU:0, one launch (start us, length us, event | category | flops | bytes accessed | tf_op | source)
XLA Modules:
  0.0 37.6 jit_solution(10709841546657294629)
XLA Ops:
  0.0 5.0 %collective-permute-start = (bf16[16,64,128]{2,1,0:T(8,128)(2,1)}, bf16[16,64,128]{2,1,0:T(8,128)(2,1)S(1)}, u32[]{:S(2)}, u32[]{:S(2)}) collective-permute-start(bf16[16,64,128]{2,1,0:T(8,128)(2,1)} %bitcast.11), channel_id=1, source_target_pairs={{0,12},{1,9},{2,14},{3,11},{4,8},{5,13},{6,10},{7,15},{8,4},{9,1},... | collective-permute-start | bytes 786440 | tf_op jit(solution)/shard_map/ppermute | solution.py:51
  5.0 3.1 %precond.2 = (bf16[16,8192]{1,0:T(8,128)(2,1)S(1)}, f32[2,64,128]{2,1,0:T(8,128)S(1)}, bf16[2,96,128]{2,1,0:T(8,128)(2,1)S(1)}, bf16[2,64,192]{2,1,0:T(8,128)(2,...) custom-call(bf16[16,64,128]{2,1,0:T(8,128)(2,1)} %bitcast.12, f32[2,64,64]{2,1,0:T(8,128)} %refs_1_.1, ...), custom_call_target="tpu_custom_call" | custom-call | flops 1000000000 | bytes 4194304 | tf_op jit(solution)/shard_map/precond/pallas_call | solution.py:222
  8.1 1.6 %collective-permute-start.2 = (bf16[16,8192]{1,0:T(8,128)(2,1)S(1)}, bf16[16,8192]{1,0:T(8,128)(2,1)S(1)}, u32[]{:S(2)}, u32[]{:S(2)}) collective-permute-start(bf16[16,8192]{1,0:T(8,128)(2,1)S(1)} %get-tuple-element.29.refs_0_), channel_id=1, source_target_pairs={{0,2},{1,3},{2,0},{3,1},{4,6},{5,7},{6,4},{7,5},{8,10},{9,11},{10,... | collective-permute-start | bytes 786440 | tf_op jit(solution)/shard_map/ppermute | solution.py:51
  9.7 0.0 collective-permute-start.1
  9.7 5.1 %split.1.slabs_ref = bf16[64,512,128]{2,1,0:T(8,128)(2,1)S(1)} custom-call(bf16[512,64,128]{2,1,0:T(8,128)(2,1)} %bitcast.10), custom_call_target="tpu_custom_call" | custom-call | flops 1000000000 | bytes 16777216 | tf_op jit(solution)/shard_map/split/pallas_call | solution.py:295
  14.8 0.1 collective-permute-start.3
  14.8 0.0 collective-permute-done.q_ref
  14.8 1.9 %precond.3.refs_4_ = bf16[16,8192]{1,0:T(8,128)(2,1)S(1)} custom-call(bf16[16,64,128]{2,1,0:T(8,128)(2,1)S(1)} %collective-permute-done.q_ref, f32[2,64,128]{2,1,0:T(8,128)S(1)} %get-tuple-element.31.refs_0_, bf16[2,96,128]{2,1,0:T(8,128)(2,1)S(1)} %get-tuple-element.32.refs_1_, bf16[2,64,192]{2,1,0:T(8,128)(2,1)S(1)} %get-tuple-element.33.refs_2_, ...), custom_call_target="tpu_custom_call" | custom-call | flops 1000000000 | bytes 4194304 | tf_op jit(solution)/shard_map/precond/pallas_call | solution.py:243
  16.7 0.6 %collective-permute-start.5 = (bf16[16,8192]{1,0:T(8,128)(2,1)S(1)}, bf16[16,8192]{1,0:T(8,128)(2,1)S(1)}, u32[]{:S(2)}, u32[]{:S(2)}) collective-permute-start(bf16[16,8192]{1,0:T(8,128)(2,1)S(1)} %precond.3.refs_4_), channel_id=1, source_target_pairs={{0,2},{1,3},{2,0},{3,1},{4,6},{5,7},{6,4},{7,5},{8,10},{9,11},{10,... | collective-permute-start | bytes 786440 | tf_op jit(solution)/shard_map/ppermute | solution.py:51
  17.3 4.0 %collective-permute-start.7 = (bf16[16,8192]{1,0:T(8,128)(2,1)S(1)}, bf16[16,8192]{1,0:T(8,128)(2,1)S(1)}, u32[]{:S(2)}, u32[]{:S(2)}) collective-permute-start(bf16[16,8192]{1,0:T(8,128)(2,1)S(1)} %precond.3.refs_4_), channel_id=1, source_target_pairs={{0,16},{1,17},{2,18},{3,19},{4,20},{5,21},{6,22},{7,23},{8,24},{9,... | collective-permute-start | bytes 786440 | tf_op jit(solution)/shard_map/ppermute | solution.py:51
  21.3 0.0 collective-permute-done.2.refs_2_
  21.3 0.0 collective-permute-start.4
  21.4 4.1 %collective-permute-done.5.refs_7_ = bf16[16,8192]{1,0:T(8,128)(2,1)S(1)} collective-permute-done((bf16[16,8192]{1,0:T(8,128)(2,1)S(1)}, bf16[16,8192]{1,0:T(8,128)(2,1)S(1)}, u32[]{:S(2)}, u32[]{:S(2)}) %collective-permute-start.5) | collective-permute-done | bytes 262176 | tf_op jit(solution)/shard_map/ppermute | solution.py:51
  25.5 1.9 %collective-permute-start.9 = (bf16[16,5120]{1,0:T(8,128)(2,1)S(1)}, bf16[16,5120]{1,0:T(8,128)(2,1)S(1)}, u32[]{:S(2)}, u32[]{:S(2)}) collective-permute-start(bf16[16,5120]{1,0:T(8,128)(2,1)S(1)} %slice.6), channel_id=1, source_target_pairs={{0,16},{1,17},{2,18},{3,19},{4,20},{5,21},{6,22},{7,23},{8,24},{9,... | collective-permute-start | bytes 491528 | tf_op jit(solution)/shard_map/ppermute | solution.py:51
  27.4 0.0 collective-permute-done.7.refs_8_
  27.4 0.6 %collective-permute-start.11 = (bf16[16,3072]{1,0:T(8,128)(2,1)S(1)}, bf16[16,3072]{1,0:T(8,128)(2,1)S(1)}, u32[]{:S(2)}, u32[]{:S(2)}) collective-permute-start(bf16[16,3072]{1,0:T(8,128)(2,1)S(1)} %slice.8), channel_id=1, source_target_pairs={{0,2},{1,3},{2,0},{3,1},{4,6},{5,7},{6,4},{7,5},{8,10},{9,11},{10,... | collective-permute-start | bytes 294920 | tf_op jit(solution)/shard_map/ppermute | solution.py:51
  28.1 0.0 collective-permute-done.3.refs_3_
  28.1 0.1 collective-permute-start.8
  28.1 1.0 %collective-permute-done.4.refs_5_ = bf16[16,8192]{1,0:T(8,128)(2,1)S(1)} collective-permute-done((bf16[16,8192]{1,0:T(8,128)(2,1)S(1)}, bf16[16,8192]{1,0:T(8,128)(2,1)S(1)}, u32[]{:S(2)}, u32[]{:S(2)}) %collective-permute-start.4) | collective-permute-done | bytes 262176 | tf_op jit(solution)/shard_map/ppermute | solution.py:51
  29.2 0.0 collective-permute-start.6
  29.2 2.3 %collective-permute-done.9 = bf16[16,5120]{1,0:T(8,128)(2,1)S(1)} collective-permute-done((bf16[16,5120]{1,0:T(8,128)(2,1)S(1)}, bf16[16,5120]{1,0:T(8,128)(2,1)S(1)}, u32[]{:S(2)}, u32[]{:S(2)}) %collective-permute-start.9) | collective-permute-done | bytes 163872 | tf_op jit(solution)/shard_map/ppermute | solution.py:51
  31.5 0.1 collective-permute-start.10
  31.6 0.5 %collective-permute-done.11 = bf16[16,3072]{1,0:T(8,128)(2,1)S(1)} collective-permute-done((bf16[16,3072]{1,0:T(8,128)(2,1)S(1)}, bf16[16,3072]{1,0:T(8,128)(2,1)S(1)}, u32[]{:S(2)}, u32[]{:S(2)}) %collective-permute-start.11) | collective-permute-done | bytes 98336 | tf_op jit(solution)/shard_map/ppermute | solution.py:51
  32.1 0.1 collective-permute-start.12
  32.2 0.0 collective-permute-done.1.refs_1_
  32.2 1.7 %collective-permute-done.12.refs_12_ = bf16[16,8192]{1,0:T(8,128)(2,1)S(1)} collective-permute-done((bf16[16,8192]{1,0:T(8,128)(2,1)S(1)}, bf16[16,8192]{1,0:T(8,128)(2,1)S(1)}, u32[]{:S(2)}, u32[]{:S(2)}) %collective-permute-start.12) | collective-permute-done | bytes 262176 | tf_op jit(solution)/shard_map/ppermute | solution.py:51
  33.8 0.0 collective-permute-done.8.refs_9_
  33.8 0.0 collective-permute-done.6.refs_6_
  33.8 0.0 collective-permute-done.10.refs_10_
  33.9 3.8 %scores.1 = f32[512,256]{1,0:T(8,128)} custom-call(bf16[64,512,128]{2,1,0:T(8,128)(2,1)S(1)} %split.1.slabs_ref, bf16[16,8192]{1,0:T(8,128)(2,1)S(1)} %get-tuple-element.29.refs_0_, bf16[16,8192]{1,0:T(8,128)(2,1)S(1)} %collective-permute-done.1.refs_1_, bf16[16,8192]{1,0:T(8,128)(2,1)S(1)} %collective-permute-done.2.refs_2_, ...), custom_call_target="tpu_custom_call" | custom-call | flops 2147483648 | bytes 12582912 | tf_op jit(solution)/shard_map/scores/pallas_call | solution.py:387
  (7 shorter events, 0.1 us)
Async XLA Ops:
  0.0 14.8 %collective-permute-start = (bf16[16,64,128]{2,1,0:T(8,128)(2,1)}, bf16[16,64,128]{2,1,0:T(8,128)(2,1)S(1)}, u32[]{:S(2)}, u32[]{:S(2)}) collective-permute-start(bf16[16,64,128]{2,1,0:T(8,128)(2,1)} %bitcast.11), channel_id=1, source_target_pairs={{0,12},{1,9},{2,14},{3,11},{4,8},{5,13},{6,10},{7,15},{8,4},{9,1},... | collective-permute-start | bytes 786440 | tf_op jit(solution)/shard_map/ppermute | solution.py:51
  8.1 13.2 %collective-permute-start.2 = (bf16[16,8192]{1,0:T(8,128)(2,1)S(1)}, bf16[16,8192]{1,0:T(8,128)(2,1)S(1)}, u32[]{:S(2)}, u32[]{:S(2)}) collective-permute-start(bf16[16,8192]{1,0:T(8,128)(2,1)S(1)} %get-tuple-element.29.refs_0_), channel_id=1, source_target_pairs={{0,2},{1,3},{2,0},{3,1},{4,6},{5,7},{6,4},{7,5},{8,10},{9,11},{10,... | collective-permute-start | bytes 786440 | tf_op jit(solution)/shard_map/ppermute | solution.py:51
  9.7 22.5 %collective-permute-start.1 = (bf16[16,8192]{1,0:T(8,128)(2,1)S(1)}, bf16[16,8192]{1,0:T(8,128)(2,1)S(1)}, u32[]{:S(2)}, u32[]{:S(2)}) collective-permute-start(bf16[16,8192]{1,0:T(8,128)(2,1)S(1)} %get-tuple-element.29.refs_0_), channel_id=1, source_target_pairs={{0,1},{1,0},{2,3},{3,2},{4,5},{5,4},{6,7},{7,6},{8,9},{9,8},{10,11... | collective-permute-start | bytes 786440 | tf_op jit(solution)/shard_map/ppermute | solution.py:51
  14.8 13.3 %collective-permute-start.3 = (bf16[16,8192]{1,0:T(8,128)(2,1)S(1)}, bf16[16,8192]{1,0:T(8,128)(2,1)S(1)}, u32[]{:S(2)}, u32[]{:S(2)}) collective-permute-start(bf16[16,8192]{1,0:T(8,128)(2,1)S(1)} %get-tuple-element.29.refs_0_), channel_id=1, source_target_pairs={{0,4},{1,5},{2,6},{3,7},{4,0},{5,1},{6,2},{7,3},{8,12},{9,13},{10,... | collective-permute-start | bytes 786440 | tf_op jit(solution)/shard_map/ppermute | solution.py:51
  16.7 8.8 %collective-permute-start.5 = (bf16[16,8192]{1,0:T(8,128)(2,1)S(1)}, bf16[16,8192]{1,0:T(8,128)(2,1)S(1)}, u32[]{:S(2)}, u32[]{:S(2)}) collective-permute-start(bf16[16,8192]{1,0:T(8,128)(2,1)S(1)} %precond.3.refs_4_), channel_id=1, source_target_pairs={{0,2},{1,3},{2,0},{3,1},{4,6},{5,7},{6,4},{7,5},{8,10},{9,11},{10,... | collective-permute-start | bytes 786440 | tf_op jit(solution)/shard_map/ppermute | solution.py:51
  17.3 10.1 %collective-permute-start.7 = (bf16[16,8192]{1,0:T(8,128)(2,1)S(1)}, bf16[16,8192]{1,0:T(8,128)(2,1)S(1)}, u32[]{:S(2)}, u32[]{:S(2)}) collective-permute-start(bf16[16,8192]{1,0:T(8,128)(2,1)S(1)} %precond.3.refs_4_), channel_id=1, source_target_pairs={{0,16},{1,17},{2,18},{3,19},{4,20},{5,21},{6,22},{7,23},{8,24},{9,... | collective-permute-start | bytes 786440 | tf_op jit(solution)/shard_map/ppermute | solution.py:51
  21.3 7.8 %collective-permute-start.4 = (bf16[16,8192]{1,0:T(8,128)(2,1)S(1)}, bf16[16,8192]{1,0:T(8,128)(2,1)S(1)}, u32[]{:S(2)}, u32[]{:S(2)}) collective-permute-start(bf16[16,8192]{1,0:T(8,128)(2,1)S(1)} %collective-permute-done.2.refs_2_), channel_id=1, source_target_pairs={{0,4},{1,5},{2,6},{3,7},{4,0},{5,1},{6,2},{7,3},{8,12},{9,13},{10,... | collective-permute-start | bytes 786440 | tf_op jit(solution)/shard_map/ppermute | solution.py:51
  25.5 5.9 %collective-permute-start.9 = (bf16[16,5120]{1,0:T(8,128)(2,1)S(1)}, bf16[16,5120]{1,0:T(8,128)(2,1)S(1)}, u32[]{:S(2)}, u32[]{:S(2)}) collective-permute-start(bf16[16,5120]{1,0:T(8,128)(2,1)S(1)} %slice.6), channel_id=1, source_target_pairs={{0,16},{1,17},{2,18},{3,19},{4,20},{5,21},{6,22},{7,23},{8,24},{9,... | collective-permute-start | bytes 491528 | tf_op jit(solution)/shard_map/ppermute | solution.py:51
  27.4 4.7 %collective-permute-start.11 = (bf16[16,3072]{1,0:T(8,128)(2,1)S(1)}, bf16[16,3072]{1,0:T(8,128)(2,1)S(1)}, u32[]{:S(2)}, u32[]{:S(2)}) collective-permute-start(bf16[16,3072]{1,0:T(8,128)(2,1)S(1)} %slice.8), channel_id=1, source_target_pairs={{0,2},{1,3},{2,0},{3,1},{4,6},{5,7},{6,4},{7,5},{8,10},{9,11},{10,... | collective-permute-start | bytes 294920 | tf_op jit(solution)/shard_map/ppermute | solution.py:51
  28.1 5.8 %collective-permute-start.8 = (bf16[32,8192]{1,0:T(8,128)(2,1)S(1)}, bf16[32,8192]{1,0:T(8,128)(2,1)S(1)}, u32[]{:S(2)}, u32[]{:S(2)}) collective-permute-start(bf16[32,8192]{1,0:T(8,128)(2,1)S(1)} %pad_maximum_fusion.1), channel_id=1, source_target_pairs={{0,1},{1,0},{2,3},{3,2},{4,5},{5,4},{6,7},{7,6},{8,9},{9,8},{10,11... | collective-permute-start | bytes 1572872 | tf_op jit(solution)/shard_map/ppermute | solution.py:51
  29.2 4.7 %collective-permute-start.6 = (bf16[32,8192]{1,0:T(8,128)(2,1)S(1)}, bf16[32,8192]{1,0:T(8,128)(2,1)S(1)}, u32[]{:S(2)}, u32[]{:S(2)}) collective-permute-start(bf16[32,8192]{1,0:T(8,128)(2,1)S(1)} %pad_maximum_fusion), channel_id=1, source_target_pairs={{0,1},{1,0},{2,3},{3,2},{4,5},{5,4},{6,7},{7,6},{8,9},{9,8},{10,11... | collective-permute-start | bytes 1572872 | tf_op jit(solution)/shard_map/ppermute | solution.py:51
  31.5 2.4 %collective-permute-start.10 = (bf16[32,8192]{1,0:T(8,128)(2,1)S(1)}, bf16[32,8192]{1,0:T(8,128)(2,1)S(1)}, u32[]{:S(2)}, u32[]{:S(2)}) collective-permute-start(bf16[32,8192]{1,0:T(8,128)(2,1)S(1)} %pad_maximum_fusion.2), channel_id=1, source_target_pairs={{0,1},{1,0},{2,3},{3,2},{4,5},{5,4},{6,7},{7,6},{8,9},{9,8},{10,11... | collective-permute-start | bytes 1572872 | tf_op jit(solution)/shard_map/ppermute | solution.py:51
  32.1 1.7 %collective-permute-start.12 = (bf16[16,8192]{1,0:T(8,128)(2,1)S(1)}, bf16[16,8192]{1,0:T(8,128)(2,1)S(1)}, u32[]{:S(2)}, u32[]{:S(2)}) collective-permute-start(bf16[16,8192]{1,0:T(8,128)(2,1)S(1)} %constant_dynamic-update-slice_fusion.refs_11_), channel_id=1, source_target_pairs={{0,1},{1,0},{2,3},{3,2},{4,5},{5,4},{6,7},{7,6},{8,9},{9,8},{10,11... | collective-permute-start | bytes 786440 | tf_op jit(solution)/shard_map/ppermute | solution.py:51
